TPU v7x, 256 devices: a whole 4x4x8 slice. The times are simulated.
256 devices in a mesh: dp: 32 (over y, x, core), rep: 8 (over z).
Axes of the slice: x: 4, y: 4, z: 8, core: 2. Of those that a mesh axis runs over, the one named last changes fastest.
Arguments:
- queries: bfloat16 [4096, 6144], P(('rep', 'dp')), parts along dimension 0, may hold values from -240 to 240
- cache_keys: bfloat16 [262144, 512], P(('rep', 'dp')), parts along dimension 0, may hold values from -6 to 6
- cache_values: bfloat16 [262144, 512], P(('rep', 'dp')), parts along dimension 0, may hold values from -6 to 6
- lengths: int32 [4096], P(('rep', 'dp')), parts along dimension 0, may hold values from 1 to 512, as said below
- counts: int32 [256], P(('rep', 'dp')), parts along dimension 0, may hold values from 1 to 16, 320 in all
- norm_gain: float32 [6144], replicated, may hold values from 0.1 to 1.9
- up_weight: bfloat16 [6144, 14336], P(None, 'dp'), may hold values from -0.078125 to 0.078125
- down_weight: bfloat16 [14336, 6144], P('dp'), may hold values from -0.046875 to 0.046875
Outputs:
- mixed: bfloat16 [4096, 6144], P(('rep', 'dp')), parts along dimension 0
There are 8 independent parts, one for each index of `rep`. A program takes and returns all parts, laid end to end along the dimension named above; an argument that names none is the same for every part. Nothing has to cross between parts.
Inputs may be any that keep to these rules, and one draw needn't show every extreme that they name: The 16 slots of one device have lengths summing to at most 1024; on every device one slot holds exactly half of 1024 positions. Over the devices of one replica the counts sum to exactly 320.
All inputs are finite; a program needn't handle non-finite values.
Results may differ from a plain program's by a relative error of at most 0.02.
Values may be sent and summed in bfloat16 or wider, within the bound.
No kernel may reach another device: no remote copies, remote signals or barrier semaphores. Data moves between devices by JAX's collectives and lax.ppermute only.
A program may use at most 128 MiB of HBM per device.

v0:
```python
import jax
import jax.numpy as jnp
from jax import lax
from jax.sharding import PartitionSpec as P

HQ = 48
KVH = 4
HD = 128


def attend(query_rows, key_rows, value_rows, cache_lengths, live_count):
    slot_count = query_rows.shape[0]
    pool_size = key_rows.shape[0]
    group = HQ // KVH
    query_heads = query_rows.reshape(slot_count, KVH, group, HD)
    key_heads = key_rows.reshape(pool_size, KVH, HD)
    value_heads = value_rows.reshape(pool_size, KVH, HD)
    scores = jnp.einsum(
        "ckgd,pkd->ckgp", query_heads, key_heads, preferred_element_type=jnp.float32
    ) * HD ** (-0.5)
    ends = jnp.cumsum(cache_lengths)
    starts = ends - cache_lengths
    positions = jnp.arange(pool_size, dtype=jnp.int32)
    inside = (positions[None, :] >= starts[:, None]) & (positions[None, :] < ends[:, None])
    inside = inside[:, None, None, :]
    masked = jnp.where(inside, scores, jnp.float32(-1e30))
    row_max = jnp.max(masked, axis=-1, keepdims=True)
    raised = jnp.where(inside, jnp.exp(masked - row_max), jnp.float32(0.0))
    row_total = jnp.sum(raised, axis=-1, keepdims=True)
    weights = (raised / row_total).astype(jnp.bfloat16)
    mixed_heads = jnp.einsum(
        "ckgp,pkd->ckgd", weights, value_heads, preferred_element_type=jnp.float32
    )
    live_mask = jnp.arange(slot_count, dtype=jnp.int32) < live_count
    flat_rows = mixed_heads.reshape(slot_count, HQ * HD)
    return jnp.where(live_mask[:, None], flat_rows, jnp.float32(0.0)).astype(jnp.bfloat16)


def normalize(row_block, norm_gain):
    values = row_block.astype(jnp.float32)
    mean_square = jnp.mean(values * values, axis=-1, keepdims=True)
    return (values * lax.rsqrt(mean_square + 1e-05) * norm_gain).astype(jnp.bfloat16)


def feed_forward(row_block, up_weight, down_weight):
    up_proj = jnp.dot(row_block, up_weight, preferred_element_type=jnp.float32)
    activated = jax.nn.silu(up_proj).astype(jnp.bfloat16)
    return jnp.dot(activated, down_weight, preferred_element_type=jnp.float32)


def on_device(
    queries, cache_keys, cache_values, lengths, counts, norm_gain, up_weight, down_weight
):
    attended = attend(queries, cache_keys, cache_values, lengths, counts[0])
    payload = normalize(attended, norm_gain)
    partial_value = feed_forward(
        lax.all_gather(payload, "dp", axis=0, tiled=True), up_weight, down_weight
    )
    summed = lax.psum_scatter(
        partial_value.astype(jnp.bfloat16), "dp", scatter_dimension=0, tiled=True
    ).astype(jnp.float32)
    return (attended.astype(jnp.float32) + summed).astype(jnp.bfloat16)


def solution(mesh):
    in_specs = (
        P(("rep", "dp"), None),
        P(("rep", "dp"), None),
        P(("rep", "dp"), None),
        P(("rep", "dp")),
        P(("rep", "dp")),
        P(),
        P(None, "dp"),
        P("dp", None),
    )
    out_specs = P(("rep", "dp"), None)
    return jax.shard_map(
        on_device, mesh=mesh, in_specs=in_specs, out_specs=out_specs, check_vma=False
    )
```

profile of v0, /device:TPU:128, one launch (start us, length us, event | category | flops | bytes accessed | tf_op | source)
XLA Modules:
  0.0 187.8 jit_solution(1654417664949247617)
XLA Ops:
  6.5 0.0 copy-start
  6.5 0.0 all-gather.2.cloned.1.call-start
  7.3 0.7 copy.13
  8.1 0.1 reduce.1
  8.2 0.7 sub.11
  8.8 0.1 fusion.15
  8.9 1.1 reshape.93
  10.0 1.3 reshape.92
  11.4 0.0 copy-done
  11.4 0.3 reshape.94
  11.7 0.6 fusion.8
  12.3 1.2 fusion.19
  13.5 0.0 copy-start.1
  13.5 0.9 multiply_reduce_fusion
  14.4 0.1 copy.17
  14.5 0.1 reshape.95
  14.6 0.0 copy-done.1
  14.6 0.8 fusion.12
  15.4 0.0 all-gather.2.cloned.1.call-update
  15.4 0.0 reduce-scatter.2.cloned.1.call-start
  15.5 55.8 %all-gather.2.cloned.1.call-done = bf16[512,6144]{1,0:T(8,128)(2,1)} async-done(((bf16[16,6144]{1,0:T(8,128)(2,1)}), bf16[512,6144]{1,0:T(8,128)(2,1)}) %all-gather.2.cloned.1.call-update) | async-done | bytes 6291472 | tf_op jit(solution)/shard_map/all_gather | solution.py:57
  71.3 6.8 %fusion.20 = f32[512,448]{0,1:T(8,128)S(1)} fusion(bf16[512,6144]{1,0:T(8,128)(2,1)} %all-gather.2.cloned.1.call-done, bf16[6144,448]{0,1:T(8,128)(2,1)} %param.14), kind=kOutput, calls=%fused_computation.34 | convolution fusion | flops 2818572288 | bytes 12713984 | tf_op jit(solution)/shard_map/dot_general | solution.py:46
  78.1 8.0 %convolution_convert_fusion = bf16[512,6144]{1,0:T(8,128)(2,1)} fusion(bf16[448,6144]{1,0:T(8,128)(2,1)} %param.15, f32[512,448]{0,1:T(8,128)S(1)} %fusion.20), kind=kOutput, calls=%fused_computation.1 | convolution fusion | flops 2822864896 | bytes 12713984 | tf_op jit(solution)/shard_map/dot_general | solution.py:48
  86.1 0.0 reduce-scatter.2.cloned.1.call-update
  86.2 93.1 %reduce-scatter.2.cloned.1.call-done = bf16[16,6144]{1,0:T(8,128)(2,1)} async-done(((bf16[512,6144]{1,0:T(8,128)(2,1)}), bf16[16,6144]{1,0:T(8,128)(2,1)}) %reduce-scatter.2.cloned.1.call-update) | async-done | bytes 196624 | tf_op jit(solution)/shard_map/reduce_scatter | solution.py:59
  179.2 1.7 fusion.13
  (3 shorter events, 0.1 us)
Async XLA Ops:
  6.5 4.8 %copy-start = (bf16[1024,512]{1,0:T(8,128)(2,1)S(1)}, bf16[1024,512]{1,0:T(8,128)(2,1)}, u32[]{:S(2)}) copy-start(bf16[1024,512]{1,0:T(8,128)(2,1)} %param.10) | copy-start | bytes 3145732
  6.5 64.7 %all-gather.2.cloned.1.call-start = ((), (), s32[]{:S(2)}) async-start(), calls=%async_computation.1 | async-start | bytes 6488064 | tf_op jit(solution)/shard_map/all_gather | solution.py:57
  13.5 1.1 copy-start.1
  15.4 163.8 %reduce-scatter.2.cloned.1.call-start = ((), (), s32[]{:S(2)}) async-start(), calls=%async_computation.2 | async-start | bytes 6488064 | tf_op jit(solution)/shard_map/reduce_scatter | solution.py:59
Sparse Core Ops, SparseCore 0:
  15.6 55.6 all-gather.1
  86.3 92.9 reduce-scatter.1
where the time goes:
time: 189 us; the launch traced here: 188 us
  waiting for transfers between devices  149 us (79%)
  matrix products  16.3 us (9%)
  between operations  14.2 us (8%)
  other arithmetic  4.68 us (2%)
  local copies, waits for them, and re-layouts  3.67 us (2%)
    reduce_scatter x1, waiting for transfers between devices, on_device(): lax.psum_scatter(partial_value.astype(jnp.bfloat16), 'dp', scatter_dimens...  93.1 us
    all_gather x1, waiting for transfers between devices, on_device(): lax.all_gather(payload, 'dp', axis=0, tiled=True)  55.8 us
    dot_general x1, matrix products, feed_forward(): return jnp.dot(activated, down_weight, preferred_element_type=jnp.float32)  8.02 us
    dot_general x1, matrix products, feed_forward(): up_proj = jnp.dot(row_block, up_weight, preferred_element_type=jnp.float32)  6.85 us
  transfers between devices with their start and end apart: 2, of which 2 were waited for; matrix products, arithmetic and copies ran while one was open for 0% of the time, Pallas kernels for 0%

commit v1 on v0

v1 whole, which is shorter than its diff:
```python
import functools

import jax
import jax.numpy as jnp
from jax import lax
from jax.experimental import pallas as pl
from jax.experimental.pallas import tpu as pltpu
from jax.sharding import PartitionSpec as P

HQ = 48
KVH = 4
HD = 128
GROUP = HQ // KVH
D = HQ * HD
HALF = D // 2
SLOTS = 16
POOL = 1024
HIDDEN = 448
SIDE = 4
N_DP = 32
WIDE = SIDE * SLOTS
CHUNK = 512


def device(y, x, c):
    return ((y % SIDE) * SIDE + x % SIDE) * 2 + c


def routes():
    out = {name: [] for name in ("xa", "xb", "x2", "ya", "yb", "y2", "core")}
    for y in range(SIDE):
        for x in range(SIDE):
            for c in range(2):
                way = 1 if c == 0 else -1
                me = device(y, x, c)
                out["xa"].append((me, device(y, x + way, c)))
                out["xb"].append((me, device(y, x - way, c)))
                out["x2"].append((me, device(y, x + 2, c)))
                out["ya"].append((me, device(y + way, x, c)))
                out["yb"].append((me, device(y - way, x, c)))
                out["y2"].append((me, device(y + 2, x, c)))
                out["core"].append((me, device(y, x, 1 - c)))
    return out


ROUTES = routes()


def send(value, route):
    return lax.ppermute(value, "dp", ROUTES[route])


def attend_kernel(lengths, counts, q, k, v, gain, attended, first, second):
    row = lax.broadcasted_iota(jnp.int32, (SLOTS, 1), 0)
    starts = jnp.zeros((SLOTS, 1), jnp.int32)
    ends = jnp.zeros((SLOTS, 1), jnp.int32)
    at = jnp.int32(0)
    for i in range(SLOTS):
        after = at + lengths[i]
        starts = jnp.where(row == i, at, starts)
        ends = jnp.where(row == i, after, ends)
        at = after
    position = lax.broadcasted_iota(jnp.int32, (SLOTS, POOL), 1)
    inside = (position >= starts) & (position < ends)
    offset = jnp.where(inside, jnp.float32(0.0), jnp.float32(-1e30))
    live = row < counts[0]
    squares = jnp.zeros((SLOTS, HD), jnp.float32)
    for kv in range(KVH):
        heads = range(kv * GROUP, (kv + 1) * GROUP)
        rows = jnp.concatenate([q[:, h * HD : (h + 1) * HD] for h in heads], axis=0)
        scores = lax.dot_general(
            rows,
            k[:, kv * HD : (kv + 1) * HD],
            (((1,), (1,)), ((), ())),
            preferred_element_type=jnp.float32,
        )
        masked = scores.reshape(GROUP, SLOTS, POOL) + offset[None]
        top = jnp.max(masked, axis=-1, keepdims=True)
        raised = jnp.exp((masked - top) * jnp.float32(HD ** (-0.5)))
        total = jnp.sum(raised, axis=-1, keepdims=True)
        mixed = lax.dot_general(
            raised.astype(jnp.bfloat16).reshape(GROUP * SLOTS, POOL),
            v[:, kv * HD : (kv + 1) * HD],
            (((1,), (0,)), ((), ())),
            preferred_element_type=jnp.float32,
        )
        mixed = mixed.reshape(GROUP, SLOTS, HD) / total
        for g, h in enumerate(heads):
            part = jnp.where(live, mixed[g], jnp.float32(0.0)).astype(jnp.bfloat16)
            attended[:, h * HD : (h + 1) * HD] = part
            wide = part.astype(jnp.float32)
            squares = squares + wide * wide
    mean_square = jnp.sum(squares, axis=-1, keepdims=True) / D
    factor = lax.rsqrt(mean_square + 1e-05)
    for out, base in ((first, 0), (second, HALF)):
        wide = attended[:, base : base + HALF].astype(jnp.float32)
        out[...] = (wide * factor * gain[:, base : base + HALF]).astype(jnp.bfloat16)


def attend(queries, cache_keys, cache_values, lengths, counts, norm_gain):
    vmem = pl.BlockSpec(memory_space=pltpu.VMEM)
    smem = pl.BlockSpec(memory_space=pltpu.SMEM)
    return pl.pallas_call(
        attend_kernel,
        out_shape=(
            jax.ShapeDtypeStruct((SLOTS, D), jnp.bfloat16),
            jax.ShapeDtypeStruct((SLOTS, HALF), jnp.bfloat16),
            jax.ShapeDtypeStruct((SLOTS, HALF), jnp.bfloat16),
        ),
        in_specs=[smem, smem, vmem, vmem, vmem, vmem],
        out_specs=(vmem, vmem, vmem),
        compiler_params=pltpu.CompilerParams(vmem_limit_bytes=24 * 2**20),
        name="attend",
    )(lengths, counts, queries, cache_keys, cache_values, norm_gain.reshape(1, D))


def block_copies(refs, rows, sems):
    pairs = []
    for core in range(2):
        for i in range(SIDE):
            pairs.append((refs[core * 8 + i], rows.at[core, i, :, :, pl.ds(0, HALF)]))
            pairs.append((refs[core * 8 + 4 + i], rows.at[core, :, i, :, pl.ds(HALF, HALF)]))
    return pairs


def ffn_kernel(*args):
    ins, up, down, outs = args[:16], args[16], args[17], args[18:34]
    rows, up_held, down_held, total, hidden, sem_in, sem_w, sem_out = args[34:]
    copies = [
        pltpu.make_async_copy(a, b, sem_in.at[i])
        for i, (a, b) in enumerate(block_copies(ins, rows, None))
    ]
    for copy in copies:
        copy.start()
    up_copy = pltpu.make_async_copy(up, up_held, sem_w.at[0])
    up_copy.start()
    down_copy = pltpu.make_async_copy(down, down_held, sem_w.at[1])
    down_copy.start()
    up_copy.wait()
    for copy in copies:
        copy.wait()
    m = 2 * SIDE * SIDE * SLOTS
    total[...] = jnp.zeros_like(total)

    @pl.loop(0, D // CHUNK)
    def _(step):
        cols = pl.ds(pl.multiple_of(step * CHUNK, CHUNK), CHUNK)
        total[...] += lax.dot_general(
            rows[:, :, :, :, cols].reshape(m, CHUNK),
            up_held[:, cols],
            (((1,), (1,)), ((), ())),
            preferred_element_type=jnp.float32,
        )

    value = total[...]
    hidden[...] = (value / (1.0 + jnp.exp(-value))).astype(jnp.bfloat16)
    down_copy.wait()

    @pl.loop(0, D // CHUNK)
    def _(step):
        cols = pl.ds(pl.multiple_of(step * CHUNK, CHUNK), CHUNK)
        product = jnp.dot(hidden[...], down_held[:, cols], preferred_element_type=jnp.float32)
        rows[:, :, :, :, cols] = product.astype(jnp.bfloat16).reshape(
            2, SIDE, SIDE, SLOTS, CHUNK
        )

    back = [
        pltpu.make_async_copy(b, a, sem_out.at[i])
        for i, (a, b) in enumerate(block_copies(outs, rows, None))
    ]
    for copy in back:
        copy.start()
    for copy in back:
        copy.wait()


def feed_forward(blocks, up_rows, down_rows):
    any_space = pl.BlockSpec(memory_space=pl.ANY)
    m = 2 * SIDE * SIDE * SLOTS
    return pl.pallas_call(
        ffn_kernel,
        out_shape=[jax.ShapeDtypeStruct((SIDE, SLOTS, HALF), jnp.bfloat16)] * 16,
        in_specs=[any_space] * 18,
        out_specs=[any_space] * 16,
        scratch_shapes=[
            pltpu.VMEM((2, SIDE, SIDE, SLOTS, D), jnp.bfloat16),
            pltpu.VMEM((HIDDEN, D), jnp.bfloat16),
            pltpu.VMEM((HIDDEN, D), jnp.bfloat16),
            pltpu.VMEM((m, HIDDEN), jnp.float32),
            pltpu.VMEM((m, HIDDEN), jnp.bfloat16),
            pltpu.SemaphoreType.DMA((16,)),
            pltpu.SemaphoreType.DMA((2,)),
            pltpu.SemaphoreType.DMA((16,)),
        ],
        compiler_params=pltpu.CompilerParams(vmem_limit_bytes=48 * 2**20),
        name="feed_forward",
    )(*blocks, up_rows, down_rows)


def ring_gather(own, axis):
    from_a = send(own, axis + "a")
    from_b = send(own, axis + "b")
    return own, from_a, from_b, send(from_a, axis + "a")


def ring_reduce(blocks, axis):
    own, of_a, of_b, of_2 = blocks
    far = send(of_2, axis + "b")
    near = send(of_b, axis + "a")
    back = send((of_a.astype(jnp.float32) + far.astype(jnp.float32)).astype(jnp.bfloat16), axis + "b")
    return own.astype(jnp.float32) + near.astype(jnp.float32) + back.astype(jnp.float32)


def on_device(
    queries, cache_keys, cache_values, lengths, counts, norm_gain, up_weight, down_weight
):
    attended, first, second = attend(
        queries, cache_keys, cache_values, lengths, counts, norm_gain
    )
    row = jnp.stack(ring_gather(first, "x"))
    column = jnp.stack(ring_gather(second, "y"))
    own = [*ring_gather(row, "y"), *ring_gather(column, "x")]
    blocks = own + [send(b, "core") for b in own]
    parts = feed_forward(blocks, up_weight.T, down_weight)
    summed = [
        (a.astype(jnp.float32) + send(b, "core").astype(jnp.float32)).astype(jnp.bfloat16)
        for a, b in zip(parts[:8], parts[8:])
    ]
    row = ring_reduce(summed[:4], "y").astype(jnp.bfloat16)
    column = ring_reduce(summed[4:], "x").astype(jnp.bfloat16)
    first = ring_reduce([row[i] for i in range(SIDE)], "x")
    second = ring_reduce([column[i] for i in range(SIDE)], "y")
    projected = jnp.concatenate([first, second], axis=1)
    return (attended.astype(jnp.float32) + projected).astype(jnp.bfloat16)


def solution(mesh):
    in_specs = (
        P(("rep", "dp"), None),
        P(("rep", "dp"), None),
        P(("rep", "dp"), None),
        P(("rep", "dp")),
        P(("rep", "dp")),
        P(),
        P(None, "dp"),
        P("dp", None),
    )
    out_specs = P(("rep", "dp"), None)
    return jax.shard_map(
        on_device, mesh=mesh, in_specs=in_specs, out_specs=out_specs, check_vma=False
    )
```

time: 189 us -> 120 us (0.63)
  waiting for transfers between devices: 149 us -> 48 us
  starting transfers between devices: 0.04 us -> 42.9 us
  Pallas kernels: 0 us -> 19.9 us
  matrix products: 16.3 us -> 0 us
  between operations: 14.2 us -> 1.05 us
  other arithmetic: 4.68 us -> 2.04 us
    reduce_scatter x1 -> x0, waiting for transfers between devices: 93.1 us -> none  [on_device(): lax.psum_scatter(partial_value.astype(jnp.bfloat16), 'dp', scatter_dimens...]
    all_gather x1 -> x0, waiting for transfers between devices: 55.8 us -> none  [on_device(): lax.all_gather(payload, 'dp', axis=0, tiled=True)]
    ppermute x0 -> x40, waiting for transfers between devices: none -> 48 us  [send(): return lax.ppermute(value, 'dp', ROUTES[route])]
    ppermute x0 -> x40, starting transfers between devices: none -> 42.9 us  [send(): return lax.ppermute(value, 'dp', ROUTES[route])]
    pallas_call x0 -> x2, Pallas kernels: none -> 19.9 us  [the longest x1 17.3 us: feed_forward(): pl.pallas_call(ffn_kernel, out_shape=[jax.ShapeDtypeStruct((SIDE, SLOTS,...]
    dot_general x4 -> x0, matrix products: 16.3 us -> none  [the longest x1 8.02 us: feed_forward(): return jnp.dot(activated, down_weight, preferred_element_type=jnp.float32)]
    unnamed x4 -> x42, local copies, waits for them, and re-layouts: 0.01 us -> 5.45 us
    reshape x4 -> x0, local copies, waits for them, and re-layouts: 2.86 us -> none  [the longest x1 1.35 us: attend(): key_heads = key_rows.reshape(pool_size, KVH, HD)]
  transfers between devices with their start and end apart: 2 -> 40, of which waited for: 2 -> 17; matrix products, arithmetic and copies ran while one was open for 0% -> 1% of each run, Pallas kernels for 0% -> 0%
where the time goes in v1:
time: 120 us; the launch traced here: 119 us
  waiting for transfers between devices  48 us (40%)
  starting transfers between devices  42.9 us (36%)
  Pallas kernels  19.9 us (17%)
  local copies, waits for them, and re-layouts  5.48 us (5%)
  other arithmetic  2.04 us (2%)
    ppermute x40, waiting for transfers between devices, send(): return lax.ppermute(value, 'dp', ROUTES[route])  48 us
    ppermute x40, starting transfers between devices, send(): return lax.ppermute(value, 'dp', ROUTES[route])  42.9 us
    pallas_call x1, Pallas kernels, feed_forward(): pl.pallas_call(ffn_kernel, out_shape=[jax.ShapeDtypeStruct((SIDE, SLOTS,...  17.3 us
    unnamed x42, local copies, waits for them, and re-layouts  5.45 us
    pallas_call x1, Pallas kernels, attend(): pl.pallas_call(attend_kernel, out_shape=(jax.ShapeDtypeStruct((SLOTS, D),...  2.59 us
  transfers between devices with their start and end apart: 40, of which 17 were waited for; matrix products, arithmetic and copies ran while one was open for 1% of the time, Pallas kernels for 0%

profile of v1, /device:TPU:128, one launch (start us, length us, event | category | flops | bytes accessed | tf_op | source)
XLA Modules:
  0.0 119.3 jit_solution(11180266123747740071)
XLA Ops:
  0.7 1.2 %copy-done = bf16[1024,512]{1,0:T(8,128)(2,1)S(1)} copy-done((bf16[1024,512]{1,0:T(8,128)(2,1)S(1)}, bf16[1024,512]{1,0:T(8,128)(2,1)}, u32[]{:S(2)}) %copy-start) | copy-done | bytes 1048600
  1.9 1.2 %copy-done.1 = bf16[1024,512]{1,0:T(8,128)(2,1)S(1)} copy-done((bf16[1024,512]{1,0:T(8,128)(2,1)S(1)}, bf16[1024,512]{1,0:T(8,128)(2,1)}, u32[]{:S(2)}) %copy-start.1) | copy-done | bytes 1048600
  3.1 0.9 copy-done.2
  4.0 0.7 copy-done.3
  4.8 0.7 copy-done.4
  5.4 2.6 %attend.1 = (bf16[16,6144]{1,0:T(8,128)(2,1)S(1)}, bf16[16,3072]{1,0:T(8,128)(2,1)S(1)}, bf16[16,3072]{1,0:T(8,128)(2,1)S(1)}) custom-call(s32[16]{0:T(128)S(1)} %copy-done.4, s32[1]{0:T(128)S(6)} %copy.9.counts, bf16[16,6144]{1,0:T(8,128)(2,1)S(1)} %copy-done.2, bf16[1024,512]{1,0:T(8,128)(2,1)S(1)} %copy-done, bf16[1024,512]{1,0:T(8,128)(2,1)S(1)} %copy-done.1, ...), custom_call_target="tpu_custom_call" | custom-call | tf_op jit(solution)/shard_map/attend/pallas_call | solution.py:103
  8.0 1.7 %collective-permute-start.6 = (bf16[16,3072]{1,0:T(8,128)(2,1)S(1)}, bf16[16,3072]{1,0:T(8,128)(2,1)S(1)}, u32[]{:S(2)}, u32[]{:S(2)}) collective-permute-start(bf16[16,3072]{1,0:T(8,128)(2,1)S(1)} %get-tuple-element.26), channel_id=1, source_target_pairs={{0,64},{8,200},{16,80},{24,216},{32,96},{40,232},{48,112},{56,248}... | collective-permute-start | bytes 294920 | tf_op jit(solution)/shard_map/ppermute | solution.py:50
  9.7 1.5 %collective-permute-start = (bf16[16,3072]{1,0:T(8,128)(2,1)S(1)}, bf16[16,3072]{1,0:T(8,128)(2,1)S(1)}, u32[]{:S(2)}, u32[]{:S(2)}) collective-permute-start(bf16[16,3072]{1,0:T(8,128)(2,1)S(1)} %get-tuple-element.25), channel_id=1, source_target_pairs={{0,16},{8,56},{16,32},{24,8},{32,48},{40,24},{48,0},{56,40},{64,80... | collective-permute-start | bytes 294920 | tf_op jit(solution)/shard_map/ppermute | solution.py:50
  11.2 1.7 %collective-permute-start.7 = (bf16[16,3072]{1,0:T(8,128)(2,1)S(1)}, bf16[16,3072]{1,0:T(8,128)(2,1)S(1)}, u32[]{:S(2)}, u32[]{:S(2)}) collective-permute-start(bf16[16,3072]{1,0:T(8,128)(2,1)S(1)} %get-tuple-element.26), channel_id=1, source_target_pairs={{0,192},{8,72},{16,208},{24,88},{32,224},{40,104},{48,240},{56,120... | collective-permute-start | bytes 294920 | tf_op jit(solution)/shard_map/ppermute | solution.py:50
  12.8 1.1 collective-permute-done.6
  13.9 0.4 collective-permute-start.8
  14.3 3.0 %collective-permute-start.1 = (bf16[16,3072]{1,0:T(8,128)(2,1)S(1)}, bf16[16,3072]{1,0:T(8,128)(2,1)S(1)}, u32[]{:S(2)}, u32[]{:S(2)}) collective-permute-start(bf16[16,3072]{1,0:T(8,128)(2,1)S(1)} %get-tuple-element.25), channel_id=1, source_target_pairs={{0,48},{8,24},{16,0},{24,40},{32,16},{40,56},{48,32},{56,8},{64,11... | collective-permute-start | bytes 294920 | tf_op jit(solution)/shard_map/ppermute | solution.py:50
  17.3 2.5 %collective-permute-done.8 = bf16[16,3072]{1,0:T(8,128)(2,1)S(1)} collective-permute-done((bf16[16,3072]{1,0:T(8,128)(2,1)S(1)}, bf16[16,3072]{1,0:T(8,128)(2,1)S(1)}, u32[]{:S(2)}, u32[]{:S(2)}) %collective-permute-start.8) | collective-permute-done | bytes 98336 | tf_op jit(solution)/shard_map/ppermute | solution.py:50
  19.9 2.8 %collective-permute-start.10 = (bf16[4,16,3072]{2,1,0:T(8,128)(2,1)S(1)}, bf16[4,16,3072]{2,1,0:T(8,128)(2,1)S(1)}, u32[]{:S(2)}, u32[]{:S(2)}) collective-permute-start(bf16[4,16,3072]{2,1,0:T(8,128)(2,1)S(1)} %pad_maximum_fusion.1.args_4_), channel_id=1, source_target_pairs={{0,48},{8,24},{16,0},{24,40},{32,16},{40,56},{48,32},{56,8},{64,11... | collective-permute-start | bytes 1179656 | tf_op jit(solution)/shard_map/ppermute | solution.py:50
  22.8 0.3 collective-permute-done.2
  23.2 3.1 %collective-permute-start.3 = (bf16[4,16,3072]{2,1,0:T(8,128)(2,1)S(1)}, bf16[4,16,3072]{2,1,0:T(8,128)(2,1)S(1)}, u32[]{:S(2)}, u32[]{:S(2)}) collective-permute-start(bf16[4,16,3072]{2,1,0:T(8,128)(2,1)S(1)} %pad_maximum_fusion.args_0_), channel_id=1, source_target_pairs={{0,64},{8,200},{16,80},{24,216},{32,96},{40,232},{48,112},{56,248}... | collective-permute-start | bytes 1179656 | tf_op jit(solution)/shard_map/ppermute | solution.py:50
  26.3 0.3 collective-permute-start.4
  26.6 5.4 %collective-permute-done.10.args_6_ = bf16[4,16,3072]{2,1,0:T(8,128)(2,1)S(1)} collective-permute-done((bf16[4,16,3072]{2,1,0:T(8,128)(2,1)S(1)}, bf16[4,16,3072]{2,1,0:T(8,128)(2,1)S(1)}, u32[]{:S(2)}, u32[]{:S(2)}) %collective-permute-start.10) | collective-permute-done | bytes 393248 | tf_op jit(solution)/shard_map/ppermute | solution.py:50
  31.9 0.7 collective-permute-done.9.args_5_
  32.7 0.3 collective-permute-start.11
  33.0 1.7 %collective-permute-done.3.args_1_ = bf16[4,16,3072]{2,1,0:T(8,128)(2,1)S(1)} collective-permute-done((bf16[4,16,3072]{2,1,0:T(8,128)(2,1)S(1)}, bf16[4,16,3072]{2,1,0:T(8,128)(2,1)S(1)}, u32[]{:S(2)}, u32[]{:S(2)}) %collective-permute-start.3) | collective-permute-done | bytes 393248 | tf_op jit(solution)/shard_map/ppermute | solution.py:50
  34.7 2.5 %collective-permute-start.5 = (bf16[4,16,3072]{2,1,0:T(8,128)(2,1)S(1)}, bf16[4,16,3072]{2,1,0:T(8,128)(2,1)S(1)}, u32[]{:S(2)}, u32[]{:S(2)}) collective-permute-start(bf16[4,16,3072]{2,1,0:T(8,128)(2,1)S(1)} %collective-permute-done.3.args_1_), channel_id=1, source_target_pairs={{0,64},{8,200},{16,80},{24,216},{32,96},{40,232},{48,112},{56,248}... | collective-permute-start | bytes 1179656 | tf_op jit(solution)/shard_map/ppermute | solution.py:50
  37.2 0.5 collective-permute-start.13
  37.8 3.8 %collective-permute-done.11.args_7_ = bf16[4,16,3072]{2,1,0:T(8,128)(2,1)S(1)} collective-permute-done((bf16[4,16,3072]{2,1,0:T(8,128)(2,1)S(1)}, bf16[4,16,3072]{2,1,0:T(8,128)(2,1)S(1)}, u32[]{:S(2)}, u32[]{:S(2)}) %collective-permute-start.11) | collective-permute-done | bytes 393248 | tf_op jit(solution)/shard_map/ppermute | solution.py:50
  41.6 2.5 %collective-permute-done.5.args_3_ = bf16[4,16,3072]{2,1,0:T(8,128)(2,1)S(1)} collective-permute-done((bf16[4,16,3072]{2,1,0:T(8,128)(2,1)S(1)}, bf16[4,16,3072]{2,1,0:T(8,128)(2,1)S(1)}, u32[]{:S(2)}, u32[]{:S(2)}) %collective-permute-start.5) | collective-permute-done | bytes 393248 | tf_op jit(solution)/shard_map/ppermute | solution.py:50
  44.2 1.6 %collective-permute-done.15.args_11_ = bf16[4,16,3072]{2,1,0:T(8,128)(2,1)S(1)} collective-permute-done((bf16[4,16,3072]{2,1,0:T(8,128)(2,1)S(1)}, bf16[4,16,3072]{2,1,0:T(8,128)(2,1)S(1)}, u32[]{:S(2)}, u32[]{:S(2)}) %collective-permute-start.15) | collective-permute-done | bytes 393248 | tf_op jit(solution)/shard_map/ppermute | solution.py:50
  46.0 0.6 copy-done.20
  46.6 17.3 %feed_forward.1 = (bf16[4,16,3072]{2,1,0:T(8,128)(2,1)S(1)}, bf16[4,16,3072]{2,1,0:T(8,128)(2,1)S(1)}, bf16[4,16,3072]{2,1,0:T(8,128)(2,1)S(1)}, bf16[4,16,3072]...) custom-call(bf16[4,16,3072]{2,1,0:T(8,128)(2,1)} %copy-done.6, ...), custom_call_target="tpu_custom_call" | custom-call | tf_op jit(solution)/shard_map/feed_forward/pallas_call | solution.py:180
  64.2 0.4 collective-permute-start.20
  64.7 0.4 collective-permute-start.24
  65.2 0.6 collective-permute-done.21
  66.0 1.4 %collective-permute-done.24 = bf16[4,16,3072]{2,1,0:T(8,128)(2,1)S(1)} collective-permute-done((bf16[4,16,3072]{2,1,0:T(8,128)(2,1)S(1)}, bf16[4,16,3072]{2,1,0:T(8,128)(2,1)S(1)}, u32[]{:S(2)}, u32[]{:S(2)}) %collective-permute-start.24) | collective-permute-done | bytes 393248 | tf_op jit(solution)/shard_map/ppermute | solution.py:50
  67.7 0.9 collective-permute-done.31
  68.8 1.7 %collective-permute-done.34 = bf16[4,16,3072]{2,1,0:T(8,128)(2,1)S(1)} collective-permute-done((bf16[4,16,3072]{2,1,0:T(8,128)(2,1)}, bf16[4,16,3072]{2,1,0:T(8,128)(2,1)S(1)}, u32[]{:S(2)}, u32[]{:S(2)}) %collective-permute-start.34) | collective-permute-done | bytes 393248 | tf_op jit(solution)/shard_map/ppermute | solution.py:50
  70.5 2.0 %collective-permute-start.25 = (bf16[4,16,3072]{2,1,0:T(8,128)(2,1)S(1)}, bf16[4,16,3072]{2,1,0:T(8,128)(2,1)S(1)}, u32[]{:S(2)}, u32[]{:S(2)}) collective-permute-start(bf16[4,16,3072]{2,1,0:T(8,128)(2,1)S(1)} %add_convert_fusion.8), channel_id=1, source_target_pairs={{0,192},{8,72},{16,208},{24,88},{32,224},{40,104},{48,240},{56,120... | collective-permute-start | bytes 1179656 | tf_op jit(solution)/shard_map/ppermute | solution.py:50
  72.7 9.1 %collective-permute-done.25 = bf16[4,16,3072]{2,1,0:T(8,128)(2,1)S(1)} collective-permute-done((bf16[4,16,3072]{2,1,0:T(8,128)(2,1)S(1)}, bf16[4,16,3072]{2,1,0:T(8,128)(2,1)S(1)}, u32[]{:S(2)}, u32[]{:S(2)}) %collective-permute-start.25) | collective-permute-done | bytes 393248 | tf_op jit(solution)/shard_map/ppermute | solution.py:50
  81.9 4.0 %collective-permute-start.35 = (bf16[4,16,3072]{2,1,0:T(8,128)(2,1)S(1)}, bf16[4,16,3072]{2,1,0:T(8,128)(2,1)S(1)}, u32[]{:S(2)}, u32[]{:S(2)}) collective-permute-start(bf16[4,16,3072]{2,1,0:T(8,128)(2,1)S(1)} %add_convert_fusion.2), channel_id=1, source_target_pairs={{0,48},{8,24},{16,0},{24,40},{32,16},{40,56},{48,32},{56,8},{64,11... | collective-permute-start | bytes 1179656 | tf_op jit(solution)/shard_map/ppermute | solution.py:50
  86.1 0.3 collective-permute-start.32
  86.4 8.6 %collective-permute-done.35 = bf16[4,16,3072]{2,1,0:T(8,128)(2,1)S(1)} collective-permute-done((bf16[4,16,3072]{2,1,0:T(8,128)(2,1)S(1)}, bf16[4,16,3072]{2,1,0:T(8,128)(2,1)S(1)}, u32[]{:S(2)}, u32[]{:S(2)}) %collective-permute-start.35) | collective-permute-done | bytes 393248 | tf_op jit(solution)/shard_map/ppermute | solution.py:50
  95.2 3.8 %collective-permute-start.36 = (bf16[4,16,3072]{2,1,0:T(8,128)(2,1)S(1)}, bf16[4,16,3072]{2,1,0:T(8,128)(2,1)S(1)}, u32[]{:S(2)}, u32[]{:S(2)}) collective-permute-start(bf16[4,16,3072]{2,1,0:T(8,128)(2,1)S(1)} %add_convert_fusion.1), channel_id=1, source_target_pairs={{0,48},{8,24},{16,0},{24,40},{32,16},{40,56},{48,32},{56,8},{64,11... | collective-permute-start | bytes 1179656 | tf_op jit(solution)/shard_map/ppermute | solution.py:50
  98.9 3.8 %collective-permute-done.26 = bf16[4,16,3072]{2,1,0:T(8,128)(2,1)S(1)} collective-permute-done((bf16[4,16,3072]{2,1,0:T(8,128)(2,1)S(1)}, bf16[4,16,3072]{2,1,0:T(8,128)(2,1)S(1)}, u32[]{:S(2)}, u32[]{:S(2)}) %collective-permute-start.26) | collective-permute-done | bytes 393248 | tf_op jit(solution)/shard_map/ppermute | solution.py:50
  103.1 3.8 %collective-permute-start.28 = (bf16[16,3072]{1,0:T(8,128)(2,1)S(1)}, bf16[16,3072]{1,0:T(8,128)(2,1)S(1)}, u32[]{:S(2)}, u32[]{:S(2)}) collective-permute-start(bf16[16,3072]{1,0:T(8,128)(2,1)S(1)} %get-tuple-element.44), channel_id=1, source_target_pairs={{0,48},{8,24},{16,0},{24,40},{32,16},{40,56},{48,32},{56,8},{64,11... | collective-permute-start | bytes 294920 | tf_op jit(solution)/shard_map/ppermute | solution.py:50
  107.1 0.5 collective-permute-start.37
  107.6 2.8 %collective-permute-start.38 = (bf16[16,3072]{1,0:T(8,128)(2,1)S(1)}, bf16[16,3072]{1,0:T(8,128)(2,1)S(1)}, u32[]{:S(2)}, u32[]{:S(2)}) collective-permute-start(bf16[16,3072]{1,0:T(8,128)(2,1)S(1)} %get-tuple-element.46), channel_id=1, source_target_pairs={{0,192},{8,72},{16,208},{24,88},{32,224},{40,104},{48,240},{56,120... | collective-permute-start | bytes 294920 | tf_op jit(solution)/shard_map/ppermute | solution.py:50
  110.5 2.3 %collective-permute-start.29 = (bf16[16,3072]{1,0:T(8,128)(2,1)S(1)}, bf16[16,3072]{1,0:T(8,128)(2,1)S(1)}, u32[]{:S(2)}, u32[]{:S(2)}) collective-permute-start(bf16[16,3072]{1,0:T(8,128)(2,1)S(1)} %fusion.3), channel_id=1, source_target_pairs={{0,48},{8,24},{16,0},{24,40},{32,16},{40,56},{48,32},{56,8},{64,11... | collective-permute-start | bytes 294920 | tf_op jit(solution)/shard_map/ppermute | solution.py:50
  112.8 3.5 %collective-permute-start.39 = (bf16[16,3072]{1,0:T(8,128)(2,1)S(1)}, bf16[16,3072]{1,0:T(8,128)(2,1)S(1)}, u32[]{:S(2)}, u32[]{:S(2)}) collective-permute-start(bf16[16,3072]{1,0:T(8,128)(2,1)S(1)} %fusion.1), channel_id=1, source_target_pairs={{0,192},{8,72},{16,208},{24,88},{32,224},{40,104},{48,240},{56,120... | collective-permute-start | bytes 294920 | tf_op jit(solution)/shard_map/ppermute | solution.py:50
  116.4 2.2 %collective-permute-done.39 = bf16[16,3072]{1,0:T(8,128)(2,1)S(1)} collective-permute-done((bf16[16,3072]{1,0:T(8,128)(2,1)S(1)}, bf16[16,3072]{1,0:T(8,128)(2,1)S(1)}, u32[]{:S(2)}, u32[]{:S(2)}) %collective-permute-start.39) | collective-permute-done | bytes 98336 | tf_op jit(solution)/shard_map/ppermute | solution.py:50
  118.6 0.7 fusion
  (93 shorter events, 2.8 us)
Async XLA Ops:
  8.0 5.9 %collective-permute-start.6 = (bf16[16,3072]{1,0:T(8,128)(2,1)S(1)}, bf16[16,3072]{1,0:T(8,128)(2,1)S(1)}, u32[]{:S(2)}, u32[]{:S(2)}) collective-permute-start(bf16[16,3072]{1,0:T(8,128)(2,1)S(1)} %get-tuple-element.26), channel_id=1, source_target_pairs={{0,64},{8,200},{16,80},{24,216},{32,96},{40,232},{48,112},{56,248}... | collective-permute-start | bytes 294920 | tf_op jit(solution)/shard_map/ppermute | solution.py:50
  9.7 7.6 %collective-permute-start = (bf16[16,3072]{1,0:T(8,128)(2,1)S(1)}, bf16[16,3072]{1,0:T(8,128)(2,1)S(1)}, u32[]{:S(2)}, u32[]{:S(2)}) collective-permute-start(bf16[16,3072]{1,0:T(8,128)(2,1)S(1)} %get-tuple-element.25), channel_id=1, source_target_pairs={{0,16},{8,56},{16,32},{24,8},{32,48},{40,24},{48,0},{56,40},{64,80... | collective-permute-start | bytes 294920 | tf_op jit(solution)/shard_map/ppermute | solution.py:50
  11.2 6.1 %collective-permute-start.7 = (bf16[16,3072]{1,0:T(8,128)(2,1)S(1)}, bf16[16,3072]{1,0:T(8,128)(2,1)S(1)}, u32[]{:S(2)}, u32[]{:S(2)}) collective-permute-start(bf16[16,3072]{1,0:T(8,128)(2,1)S(1)} %get-tuple-element.26), channel_id=1, source_target_pairs={{0,192},{8,72},{16,208},{24,88},{32,224},{40,104},{48,240},{56,120... | collective-permute-start | bytes 294920 | tf_op jit(solution)/shard_map/ppermute | solution.py:50
  13.9 5.8 %collective-permute-start.8 = (bf16[16,3072]{1,0:T(8,128)(2,1)S(1)}, bf16[16,3072]{1,0:T(8,128)(2,1)S(1)}, u32[]{:S(2)}, u32[]{:S(2)}) collective-permute-start(bf16[16,3072]{1,0:T(8,128)(2,1)S(1)} %collective-permute-done.6), channel_id=1, source_target_pairs={{0,64},{8,200},{16,80},{24,216},{32,96},{40,232},{48,112},{56,248}... | collective-permute-start | bytes 294920 | tf_op jit(solution)/shard_map/ppermute | solution.py:50
  14.3 8.5 %collective-permute-start.1 = (bf16[16,3072]{1,0:T(8,128)(2,1)S(1)}, bf16[16,3072]{1,0:T(8,128)(2,1)S(1)}, u32[]{:S(2)}, u32[]{:S(2)}) collective-permute-start(bf16[16,3072]{1,0:T(8,128)(2,1)S(1)} %get-tuple-element.25), channel_id=1, source_target_pairs={{0,48},{8,24},{16,0},{24,40},{32,16},{40,56},{48,32},{56,8},{64,11... | collective-permute-start | bytes 294920 | tf_op jit(solution)/shard_map/ppermute | solution.py:50
  17.3 5.8 %collective-permute-start.2 = (bf16[16,3072]{1,0:T(8,128)(2,1)S(1)}, bf16[16,3072]{1,0:T(8,128)(2,1)S(1)}, u32[]{:S(2)}, u32[]{:S(2)}) collective-permute-start(bf16[16,3072]{1,0:T(8,128)(2,1)S(1)} %collective-permute-done), channel_id=1, source_target_pairs={{0,16},{8,56},{16,32},{24,8},{32,48},{40,24},{48,0},{56,40},{64,80... | collective-permute-start | bytes 294920 | tf_op jit(solution)/shard_map/ppermute | solution.py:50
  19.8 26.0 %copy-start.5 = (bf16[4,16,3072]{2,1,0:T(8,128)(2,1)}, bf16[4,16,3072]{2,1,0:T(8,128)(2,1)S(1)}, u32[]{:S(2)}) copy-start(bf16[4,16,3072]{2,1,0:T(8,128)(2,1)S(1)} %pad_maximum_fusion.1.args_4_) | copy-start | bytes 1179652
  19.8 6.5 %collective-permute-start.16 = (bf16[4,16,3072]{2,1,0:T(8,128)(2,1)S(1)}, bf16[4,16,3072]{2,1,0:T(8,128)(2,1)S(1)}, u32[]{:S(2)}, u32[]{:S(2)}) collective-permute-start(bf16[4,16,3072]{2,1,0:T(8,128)(2,1)S(1)} %pad_maximum_fusion.1.args_4_), channel_id=1, source_target_pairs={{0,8},{8,0},{16,24},{24,16},{32,40},{40,32},{48,56},{56,48},{64,72... | collective-permute-start | bytes 1179656 | tf_op jit(solution)/shard_map/ppermute | solution.py:50
  19.9 12.0 %collective-permute-start.10 = (bf16[4,16,3072]{2,1,0:T(8,128)(2,1)S(1)}, bf16[4,16,3072]{2,1,0:T(8,128)(2,1)S(1)}, u32[]{:S(2)}, u32[]{:S(2)}) collective-permute-start(bf16[4,16,3072]{2,1,0:T(8,128)(2,1)S(1)} %pad_maximum_fusion.1.args_4_), channel_id=1, source_target_pairs={{0,48},{8,24},{16,0},{24,40},{32,16},{40,56},{48,32},{56,8},{64,11... | collective-permute-start | bytes 1179656 | tf_op jit(solution)/shard_map/ppermute | solution.py:50
  22.8 9.9 %collective-permute-start.9 = (bf16[4,16,3072]{2,1,0:T(8,128)(2,1)S(1)}, bf16[4,16,3072]{2,1,0:T(8,128)(2,1)S(1)}, u32[]{:S(2)}, u32[]{:S(2)}) collective-permute-start(bf16[4,16,3072]{2,1,0:T(8,128)(2,1)S(1)} %pad_maximum_fusion.1.args_4_), channel_id=1, source_target_pairs={{0,16},{8,56},{16,32},{24,8},{32,48},{40,24},{48,0},{56,40},{64,80... | collective-permute-start | bytes 1179656 | tf_op jit(solution)/shard_map/ppermute | solution.py:50
  23.1 22.7 %copy-start.6 = (bf16[4,16,3072]{2,1,0:T(8,128)(2,1)}, bf16[4,16,3072]{2,1,0:T(8,128)(2,1)S(1)}, u32[]{:S(2)}) copy-start(bf16[4,16,3072]{2,1,0:T(8,128)(2,1)S(1)} %pad_maximum_fusion.args_0_) | copy-start | bytes 1179652
  23.2 11.5 %collective-permute-start.3 = (bf16[4,16,3072]{2,1,0:T(8,128)(2,1)S(1)}, bf16[4,16,3072]{2,1,0:T(8,128)(2,1)S(1)}, u32[]{:S(2)}, u32[]{:S(2)}) collective-permute-start(bf16[4,16,3072]{2,1,0:T(8,128)(2,1)S(1)} %pad_maximum_fusion.args_0_), channel_id=1, source_target_pairs={{0,64},{8,200},{16,80},{24,216},{32,96},{40,232},{48,112},{56,248}... | collective-permute-start | bytes 1179656 | tf_op jit(solution)/shard_map/ppermute | solution.py:50
  26.3 10.9 %collective-permute-start.12 = (bf16[4,16,3072]{2,1,0:T(8,128)(2,1)S(1)}, bf16[4,16,3072]{2,1,0:T(8,128)(2,1)S(1)}, u32[]{:S(2)}, u32[]{:S(2)}) collective-permute-start(bf16[4,16,3072]{2,1,0:T(8,128)(2,1)S(1)} %pad_maximum_fusion.args_0_), channel_id=1, source_target_pairs={{0,8},{8,0},{16,24},{24,16},{32,40},{40,32},{48,56},{56,48},{64,72... | collective-permute-start | bytes 1179656 | tf_op jit(solution)/shard_map/ppermute | solution.py:50
  26.3 19.6 %copy-start.7 = (bf16[4,16,3072]{2,1,0:T(8,128)(2,1)}, bf16[4,16,3072]{2,1,0:T(8,128)(2,1)S(1)}, u32[]{:S(2)}) copy-start(bf16[4,16,3072]{2,1,0:T(8,128)(2,1)S(1)} %collective-permute-done.16.args_12_) | copy-start | bytes 1179652
  26.3 10.9 %collective-permute-start.4 = (bf16[4,16,3072]{2,1,0:T(8,128)(2,1)S(1)}, bf16[4,16,3072]{2,1,0:T(8,128)(2,1)S(1)}, u32[]{:S(2)}, u32[]{:S(2)}) collective-permute-start(bf16[4,16,3072]{2,1,0:T(8,128)(2,1)S(1)} %pad_maximum_fusion.args_0_), channel_id=1, source_target_pairs={{0,192},{8,72},{16,208},{24,88},{32,224},{40,104},{48,240},{56,120... | collective-permute-start | bytes 1179656 | tf_op jit(solution)/shard_map/ppermute | solution.py:50
  31.9 13.9 %copy-start.8 = (bf16[4,16,3072]{2,1,0:T(8,128)(2,1)}, bf16[4,16,3072]{2,1,0:T(8,128)(2,1)S(1)}, u32[]{:S(2)}) copy-start(bf16[4,16,3072]{2,1,0:T(8,128)(2,1)S(1)} %collective-permute-done.10.args_6_) | copy-start | bytes 1179652
  31.9 5.8 %collective-permute-start.18 = (bf16[4,16,3072]{2,1,0:T(8,128)(2,1)S(1)}, bf16[4,16,3072]{2,1,0:T(8,128)(2,1)S(1)}, u32[]{:S(2)}, u32[]{:S(2)}) collective-permute-start(bf16[4,16,3072]{2,1,0:T(8,128)(2,1)S(1)} %collective-permute-done.10.args_6_), channel_id=1, source_target_pairs={{0,8},{8,0},{16,24},{24,16},{32,40},{40,32},{48,56},{56,48},{64,72... | collective-permute-start | bytes 1179656 | tf_op jit(solution)/shard_map/ppermute | solution.py:50
  32.6 13.2 %copy-start.9 = (bf16[4,16,3072]{2,1,0:T(8,128)(2,1)}, bf16[4,16,3072]{2,1,0:T(8,128)(2,1)S(1)}, u32[]{:S(2)}) copy-start(bf16[4,16,3072]{2,1,0:T(8,128)(2,1)S(1)} %collective-permute-done.9.args_5_) | copy-start | bytes 1179652
  32.7 9.0 %collective-permute-start.11 = (bf16[4,16,3072]{2,1,0:T(8,128)(2,1)S(1)}, bf16[4,16,3072]{2,1,0:T(8,128)(2,1)S(1)}, u32[]{:S(2)}, u32[]{:S(2)}) collective-permute-start(bf16[4,16,3072]{2,1,0:T(8,128)(2,1)S(1)} %collective-permute-done.9.args_5_), channel_id=1, source_target_pairs={{0,16},{8,56},{16,32},{24,8},{32,48},{40,24},{48,0},{56,40},{64,80... | collective-permute-start | bytes 1179656 | tf_op jit(solution)/shard_map/ppermute | solution.py:50
  34.7 11.2 %copy-start.10 = (bf16[4,16,3072]{2,1,0:T(8,128)(2,1)}, bf16[4,16,3072]{2,1,0:T(8,128)(2,1)S(1)}, u32[]{:S(2)}) copy-start(bf16[4,16,3072]{2,1,0:T(8,128)(2,1)S(1)} %collective-permute-done.3.args_1_) | copy-start | bytes 1179652
  34.7 9.5 %collective-permute-start.5 = (bf16[4,16,3072]{2,1,0:T(8,128)(2,1)S(1)}, bf16[4,16,3072]{2,1,0:T(8,128)(2,1)S(1)}, u32[]{:S(2)}, u32[]{:S(2)}) collective-permute-start(bf16[4,16,3072]{2,1,0:T(8,128)(2,1)S(1)} %collective-permute-done.3.args_1_), channel_id=1, source_target_pairs={{0,64},{8,200},{16,80},{24,216},{32,96},{40,232},{48,112},{56,248}... | collective-permute-start | bytes 1179656 | tf_op jit(solution)/shard_map/ppermute | solution.py:50
  37.2 8.7 %copy-start.11 = (bf16[4,16,3072]{2,1,0:T(8,128)(2,1)}, bf16[4,16,3072]{2,1,0:T(8,128)(2,1)S(1)}, u32[]{:S(2)}) copy-start(bf16[4,16,3072]{2,1,0:T(8,128)(2,1)S(1)} %collective-permute-done.12.args_8_) | copy-start | bytes 1179652
  37.2 6.9 %collective-permute-start.17 = (bf16[4,16,3072]{2,1,0:T(8,128)(2,1)S(1)}, bf16[4,16,3072]{2,1,0:T(8,128)(2,1)S(1)}, u32[]{:S(2)}, u32[]{:S(2)}) collective-permute-start(bf16[4,16,3072]{2,1,0:T(8,128)(2,1)S(1)} %collective-permute-done.9.args_5_), channel_id=1, source_target_pairs={{0,8},{8,0},{16,24},{24,16},{32,40},{40,32},{48,56},{56,48},{64,72... | collective-permute-start | bytes 1179656 | tf_op jit(solution)/shard_map/ppermute | solution.py:50
  37.2 8.7 %copy-start.12 = (bf16[4,16,3072]{2,1,0:T(8,128)(2,1)}, bf16[4,16,3072]{2,1,0:T(8,128)(2,1)S(1)}, u32[]{:S(2)}) copy-start(bf16[4,16,3072]{2,1,0:T(8,128)(2,1)S(1)} %collective-permute-done.4.args_2_) | copy-start | bytes 1179652
  37.2 6.9 %collective-permute-start.13 = (bf16[4,16,3072]{2,1,0:T(8,128)(2,1)S(1)}, bf16[4,16,3072]{2,1,0:T(8,128)(2,1)S(1)}, u32[]{:S(2)}, u32[]{:S(2)}) collective-permute-start(bf16[4,16,3072]{2,1,0:T(8,128)(2,1)S(1)} %collective-permute-done.3.args_1_), channel_id=1, source_target_pairs={{0,8},{8,0},{16,24},{24,16},{32,40},{40,32},{48,56},{56,48},{64,72... | collective-permute-start | bytes 1179656 | tf_op jit(solution)/shard_map/ppermute | solution.py:50
  37.7 6.4 %collective-permute-start.14 = (bf16[4,16,3072]{2,1,0:T(8,128)(2,1)S(1)}, bf16[4,16,3072]{2,1,0:T(8,128)(2,1)S(1)}, u32[]{:S(2)}, u32[]{:S(2)}) collective-permute-start(bf16[4,16,3072]{2,1,0:T(8,128)(2,1)S(1)} %collective-permute-done.4.args_2_), channel_id=1, source_target_pairs={{0,8},{8,0},{16,24},{24,16},{32,40},{40,32},{48,56},{56,48},{64,72... | collective-permute-start | bytes 1179656 | tf_op jit(solution)/shard_map/ppermute | solution.py:50
  41.6 2.5 %collective-permute-start.19 = (bf16[4,16,3072]{2,1,0:T(8,128)(2,1)S(1)}, bf16[4,16,3072]{2,1,0:T(8,128)(2,1)S(1)}, u32[]{:S(2)}, u32[]{:S(2)}) collective-permute-start(bf16[4,16,3072]{2,1,0:T(8,128)(2,1)S(1)} %collective-permute-done.11.args_7_), channel_id=1, source_target_pairs={{0,8},{8,0},{16,24},{24,16},{32,40},{40,32},{48,56},{56,48},{64,72... | collective-permute-start | bytes 1179656 | tf_op jit(solution)/shard_map/ppermute | solution.py:50
  44.1 1.7 %collective-permute-start.15 = (bf16[4,16,3072]{2,1,0:T(8,128)(2,1)S(1)}, bf16[4,16,3072]{2,1,0:T(8,128)(2,1)S(1)}, u32[]{:S(2)}, u32[]{:S(2)}) collective-permute-start(bf16[4,16,3072]{2,1,0:T(8,128)(2,1)S(1)} %collective-permute-done.5.args_3_), channel_id=1, source_target_pairs={{0,8},{8,0},{16,24},{24,16},{32,40},{40,32},{48,56},{56,48},{64,72... | collective-permute-start | bytes 1179656 | tf_op jit(solution)/shard_map/ppermute | solution.py:50
  63.9 1.8 %collective-permute-start.21 = (bf16[4,16,3072]{2,1,0:T(8,128)(2,1)S(1)}, bf16[4,16,3072]{2,1,0:T(8,128)(2,1)S(1)}, u32[]{:S(2)}, u32[]{:S(2)}) collective-permute-start(bf16[4,16,3072]{2,1,0:T(8,128)(2,1)S(1)} %get-tuple-element.30), channel_id=1, source_target_pairs={{0,8},{8,0},{16,24},{24,16},{32,40},{40,32},{48,56},{56,48},{64,72... | collective-permute-start | bytes 1179656 | tf_op jit(solution)/shard_map/ppermute | solution.py:50
  64.2 31.0 %collective-permute-start.20 = (bf16[4,16,3072]{2,1,0:T(8,128)(2,1)S(1)}, bf16[4,16,3072]{2,1,0:T(8,128)(2,1)S(1)}, u32[]{:S(2)}, u32[]{:S(2)}) collective-permute-start(bf16[4,16,3072]{2,1,0:T(8,128)(2,1)S(1)} %get-tuple-element.28), channel_id=1, source_target_pairs={{0,8},{8,0},{16,24},{24,16},{32,40},{40,32},{48,56},{56,48},{64,72... | collective-permute-start | bytes 1179656 | tf_op jit(solution)/shard_map/ppermute | solution.py:50
  64.5 8.1 %collective-permute-start.23 = (bf16[4,16,3072]{2,1,0:T(8,128)(2,1)S(1)}, bf16[4,16,3072]{2,1,0:T(8,128)(2,1)S(1)}, u32[]{:S(2)}, u32[]{:S(2)}) collective-permute-start(bf16[4,16,3072]{2,1,0:T(8,128)(2,1)S(1)} %get-tuple-element.32), channel_id=1, source_target_pairs={{0,8},{8,0},{16,24},{24,16},{32,40},{40,32},{48,56},{56,48},{64,72... | collective-permute-start | bytes 1179656 | tf_op jit(solution)/shard_map/ppermute | solution.py:50
  64.7 2.8 %collective-permute-start.24 = (bf16[4,16,3072]{2,1,0:T(8,128)(2,1)S(1)}, bf16[4,16,3072]{2,1,0:T(8,128)(2,1)S(1)}, u32[]{:S(2)}, u32[]{:S(2)}) collective-permute-start(bf16[4,16,3072]{2,1,0:T(8,128)(2,1)S(1)} %get-tuple-element.34), channel_id=1, source_target_pairs={{0,8},{8,0},{16,24},{24,16},{32,40},{40,32},{48,56},{56,48},{64,72... | collective-permute-start | bytes 1179656 | tf_op jit(solution)/shard_map/ppermute | solution.py:50
  65.0 41.8 %collective-permute-start.30 = (bf16[4,16,3072]{2,1,0:T(8,128)(2,1)S(1)}, bf16[4,16,3072]{2,1,0:T(8,128)(2,1)S(1)}, u32[]{:S(2)}, u32[]{:S(2)}) collective-permute-start(bf16[4,16,3072]{2,1,0:T(8,128)(2,1)S(1)} %get-tuple-element.36), channel_id=1, source_target_pairs={{0,8},{8,0},{16,24},{24,16},{32,40},{40,32},{48,56},{56,48},{64,72... | collective-permute-start | bytes 1179656 | tf_op jit(solution)/shard_map/ppermute | solution.py:50
  65.8 2.8 %collective-permute-start.31 = (bf16[4,16,3072]{2,1,0:T(8,128)(2,1)S(1)}, bf16[4,16,3072]{2,1,0:T(8,128)(2,1)S(1)}, u32[]{:S(2)}, u32[]{:S(2)}) collective-permute-start(bf16[4,16,3072]{2,1,0:T(8,128)(2,1)S(1)} %get-tuple-element.38), channel_id=1, source_target_pairs={{0,8},{8,0},{16,24},{24,16},{32,40},{40,32},{48,56},{56,48},{64,72... | collective-permute-start | bytes 1179656 | tf_op jit(solution)/shard_map/ppermute | solution.py:50
  67.4 18.6 %collective-permute-start.33 = (bf16[4,16,3072]{2,1,0:T(8,128)(2,1)S(1)}, bf16[4,16,3072]{2,1,0:T(8,128)(2,1)S(1)}, u32[]{:S(2)}, u32[]{:S(2)}) collective-permute-start(bf16[4,16,3072]{2,1,0:T(8,128)(2,1)S(1)} %get-tuple-element.40), channel_id=1, source_target_pairs={{0,8},{8,0},{16,24},{24,16},{32,40},{40,32},{48,56},{56,48},{64,72... | collective-permute-start | bytes 1179656 | tf_op jit(solution)/shard_map/ppermute | solution.py:50
  68.6 1.9 %collective-permute-start.34 = (bf16[4,16,3072]{2,1,0:T(8,128)(2,1)}, bf16[4,16,3072]{2,1,0:T(8,128)(2,1)S(1)}, u32[]{:S(2)}, u32[]{:S(2)}) collective-permute-start(bf16[4,16,3072]{2,1,0:T(8,128)(2,1)} %get-tuple-element.42), channel_id=1, source_target_pairs={{0,8},{8,0},{16,24},{24,16},{32,40},{40,32},{48,56},{56,48},{64,72... | collective-permute-start | bytes 1179656 | tf_op jit(solution)/shard_map/ppermute | solution.py:50
  70.5 11.4 %collective-permute-start.25 = (bf16[4,16,3072]{2,1,0:T(8,128)(2,1)S(1)}, bf16[4,16,3072]{2,1,0:T(8,128)(2,1)S(1)}, u32[]{:S(2)}, u32[]{:S(2)}) collective-permute-start(bf16[4,16,3072]{2,1,0:T(8,128)(2,1)S(1)} %add_convert_fusion.8), channel_id=1, source_target_pairs={{0,192},{8,72},{16,208},{24,88},{32,224},{40,104},{48,240},{56,120... | collective-permute-start | bytes 1179656 | tf_op jit(solution)/shard_map/ppermute | solution.py:50
  72.6 26.3 %collective-permute-start.22 = (bf16[4,16,3072]{2,1,0:T(8,128)(2,1)S(1)}, bf16[4,16,3072]{2,1,0:T(8,128)(2,1)S(1)}, u32[]{:S(2)}, u32[]{:S(2)}) collective-permute-start(bf16[4,16,3072]{2,1,0:T(8,128)(2,1)S(1)} %add_convert_fusion.10), channel_id=1, source_target_pairs={{0,64},{8,200},{16,80},{24,216},{32,96},{40,232},{48,112},{56,248}... | collective-permute-start | bytes 1179656 | tf_op jit(solution)/shard_map/ppermute | solution.py:50
  81.9 13.2 %collective-permute-start.35 = (bf16[4,16,3072]{2,1,0:T(8,128)(2,1)S(1)}, bf16[4,16,3072]{2,1,0:T(8,128)(2,1)S(1)}, u32[]{:S(2)}, u32[]{:S(2)}) collective-permute-start(bf16[4,16,3072]{2,1,0:T(8,128)(2,1)S(1)} %add_convert_fusion.2), channel_id=1, source_target_pairs={{0,48},{8,24},{16,0},{24,40},{32,16},{40,56},{48,32},{56,8},{64,11... | collective-permute-start | bytes 1179656 | tf_op jit(solution)/shard_map/ppermute | solution.py:50
  86.1 20.8 %collective-permute-start.32 = (bf16[4,16,3072]{2,1,0:T(8,128)(2,1)S(1)}, bf16[4,16,3072]{2,1,0:T(8,128)(2,1)S(1)}, u32[]{:S(2)}, u32[]{:S(2)}) collective-permute-start(bf16[4,16,3072]{2,1,0:T(8,128)(2,1)S(1)} %add_convert_fusion.4), channel_id=1, source_target_pairs={{0,16},{8,56},{16,32},{24,8},{32,48},{40,24},{48,0},{56,40},{64,80... | collective-permute-start | bytes 1179656 | tf_op jit(solution)/shard_map/ppermute | solution.py:50
  95.0 7.8 %collective-permute-start.26 = (bf16[4,16,3072]{2,1,0:T(8,128)(2,1)S(1)}, bf16[4,16,3072]{2,1,0:T(8,128)(2,1)S(1)}, u32[]{:S(2)}, u32[]{:S(2)}) collective-permute-start(bf16[4,16,3072]{2,1,0:T(8,128)(2,1)S(1)} %add_convert_fusion.7), channel_id=1, source_target_pairs={{0,192},{8,72},{16,208},{24,88},{32,224},{40,104},{48,240},{56,120... | collective-permute-start | bytes 1179656 | tf_op jit(solution)/shard_map/ppermute | solution.py:50
  95.2 11.7 %collective-permute-start.36 = (bf16[4,16,3072]{2,1,0:T(8,128)(2,1)S(1)}, bf16[4,16,3072]{2,1,0:T(8,128)(2,1)S(1)}, u32[]{:S(2)}, u32[]{:S(2)}) collective-permute-start(bf16[4,16,3072]{2,1,0:T(8,128)(2,1)S(1)} %add_convert_fusion.1), channel_id=1, source_target_pairs={{0,48},{8,24},{16,0},{24,40},{32,16},{40,56},{48,32},{56,8},{64,11... | collective-permute-start | bytes 1179656 | tf_op jit(solution)/shard_map/ppermute | solution.py:50
  103.0 13.4 %collective-permute-start.27 = (bf16[16,3072]{1,0:T(8,128)(2,1)S(1)}, bf16[16,3072]{1,0:T(8,128)(2,1)S(1)}, u32[]{:S(2)}, u32[]{:S(2)}) collective-permute-start(bf16[16,3072]{1,0:T(8,128)(2,1)S(1)} %get-tuple-element.43), channel_id=1, source_target_pairs={{0,16},{8,56},{16,32},{24,8},{32,48},{40,24},{48,0},{56,40},{64,80... | collective-permute-start | bytes 294920 | tf_op jit(solution)/shard_map/ppermute | solution.py:50
  103.1 7.3 %collective-permute-start.28 = (bf16[16,3072]{1,0:T(8,128)(2,1)S(1)}, bf16[16,3072]{1,0:T(8,128)(2,1)S(1)}, u32[]{:S(2)}, u32[]{:S(2)}) collective-permute-start(bf16[16,3072]{1,0:T(8,128)(2,1)S(1)} %get-tuple-element.44), channel_id=1, source_target_pairs={{0,48},{8,24},{16,0},{24,40},{32,16},{40,56},{48,32},{56,8},{64,11... | collective-permute-start | bytes 294920 | tf_op jit(solution)/shard_map/ppermute | solution.py:50
  107.1 9.3 %collective-permute-start.37 = (bf16[16,3072]{1,0:T(8,128)(2,1)S(1)}, bf16[16,3072]{1,0:T(8,128)(2,1)S(1)}, u32[]{:S(2)}, u32[]{:S(2)}) collective-permute-start(bf16[16,3072]{1,0:T(8,128)(2,1)S(1)} %get-tuple-element.45), channel_id=1, source_target_pairs={{0,64},{8,200},{16,80},{24,216},{32,96},{40,232},{48,112},{56,248}... | collective-permute-start | bytes 294920 | tf_op jit(solution)/shard_map/ppermute | solution.py:50
  107.6 5.2 %collective-permute-start.38 = (bf16[16,3072]{1,0:T(8,128)(2,1)S(1)}, bf16[16,3072]{1,0:T(8,128)(2,1)S(1)}, u32[]{:S(2)}, u32[]{:S(2)}) collective-permute-start(bf16[16,3072]{1,0:T(8,128)(2,1)S(1)} %get-tuple-element.46), channel_id=1, source_target_pairs={{0,192},{8,72},{16,208},{24,88},{32,224},{40,104},{48,240},{56,120... | collective-permute-start | bytes 294920 | tf_op jit(solution)/shard_map/ppermute | solution.py:50
  110.5 5.9 %collective-permute-start.29 = (bf16[16,3072]{1,0:T(8,128)(2,1)S(1)}, bf16[16,3072]{1,0:T(8,128)(2,1)S(1)}, u32[]{:S(2)}, u32[]{:S(2)}) collective-permute-start(bf16[16,3072]{1,0:T(8,128)(2,1)S(1)} %fusion.3), channel_id=1, source_target_pairs={{0,48},{8,24},{16,0},{24,40},{32,16},{40,56},{48,32},{56,8},{64,11... | collective-permute-start | bytes 294920 | tf_op jit(solution)/shard_map/ppermute | solution.py:50
  112.8 5.7 %collective-permute-start.39 = (bf16[16,3072]{1,0:T(8,128)(2,1)S(1)}, bf16[16,3072]{1,0:T(8,128)(2,1)S(1)}, u32[]{:S(2)}, u32[]{:S(2)}) collective-permute-start(bf16[16,3072]{1,0:T(8,128)(2,1)S(1)} %fusion.1), channel_id=1, source_target_pairs={{0,192},{8,72},{16,208},{24,88},{32,224},{40,104},{48,240},{56,120... | collective-permute-start | bytes 294920 | tf_op jit(solution)/shard_map/ppermute | solution.py:50
  (13 other events, 27.0 us)

commit v2 on v1

v2 whole, which is shorter than its diff:
```python
import jax
import jax.numpy as jnp
from jax import lax
from jax.experimental import pallas as pl
from jax.experimental.pallas import tpu as pltpu
from jax.sharding import PartitionSpec as P

HQ = 48
KVH = 4
HD = 128
GROUP = HQ // KVH
D = HQ * HD
SLOTS = 16
POOL = 1024
HIDDEN = 448
SIDE = 4
PAIR = 2 * SLOTS
CHUNK = 3072


def device(y, x, c):
    return ((y % SIDE) * SIDE + x % SIDE) * 2 + c


def routes():
    out = {name: [] for name in ("sa", "sb", "s2", "ta", "tb", "core")}
    for y in range(SIDE):
        for x in range(SIDE):
            for c in range(2):
                me = device(y, x, c)
                for name, by in (("a", 1), ("b", -1), ("2", 2)):
                    along_x, along_y = device(y, x + by, c), device(y + by, x, c)
                    out["s" + name].append((me, along_x if c == 0 else along_y))
                    if name != "2":
                        out["t" + name].append((me, along_y if c == 0 else along_x))
                out["core"].append((me, device(y, x, 1 - c)))
    return out


ROUTES = routes()


def send(value, route, what):
    with jax.named_scope(what + "_" + route):
        return lax.ppermute(value, "dp", ROUTES[route])


def in_hbm(x):
    return pltpu.with_memory_space_constraint(x, pltpu.HBM)


def attend_kernel(
    counts, lengths_in, q_in, k_in, v_in, gain_in, attended, normed, lengths, q, k, v, gain, sems
):
    copies = [
        pltpu.make_async_copy(a, b, sems.at[i])
        for i, (a, b) in enumerate(
            (
                (lengths_in, lengths),
                (k_in, k),
                (q_in, q),
                (v_in, v),
                (gain_in, gain),
            )
        )
    ]
    for copy in copies:
        copy.start()
    copies[0].wait()
    row = lax.broadcasted_iota(jnp.int32, (SLOTS, 1), 0)
    starts = jnp.zeros((SLOTS, 1), jnp.int32)
    ends = jnp.zeros((SLOTS, 1), jnp.int32)
    at = jnp.int32(0)
    for i in range(SLOTS):
        after = at + lengths[i]
        starts = jnp.where(row == i, at, starts)
        ends = jnp.where(row == i, after, ends)
        at = after
    position = lax.broadcasted_iota(jnp.int32, (SLOTS, POOL), 1)
    inside = (position >= starts) & (position < ends)
    offset = jnp.where(inside, jnp.float32(0.0), jnp.float32(-1e30))
    live = row < counts[0]
    squares = jnp.zeros((SLOTS, HD), jnp.float32)
    copies[1].wait()
    copies[2].wait()
    for kv in range(KVH):
        heads = range(kv * GROUP, (kv + 1) * GROUP)
        rows = jnp.concatenate([q[:, h * HD : (h + 1) * HD] for h in heads], axis=0)
        scores = lax.dot_general(
            rows,
            k[:, kv * HD : (kv + 1) * HD],
            (((1,), (1,)), ((), ())),
            preferred_element_type=jnp.float32,
        )
        masked = scores.reshape(GROUP, SLOTS, POOL) + offset[None]
        top = jnp.max(masked, axis=-1, keepdims=True)
        raised = jnp.exp((masked - top) * jnp.float32(HD ** (-0.5)))
        total = jnp.sum(raised, axis=-1, keepdims=True)
        if kv == 0:
            copies[3].wait()
        mixed = lax.dot_general(
            raised.astype(jnp.bfloat16).reshape(GROUP * SLOTS, POOL),
            v[:, kv * HD : (kv + 1) * HD],
            (((1,), (0,)), ((), ())),
            preferred_element_type=jnp.float32,
        )
        mixed = mixed.reshape(GROUP, SLOTS, HD) / total
        for g, h in enumerate(heads):
            part = jnp.where(live, mixed[g], jnp.float32(0.0)).astype(jnp.bfloat16)
            attended[:, h * HD : (h + 1) * HD] = part
            wide = part.astype(jnp.float32)
            squares = squares + wide * wide
    mean_square = jnp.sum(squares, axis=-1, keepdims=True) / D
    factor = lax.rsqrt(mean_square + 1e-05)
    copies[4].wait()
    normed[...] = (attended[...].astype(jnp.float32) * factor * gain[...]).astype(jnp.bfloat16)


def attend(queries, cache_keys, cache_values, lengths, counts, norm_gain):
    vmem = pl.BlockSpec(memory_space=pltpu.VMEM)
    any_space = pl.BlockSpec(memory_space=pl.ANY)
    return pl.pallas_call(
        attend_kernel,
        out_shape=(jax.ShapeDtypeStruct((SLOTS, D), jnp.bfloat16),) * 2,
        in_specs=[pl.BlockSpec(memory_space=pltpu.SMEM)] + [any_space] * 5,
        out_specs=(vmem, vmem),
        scratch_shapes=[
            pltpu.SMEM((SLOTS,), jnp.int32),
            pltpu.VMEM((SLOTS, D), jnp.bfloat16),
            pltpu.VMEM((POOL, KVH * HD), jnp.bfloat16),
            pltpu.VMEM((POOL, KVH * HD), jnp.bfloat16),
            pltpu.VMEM((1, D), jnp.float32),
            pltpu.SemaphoreType.DMA((5,)),
        ],
        compiler_params=pltpu.CompilerParams(vmem_limit_bytes=16 * 2**20),
        name="attend",
    )(counts, *map(in_hbm, (lengths, queries, cache_keys, cache_values, norm_gain.reshape(1, D))))


def fetch_kernel(up, down, after, up_held, down_held, sems):
    copies = [
        pltpu.make_async_copy(up, up_held, sems.at[0]),
        pltpu.make_async_copy(down, down_held, sems.at[1]),
    ]
    for copy in copies:
        copy.start()
    for copy in copies:
        copy.wait()


def fetch(up_rows, down_rows, after):
    any_space = pl.BlockSpec(memory_space=pl.ANY)
    vmem = pl.BlockSpec(memory_space=pltpu.VMEM)
    return pl.pallas_call(
        fetch_kernel,
        out_shape=[jax.ShapeDtypeStruct((HIDDEN, D), jnp.bfloat16)] * 2,
        in_specs=[any_space] * 3,
        out_specs=[vmem] * 2,
        scratch_shapes=[pltpu.SemaphoreType.DMA((2,))],
        compiler_params=pltpu.CompilerParams(vmem_limit_bytes=16 * 2**20),
        cost_estimate=pl.CostEstimate(flops=0, bytes_accessed=4 * HIDDEN * D, transcendentals=0),
        name="fetch",
    )(in_hbm(up_rows), in_hbm(down_rows), after)


def ffn_kernel(*args):
    blocks, up, down, outs, (total, hidden) = args[:8], args[8:10], args[10:12], args[12:20], args[20:]
    total[...] = jnp.zeros_like(total)

    @pl.loop(0, D // CHUNK)
    def _(step):
        cols = pl.ds(pl.multiple_of(step * CHUNK, CHUNK), CHUNK)
        total[...] += lax.dot_general(
            jnp.concatenate([w[:, cols] for w in up], axis=0),
            jnp.concatenate([b[:, cols] for b in blocks], axis=0),
            (((1,), (1,)), ((), ())),
            preferred_element_type=jnp.float32,
        )

    value = total[...]
    hidden[...] = (value / (1.0 + jnp.exp(-value))).astype(jnp.bfloat16).T

    @pl.loop(0, D // CHUNK)
    def _(step):
        cols = pl.ds(pl.multiple_of(step * CHUNK, CHUNK), CHUNK)
        product = jnp.dot(
            hidden[...],
            jnp.concatenate([w[:, cols] for w in down], axis=0),
            preferred_element_type=jnp.float32,
        ).astype(jnp.bfloat16)
        for i, out in enumerate(outs):
            out[:, cols] = product[i * PAIR : (i + 1) * PAIR]


def feed_forward(blocks, up, down):
    vmem = pl.BlockSpec(memory_space=pltpu.VMEM)
    return pl.pallas_call(
        ffn_kernel,
        out_shape=[jax.ShapeDtypeStruct((PAIR, D), jnp.bfloat16)] * 8,
        in_specs=[vmem] * 12,
        out_specs=[vmem] * 8,
        scratch_shapes=[
            pltpu.VMEM((2 * HIDDEN, 8 * PAIR), jnp.float32),
            pltpu.VMEM((8 * PAIR, 2 * HIDDEN), jnp.bfloat16),
        ],
        compiler_params=pltpu.CompilerParams(vmem_limit_bytes=16 * 2**20),
        name="feed_forward",
    )(*blocks, *up, *down)


def f32(x):
    return x.astype(jnp.float32)


def add(*terms):
    return sum(map(f32, terms)).astype(jnp.bfloat16)


def on_device(
    queries, cache_keys, cache_values, lengths, counts, norm_gain, up_weight, down_weight
):
    up_own, down_own = up_weight.T, down_weight
    up_other = send(up_own, "core", "up")
    down_other = send(down_own, "core", "down")
    attended, normed = attend(queries, cache_keys, cache_values, lengths, counts, norm_gain)
    by_a, by_b, by_2 = [send(normed, r, "gather") for r in ("sa", "sb", "s2")]
    first = jnp.concatenate([normed, by_a], axis=0)
    second = jnp.concatenate([by_b, by_2], axis=0)
    first_a, second_b = send(first, "ta", "gather"), send(second, "tb", "gather")
    first_b, second_a = send(first, "tb", "gather"), send(second, "ta", "gather")
    first_2, second_2 = send(first_a, "ta", "gather2"), send(second_b, "tb", "gather2")
    up_held, down_held = fetch(up_own, down_own, second)
    blocks = [first, second, first_a, second_b, first_b, second_a, first_2, second_2]
    first, second, first_a, second_b, first_b, second_a, first_2, second_2 = feed_forward(
        blocks, (up_held, up_other), (down_held, down_other)
    )
    far_first = send(first_2, "tb", "reduce2")
    far_second = send(second_2, "ta", "reduce2")
    near_first = send(first_b, "ta", "reduce")
    near_second = send(second_a, "tb", "reduce")
    back_first = send(add(first_a, far_first), "tb", "reduce")
    back_second = send(add(second_b, far_second), "ta", "reduce")
    first = f32(first) + f32(near_first) + f32(back_first)
    second = f32(second) + f32(near_second) + f32(back_second)
    home_a = send(first[SLOTS:].astype(jnp.bfloat16), "sb", "home")
    home_b = send(second[:SLOTS].astype(jnp.bfloat16), "sa", "home")
    home_2 = send(second[SLOTS:].astype(jnp.bfloat16), "s2", "home")
    projected = first[:SLOTS] + f32(home_a) + f32(home_b) + f32(home_2)
    return (f32(attended) + projected).astype(jnp.bfloat16)


def solution(mesh):
    in_specs = (
        P(("rep", "dp"), None),
        P(("rep", "dp"), None),
        P(("rep", "dp"), None),
        P(("rep", "dp")),
        P(("rep", "dp")),
        P(),
        P(None, "dp"),
        P("dp", None),
    )
    out_specs = P(("rep", "dp"), None)
    return jax.shard_map(
        on_device, mesh=mesh, in_specs=in_specs, out_specs=out_specs, check_vma=False
    )
```

time: 120 us -> 84.7 us (0.71)
  starting transfers between devices: 42.9 us -> 28.5 us
  waiting for transfers between devices: 48 us -> 39.1 us
  local copies, waits for them, and re-layouts: 5.48 us -> 0.11 us
  Pallas kernels: 19.9 us -> 14.9 us
    ppermute x40 -> x20, starting transfers between devices: 42.9 us -> 28.5 us  [send(): return lax.ppermute(value, 'dp', ROUTES[route])]
    ppermute x40 -> x20, waiting for transfers between devices: 48 us -> 39.1 us  [send(): return lax.ppermute(value, 'dp', ROUTES[route])]
    pallas_call x1 -> x2, Pallas kernels: 17.3 us -> 11.4 us  [the longest x1 7.19 us: feed_forward(): pl.pallas_call(ffn_kernel, out_shape=[jax.ShapeDtypeStruct((PAIR, D), jnp...]
    unnamed x42 -> x2, local copies, waits for them, and re-layouts: 5.45 us -> 0.03 us
  transfers between devices with their start and end apart: 40 -> 20, of which waited for: 17 -> 10; matrix products, arithmetic and copies ran while one was open for 1% -> 1% of each run, Pallas kernels for 0% -> 9%
where the time goes in v2:
time: 84.7 us; the launch traced here: 84.6 us
  waiting for transfers between devices  39.1 us (46%)
  starting transfers between devices  28.5 us (34%)
  Pallas kernels  14.9 us (18%)
  other arithmetic  1.25 us (1%)
    ppermute x20, waiting for transfers between devices, send(): return lax.ppermute(value, 'dp', ROUTES[route])  39.1 us
    ppermute x20, starting transfers between devices, send(): return lax.ppermute(value, 'dp', ROUTES[route])  28.5 us
    pallas_call x1, Pallas kernels, feed_forward(): pl.pallas_call(ffn_kernel, out_shape=[jax.ShapeDtypeStruct((PAIR, D), jnp...  7.19 us
    pallas_call x1, Pallas kernels, fetch(): pl.pallas_call(fetch_kernel, out_shape=[jax.ShapeDtypeStruct((HIDDEN, D),...  4.21 us
    pallas_call x1, Pallas kernels, attend(): pl.pallas_call(attend_kernel, out_shape=(jax.ShapeDtypeStruct((SLOTS, D),...  3.48 us
  transfers between devices with their start and end apart: 20, of which 10 were waited for; matrix products, arithmetic and copies ran while one was open for 1% of the time, Pallas kernels for 9%

profile of v2, /device:TPU:128, one launch (start us, length us, event | category | flops | bytes accessed | tf_op | source)
XLA Modules:
  0.0 84.6 jit_solution(4495839047723158735)
XLA Ops:
  0.0 0.0 collective-permute-start.9
  0.0 0.5 collective-permute-start.10
  1.2 3.5 %attend.1 = (bf16[16,6144]{1,0:T(8,128)(2,1)S(1)}, bf16[16,6144]{1,0:T(8,128)(2,1)S(1)}) custom-call(s32[1]{0:T(128)S(6)} %copy.11.counts, s32[16]{0:T(128)} %lengths_in.1, bf16[16,6144]{1,0:T(8,128)(2,1)} %q_in.1, bf16[1024,512]{1,0:T(8,128)(2,1)} %k_in.1, bf16[1024,512]{1,0:T(8,128)(2,1)} %v_in.1, f32[1,6144]{1,0:T(1,128)} %bitcast.4), custom_call_target="tpu_custom_call" | custom-call | tf_op jit(solution)/shard_map/attend/pallas_call | solution.py:122
  4.6 3.1 %collective-permute-start.2 = (bf16[16,6144]{1,0:T(8,128)(2,1)S(1)}, bf16[16,6144]{1,0:T(8,128)(2,1)S(1)}, u32[]{:S(2)}, u32[]{:S(2)}) collective-permute-start(bf16[16,6144]{1,0:T(8,128)(2,1)S(1)} %get-tuple-element.18), channel_id=1, source_target_pairs={{0,32},{8,136},{16,48},{24,152},{32,0},{40,168},{48,16},{56,184},{... | collective-permute-start | bytes 589832 | tf_op jit(solution)/shard_map/gather_s2/ppermute | solution.py:45
  7.8 1.1 %collective-permute-start.1 = (bf16[16,6144]{1,0:T(8,128)(2,1)S(1)}, bf16[16,6144]{1,0:T(8,128)(2,1)S(1)}, u32[]{:S(2)}, u32[]{:S(2)}) collective-permute-start(bf16[16,6144]{1,0:T(8,128)(2,1)S(1)} %get-tuple-element.18), channel_id=1, source_target_pairs={{0,48},{8,200},{16,0},{24,216},{32,16},{40,232},{48,32},{56,248},{... | collective-permute-start | bytes 589832 | tf_op jit(solution)/shard_map/gather_sb/ppermute | solution.py:45
  8.9 0.9 %collective-permute-start = (bf16[16,6144]{1,0:T(8,128)(2,1)S(1)}, bf16[16,6144]{1,0:T(8,128)(2,1)S(1)}, u32[]{:S(2)}, u32[]{:S(2)}) collective-permute-start(bf16[16,6144]{1,0:T(8,128)(2,1)S(1)} %get-tuple-element.18), channel_id=1, source_target_pairs={{0,16},{8,72},{16,32},{24,88},{32,48},{40,104},{48,0},{56,120},{64... | collective-permute-start | bytes 589832 | tf_op jit(solution)/shard_map/gather_sa/ppermute | solution.py:45
  9.8 6.0 %collective-permute-done = bf16[16,6144]{1,0:T(8,128)(2,1)S(1)} collective-permute-done((bf16[16,6144]{1,0:T(8,128)(2,1)S(1)}, bf16[16,6144]{1,0:T(8,128)(2,1)S(1)}, u32[]{:S(2)}, u32[]{:S(2)}) %collective-permute-start) | collective-permute-done | bytes 196640 | tf_op jit(solution)/shard_map/gather_sa/ppermute | solution.py:45
  15.8 3.1 %collective-permute-start.5 = (bf16[32,6144]{1,0:T(8,128)(2,1)S(1)}, bf16[32,6144]{1,0:T(8,128)(2,1)S(1)}, u32[]{:S(2)}, u32[]{:S(2)}) collective-permute-start(bf16[32,6144]{1,0:T(8,128)(2,1)S(1)} %constant_dynamic-update-slice_fusion.args_0_), channel_id=1, source_target_pairs={{0,192},{8,56},{16,208},{24,8},{32,224},{40,24},{48,240},{56,40},{... | collective-permute-start | bytes 1179656 | tf_op jit(solution)/shard_map/gather_tb/ppermute | solution.py:45
  18.9 0.0 collective-permute-done.1
  18.9 0.0 collective-permute-start.3
  18.9 0.0 collective-permute-done.2
  18.9 3.3 %collective-permute-start.4 = (bf16[32,6144]{1,0:T(8,128)(2,1)S(1)}, bf16[32,6144]{1,0:T(8,128)(2,1)S(1)}, u32[]{:S(2)}, u32[]{:S(2)}) collective-permute-start(bf16[32,6144]{1,0:T(8,128)(2,1)S(1)} %constant_dynamic-update-slice_fusion.2.after.args_1_), channel_id=1, source_target_pairs={{0,192},{8,56},{16,208},{24,8},{32,224},{40,24},{48,240},{56,40},{... | collective-permute-start | bytes 1179656 | tf_op jit(solution)/shard_map/gather_tb/ppermute | solution.py:45
  22.3 1.9 %collective-permute-done.5.args_4_ = bf16[32,6144]{1,0:T(8,128)(2,1)S(1)} collective-permute-done((bf16[32,6144]{1,0:T(8,128)(2,1)S(1)}, bf16[32,6144]{1,0:T(8,128)(2,1)S(1)}, u32[]{:S(2)}, u32[]{:S(2)}) %collective-permute-start.5) | collective-permute-done | bytes 393248 | tf_op jit(solution)/shard_map/gather_tb/ppermute | solution.py:45
  24.2 1.0 %collective-permute-start.6 = (bf16[32,6144]{1,0:T(8,128)(2,1)S(1)}, bf16[32,6144]{1,0:T(8,128)(2,1)S(1)}, u32[]{:S(2)}, u32[]{:S(2)}) collective-permute-start(bf16[32,6144]{1,0:T(8,128)(2,1)S(1)} %constant_dynamic-update-slice_fusion.2.after.args_1_), channel_id=1, source_target_pairs={{0,64},{8,24},{16,80},{24,40},{32,96},{40,56},{48,112},{56,8},{64,... | collective-permute-start | bytes 1179656 | tf_op jit(solution)/shard_map/gather_ta/ppermute | solution.py:45
  25.2 2.7 %collective-permute-done.3.args_2_ = bf16[32,6144]{1,0:T(8,128)(2,1)S(1)} collective-permute-done((bf16[32,6144]{1,0:T(8,128)(2,1)S(1)}, bf16[32,6144]{1,0:T(8,128)(2,1)S(1)}, u32[]{:S(2)}, u32[]{:S(2)}) %collective-permute-start.3) | collective-permute-done | bytes 393248 | tf_op jit(solution)/shard_map/gather_ta/ppermute | solution.py:45
  27.9 0.0 collective-permute-start.7
  27.9 0.5 collective-permute-done.4.args_3_
  28.4 3.7 %collective-permute-start.8 = (bf16[32,6144]{1,0:T(8,128)(2,1)S(1)}, bf16[32,6144]{1,0:T(8,128)(2,1)S(1)}, u32[]{:S(2)}, u32[]{:S(2)}) collective-permute-start(bf16[32,6144]{1,0:T(8,128)(2,1)S(1)} %collective-permute-done.4.args_3_), channel_id=1, source_target_pairs={{0,192},{8,56},{16,208},{24,8},{32,224},{40,24},{48,240},{56,40},{... | collective-permute-start | bytes 1179656 | tf_op jit(solution)/shard_map/gather2_tb/ppermute | solution.py:45
  32.1 4.2 %fetch.1 = (bf16[448,6144]{1,0:T(8,128)(2,1)S(1)}, bf16[448,6144]{1,0:T(8,128)(2,1)S(1)}) custom-call(bf16[448,6144]{1,0:T(8,128)(2,1)} %bitcast.3, bf16[448,6144]{1,0:T(8,128)(2,1)} %down.1, bf16[32,6144]{1,0:T(8,128)(2,1)S(1)} %constant_dynamic-update-slice_fusion.2.after.args_1_), custom_call_target="tpu_custom_call" | custom-call | bytes 11010048 | tf_op jit(solution)/shard_map/fetch/pallas_call | solution.py:154
  36.3 0.0 collective-permute-done.6.args_5_
  36.3 1.5 %collective-permute-done.7.args_6_ = bf16[32,6144]{1,0:T(8,128)(2,1)S(1)} collective-permute-done((bf16[32,6144]{1,0:T(8,128)(2,1)S(1)}, bf16[32,6144]{1,0:T(8,128)(2,1)S(1)}, u32[]{:S(2)}, u32[]{:S(2)}) %collective-permute-start.7) | collective-permute-done | bytes 393248 | tf_op jit(solution)/shard_map/gather2_ta/ppermute | solution.py:45
  37.8 0.0 collective-permute-done.8.args_7_
  37.8 0.0 collective-permute-done.9.args_9_
  37.9 0.0 collective-permute-done.10.args_11_
  37.9 7.2 %feed_forward.1 = (bf16[32,6144]{1,0:T(8,128)(2,1)S(1)}, bf16[32,6144]{1,0:T(8,128)(2,1)S(1)}, bf16[32,6144]{1,0:T(8,128)(2,1)S(1)}, bf16[32,6144]{1,0:T(8,128)(...) custom-call(bf16[32,6144]{1,0:T(8,128)(2,1)S(1)} %constant_dynamic-u, ...), custom_call_target="tpu_custom_call" | custom-call | tf_op jit(solution)/shard_map/feed_forward/pallas_call | solution.py:197
  45.1 3.3 %collective-permute-start.12 = (bf16[32,6144]{1,0:T(8,128)(2,1)S(1)}, bf16[32,6144]{1,0:T(8,128)(2,1)S(1)}, u32[]{:S(2)}, u32[]{:S(2)}) collective-permute-start(bf16[32,6144]{1,0:T(8,128)(2,1)S(1)} %get-tuple-element.24), channel_id=1, source_target_pairs={{0,192},{8,56},{16,208},{24,8},{32,224},{40,24},{48,240},{56,40},{... | collective-permute-start | bytes 1179656 | tf_op jit(solution)/shard_map/reduce2_tb/ppermute | solution.py:45
  48.4 0.0 collective-permute-start.11
  48.4 3.2 %collective-permute-start.15 = (bf16[32,6144]{1,0:T(8,128)(2,1)S(1)}, bf16[32,6144]{1,0:T(8,128)(2,1)S(1)}, u32[]{:S(2)}, u32[]{:S(2)}) collective-permute-start(bf16[32,6144]{1,0:T(8,128)(2,1)S(1)} %get-tuple-element.26), channel_id=1, source_target_pairs={{0,192},{8,56},{16,208},{24,8},{32,224},{40,24},{48,240},{56,40},{... | collective-permute-start | bytes 1179656 | tf_op jit(solution)/shard_map/reduce_tb/ppermute | solution.py:45
  51.6 0.0 collective-permute-start.16
  51.6 2.1 %collective-permute-done.12 = bf16[32,6144]{1,0:T(8,128)(2,1)S(1)} collective-permute-done((bf16[32,6144]{1,0:T(8,128)(2,1)S(1)}, bf16[32,6144]{1,0:T(8,128)(2,1)S(1)}, u32[]{:S(2)}, u32[]{:S(2)}) %collective-permute-start.12) | collective-permute-done | bytes 393248 | tf_op jit(solution)/shard_map/reduce2_tb/ppermute | solution.py:45
  53.7 0.1 add_convert_fusion.2
  53.8 3.8 %collective-permute-start.13 = (bf16[32,6144]{1,0:T(8,128)(2,1)S(1)}, bf16[32,6144]{1,0:T(8,128)(2,1)S(1)}, u32[]{:S(2)}, u32[]{:S(2)}) collective-permute-start(bf16[32,6144]{1,0:T(8,128)(2,1)S(1)} %add_convert_fusion.2), channel_id=1, source_target_pairs={{0,192},{8,56},{16,208},{24,8},{32,224},{40,24},{48,240},{56,40},{... | collective-permute-start | bytes 1179656 | tf_op jit(solution)/shard_map/reduce_tb/ppermute | solution.py:45
  57.5 4.0 %collective-permute-done.16 = bf16[32,6144]{1,0:T(8,128)(2,1)S(1)} collective-permute-done((bf16[32,6144]{1,0:T(8,128)(2,1)S(1)}, bf16[32,6144]{1,0:T(8,128)(2,1)S(1)}, u32[]{:S(2)}, u32[]{:S(2)}) %collective-permute-start.16) | collective-permute-done | bytes 393248 | tf_op jit(solution)/shard_map/reduce2_ta/ppermute | solution.py:45
  61.6 0.1 add_convert_fusion.1
  61.7 0.1 collective-permute-start.17
  61.8 0.0 collective-permute-done.11
  61.8 2.8 %collective-permute-done.13 = bf16[32,6144]{1,0:T(8,128)(2,1)S(1)} collective-permute-done((bf16[32,6144]{1,0:T(8,128)(2,1)S(1)}, bf16[32,6144]{1,0:T(8,128)(2,1)S(1)}, u32[]{:S(2)}, u32[]{:S(2)}) %collective-permute-start.13) | collective-permute-done | bytes 393248 | tf_op jit(solution)/shard_map/reduce_tb/ppermute | solution.py:45
  64.6 0.1 convert_add_fusion
  64.8 0.1 collective-permute-start.14
  64.9 0.0 collective-permute-done.15
  64.9 9.7 %collective-permute-done.17 = bf16[32,6144]{1,0:T(8,128)(2,1)S(1)} collective-permute-done((bf16[32,6144]{1,0:T(8,128)(2,1)S(1)}, bf16[32,6144]{1,0:T(8,128)(2,1)S(1)}, u32[]{:S(2)}, u32[]{:S(2)}) %collective-permute-start.17) | collective-permute-done | bytes 393248 | tf_op jit(solution)/shard_map/reduce_ta/ppermute | solution.py:45
  74.6 0.1 add_convert_fusion
  74.8 0.2 collective-permute-start.18
  74.9 1.0 %collective-permute-start.19 = (bf16[16,6144]{1,0:T(8,128)(2,1)S(1)}, bf16[16,6144]{1,0:T(8,128)(2,1)S(1)}, u32[]{:S(2)}, u32[]{:S(2)}) collective-permute-start(bf16[16,6144]{1,0:T(8,128)(2,1)S(1)} %get-tuple-element.30), channel_id=1, source_target_pairs={{0,32},{8,136},{16,48},{24,152},{32,0},{40,168},{48,16},{56,184},{... | collective-permute-start | bytes 589832 | tf_op jit(solution)/shard_map/home_s2/ppermute | solution.py:45
  75.9 0.0 collective-permute-done.14
  76.0 7.9 %collective-permute-done.18 = bf16[16,6144]{1,0:T(8,128)(2,1)S(1)} collective-permute-done((bf16[16,6144]{1,0:T(8,128)(2,1)S(1)}, bf16[16,6144]{1,0:T(8,128)(2,1)S(1)}, u32[]{:S(2)}, u32[]{:S(2)}) %collective-permute-start.18) | collective-permute-done | bytes 196640 | tf_op jit(solution)/shard_map/home_sa/ppermute | solution.py:45
  83.8 0.0 collective-permute-done.19
  83.8 0.8 fusion.3
  (6 shorter events, 0.1 us)
Async XLA Ops:
  0.0 37.9 %collective-permute-start.9 = (bf16[448,6144]{1,0:T(8,128)(2,1)}, bf16[448,6144]{1,0:T(8,128)(2,1)S(1)}, u32[]{:S(2)}, u32[]{:S(2)}) collective-permute-start(bf16[448,6144]{1,0:T(8,128)(2,1)} %bitcast.2), channel_id=1, source_target_pairs={{0,8},{8,0},{16,24},{24,16},{32,40},{40,32},{48,56},{56,48},{64,72... | collective-permute-start | bytes 16515080 | tf_op jit(solution)/shard_map/up_core/ppermute | solution.py:45
  0.0 37.9 %collective-permute-start.10 = (bf16[448,6144]{1,0:T(8,128)(2,1)}, bf16[448,6144]{1,0:T(8,128)(2,1)S(1)}, u32[]{:S(2)}, u32[]{:S(2)}) collective-permute-start(bf16[448,6144]{1,0:T(8,128)(2,1)} %down.1), channel_id=1, source_target_pairs={{0,8},{8,0},{16,24},{24,16},{32,40},{40,32},{48,56},{56,48},{64,72... | collective-permute-start | bytes 16515080 | tf_op jit(solution)/shard_map/down_core/ppermute | solution.py:45
  4.6 14.3 %collective-permute-start.2 = (bf16[16,6144]{1,0:T(8,128)(2,1)S(1)}, bf16[16,6144]{1,0:T(8,128)(2,1)S(1)}, u32[]{:S(2)}, u32[]{:S(2)}) collective-permute-start(bf16[16,6144]{1,0:T(8,128)(2,1)S(1)} %get-tuple-element.18), channel_id=1, source_target_pairs={{0,32},{8,136},{16,48},{24,152},{32,0},{40,168},{48,16},{56,184},{... | collective-permute-start | bytes 589832 | tf_op jit(solution)/shard_map/gather_s2/ppermute | solution.py:45
  7.8 11.1 %collective-permute-start.1 = (bf16[16,6144]{1,0:T(8,128)(2,1)S(1)}, bf16[16,6144]{1,0:T(8,128)(2,1)S(1)}, u32[]{:S(2)}, u32[]{:S(2)}) collective-permute-start(bf16[16,6144]{1,0:T(8,128)(2,1)S(1)} %get-tuple-element.18), channel_id=1, source_target_pairs={{0,48},{8,200},{16,0},{24,216},{32,16},{40,232},{48,32},{56,248},{... | collective-permute-start | bytes 589832 | tf_op jit(solution)/shard_map/gather_sb/ppermute | solution.py:45
  8.9 6.9 %collective-permute-start = (bf16[16,6144]{1,0:T(8,128)(2,1)S(1)}, bf16[16,6144]{1,0:T(8,128)(2,1)S(1)}, u32[]{:S(2)}, u32[]{:S(2)}) collective-permute-start(bf16[16,6144]{1,0:T(8,128)(2,1)S(1)} %get-tuple-element.18), channel_id=1, source_target_pairs={{0,16},{8,72},{16,32},{24,88},{32,48},{40,104},{48,0},{56,120},{64... | collective-permute-start | bytes 589832 | tf_op jit(solution)/shard_map/gather_sa/ppermute | solution.py:45
  15.8 8.4 %collective-permute-start.5 = (bf16[32,6144]{1,0:T(8,128)(2,1)S(1)}, bf16[32,6144]{1,0:T(8,128)(2,1)S(1)}, u32[]{:S(2)}, u32[]{:S(2)}) collective-permute-start(bf16[32,6144]{1,0:T(8,128)(2,1)S(1)} %constant_dynamic-update-slice_fusion.args_0_), channel_id=1, source_target_pairs={{0,192},{8,56},{16,208},{24,8},{32,224},{40,24},{48,240},{56,40},{... | collective-permute-start | bytes 1179656 | tf_op jit(solution)/shard_map/gather_tb/ppermute | solution.py:45
  18.9 9.0 %collective-permute-start.3 = (bf16[32,6144]{1,0:T(8,128)(2,1)S(1)}, bf16[32,6144]{1,0:T(8,128)(2,1)S(1)}, u32[]{:S(2)}, u32[]{:S(2)}) collective-permute-start(bf16[32,6144]{1,0:T(8,128)(2,1)S(1)} %constant_dynamic-update-slice_fusion.args_0_), channel_id=1, source_target_pairs={{0,64},{8,24},{16,80},{24,40},{32,96},{40,56},{48,112},{56,8},{64,... | collective-permute-start | bytes 1179656 | tf_op jit(solution)/shard_map/gather_ta/ppermute | solution.py:45
  18.9 9.4 %collective-permute-start.4 = (bf16[32,6144]{1,0:T(8,128)(2,1)S(1)}, bf16[32,6144]{1,0:T(8,128)(2,1)S(1)}, u32[]{:S(2)}, u32[]{:S(2)}) collective-permute-start(bf16[32,6144]{1,0:T(8,128)(2,1)S(1)} %constant_dynamic-update-slice_fusion.2.after.args_1_), channel_id=1, source_target_pairs={{0,192},{8,56},{16,208},{24,8},{32,224},{40,24},{48,240},{56,40},{... | collective-permute-start | bytes 1179656 | tf_op jit(solution)/shard_map/gather_tb/ppermute | solution.py:45
  24.2 12.1 %collective-permute-start.6 = (bf16[32,6144]{1,0:T(8,128)(2,1)S(1)}, bf16[32,6144]{1,0:T(8,128)(2,1)S(1)}, u32[]{:S(2)}, u32[]{:S(2)}) collective-permute-start(bf16[32,6144]{1,0:T(8,128)(2,1)S(1)} %constant_dynamic-update-slice_fusion.2.after.args_1_), channel_id=1, source_target_pairs={{0,64},{8,24},{16,80},{24,40},{32,96},{40,56},{48,112},{56,8},{64,... | collective-permute-start | bytes 1179656 | tf_op jit(solution)/shard_map/gather_ta/ppermute | solution.py:45
  27.9 10.0 %collective-permute-start.7 = (bf16[32,6144]{1,0:T(8,128)(2,1)S(1)}, bf16[32,6144]{1,0:T(8,128)(2,1)S(1)}, u32[]{:S(2)}, u32[]{:S(2)}) collective-permute-start(bf16[32,6144]{1,0:T(8,128)(2,1)S(1)} %collective-permute-done.3.args_2_), channel_id=1, source_target_pairs={{0,64},{8,24},{16,80},{24,40},{32,96},{40,56},{48,112},{56,8},{64,... | collective-permute-start | bytes 1179656 | tf_op jit(solution)/shard_map/gather2_ta/ppermute | solution.py:45
  28.4 9.4 %collective-permute-start.8 = (bf16[32,6144]{1,0:T(8,128)(2,1)S(1)}, bf16[32,6144]{1,0:T(8,128)(2,1)S(1)}, u32[]{:S(2)}, u32[]{:S(2)}) collective-permute-start(bf16[32,6144]{1,0:T(8,128)(2,1)S(1)} %collective-permute-done.4.args_3_), channel_id=1, source_target_pairs={{0,192},{8,56},{16,208},{24,8},{32,224},{40,24},{48,240},{56,40},{... | collective-permute-start | bytes 1179656 | tf_op jit(solution)/shard_map/gather2_tb/ppermute | solution.py:45
  45.1 8.6 %collective-permute-start.12 = (bf16[32,6144]{1,0:T(8,128)(2,1)S(1)}, bf16[32,6144]{1,0:T(8,128)(2,1)S(1)}, u32[]{:S(2)}, u32[]{:S(2)}) collective-permute-start(bf16[32,6144]{1,0:T(8,128)(2,1)S(1)} %get-tuple-element.24), channel_id=1, source_target_pairs={{0,192},{8,56},{16,208},{24,8},{32,224},{40,24},{48,240},{56,40},{... | collective-permute-start | bytes 1179656 | tf_op jit(solution)/shard_map/reduce2_tb/ppermute | solution.py:45
  48.4 13.4 %collective-permute-start.11 = (bf16[32,6144]{1,0:T(8,128)(2,1)S(1)}, bf16[32,6144]{1,0:T(8,128)(2,1)S(1)}, u32[]{:S(2)}, u32[]{:S(2)}) collective-permute-start(bf16[32,6144]{1,0:T(8,128)(2,1)S(1)} %get-tuple-element.22), channel_id=1, source_target_pairs={{0,64},{8,24},{16,80},{24,40},{32,96},{40,56},{48,112},{56,8},{64,... | collective-permute-start | bytes 1179656 | tf_op jit(solution)/shard_map/reduce_ta/ppermute | solution.py:45
  48.4 16.5 %collective-permute-start.15 = (bf16[32,6144]{1,0:T(8,128)(2,1)S(1)}, bf16[32,6144]{1,0:T(8,128)(2,1)S(1)}, u32[]{:S(2)}, u32[]{:S(2)}) collective-permute-start(bf16[32,6144]{1,0:T(8,128)(2,1)S(1)} %get-tuple-element.26), channel_id=1, source_target_pairs={{0,192},{8,56},{16,208},{24,8},{32,224},{40,24},{48,240},{56,40},{... | collective-permute-start | bytes 1179656 | tf_op jit(solution)/shard_map/reduce_tb/ppermute | solution.py:45
  51.6 10.0 %collective-permute-start.16 = (bf16[32,6144]{1,0:T(8,128)(2,1)S(1)}, bf16[32,6144]{1,0:T(8,128)(2,1)S(1)}, u32[]{:S(2)}, u32[]{:S(2)}) collective-permute-start(bf16[32,6144]{1,0:T(8,128)(2,1)S(1)} %get-tuple-element.28), channel_id=1, source_target_pairs={{0,64},{8,24},{16,80},{24,40},{32,96},{40,56},{48,112},{56,8},{64,... | collective-permute-start | bytes 1179656 | tf_op jit(solution)/shard_map/reduce2_ta/ppermute | solution.py:45
  53.8 10.9 %collective-permute-start.13 = (bf16[32,6144]{1,0:T(8,128)(2,1)S(1)}, bf16[32,6144]{1,0:T(8,128)(2,1)S(1)}, u32[]{:S(2)}, u32[]{:S(2)}) collective-permute-start(bf16[32,6144]{1,0:T(8,128)(2,1)S(1)} %add_convert_fusion.2), channel_id=1, source_target_pairs={{0,192},{8,56},{16,208},{24,8},{32,224},{40,24},{48,240},{56,40},{... | collective-permute-start | bytes 1179656 | tf_op jit(solution)/shard_map/reduce_tb/ppermute | solution.py:45
  61.7 12.9 %collective-permute-start.17 = (bf16[32,6144]{1,0:T(8,128)(2,1)S(1)}, bf16[32,6144]{1,0:T(8,128)(2,1)S(1)}, u32[]{:S(2)}, u32[]{:S(2)}) collective-permute-start(bf16[32,6144]{1,0:T(8,128)(2,1)S(1)} %add_convert_fusion.1), channel_id=1, source_target_pairs={{0,64},{8,24},{16,80},{24,40},{32,96},{40,56},{48,112},{56,8},{64,... | collective-permute-start | bytes 1179656 | tf_op jit(solution)/shard_map/reduce_ta/ppermute | solution.py:45
  64.8 11.2 %collective-permute-start.14 = (bf16[16,6144]{1,0:T(8,128)(2,1)S(1)}, bf16[16,6144]{1,0:T(8,128)(2,1)S(1)}, u32[]{:S(2)}, u32[]{:S(2)}) collective-permute-start(bf16[16,6144]{1,0:T(8,128)(2,1)S(1)} %slice.33), channel_id=1, source_target_pairs={{0,48},{8,200},{16,0},{24,216},{32,16},{40,232},{48,32},{56,248},{... | collective-permute-start | bytes 589832 | tf_op jit(solution)/shard_map/home_sb/ppermute | solution.py:45
  74.8 9.1 %collective-permute-start.18 = (bf16[16,6144]{1,0:T(8,128)(2,1)S(1)}, bf16[16,6144]{1,0:T(8,128)(2,1)S(1)}, u32[]{:S(2)}, u32[]{:S(2)}) collective-permute-start(bf16[16,6144]{1,0:T(8,128)(2,1)S(1)} %get-tuple-element.29), channel_id=1, source_target_pairs={{0,16},{8,72},{16,32},{24,88},{32,48},{40,104},{48,0},{56,120},{64... | collective-permute-start | bytes 589832 | tf_op jit(solution)/shard_map/home_sa/ppermute | solution.py:45
  74.9 8.9 %collective-permute-start.19 = (bf16[16,6144]{1,0:T(8,128)(2,1)S(1)}, bf16[16,6144]{1,0:T(8,128)(2,1)S(1)}, u32[]{:S(2)}, u32[]{:S(2)}) collective-permute-start(bf16[16,6144]{1,0:T(8,128)(2,1)S(1)} %get-tuple-element.30), channel_id=1, source_target_pairs={{0,32},{8,136},{16,48},{24,152},{32,0},{40,168},{48,16},{56,184},{... | collective-permute-start | bytes 589832 | tf_op jit(solution)/shard_map/home_s2/ppermute | solution.py:45

commit v3 on v2

--- a/solution.py
+++ b/solution.py
@@ -19,20 +19,20 @@
 
 
 def device(y, x, c):
-    return ((y % SIDE) * SIDE + x % SIDE) * 2 + c
+    return (y * SIDE + x) * 2 + c
 
 
 def routes():
-    out = {name: [] for name in ("sa", "sb", "s2", "ta", "tb", "core")}
+    other = {"near": (1, 0, 3, 2), "wrap": (3, 2, 1, 0), "far": (2, 3, 0, 1)}
+    out = {"core": [], **{axis + name: [] for axis in "st" for name in other}}
     for y in range(SIDE):
         for x in range(SIDE):
             for c in range(2):
                 me = device(y, x, c)
-                for name, by in (("a", 1), ("b", -1), ("2", 2)):
-                    along_x, along_y = device(y, x + by, c), device(y + by, x, c)
+                for name, to in other.items():
+                    along_x, along_y = device(y, to[x], c), device(to[y], x, c)
                     out["s" + name].append((me, along_x if c == 0 else along_y))
-                    if name != "2":
-                        out["t" + name].append((me, along_y if c == 0 else along_x))
+                    out["t" + name].append((me, along_y if c == 0 else along_x))
                 out["core"].append((me, device(y, x, 1 - c)))
     return out
 
@@ -223,29 +223,29 @@
     up_other = send(up_own, "core", "up")
     down_other = send(down_own, "core", "down")
     attended, normed = attend(queries, cache_keys, cache_values, lengths, counts, norm_gain)
-    by_a, by_b, by_2 = [send(normed, r, "gather") for r in ("sa", "sb", "s2")]
-    first = jnp.concatenate([normed, by_a], axis=0)
-    second = jnp.concatenate([by_b, by_2], axis=0)
-    first_a, second_b = send(first, "ta", "gather"), send(second, "tb", "gather")
-    first_b, second_a = send(first, "tb", "gather"), send(second, "ta", "gather")
-    first_2, second_2 = send(first_a, "ta", "gather2"), send(second_b, "tb", "gather2")
+    by_wrap, by_far, by_near = [send(normed, r, "gather") for r in ("swrap", "sfar", "snear")]
+    first = jnp.concatenate([normed, by_near], axis=0)
+    second = jnp.concatenate([by_wrap, by_far], axis=0)
+    first_w, second_n = send(first, "twrap", "gather"), send(second, "tnear", "gather")
+    second_w, first_n = send(second, "twrap", "gather"), send(first, "tnear", "gather")
+    first_f, second_f = send(first_w, "tnear", "gather2"), send(second_n, "twrap", "gather2")
     up_held, down_held = fetch(up_own, down_own, second)
-    blocks = [first, second, first_a, second_b, first_b, second_a, first_2, second_2]
-    first, second, first_a, second_b, first_b, second_a, first_2, second_2 = feed_forward(
+    blocks = [first, second, first_w, second_n, first_n, second_w, first_f, second_f]
+    first, second, first_w, second_n, first_n, second_w, first_f, second_f = feed_forward(
         blocks, (up_held, up_other), (down_held, down_other)
     )
-    far_first = send(first_2, "tb", "reduce2")
-    far_second = send(second_2, "ta", "reduce2")
-    near_first = send(first_b, "ta", "reduce")
-    near_second = send(second_a, "tb", "reduce")
-    back_first = send(add(first_a, far_first), "tb", "reduce")
-    back_second = send(add(second_b, far_second), "ta", "reduce")
+    far_first = send(first_f, "tnear", "reduce2")
+    far_second = send(second_f, "twrap", "reduce2")
+    near_first = send(first_n, "tnear", "reduce")
+    near_second = send(second_w, "twrap", "reduce")
+    back_first = send(add(first_w, far_first), "twrap", "reduce")
+    back_second = send(add(second_n, far_second), "tnear", "reduce")
     first = f32(first) + f32(near_first) + f32(back_first)
     second = f32(second) + f32(near_second) + f32(back_second)
-    home_a = send(first[SLOTS:].astype(jnp.bfloat16), "sb", "home")
-    home_b = send(second[:SLOTS].astype(jnp.bfloat16), "sa", "home")
-    home_2 = send(second[SLOTS:].astype(jnp.bfloat16), "s2", "home")
-    projected = first[:SLOTS] + f32(home_a) + f32(home_b) + f32(home_2)
+    home_near = send(first[SLOTS:].astype(jnp.bfloat16), "snear", "home")
+    home_wrap = send(second[:SLOTS].astype(jnp.bfloat16), "swrap", "home")
+    home_far = send(second[SLOTS:].astype(jnp.bfloat16), "sfar", "home")
+    projected = first[:SLOTS] + f32(home_near) + f32(home_wrap) + f32(home_far)
     return (f32(attended) + projected).astype(jnp.bfloat16)
 
 

time: 84.7 us -> 80 us (0.945)
  waiting for transfers between devices: 39.1 us -> 34.9 us
    ppermute x20, waiting for transfers between devices: 39.1 us -> 34.9 us  [send(): return lax.ppermute(value, 'dp', ROUTES[route])]
  transfers between devices with their start and end apart: 20 -> 20, of which waited for: 10 -> 10; matrix products, arithmetic and copies ran while one was open for 1% -> 1% of each run, Pallas kernels for 9% -> 10%
where the time goes in v3:
time: 80 us; the launch traced here: 79.9 us
  waiting for transfers between devices  34.9 us (44%)
  starting transfers between devices  28 us (35%)
  Pallas kernels  14.9 us (19%)
  other arithmetic  1.25 us (2%)
    ppermute x20, waiting for transfers between devices, send(): return lax.ppermute(value, 'dp', ROUTES[route])  34.9 us
    ppermute x20, starting transfers between devices, send(): return lax.ppermute(value, 'dp', ROUTES[route])  28 us
    pallas_call x1, Pallas kernels, feed_forward(): pl.pallas_call(ffn_kernel, out_shape=[jax.ShapeDtypeStruct((PAIR, D), jnp...  7.2 us
    pallas_call x1, Pallas kernels, fetch(): pl.pallas_call(fetch_kernel, out_shape=[jax.ShapeDtypeStruct((HIDDEN, D),...  4.21 us
    pallas_call x1, Pallas kernels, attend(): pl.pallas_call(attend_kernel, out_shape=(jax.ShapeDtypeStruct((SLOTS, D),...  3.48 us
  transfers between devices with their start and end apart: 20, of which 10 were waited for; matrix products, arithmetic and copies ran while one was open for 1% of the time, Pallas kernels for 10%

profile of v3, /device:TPU:128, one launch (start us, length us, event | category | flops | bytes accessed | tf_op | source)
XLA Modules:
  0.0 79.9 jit_solution(297698279202669939)
XLA Ops:
  0.0 0.0 collective-permute-start.9
  0.0 0.5 collective-permute-start.10
  1.2 3.5 %attend.1 = (bf16[16,6144]{1,0:T(8,128)(2,1)S(1)}, bf16[16,6144]{1,0:T(8,128)(2,1)S(1)}) custom-call(s32[1]{0:T(128)S(6)} %copy.11.counts, s32[16]{0:T(128)} %lengths_in.1, bf16[16,6144]{1,0:T(8,128)(2,1)} %q_in.1, bf16[1024,512]{1,0:T(8,128)(2,1)} %k_in.1, bf16[1024,512]{1,0:T(8,128)(2,1)} %v_in.1, f32[1,6144]{1,0:T(1,128)} %bitcast.4), custom_call_target="tpu_custom_call" | custom-call | tf_op jit(solution)/shard_map/attend/pallas_call | solution.py:122
  4.6 3.1 %collective-permute-start.2 = (bf16[16,6144]{1,0:T(8,128)(2,1)S(1)}, bf16[16,6144]{1,0:T(8,128)(2,1)S(1)}, u32[]{:S(2)}, u32[]{:S(2)}) collective-permute-start(bf16[16,6144]{1,0:T(8,128)(2,1)S(1)} %get-tuple-element.18), channel_id=1, source_target_pairs={{0,32},{8,136},{16,48},{24,152},{32,0},{40,168},{48,16},{56,184},{... | collective-permute-start | bytes 589832 | tf_op jit(solution)/shard_map/gather_sfar/ppermute | solution.py:45
  7.8 1.1 %collective-permute-start.1 = (bf16[16,6144]{1,0:T(8,128)(2,1)S(1)}, bf16[16,6144]{1,0:T(8,128)(2,1)S(1)}, u32[]{:S(2)}, u32[]{:S(2)}) collective-permute-start(bf16[16,6144]{1,0:T(8,128)(2,1)S(1)} %get-tuple-element.18), channel_id=1, source_target_pairs={{0,48},{8,200},{16,32},{24,216},{32,16},{40,232},{48,0},{56,248},{... | collective-permute-start | bytes 589832 | tf_op jit(solution)/shard_map/gather_swrap/ppermute | solution.py:45
  8.9 0.0 collective-permute-start
  8.9 5.6 %collective-permute-done = bf16[16,6144]{1,0:T(8,128)(2,1)S(1)} collective-permute-done((bf16[16,6144]{1,0:T(8,128)(2,1)S(1)}, bf16[16,6144]{1,0:T(8,128)(2,1)S(1)}, u32[]{:S(2)}, u32[]{:S(2)}) %collective-permute-start) | collective-permute-done | bytes 196640 | tf_op jit(solution)/shard_map/gather_snear/ppermute | solution.py:45
  14.6 1.7 %collective-permute-start.5 = (bf16[32,6144]{1,0:T(8,128)(2,1)S(1)}, bf16[32,6144]{1,0:T(8,128)(2,1)S(1)}, u32[]{:S(2)}, u32[]{:S(2)}) collective-permute-start(bf16[32,6144]{1,0:T(8,128)(2,1)S(1)} %constant_dynamic-update-slice_fusion.args_0_), channel_id=1, source_target_pairs={{0,64},{8,24},{16,80},{24,8},{32,96},{40,56},{48,112},{56,40},{64,... | collective-permute-start | bytes 1179656 | tf_op jit(solution)/shard_map/gather_tnear/ppermute | solution.py:45
  16.3 0.0 collective-permute-done.1
  16.3 2.2 %collective-permute-start.3 = (bf16[32,6144]{1,0:T(8,128)(2,1)S(1)}, bf16[32,6144]{1,0:T(8,128)(2,1)S(1)}, u32[]{:S(2)}, u32[]{:S(2)}) collective-permute-start(bf16[32,6144]{1,0:T(8,128)(2,1)S(1)} %constant_dynamic-update-slice_fusion.args_0_), channel_id=1, source_target_pairs={{0,192},{8,56},{16,208},{24,40},{32,224},{40,24},{48,240},{56,8},{... | collective-permute-start | bytes 1179656 | tf_op jit(solution)/shard_map/gather_twrap/ppermute | solution.py:45
  18.5 0.0 collective-permute-done.2
  18.5 0.8 collective-permute-start.4
  19.3 3.2 %collective-permute-done.5.args_4_ = bf16[32,6144]{1,0:T(8,128)(2,1)S(1)} collective-permute-done((bf16[32,6144]{1,0:T(8,128)(2,1)S(1)}, bf16[32,6144]{1,0:T(8,128)(2,1)S(1)}, u32[]{:S(2)}, u32[]{:S(2)}) %collective-permute-start.5) | collective-permute-done | bytes 393248 | tf_op jit(solution)/shard_map/gather_tnear/ppermute | solution.py:45
  22.5 3.0 %collective-permute-start.6 = (bf16[32,6144]{1,0:T(8,128)(2,1)S(1)}, bf16[32,6144]{1,0:T(8,128)(2,1)S(1)}, u32[]{:S(2)}, u32[]{:S(2)}) collective-permute-start(bf16[32,6144]{1,0:T(8,128)(2,1)S(1)} %constant_dynamic-update-slice_fusion.2.after.args_1_), channel_id=1, source_target_pairs={{0,192},{8,56},{16,208},{24,40},{32,224},{40,24},{48,240},{56,8},{... | collective-permute-start | bytes 1179656 | tf_op jit(solution)/shard_map/gather_twrap/ppermute | solution.py:45
  25.5 0.0 collective-permute-done.3.args_2_
  25.5 0.1 collective-permute-start.7
  25.6 1.1 %collective-permute-done.4.args_3_ = bf16[32,6144]{1,0:T(8,128)(2,1)S(1)} collective-permute-done((bf16[32,6144]{1,0:T(8,128)(2,1)S(1)}, bf16[32,6144]{1,0:T(8,128)(2,1)S(1)}, u32[]{:S(2)}, u32[]{:S(2)}) %collective-permute-start.4) | collective-permute-done | bytes 393248 | tf_op jit(solution)/shard_map/gather_tnear/ppermute | solution.py:45
  26.7 3.0 %collective-permute-start.8 = (bf16[32,6144]{1,0:T(8,128)(2,1)S(1)}, bf16[32,6144]{1,0:T(8,128)(2,1)S(1)}, u32[]{:S(2)}, u32[]{:S(2)}) collective-permute-start(bf16[32,6144]{1,0:T(8,128)(2,1)S(1)} %collective-permute-done.4.args_3_), channel_id=1, source_target_pairs={{0,192},{8,56},{16,208},{24,40},{32,224},{40,24},{48,240},{56,8},{... | collective-permute-start | bytes 1179656 | tf_op jit(solution)/shard_map/gather2_twrap/ppermute | solution.py:45
  29.7 4.2 %fetch.1 = (bf16[448,6144]{1,0:T(8,128)(2,1)S(1)}, bf16[448,6144]{1,0:T(8,128)(2,1)S(1)}) custom-call(bf16[448,6144]{1,0:T(8,128)(2,1)} %bitcast.3, bf16[448,6144]{1,0:T(8,128)(2,1)} %down.1, bf16[32,6144]{1,0:T(8,128)(2,1)S(1)} %constant_dynamic-update-slice_fusion.2.after.args_1_), custom_call_target="tpu_custom_call" | custom-call | bytes 11010048 | tf_op jit(solution)/shard_map/fetch/pallas_call | solution.py:154
  33.9 0.0 collective-permute-done.6.args_5_
  33.9 0.0 collective-permute-done.7.args_6_
  33.9 1.7 %collective-permute-done.8.args_7_ = bf16[32,6144]{1,0:T(8,128)(2,1)S(1)} collective-permute-done((bf16[32,6144]{1,0:T(8,128)(2,1)S(1)}, bf16[32,6144]{1,0:T(8,128)(2,1)S(1)}, u32[]{:S(2)}, u32[]{:S(2)}) %collective-permute-start.8) | collective-permute-done | bytes 393248 | tf_op jit(solution)/shard_map/gather2_twrap/ppermute | solution.py:45
  35.7 0.0 collective-permute-done.9.args_9_
  35.7 0.0 collective-permute-done.10.args_11_
  35.7 7.2 %feed_forward.1 = (bf16[32,6144]{1,0:T(8,128)(2,1)S(1)}, bf16[32,6144]{1,0:T(8,128)(2,1)S(1)}, bf16[32,6144]{1,0:T(8,128)(2,1)S(1)}, bf16[32,6144]{1,0:T(8,128)(...) custom-call(bf16[32,6144]{1,0:T(8,128)(2,1)S(1)} %constant_dynamic-u, ...), custom_call_target="tpu_custom_call" | custom-call | tf_op jit(solution)/shard_map/feed_forward/pallas_call | solution.py:197
  42.9 0.4 collective-permute-start.12
  43.3 1.7 %collective-permute-start.11 = (bf16[32,6144]{1,0:T(8,128)(2,1)S(1)}, bf16[32,6144]{1,0:T(8,128)(2,1)S(1)}, u32[]{:S(2)}, u32[]{:S(2)}) collective-permute-start(bf16[32,6144]{1,0:T(8,128)(2,1)S(1)} %get-tuple-element.22), channel_id=1, source_target_pairs={{0,64},{8,24},{16,80},{24,8},{32,96},{40,56},{48,112},{56,40},{64,... | collective-permute-start | bytes 1179656 | tf_op jit(solution)/shard_map/reduce_tnear/ppermute | solution.py:45
  45.0 3.0 %collective-permute-start.15 = (bf16[32,6144]{1,0:T(8,128)(2,1)S(1)}, bf16[32,6144]{1,0:T(8,128)(2,1)S(1)}, u32[]{:S(2)}, u32[]{:S(2)}) collective-permute-start(bf16[32,6144]{1,0:T(8,128)(2,1)S(1)} %get-tuple-element.26), channel_id=1, source_target_pairs={{0,192},{8,56},{16,208},{24,40},{32,224},{40,24},{48,240},{56,8},{... | collective-permute-start | bytes 1179656 | tf_op jit(solution)/shard_map/reduce_twrap/ppermute | solution.py:45
  48.0 0.2 collective-permute-start.16
  48.2 2.5 %collective-permute-done.12 = bf16[32,6144]{1,0:T(8,128)(2,1)S(1)} collective-permute-done((bf16[32,6144]{1,0:T(8,128)(2,1)S(1)}, bf16[32,6144]{1,0:T(8,128)(2,1)S(1)}, u32[]{:S(2)}, u32[]{:S(2)}) %collective-permute-start.12) | collective-permute-done | bytes 393248 | tf_op jit(solution)/shard_map/reduce2_tnear/ppermute | solution.py:45
  50.7 0.1 add_convert_fusion.2
  50.8 3.1 %collective-permute-start.13 = (bf16[32,6144]{1,0:T(8,128)(2,1)S(1)}, bf16[32,6144]{1,0:T(8,128)(2,1)S(1)}, u32[]{:S(2)}, u32[]{:S(2)}) collective-permute-start(bf16[32,6144]{1,0:T(8,128)(2,1)S(1)} %add_convert_fusion.2), channel_id=1, source_target_pairs={{0,192},{8,56},{16,208},{24,40},{32,224},{40,24},{48,240},{56,8},{... | collective-permute-start | bytes 1179656 | tf_op jit(solution)/shard_map/reduce_twrap/ppermute | solution.py:45
  53.9 4.3 %collective-permute-done.16 = bf16[32,6144]{1,0:T(8,128)(2,1)S(1)} collective-permute-done((bf16[32,6144]{1,0:T(8,128)(2,1)S(1)}, bf16[32,6144]{1,0:T(8,128)(2,1)S(1)}, u32[]{:S(2)}, u32[]{:S(2)}) %collective-permute-start.16) | collective-permute-done | bytes 393248 | tf_op jit(solution)/shard_map/reduce2_twrap/ppermute | solution.py:45
  58.2 0.1 add_convert_fusion.1
  58.3 0.1 collective-permute-start.17
  58.4 0.0 collective-permute-done.11
  58.4 4.0 %collective-permute-done.13 = bf16[32,6144]{1,0:T(8,128)(2,1)S(1)} collective-permute-done((bf16[32,6144]{1,0:T(8,128)(2,1)S(1)}, bf16[32,6144]{1,0:T(8,128)(2,1)S(1)}, u32[]{:S(2)}, u32[]{:S(2)}) %collective-permute-start.13) | collective-permute-done | bytes 393248 | tf_op jit(solution)/shard_map/reduce_twrap/ppermute | solution.py:45
  62.4 0.1 convert_add_fusion
  62.6 1.1 %collective-permute-start.14 = (bf16[16,6144]{1,0:T(8,128)(2,1)S(1)}, bf16[16,6144]{1,0:T(8,128)(2,1)S(1)}, u32[]{:S(2)}, u32[]{:S(2)}) collective-permute-start(bf16[16,6144]{1,0:T(8,128)(2,1)S(1)} %slice.33), channel_id=1, source_target_pairs={{0,16},{8,72},{16,0},{24,88},{32,48},{40,104},{48,32},{56,120},{64... | collective-permute-start | bytes 589832 | tf_op jit(solution)/shard_map/home_snear/ppermute | solution.py:45
  63.7 0.0 collective-permute-done.15
  63.7 5.3 %collective-permute-done.17 = bf16[32,6144]{1,0:T(8,128)(2,1)S(1)} collective-permute-done((bf16[32,6144]{1,0:T(8,128)(2,1)S(1)}, bf16[32,6144]{1,0:T(8,128)(2,1)S(1)}, u32[]{:S(2)}, u32[]{:S(2)}) %collective-permute-start.17) | collective-permute-done | bytes 393248 | tf_op jit(solution)/shard_map/reduce_tnear/ppermute | solution.py:45
  68.9 0.1 add_convert_fusion
  69.1 2.8 %collective-permute-start.18 = (bf16[16,6144]{1,0:T(8,128)(2,1)S(1)}, bf16[16,6144]{1,0:T(8,128)(2,1)S(1)}, u32[]{:S(2)}, u32[]{:S(2)}) collective-permute-start(bf16[16,6144]{1,0:T(8,128)(2,1)S(1)} %get-tuple-element.29), channel_id=1, source_target_pairs={{0,48},{8,200},{16,32},{24,216},{32,16},{40,232},{48,0},{56,248},{... | collective-permute-start | bytes 589832 | tf_op jit(solution)/shard_map/home_swrap/ppermute | solution.py:45
  72.0 0.0 collective-permute-start.19
  72.0 0.0 collective-permute-done.14
  72.0 5.3 %collective-permute-done.18 = bf16[16,6144]{1,0:T(8,128)(2,1)S(1)} collective-permute-done((bf16[16,6144]{1,0:T(8,128)(2,1)S(1)}, bf16[16,6144]{1,0:T(8,128)(2,1)S(1)}, u32[]{:S(2)}, u32[]{:S(2)}) %collective-permute-start.18) | collective-permute-done | bytes 196640 | tf_op jit(solution)/shard_map/home_swrap/ppermute | solution.py:45
  77.2 1.9 %collective-permute-done.19 = bf16[16,6144]{1,0:T(8,128)(2,1)S(1)} collective-permute-done((bf16[16,6144]{1,0:T(8,128)(2,1)S(1)}, bf16[16,6144]{1,0:T(8,128)(2,1)S(1)}, u32[]{:S(2)}, u32[]{:S(2)}) %collective-permute-start.19) | collective-permute-done | bytes 196640 | tf_op jit(solution)/shard_map/home_sfar/ppermute | solution.py:45
  79.1 0.8 fusion.3
  (6 shorter events, 0.1 us)
Async XLA Ops:
  0.0 35.7 %collective-permute-start.9 = (bf16[448,6144]{1,0:T(8,128)(2,1)}, bf16[448,6144]{1,0:T(8,128)(2,1)S(1)}, u32[]{:S(2)}, u32[]{:S(2)}) collective-permute-start(bf16[448,6144]{1,0:T(8,128)(2,1)} %bitcast.2), channel_id=1, source_target_pairs={{0,8},{8,0},{16,24},{24,16},{32,40},{40,32},{48,56},{56,48},{64,72... | collective-permute-start | bytes 16515080 | tf_op jit(solution)/shard_map/up_core/ppermute | solution.py:45
  0.0 35.7 %collective-permute-start.10 = (bf16[448,6144]{1,0:T(8,128)(2,1)}, bf16[448,6144]{1,0:T(8,128)(2,1)S(1)}, u32[]{:S(2)}, u32[]{:S(2)}) collective-permute-start(bf16[448,6144]{1,0:T(8,128)(2,1)} %down.1), channel_id=1, source_target_pairs={{0,8},{8,0},{16,24},{24,16},{32,40},{40,32},{48,56},{56,48},{64,72... | collective-permute-start | bytes 16515080 | tf_op jit(solution)/shard_map/down_core/ppermute | solution.py:45
  4.6 13.8 %collective-permute-start.2 = (bf16[16,6144]{1,0:T(8,128)(2,1)S(1)}, bf16[16,6144]{1,0:T(8,128)(2,1)S(1)}, u32[]{:S(2)}, u32[]{:S(2)}) collective-permute-start(bf16[16,6144]{1,0:T(8,128)(2,1)S(1)} %get-tuple-element.18), channel_id=1, source_target_pairs={{0,32},{8,136},{16,48},{24,152},{32,0},{40,168},{48,16},{56,184},{... | collective-permute-start | bytes 589832 | tf_op jit(solution)/shard_map/gather_sfar/ppermute | solution.py:45
  7.8 8.5 %collective-permute-start.1 = (bf16[16,6144]{1,0:T(8,128)(2,1)S(1)}, bf16[16,6144]{1,0:T(8,128)(2,1)S(1)}, u32[]{:S(2)}, u32[]{:S(2)}) collective-permute-start(bf16[16,6144]{1,0:T(8,128)(2,1)S(1)} %get-tuple-element.18), channel_id=1, source_target_pairs={{0,48},{8,200},{16,32},{24,216},{32,16},{40,232},{48,0},{56,248},{... | collective-permute-start | bytes 589832 | tf_op jit(solution)/shard_map/gather_swrap/ppermute | solution.py:45
  8.9 5.7 %collective-permute-start = (bf16[16,6144]{1,0:T(8,128)(2,1)S(1)}, bf16[16,6144]{1,0:T(8,128)(2,1)S(1)}, u32[]{:S(2)}, u32[]{:S(2)}) collective-permute-start(bf16[16,6144]{1,0:T(8,128)(2,1)S(1)} %get-tuple-element.18), channel_id=1, source_target_pairs={{0,16},{8,72},{16,0},{24,88},{32,48},{40,104},{48,32},{56,120},{64... | collective-permute-start | bytes 589832 | tf_op jit(solution)/shard_map/gather_snear/ppermute | solution.py:45
  14.6 7.9 %collective-permute-start.5 = (bf16[32,6144]{1,0:T(8,128)(2,1)S(1)}, bf16[32,6144]{1,0:T(8,128)(2,1)S(1)}, u32[]{:S(2)}, u32[]{:S(2)}) collective-permute-start(bf16[32,6144]{1,0:T(8,128)(2,1)S(1)} %constant_dynamic-update-slice_fusion.args_0_), channel_id=1, source_target_pairs={{0,64},{8,24},{16,80},{24,8},{32,96},{40,56},{48,112},{56,40},{64,... | collective-permute-start | bytes 1179656 | tf_op jit(solution)/shard_map/gather_tnear/ppermute | solution.py:45
  16.3 9.2 %collective-permute-start.3 = (bf16[32,6144]{1,0:T(8,128)(2,1)S(1)}, bf16[32,6144]{1,0:T(8,128)(2,1)S(1)}, u32[]{:S(2)}, u32[]{:S(2)}) collective-permute-start(bf16[32,6144]{1,0:T(8,128)(2,1)S(1)} %constant_dynamic-update-slice_fusion.args_0_), channel_id=1, source_target_pairs={{0,192},{8,56},{16,208},{24,40},{32,224},{40,24},{48,240},{56,8},{... | collective-permute-start | bytes 1179656 | tf_op jit(solution)/shard_map/gather_twrap/ppermute | solution.py:45
  18.5 8.2 %collective-permute-start.4 = (bf16[32,6144]{1,0:T(8,128)(2,1)S(1)}, bf16[32,6144]{1,0:T(8,128)(2,1)S(1)}, u32[]{:S(2)}, u32[]{:S(2)}) collective-permute-start(bf16[32,6144]{1,0:T(8,128)(2,1)S(1)} %constant_dynamic-update-slice_fusion.2.after.args_1_), channel_id=1, source_target_pairs={{0,64},{8,24},{16,80},{24,8},{32,96},{40,56},{48,112},{56,40},{64,... | collective-permute-start | bytes 1179656 | tf_op jit(solution)/shard_map/gather_tnear/ppermute | solution.py:45
  22.5 11.4 %collective-permute-start.6 = (bf16[32,6144]{1,0:T(8,128)(2,1)S(1)}, bf16[32,6144]{1,0:T(8,128)(2,1)S(1)}, u32[]{:S(2)}, u32[]{:S(2)}) collective-permute-start(bf16[32,6144]{1,0:T(8,128)(2,1)S(1)} %constant_dynamic-update-slice_fusion.2.after.args_1_), channel_id=1, source_target_pairs={{0,192},{8,56},{16,208},{24,40},{32,224},{40,24},{48,240},{56,8},{... | collective-permute-start | bytes 1179656 | tf_op jit(solution)/shard_map/gather_twrap/ppermute | solution.py:45
  25.5 8.4 %collective-permute-start.7 = (bf16[32,6144]{1,0:T(8,128)(2,1)S(1)}, bf16[32,6144]{1,0:T(8,128)(2,1)S(1)}, u32[]{:S(2)}, u32[]{:S(2)}) collective-permute-start(bf16[32,6144]{1,0:T(8,128)(2,1)S(1)} %collective-permute-done.3.args_2_), channel_id=1, source_target_pairs={{0,64},{8,24},{16,80},{24,8},{32,96},{40,56},{48,112},{56,40},{64,... | collective-permute-start | bytes 1179656 | tf_op jit(solution)/shard_map/gather2_tnear/ppermute | solution.py:45
  26.7 9.0 %collective-permute-start.8 = (bf16[32,6144]{1,0:T(8,128)(2,1)S(1)}, bf16[32,6144]{1,0:T(8,128)(2,1)S(1)}, u32[]{:S(2)}, u32[]{:S(2)}) collective-permute-start(bf16[32,6144]{1,0:T(8,128)(2,1)S(1)} %collective-permute-done.4.args_3_), channel_id=1, source_target_pairs={{0,192},{8,56},{16,208},{24,40},{32,224},{40,24},{48,240},{56,8},{... | collective-permute-start | bytes 1179656 | tf_op jit(solution)/shard_map/gather2_twrap/ppermute | solution.py:45
  42.9 7.9 %collective-permute-start.12 = (bf16[32,6144]{1,0:T(8,128)(2,1)S(1)}, bf16[32,6144]{1,0:T(8,128)(2,1)S(1)}, u32[]{:S(2)}, u32[]{:S(2)}) collective-permute-start(bf16[32,6144]{1,0:T(8,128)(2,1)S(1)} %get-tuple-element.24), channel_id=1, source_target_pairs={{0,64},{8,24},{16,80},{24,8},{32,96},{40,56},{48,112},{56,40},{64,... | collective-permute-start | bytes 1179656 | tf_op jit(solution)/shard_map/reduce2_tnear/ppermute | solution.py:45
  43.3 15.1 %collective-permute-start.11 = (bf16[32,6144]{1,0:T(8,128)(2,1)S(1)}, bf16[32,6144]{1,0:T(8,128)(2,1)S(1)}, u32[]{:S(2)}, u32[]{:S(2)}) collective-permute-start(bf16[32,6144]{1,0:T(8,128)(2,1)S(1)} %get-tuple-element.22), channel_id=1, source_target_pairs={{0,64},{8,24},{16,80},{24,8},{32,96},{40,56},{48,112},{56,40},{64,... | collective-permute-start | bytes 1179656 | tf_op jit(solution)/shard_map/reduce_tnear/ppermute | solution.py:45
  45.0 18.7 %collective-permute-start.15 = (bf16[32,6144]{1,0:T(8,128)(2,1)S(1)}, bf16[32,6144]{1,0:T(8,128)(2,1)S(1)}, u32[]{:S(2)}, u32[]{:S(2)}) collective-permute-start(bf16[32,6144]{1,0:T(8,128)(2,1)S(1)} %get-tuple-element.26), channel_id=1, source_target_pairs={{0,192},{8,56},{16,208},{24,40},{32,224},{40,24},{48,240},{56,8},{... | collective-permute-start | bytes 1179656 | tf_op jit(solution)/shard_map/reduce_twrap/ppermute | solution.py:45
  48.0 10.2 %collective-permute-start.16 = (bf16[32,6144]{1,0:T(8,128)(2,1)S(1)}, bf16[32,6144]{1,0:T(8,128)(2,1)S(1)}, u32[]{:S(2)}, u32[]{:S(2)}) collective-permute-start(bf16[32,6144]{1,0:T(8,128)(2,1)S(1)} %get-tuple-element.28), channel_id=1, source_target_pairs={{0,192},{8,56},{16,208},{24,40},{32,224},{40,24},{48,240},{56,8},{... | collective-permute-start | bytes 1179656 | tf_op jit(solution)/shard_map/reduce2_twrap/ppermute | solution.py:45
  50.8 11.6 %collective-permute-start.13 = (bf16[32,6144]{1,0:T(8,128)(2,1)S(1)}, bf16[32,6144]{1,0:T(8,128)(2,1)S(1)}, u32[]{:S(2)}, u32[]{:S(2)}) collective-permute-start(bf16[32,6144]{1,0:T(8,128)(2,1)S(1)} %add_convert_fusion.2), channel_id=1, source_target_pairs={{0,192},{8,56},{16,208},{24,40},{32,224},{40,24},{48,240},{56,8},{... | collective-permute-start | bytes 1179656 | tf_op jit(solution)/shard_map/reduce_twrap/ppermute | solution.py:45
  58.3 10.6 %collective-permute-start.17 = (bf16[32,6144]{1,0:T(8,128)(2,1)S(1)}, bf16[32,6144]{1,0:T(8,128)(2,1)S(1)}, u32[]{:S(2)}, u32[]{:S(2)}) collective-permute-start(bf16[32,6144]{1,0:T(8,128)(2,1)S(1)} %add_convert_fusion.1), channel_id=1, source_target_pairs={{0,64},{8,24},{16,80},{24,8},{32,96},{40,56},{48,112},{56,40},{64,... | collective-permute-start | bytes 1179656 | tf_op jit(solution)/shard_map/reduce_tnear/ppermute | solution.py:45
  62.6 9.4 %collective-permute-start.14 = (bf16[16,6144]{1,0:T(8,128)(2,1)S(1)}, bf16[16,6144]{1,0:T(8,128)(2,1)S(1)}, u32[]{:S(2)}, u32[]{:S(2)}) collective-permute-start(bf16[16,6144]{1,0:T(8,128)(2,1)S(1)} %slice.33), channel_id=1, source_target_pairs={{0,16},{8,72},{16,0},{24,88},{32,48},{40,104},{48,32},{56,120},{64... | collective-permute-start | bytes 589832 | tf_op jit(solution)/shard_map/home_snear/ppermute | solution.py:45
  69.1 8.1 %collective-permute-start.18 = (bf16[16,6144]{1,0:T(8,128)(2,1)S(1)}, bf16[16,6144]{1,0:T(8,128)(2,1)S(1)}, u32[]{:S(2)}, u32[]{:S(2)}) collective-permute-start(bf16[16,6144]{1,0:T(8,128)(2,1)S(1)} %get-tuple-element.29), channel_id=1, source_target_pairs={{0,48},{8,200},{16,32},{24,216},{32,16},{40,232},{48,0},{56,248},{... | collective-permute-start | bytes 589832 | tf_op jit(solution)/shard_map/home_swrap/ppermute | solution.py:45
  72.0 7.2 %collective-permute-start.19 = (bf16[16,6144]{1,0:T(8,128)(2,1)S(1)}, bf16[16,6144]{1,0:T(8,128)(2,1)S(1)}, u32[]{:S(2)}, u32[]{:S(2)}) collective-permute-start(bf16[16,6144]{1,0:T(8,128)(2,1)S(1)} %get-tuple-element.30), channel_id=1, source_target_pairs={{0,32},{8,136},{16,48},{24,152},{32,0},{40,168},{48,16},{56,184},{... | collective-permute-start | bytes 589832 | tf_op jit(solution)/shard_map/home_sfar/ppermute | solution.py:45

commit v4 on v3

--- a/solution.py
+++ b/solution.py
@@ -50,7 +50,7 @@
 
 
 def attend_kernel(
-    counts, lengths_in, q_in, k_in, v_in, gain_in, attended, normed, lengths, q, k, v, gain, sems
+    counts, lengths_in, q_in, k_in, v_in, gain_in, down, attended, normed, down_held, lengths, q, k, v, gain, sems
 ):
     copies = [
         pltpu.make_async_copy(a, b, sems.at[i])
@@ -61,6 +61,7 @@
                 (q_in, q),
                 (v_in, v),
                 (gain_in, gain),
+                (down, down_held),
             )
         )
     ]
@@ -114,53 +115,52 @@
     factor = lax.rsqrt(mean_square + 1e-05)
     copies[4].wait()
     normed[...] = (attended[...].astype(jnp.float32) * factor * gain[...]).astype(jnp.bfloat16)
-
-
-def attend(queries, cache_keys, cache_values, lengths, counts, norm_gain):
+    copies[5].wait()
+
+
+def attend(queries, cache_keys, cache_values, lengths, counts, norm_gain, down_rows):
     vmem = pl.BlockSpec(memory_space=pltpu.VMEM)
     any_space = pl.BlockSpec(memory_space=pl.ANY)
     return pl.pallas_call(
         attend_kernel,
-        out_shape=(jax.ShapeDtypeStruct((SLOTS, D), jnp.bfloat16),) * 2,
-        in_specs=[pl.BlockSpec(memory_space=pltpu.SMEM)] + [any_space] * 5,
-        out_specs=(vmem, vmem),
+        out_shape=(
+            jax.ShapeDtypeStruct((SLOTS, D), jnp.bfloat16),
+            jax.ShapeDtypeStruct((SLOTS, D), jnp.bfloat16),
+            jax.ShapeDtypeStruct((HIDDEN, D), jnp.bfloat16),
+        ),
+        in_specs=[pl.BlockSpec(memory_space=pltpu.SMEM)] + [any_space] * 6,
+        out_specs=(vmem, vmem, vmem),
         scratch_shapes=[
             pltpu.SMEM((SLOTS,), jnp.int32),
             pltpu.VMEM((SLOTS, D), jnp.bfloat16),
             pltpu.VMEM((POOL, KVH * HD), jnp.bfloat16),
             pltpu.VMEM((POOL, KVH * HD), jnp.bfloat16),
             pltpu.VMEM((1, D), jnp.float32),
-            pltpu.SemaphoreType.DMA((5,)),
+            pltpu.SemaphoreType.DMA((6,)),
         ],
         compiler_params=pltpu.CompilerParams(vmem_limit_bytes=16 * 2**20),
         name="attend",
-    )(counts, *map(in_hbm, (lengths, queries, cache_keys, cache_values, norm_gain.reshape(1, D))))
-
-
-def fetch_kernel(up, down, after, up_held, down_held, sems):
-    copies = [
-        pltpu.make_async_copy(up, up_held, sems.at[0]),
-        pltpu.make_async_copy(down, down_held, sems.at[1]),
-    ]
-    for copy in copies:
-        copy.start()
-    for copy in copies:
-        copy.wait()
-
-
-def fetch(up_rows, down_rows, after):
+    )(counts, *map(in_hbm, (lengths, queries, cache_keys, cache_values, norm_gain.reshape(1, D), down_rows)))
+
+
+def fetch_kernel(weights, after, held, sem):
+    copy = pltpu.make_async_copy(weights, held, sem)
+    copy.start()
+    copy.wait()
+
+
+def fetch(weights, after):
     any_space = pl.BlockSpec(memory_space=pl.ANY)
-    vmem = pl.BlockSpec(memory_space=pltpu.VMEM)
     return pl.pallas_call(
         fetch_kernel,
-        out_shape=[jax.ShapeDtypeStruct((HIDDEN, D), jnp.bfloat16)] * 2,
-        in_specs=[any_space] * 3,
-        out_specs=[vmem] * 2,
-        scratch_shapes=[pltpu.SemaphoreType.DMA((2,))],
+        out_shape=jax.ShapeDtypeStruct((HIDDEN, D), jnp.bfloat16),
+        in_specs=[any_space] * 2,
+        out_specs=pl.BlockSpec(memory_space=pltpu.VMEM),
+        scratch_shapes=[pltpu.SemaphoreType.DMA],
         compiler_params=pltpu.CompilerParams(vmem_limit_bytes=16 * 2**20),
         cost_estimate=pl.CostEstimate(flops=0, bytes_accessed=4 * HIDDEN * D, transcendentals=0),
         name="fetch",
-    )(in_hbm(up_rows), in_hbm(down_rows), after)
+    )(in_hbm(weights), after)
 
 
 def ffn_kernel(*args):
@@ -212,34 +212,74 @@
     return x.astype(jnp.float32)
 
 
-def add(*terms):
-    return sum(map(f32, terms)).astype(jnp.bfloat16)
+def pack_kernel(own, near, wrap, far, held, after, first, second, handed):
+    first[:SLOTS] = own[...]
+    first[SLOTS:] = near[...]
+    second[:SLOTS] = wrap[...]
+    second[SLOTS:] = far[...]
+
+
+def pack(own, near, wrap, far, held, after):
+    vmem = pl.BlockSpec(memory_space=pltpu.VMEM)
+    block = jax.ShapeDtypeStruct((PAIR, D), jnp.bfloat16)
+    return pl.pallas_call(
+        pack_kernel,
+        out_shape=[block, block, jax.ShapeDtypeStruct(held.shape, held.dtype)],
+        in_specs=[vmem] * 5 + [pl.BlockSpec(memory_space=pl.ANY)],
+        out_specs=[vmem] * 3,
+        input_output_aliases={4: 2},
+        compiler_params=pltpu.CompilerParams(vmem_limit_bytes=16 * 2**20),
+        name="pack",
+    )(own, near, wrap, far, held, after)
+
+
+def merge_kernel(mine, arrived, *refs):
+    waiting, (total, *later) = refs[: len(refs) // 2], refs[len(refs) // 2 :]
+    total[...] = (mine[...].astype(jnp.float32) + arrived[...].astype(jnp.float32)).astype(jnp.bfloat16)
+    for source, target in zip(waiting, later):
+        target[...] = source[...]
+
+
+def merge(mine, arrived, *waiting):
+    vmem = pl.BlockSpec(memory_space=pltpu.VMEM)
+    n = 1 + len(waiting)
+    return pl.pallas_call(
+        merge_kernel,
+        out_shape=[jax.ShapeDtypeStruct((PAIR, D), jnp.bfloat16)] * n,
+        in_specs=[vmem] * (n + 1),
+        out_specs=[vmem] * n,
+        compiler_params=pltpu.CompilerParams(vmem_limit_bytes=16 * 2**20),
+        name="merge",
+    )(mine, arrived, *waiting)
 
 
 def on_device(
     queries, cache_keys, cache_values, lengths, counts, norm_gain, up_weight, down_weight
 ):
-    up_own, down_own = up_weight.T, down_weight
+    up_own = up_weight.T
     up_other = send(up_own, "core", "up")
-    down_other = send(down_own, "core", "down")
-    attended, normed = attend(queries, cache_keys, cache_values, lengths, counts, norm_gain)
+    attended, normed, down_held = attend(
+        queries, cache_keys, cache_values, lengths, counts, norm_gain, down_weight
+    )
     by_wrap, by_far, by_near = [send(normed, r, "gather") for r in ("swrap", "sfar", "snear")]
-    first = jnp.concatenate([normed, by_near], axis=0)
-    second = jnp.concatenate([by_wrap, by_far], axis=0)
+    first, second, down_held = pack(normed, by_near, by_wrap, by_far, down_held, up_other)
+    down_other = send(down_held, "core", "down")
+    up_held = fetch(up_own, second)
     first_w, second_n = send(first, "twrap", "gather"), send(second, "tnear", "gather")
     second_w, first_n = send(second, "twrap", "gather"), send(first, "tnear", "gather")
     first_f, second_f = send(first_w, "tnear", "gather2"), send(second_n, "twrap", "gather2")
-    up_held, down_held = fetch(up_own, down_own, second)
     blocks = [first, second, first_w, second_n, first_n, second_w, first_f, second_f]
     first, second, first_w, second_n, first_n, second_w, first_f, second_f = feed_forward(
         blocks, (up_held, up_other), (down_held, down_other)
     )
     far_first = send(first_f, "tnear", "reduce2")
     far_second = send(second_f, "twrap", "reduce2")
+    first_w, first_n, second_w = merge(first_w, far_first, first_n, second_w)
+    back_first = send(first_w, "twrap", "reduce")
     near_first = send(first_n, "tnear", "reduce")
     near_second = send(second_w, "twrap", "reduce")
-    back_first = send(add(first_w, far_first), "twrap", "reduce")
-    back_second = send(add(second_n, far_second), "tnear", "reduce")
+    (second_n,) = merge(second_n, far_second)
+    back_second = send(second_n, "tnear", "reduce")
     first = f32(first) + f32(near_first) + f32(back_first)
     second = f32(second) + f32(near_second) + f32(back_second)
     home_near = send(first[SLOTS:].astype(jnp.bfloat16), "snear", "home")

time: 80 us -> 74.7 us (0.934)
  starting transfers between devices: 28 us -> 22.2 us
  waiting for transfers between devices: 34.9 us -> 37 us
  Pallas kernels: 14.9 us -> 13.5 us
    ppermute x20, starting transfers between devices: 28 us -> 22.2 us  [send(): return lax.ppermute(value, 'dp', ROUTES[route])]
    ppermute x20, waiting for transfers between devices: 34.9 us -> 37 us  [send(): return lax.ppermute(value, 'dp', ROUTES[route])]
    pallas_call x1 -> x4, Pallas kernels: 4.21 us -> 2.83 us  [the longest x1 2.57 us: fetch(): pl.pallas_call(fetch_kernel, out_shape=jax.ShapeDtypeStruct((HIDDEN, D),...]
  transfers between devices with their start and end apart: 20 -> 20, of which waited for: 10 -> 14; matrix products, arithmetic and copies ran while one was open for 1% -> 0% of each run, Pallas kernels for 10% -> 8%
where the time goes in v4:
time: 74.7 us; the launch traced here: 74.5 us
  waiting for transfers between devices  37 us (50%)
  starting transfers between devices  22.2 us (30%)
  Pallas kernels  13.5 us (18%)
  other arithmetic  1.07 us (1%)
  between operations  0.76 us (1%)
    ppermute x20, waiting for transfers between devices, send(): return lax.ppermute(value, 'dp', ROUTES[route])  37 us
    ppermute x20, starting transfers between devices, send(): return lax.ppermute(value, 'dp', ROUTES[route])  22.2 us
    pallas_call x1, Pallas kernels, feed_forward(): pl.pallas_call(ffn_kernel, out_shape=[jax.ShapeDtypeStruct((PAIR, D), jnp...  7.19 us
    pallas_call x1, Pallas kernels, attend(): pl.pallas_call(attend_kernel, out_shape=(jax.ShapeDtypeStruct((SLOTS, D),...  3.49 us
    pallas_call x1, Pallas kernels, fetch(): pl.pallas_call(fetch_kernel, out_shape=jax.ShapeDtypeStruct((HIDDEN, D),...  2.57 us
  transfers between devices with their start and end apart: 20, of which 14 were waited for; matrix products, arithmetic and copies ran while one was open for 0% of the time, Pallas kernels for 8%

profile of v4, /device:TPU:128, one launch (start us, length us, event | category | flops | bytes accessed | tf_op | source)
XLA Modules:
  0.0 74.5 jit_solution(17155788098990097469)
XLA Ops:
  0.0 0.0 collective-permute-start.3
  0.7 3.5 %attend.1 = (bf16[16,6144]{1,0:T(8,128)(2,1)S(1)}, bf16[16,6144]{1,0:T(8,128)(2,1)S(1)}, bf16[448,6144]{1,0:T(8,128)(2,1)S(1)}) custom-call(s32[1]{0:T(128)S(6)} %copy.11.counts, s32[16]{0:T(128)} %lengths_in.1, bf16[16,6144]{1,0:T(8,128)(2,1)} %q_in.1, bf16[1024,512]{1,0:T(8,128)(2,1)} %k_in.1, bf16[1024,512]{1,0:T(8,128)(2,1)} %v_in.1, f32[1,6144]{1,0:T(1,128)} %bitcast.4, ...), custom_call_target="tpu_custom_call" | custom-call | tf_op jit(solution)/shard_map/attend/pallas_call | solution.py:124
  4.2 3.1 %collective-permute-start.2 = (bf16[16,6144]{1,0:T(8,128)(2,1)S(1)}, bf16[16,6144]{1,0:T(8,128)(2,1)S(1)}, u32[]{:S(2)}, u32[]{:S(2)}) collective-permute-start(bf16[16,6144]{1,0:T(8,128)(2,1)S(1)} %get-tuple-element.23.own), channel_id=1, source_target_pairs={{0,32},{8,136},{16,48},{24,152},{32,0},{40,168},{48,16},{56,184},{... | collective-permute-start | bytes 589832 | tf_op jit(solution)/shard_map/gather_sfar/ppermute | solution.py:45
  7.3 1.1 %collective-permute-start.1 = (bf16[16,6144]{1,0:T(8,128)(2,1)S(1)}, bf16[16,6144]{1,0:T(8,128)(2,1)S(1)}, u32[]{:S(2)}, u32[]{:S(2)}) collective-permute-start(bf16[16,6144]{1,0:T(8,128)(2,1)S(1)} %get-tuple-element.23.own), channel_id=1, source_target_pairs={{0,48},{8,200},{16,32},{24,216},{32,16},{40,232},{48,0},{56,248},{... | collective-permute-start | bytes 589832 | tf_op jit(solution)/shard_map/gather_swrap/ppermute | solution.py:45
  8.4 0.0 collective-permute-start
  8.4 3.0 %collective-permute-done.2.far = bf16[16,6144]{1,0:T(8,128)(2,1)S(1)} collective-permute-done((bf16[16,6144]{1,0:T(8,128)(2,1)S(1)}, bf16[16,6144]{1,0:T(8,128)(2,1)S(1)}, u32[]{:S(2)}, u32[]{:S(2)}) %collective-permute-start.2) | collective-permute-done | bytes 196640 | tf_op jit(solution)/shard_map/gather_sfar/ppermute | solution.py:45
  11.4 2.7 %collective-permute-done.1.wrap = bf16[16,6144]{1,0:T(8,128)(2,1)S(1)} collective-permute-done((bf16[16,6144]{1,0:T(8,128)(2,1)S(1)}, bf16[16,6144]{1,0:T(8,128)(2,1)S(1)}, u32[]{:S(2)}, u32[]{:S(2)}) %collective-permute-start.1) | collective-permute-done | bytes 196640 | tf_op jit(solution)/shard_map/gather_swrap/ppermute | solution.py:45
  14.1 0.0 collective-permute-done.near
  14.2 0.0 collective-permute-done.3.after.args_9_
  14.2 0.1 pack.1
  14.2 0.1 collective-permute-start.10
  14.3 3.1 %collective-permute-start.4 = (bf16[32,6144]{1,0:T(8,128)(2,1)S(1)}, bf16[32,6144]{1,0:T(8,128)(2,1)S(1)}, u32[]{:S(2)}, u32[]{:S(2)}) collective-permute-start(bf16[32,6144]{1,0:T(8,128)(2,1)S(1)} %get-tuple-element.25.args_0_), channel_id=1, source_target_pairs={{0,192},{8,56},{16,208},{24,40},{32,224},{40,24},{48,240},{56,8},{... | collective-permute-start | bytes 1179656 | tf_op jit(solution)/shard_map/gather_twrap/ppermute | solution.py:45
  17.4 0.1 collective-permute-start.5
  17.6 1.9 %collective-permute-start.6 = (bf16[32,6144]{1,0:T(8,128)(2,1)S(1)}, bf16[32,6144]{1,0:T(8,128)(2,1)S(1)}, u32[]{:S(2)}, u32[]{:S(2)}) collective-permute-start(bf16[32,6144]{1,0:T(8,128)(2,1)S(1)} %get-tuple-element.25.args_0_), channel_id=1, source_target_pairs={{0,64},{8,24},{16,80},{24,8},{32,96},{40,56},{48,112},{56,40},{64,... | collective-permute-start | bytes 1179656 | tf_op jit(solution)/shard_map/gather_tnear/ppermute | solution.py:45
  19.4 0.2 collective-permute-start.7
  19.7 3.7 %collective-permute-done.4.args_2_ = bf16[32,6144]{1,0:T(8,128)(2,1)S(1)} collective-permute-done((bf16[32,6144]{1,0:T(8,128)(2,1)S(1)}, bf16[32,6144]{1,0:T(8,128)(2,1)S(1)}, u32[]{:S(2)}, u32[]{:S(2)}) %collective-permute-start.4) | collective-permute-done | bytes 393248 | tf_op jit(solution)/shard_map/gather_twrap/ppermute | solution.py:45
  23.4 0.4 collective-permute-start.8
  23.8 1.4 %collective-permute-done.5.args_3_ = bf16[32,6144]{1,0:T(8,128)(2,1)S(1)} collective-permute-done((bf16[32,6144]{1,0:T(8,128)(2,1)S(1)}, bf16[32,6144]{1,0:T(8,128)(2,1)S(1)}, u32[]{:S(2)}, u32[]{:S(2)}) %collective-permute-start.5) | collective-permute-done | bytes 393248 | tf_op jit(solution)/shard_map/gather_tnear/ppermute | solution.py:45
  25.2 1.2 %collective-permute-start.9 = (bf16[32,6144]{1,0:T(8,128)(2,1)S(1)}, bf16[32,6144]{1,0:T(8,128)(2,1)S(1)}, u32[]{:S(2)}, u32[]{:S(2)}) collective-permute-start(bf16[32,6144]{1,0:T(8,128)(2,1)S(1)} %collective-permute-done.5.args_3_), channel_id=1, source_target_pairs={{0,192},{8,56},{16,208},{24,40},{32,224},{40,24},{48,240},{56,8},{... | collective-permute-start | bytes 1179656 | tf_op jit(solution)/shard_map/gather2_twrap/ppermute | solution.py:45
  26.4 2.6 %fetch.1.args_8_ = bf16[448,6144]{1,0:T(8,128)(2,1)S(1)} custom-call(bf16[448,6144]{1,0:T(8,128)(2,1)} %bitcast.3, bf16[32,6144]{1,0:T(8,128)(2,1)S(1)} %get-tuple-element.26.after.args_1_), custom_call_target="tpu_custom_call" | custom-call | bytes 11010048 | tf_op jit(solution)/shard_map/fetch/pallas_call | solution.py:154
  29.0 0.4 collective-permute-done.6.args_4_
  29.4 0.0 collective-permute-done.7.args_5_
  29.4 4.2 %collective-permute-done.8.args_6_ = bf16[32,6144]{1,0:T(8,128)(2,1)S(1)} collective-permute-done((bf16[32,6144]{1,0:T(8,128)(2,1)S(1)}, bf16[32,6144]{1,0:T(8,128)(2,1)S(1)}, u32[]{:S(2)}, u32[]{:S(2)}) %collective-permute-start.8) | collective-permute-done | bytes 393248 | tf_op jit(solution)/shard_map/gather2_tnear/ppermute | solution.py:45
  33.6 0.6 collective-permute-done.9.args_7_
  34.2 0.0 collective-permute-done.10.args_11_
  34.2 7.2 %feed_forward.1 = (bf16[32,6144]{1,0:T(8,128)(2,1)S(1)}, bf16[32,6144]{1,0:T(8,128)(2,1)S(1)}, bf16[32,6144]{1,0:T(8,128)(2,1)S(1)}, bf16[32,6144]{1,0:T(8,128)(...) custom-call(bf16[32,6144]{1,0:T(8,128)(2,1)S(1)} %get-tuple-element., ...), custom_call_target="tpu_custom_call" | custom-call | tf_op jit(solution)/shard_map/feed_forward/pallas_call | solution.py:197
  41.4 0.1 collective-permute-start.11
  41.5 2.0 %collective-permute-start.16 = (bf16[32,6144]{1,0:T(8,128)(2,1)S(1)}, bf16[32,6144]{1,0:T(8,128)(2,1)S(1)}, u32[]{:S(2)}, u32[]{:S(2)}) collective-permute-start(bf16[32,6144]{1,0:T(8,128)(2,1)S(1)} %get-tuple-element.38), channel_id=1, source_target_pairs={{0,192},{8,56},{16,208},{24,40},{32,224},{40,24},{48,240},{56,8},{... | collective-permute-start | bytes 1179656 | tf_op jit(solution)/shard_map/reduce2_twrap/ppermute | solution.py:45
  43.5 5.8 %collective-permute-done.11.arrived = bf16[32,6144]{1,0:T(8,128)(2,1)S(1)} collective-permute-done((bf16[32,6144]{1,0:T(8,128)(2,1)S(1)}, bf16[32,6144]{1,0:T(8,128)(2,1)S(1)}, u32[]{:S(2)}, u32[]{:S(2)}) %collective-permute-start.11) | collective-permute-done | bytes 393248 | tf_op jit(solution)/shard_map/reduce2_tnear/ppermute | solution.py:45
  49.2 0.1 merge.2
  49.4 0.3 collective-permute-start.12
  49.6 2.0 %collective-permute-start.13 = (bf16[32,6144]{1,0:T(8,128)(2,1)S(1)}, bf16[32,6144]{1,0:T(8,128)(2,1)S(1)}, u32[]{:S(2)}, u32[]{:S(2)}) collective-permute-start(bf16[32,6144]{1,0:T(8,128)(2,1)S(1)} %get-tuple-element.34), channel_id=1, source_target_pairs={{0,192},{8,56},{16,208},{24,40},{32,224},{40,24},{48,240},{56,8},{... | collective-permute-start | bytes 1179656 | tf_op jit(solution)/shard_map/reduce_twrap/ppermute | solution.py:45
  51.6 1.3 %collective-permute-start.15 = (bf16[32,6144]{1,0:T(8,128)(2,1)S(1)}, bf16[32,6144]{1,0:T(8,128)(2,1)S(1)}, u32[]{:S(2)}, u32[]{:S(2)}) collective-permute-start(bf16[32,6144]{1,0:T(8,128)(2,1)S(1)} %get-tuple-element.36), channel_id=1, source_target_pairs={{0,192},{8,56},{16,208},{24,40},{32,224},{40,24},{48,240},{56,8},{... | collective-permute-start | bytes 1179656 | tf_op jit(solution)/shard_map/reduce_twrap/ppermute | solution.py:45
  53.0 0.1 merge.3
  53.1 0.8 %collective-permute-start.17 = (bf16[32,6144]{1,0:T(8,128)(2,1)S(1)}, bf16[32,6144]{1,0:T(8,128)(2,1)S(1)}, u32[]{:S(2)}, u32[]{:S(2)}) collective-permute-start(bf16[32,6144]{1,0:T(8,128)(2,1)S(1)} %merge.3), channel_id=1, source_target_pairs={{0,64},{8,24},{16,80},{24,8},{32,96},{40,56},{48,112},{56,40},{64,... | collective-permute-start | bytes 1179656 | tf_op jit(solution)/shard_map/reduce_tnear/ppermute | solution.py:45
  53.9 3.5 %collective-permute-done.12 = bf16[32,6144]{1,0:T(8,128)(2,1)S(1)} collective-permute-done((bf16[32,6144]{1,0:T(8,128)(2,1)S(1)}, bf16[32,6144]{1,0:T(8,128)(2,1)S(1)}, u32[]{:S(2)}, u32[]{:S(2)}) %collective-permute-start.12) | collective-permute-done | bytes 393248 | tf_op jit(solution)/shard_map/reduce_tnear/ppermute | solution.py:45
  57.4 1.3 %collective-permute-done.13 = bf16[32,6144]{1,0:T(8,128)(2,1)S(1)} collective-permute-done((bf16[32,6144]{1,0:T(8,128)(2,1)S(1)}, bf16[32,6144]{1,0:T(8,128)(2,1)S(1)}, u32[]{:S(2)}, u32[]{:S(2)}) %collective-permute-start.13) | collective-permute-done | bytes 393248 | tf_op jit(solution)/shard_map/reduce_twrap/ppermute | solution.py:45
  58.7 0.1 convert_add_fusion
  58.9 1.0 %collective-permute-start.14 = (bf16[16,6144]{1,0:T(8,128)(2,1)S(1)}, bf16[16,6144]{1,0:T(8,128)(2,1)S(1)}, u32[]{:S(2)}, u32[]{:S(2)}) collective-permute-start(bf16[16,6144]{1,0:T(8,128)(2,1)S(1)} %slice.33), channel_id=1, source_target_pairs={{0,16},{8,72},{16,0},{24,88},{32,48},{40,104},{48,32},{56,120},{64... | collective-permute-start | bytes 589832 | tf_op jit(solution)/shard_map/home_snear/ppermute | solution.py:45
  59.9 3.0 %collective-permute-done.15 = bf16[32,6144]{1,0:T(8,128)(2,1)S(1)} collective-permute-done((bf16[32,6144]{1,0:T(8,128)(2,1)S(1)}, bf16[32,6144]{1,0:T(8,128)(2,1)S(1)}, u32[]{:S(2)}, u32[]{:S(2)}) %collective-permute-start.15) | collective-permute-done | bytes 393248 | tf_op jit(solution)/shard_map/reduce_twrap/ppermute | solution.py:45
  62.9 0.8 %collective-permute-done.17 = bf16[32,6144]{1,0:T(8,128)(2,1)S(1)} collective-permute-done((bf16[32,6144]{1,0:T(8,128)(2,1)S(1)}, bf16[32,6144]{1,0:T(8,128)(2,1)S(1)}, u32[]{:S(2)}, u32[]{:S(2)}) %collective-permute-start.17) | collective-permute-done | bytes 393248 | tf_op jit(solution)/shard_map/reduce_tnear/ppermute | solution.py:45
  63.7 0.1 add_convert_fusion
  63.9 2.7 %collective-permute-start.18 = (bf16[16,6144]{1,0:T(8,128)(2,1)S(1)}, bf16[16,6144]{1,0:T(8,128)(2,1)S(1)}, u32[]{:S(2)}, u32[]{:S(2)}) collective-permute-start(bf16[16,6144]{1,0:T(8,128)(2,1)S(1)} %get-tuple-element.39), channel_id=1, source_target_pairs={{0,48},{8,200},{16,32},{24,216},{32,16},{40,232},{48,0},{56,248},{... | collective-permute-start | bytes 589832 | tf_op jit(solution)/shard_map/home_swrap/ppermute | solution.py:45
  66.6 0.7 collective-permute-start.19
  67.3 0.0 collective-permute-done.14
  67.3 4.6 %collective-permute-done.18 = bf16[16,6144]{1,0:T(8,128)(2,1)S(1)} collective-permute-done((bf16[16,6144]{1,0:T(8,128)(2,1)S(1)}, bf16[16,6144]{1,0:T(8,128)(2,1)S(1)}, u32[]{:S(2)}, u32[]{:S(2)}) %collective-permute-start.18) | collective-permute-done | bytes 196640 | tf_op jit(solution)/shard_map/home_swrap/ppermute | solution.py:45
  71.9 1.8 %collective-permute-done.19 = bf16[16,6144]{1,0:T(8,128)(2,1)S(1)} collective-permute-done((bf16[16,6144]{1,0:T(8,128)(2,1)S(1)}, bf16[16,6144]{1,0:T(8,128)(2,1)S(1)}, u32[]{:S(2)}, u32[]{:S(2)}) %collective-permute-start.19) | collective-permute-done | bytes 196640 | tf_op jit(solution)/shard_map/home_sfar/ppermute | solution.py:45
  73.8 0.8 %fusion.3 = bf16[16,6144]{1,0:T(8,128)(2,1)} fusion(f32[32,6144]{1,0:T(8,128)S(1)} %convert_add_fusion, bf16[16,6144]{1,0:T(8,128)(2,1)S(1)} %collective-permute-done.19, bf16[16,6144]{1,0:T(8,128)(2,1)S(1)} %collective-permute-done.18, bf16[16,6144]{1,0:T(8,128)(2,1)S(1)} %collective-permute-done.14, bf16[16,6144]{1,0:T(8,128)(2,1)S(1)} %get-tuple-element.22), kind=kLoop, calls=%fused_computation.7 | loop fusion | flops 884736 | bytes 1376256 | tf_op jit(solution)/shard_map/convert_element_type | solution.py:289
  (3 shorter events, 0.1 us)
Async XLA Ops:
  0.0 14.2 %collective-permute-start.3 = (bf16[448,6144]{1,0:T(8,128)(2,1)}, bf16[448,6144]{1,0:T(8,128)(2,1)S(1)}, u32[]{:S(2)}, u32[]{:S(2)}) collective-permute-start(bf16[448,6144]{1,0:T(8,128)(2,1)} %bitcast.2), channel_id=1, source_target_pairs={{0,8},{8,0},{16,24},{24,16},{32,40},{40,32},{48,56},{56,48},{64,72... | collective-permute-start | bytes 16515080 | tf_op jit(solution)/shard_map/up_core/ppermute | solution.py:45
  4.2 7.3 %collective-permute-start.2 = (bf16[16,6144]{1,0:T(8,128)(2,1)S(1)}, bf16[16,6144]{1,0:T(8,128)(2,1)S(1)}, u32[]{:S(2)}, u32[]{:S(2)}) collective-permute-start(bf16[16,6144]{1,0:T(8,128)(2,1)S(1)} %get-tuple-element.23.own), channel_id=1, source_target_pairs={{0,32},{8,136},{16,48},{24,152},{32,0},{40,168},{48,16},{56,184},{... | collective-permute-start | bytes 589832 | tf_op jit(solution)/shard_map/gather_sfar/ppermute | solution.py:45
  7.3 6.9 %collective-permute-start.1 = (bf16[16,6144]{1,0:T(8,128)(2,1)S(1)}, bf16[16,6144]{1,0:T(8,128)(2,1)S(1)}, u32[]{:S(2)}, u32[]{:S(2)}) collective-permute-start(bf16[16,6144]{1,0:T(8,128)(2,1)S(1)} %get-tuple-element.23.own), channel_id=1, source_target_pairs={{0,48},{8,200},{16,32},{24,216},{32,16},{40,232},{48,0},{56,248},{... | collective-permute-start | bytes 589832 | tf_op jit(solution)/shard_map/gather_swrap/ppermute | solution.py:45
  8.4 5.7 %collective-permute-start = (bf16[16,6144]{1,0:T(8,128)(2,1)S(1)}, bf16[16,6144]{1,0:T(8,128)(2,1)S(1)}, u32[]{:S(2)}, u32[]{:S(2)}) collective-permute-start(bf16[16,6144]{1,0:T(8,128)(2,1)S(1)} %get-tuple-element.23.own), channel_id=1, source_target_pairs={{0,16},{8,72},{16,0},{24,88},{32,48},{40,104},{48,32},{56,120},{64... | collective-permute-start | bytes 589832 | tf_op jit(solution)/shard_map/gather_snear/ppermute | solution.py:45
  14.2 20.0 %collective-permute-start.10 = (bf16[448,6144]{1,0:T(8,128)(2,1)S(1)}, bf16[448,6144]{1,0:T(8,128)(2,1)S(1)}, u32[]{:S(2)}, u32[]{:S(2)}) collective-permute-start(bf16[448,6144]{1,0:T(8,128)(2,1)S(1)} %get-tuple-element.27.args_10_), channel_id=1, source_target_pairs={{0,8},{8,0},{16,24},{24,16},{32,40},{40,32},{48,56},{56,48},{64,72... | collective-permute-start | bytes 16515080 | tf_op jit(solution)/shard_map/down_core/ppermute | solution.py:45
  14.3 9.1 %collective-permute-start.4 = (bf16[32,6144]{1,0:T(8,128)(2,1)S(1)}, bf16[32,6144]{1,0:T(8,128)(2,1)S(1)}, u32[]{:S(2)}, u32[]{:S(2)}) collective-permute-start(bf16[32,6144]{1,0:T(8,128)(2,1)S(1)} %get-tuple-element.25.args_0_), channel_id=1, source_target_pairs={{0,192},{8,56},{16,208},{24,40},{32,224},{40,24},{48,240},{56,8},{... | collective-permute-start | bytes 1179656 | tf_op jit(solution)/shard_map/gather_twrap/ppermute | solution.py:45
  17.4 7.8 %collective-permute-start.5 = (bf16[32,6144]{1,0:T(8,128)(2,1)S(1)}, bf16[32,6144]{1,0:T(8,128)(2,1)S(1)}, u32[]{:S(2)}, u32[]{:S(2)}) collective-permute-start(bf16[32,6144]{1,0:T(8,128)(2,1)S(1)} %get-tuple-element.26.after.args_1_), channel_id=1, source_target_pairs={{0,64},{8,24},{16,80},{24,8},{32,96},{40,56},{48,112},{56,40},{64,... | collective-permute-start | bytes 1179656 | tf_op jit(solution)/shard_map/gather_tnear/ppermute | solution.py:45
  17.6 11.9 %collective-permute-start.6 = (bf16[32,6144]{1,0:T(8,128)(2,1)S(1)}, bf16[32,6144]{1,0:T(8,128)(2,1)S(1)}, u32[]{:S(2)}, u32[]{:S(2)}) collective-permute-start(bf16[32,6144]{1,0:T(8,128)(2,1)S(1)} %get-tuple-element.25.args_0_), channel_id=1, source_target_pairs={{0,64},{8,24},{16,80},{24,8},{32,96},{40,56},{48,112},{56,40},{64,... | collective-permute-start | bytes 1179656 | tf_op jit(solution)/shard_map/gather_tnear/ppermute | solution.py:45
  19.4 10.0 %collective-permute-start.7 = (bf16[32,6144]{1,0:T(8,128)(2,1)S(1)}, bf16[32,6144]{1,0:T(8,128)(2,1)S(1)}, u32[]{:S(2)}, u32[]{:S(2)}) collective-permute-start(bf16[32,6144]{1,0:T(8,128)(2,1)S(1)} %get-tuple-element.26.after.args_1_), channel_id=1, source_target_pairs={{0,192},{8,56},{16,208},{24,40},{32,224},{40,24},{48,240},{56,8},{... | collective-permute-start | bytes 1179656 | tf_op jit(solution)/shard_map/gather_twrap/ppermute | solution.py:45
  23.4 10.2 %collective-permute-start.8 = (bf16[32,6144]{1,0:T(8,128)(2,1)S(1)}, bf16[32,6144]{1,0:T(8,128)(2,1)S(1)}, u32[]{:S(2)}, u32[]{:S(2)}) collective-permute-start(bf16[32,6144]{1,0:T(8,128)(2,1)S(1)} %collective-permute-done.4.args_2_), channel_id=1, source_target_pairs={{0,64},{8,24},{16,80},{24,8},{32,96},{40,56},{48,112},{56,40},{64,... | collective-permute-start | bytes 1179656 | tf_op jit(solution)/shard_map/gather2_tnear/ppermute | solution.py:45
  25.2 9.0 %collective-permute-start.9 = (bf16[32,6144]{1,0:T(8,128)(2,1)S(1)}, bf16[32,6144]{1,0:T(8,128)(2,1)S(1)}, u32[]{:S(2)}, u32[]{:S(2)}) collective-permute-start(bf16[32,6144]{1,0:T(8,128)(2,1)S(1)} %collective-permute-done.5.args_3_), channel_id=1, source_target_pairs={{0,192},{8,56},{16,208},{24,40},{32,224},{40,24},{48,240},{56,8},{... | collective-permute-start | bytes 1179656 | tf_op jit(solution)/shard_map/gather2_twrap/ppermute | solution.py:45
  41.4 7.9 %collective-permute-start.11 = (bf16[32,6144]{1,0:T(8,128)(2,1)S(1)}, bf16[32,6144]{1,0:T(8,128)(2,1)S(1)}, u32[]{:S(2)}, u32[]{:S(2)}) collective-permute-start(bf16[32,6144]{1,0:T(8,128)(2,1)S(1)} %get-tuple-element.30), channel_id=1, source_target_pairs={{0,64},{8,24},{16,80},{24,8},{32,96},{40,56},{48,112},{56,40},{64,... | collective-permute-start | bytes 1179656 | tf_op jit(solution)/shard_map/reduce2_tnear/ppermute | solution.py:45
  41.5 11.5 %collective-permute-start.16 = (bf16[32,6144]{1,0:T(8,128)(2,1)S(1)}, bf16[32,6144]{1,0:T(8,128)(2,1)S(1)}, u32[]{:S(2)}, u32[]{:S(2)}) collective-permute-start(bf16[32,6144]{1,0:T(8,128)(2,1)S(1)} %get-tuple-element.38), channel_id=1, source_target_pairs={{0,192},{8,56},{16,208},{24,40},{32,224},{40,24},{48,240},{56,8},{... | collective-permute-start | bytes 1179656 | tf_op jit(solution)/shard_map/reduce2_twrap/ppermute | solution.py:45
  49.4 8.0 %collective-permute-start.12 = (bf16[32,6144]{1,0:T(8,128)(2,1)S(1)}, bf16[32,6144]{1,0:T(8,128)(2,1)S(1)}, u32[]{:S(2)}, u32[]{:S(2)}) collective-permute-start(bf16[32,6144]{1,0:T(8,128)(2,1)S(1)} %get-tuple-element.33), channel_id=1, source_target_pairs={{0,64},{8,24},{16,80},{24,8},{32,96},{40,56},{48,112},{56,40},{64,... | collective-permute-start | bytes 1179656 | tf_op jit(solution)/shard_map/reduce_tnear/ppermute | solution.py:45
  49.6 9.1 %collective-permute-start.13 = (bf16[32,6144]{1,0:T(8,128)(2,1)S(1)}, bf16[32,6144]{1,0:T(8,128)(2,1)S(1)}, u32[]{:S(2)}, u32[]{:S(2)}) collective-permute-start(bf16[32,6144]{1,0:T(8,128)(2,1)S(1)} %get-tuple-element.34), channel_id=1, source_target_pairs={{0,192},{8,56},{16,208},{24,40},{32,224},{40,24},{48,240},{56,8},{... | collective-permute-start | bytes 1179656 | tf_op jit(solution)/shard_map/reduce_twrap/ppermute | solution.py:45
  51.6 11.3 %collective-permute-start.15 = (bf16[32,6144]{1,0:T(8,128)(2,1)S(1)}, bf16[32,6144]{1,0:T(8,128)(2,1)S(1)}, u32[]{:S(2)}, u32[]{:S(2)}) collective-permute-start(bf16[32,6144]{1,0:T(8,128)(2,1)S(1)} %get-tuple-element.36), channel_id=1, source_target_pairs={{0,192},{8,56},{16,208},{24,40},{32,224},{40,24},{48,240},{56,8},{... | collective-permute-start | bytes 1179656 | tf_op jit(solution)/shard_map/reduce_twrap/ppermute | solution.py:45
  53.1 10.7 %collective-permute-start.17 = (bf16[32,6144]{1,0:T(8,128)(2,1)S(1)}, bf16[32,6144]{1,0:T(8,128)(2,1)S(1)}, u32[]{:S(2)}, u32[]{:S(2)}) collective-permute-start(bf16[32,6144]{1,0:T(8,128)(2,1)S(1)} %merge.3), channel_id=1, source_target_pairs={{0,64},{8,24},{16,80},{24,8},{32,96},{40,56},{48,112},{56,40},{64,... | collective-permute-start | bytes 1179656 | tf_op jit(solution)/shard_map/reduce_tnear/ppermute | solution.py:45
  58.9 8.4 %collective-permute-start.14 = (bf16[16,6144]{1,0:T(8,128)(2,1)S(1)}, bf16[16,6144]{1,0:T(8,128)(2,1)S(1)}, u32[]{:S(2)}, u32[]{:S(2)}) collective-permute-start(bf16[16,6144]{1,0:T(8,128)(2,1)S(1)} %slice.33), channel_id=1, source_target_pairs={{0,16},{8,72},{16,0},{24,88},{32,48},{40,104},{48,32},{56,120},{64... | collective-permute-start | bytes 589832 | tf_op jit(solution)/shard_map/home_snear/ppermute | solution.py:45
  63.9 8.0 %collective-permute-start.18 = (bf16[16,6144]{1,0:T(8,128)(2,1)S(1)}, bf16[16,6144]{1,0:T(8,128)(2,1)S(1)}, u32[]{:S(2)}, u32[]{:S(2)}) collective-permute-start(bf16[16,6144]{1,0:T(8,128)(2,1)S(1)} %get-tuple-element.39), channel_id=1, source_target_pairs={{0,48},{8,200},{16,32},{24,216},{32,16},{40,232},{48,0},{56,248},{... | collective-permute-start | bytes 589832 | tf_op jit(solution)/shard_map/home_swrap/ppermute | solution.py:45
  66.6 7.2 %collective-permute-start.19 = (bf16[16,6144]{1,0:T(8,128)(2,1)S(1)}, bf16[16,6144]{1,0:T(8,128)(2,1)S(1)}, u32[]{:S(2)}, u32[]{:S(2)}) collective-permute-start(bf16[16,6144]{1,0:T(8,128)(2,1)S(1)} %get-tuple-element.40), channel_id=1, source_target_pairs={{0,32},{8,136},{16,48},{24,152},{32,0},{40,168},{48,16},{56,184},{... | collective-permute-start | bytes 589832 | tf_op jit(solution)/shard_map/home_sfar/ppermute | solution.py:45

commit v5 on v4

--- a/solution.py
+++ b/solution.py
@@ -1,3 +1,5 @@
+import functools
+
 import jax
 import jax.numpy as jnp
 from jax import lax
@@ -50,7 +52,7 @@
 
 
 def attend_kernel(
-    counts, lengths_in, q_in, k_in, v_in, gain_in, down, attended, normed, down_held, lengths, q, k, v, gain, sems
+    counts, lengths_in, q_in, k_in, v_in, gain_in, up, down, attended, normed, weights, lengths, q, k, v, gain, sems
 ):
     copies = [
         pltpu.make_async_copy(a, b, sems.at[i])
@@ -61,7 +63,8 @@
                 (q_in, q),
                 (v_in, v),
                 (gain_in, gain),
-                (down, down_held),
+                (up, weights.at[:HIDDEN]),
+                (down, weights.at[HIDDEN:]),
             )
         )
     ]
@@ -116,9 +119,10 @@
     copies[4].wait()
     normed[...] = (attended[...].astype(jnp.float32) * factor * gain[...]).astype(jnp.bfloat16)
     copies[5].wait()
-
-
-def attend(queries, cache_keys, cache_values, lengths, counts, norm_gain, down_rows):
+    copies[6].wait()
+
+
+def attend(queries, cache_keys, cache_values, lengths, counts, norm_gain, up_rows, down_rows):
     vmem = pl.BlockSpec(memory_space=pltpu.VMEM)
     any_space = pl.BlockSpec(memory_space=pl.ANY)
     return pl.pallas_call(
@@ -126,9 +130,9 @@
         out_shape=(
             jax.ShapeDtypeStruct((SLOTS, D), jnp.bfloat16),
             jax.ShapeDtypeStruct((SLOTS, D), jnp.bfloat16),
-            jax.ShapeDtypeStruct((HIDDEN, D), jnp.bfloat16),
+            jax.ShapeDtypeStruct((2 * HIDDEN, D), jnp.bfloat16),
         ),
-        in_specs=[pl.BlockSpec(memory_space=pltpu.SMEM)] + [any_space] * 6,
+        in_specs=[pl.BlockSpec(memory_space=pltpu.SMEM)] + [any_space] * 7,
         out_specs=(vmem, vmem, vmem),
         scratch_shapes=[
             pltpu.SMEM((SLOTS,), jnp.int32),
@@ -136,42 +140,22 @@
             pltpu.VMEM((POOL, KVH * HD), jnp.bfloat16),
             pltpu.VMEM((POOL, KVH * HD), jnp.bfloat16),
             pltpu.VMEM((1, D), jnp.float32),
-            pltpu.SemaphoreType.DMA((6,)),
+            pltpu.SemaphoreType.DMA((7,)),
         ],
         compiler_params=pltpu.CompilerParams(vmem_limit_bytes=16 * 2**20),
         name="attend",
-    )(counts, *map(in_hbm, (lengths, queries, cache_keys, cache_values, norm_gain.reshape(1, D), down_rows)))
-
-
-def fetch_kernel(weights, after, held, sem):
-    copy = pltpu.make_async_copy(weights, held, sem)
-    copy.start()
-    copy.wait()
-
-
-def fetch(weights, after):
-    any_space = pl.BlockSpec(memory_space=pl.ANY)
-    return pl.pallas_call(
-        fetch_kernel,
-        out_shape=jax.ShapeDtypeStruct((HIDDEN, D), jnp.bfloat16),
-        in_specs=[any_space] * 2,
-        out_specs=pl.BlockSpec(memory_space=pltpu.VMEM),
-        scratch_shapes=[pltpu.SemaphoreType.DMA],
-        compiler_params=pltpu.CompilerParams(vmem_limit_bytes=16 * 2**20),
-        cost_estimate=pl.CostEstimate(flops=0, bytes_accessed=4 * HIDDEN * D, transcendentals=0),
-        name="fetch",
-    )(in_hbm(weights), after)
-
-
-def ffn_kernel(*args):
-    blocks, up, down, outs, (total, hidden) = args[:8], args[8:10], args[10:12], args[12:20], args[20:]
+    )(counts, *map(in_hbm, (lengths, queries, cache_keys, cache_values, norm_gain.reshape(1, D), up_rows, down_rows)))
+
+
+def up_kernel(*args):
+    blocks, weights, (hidden, total) = args[:8], args[8:10], args[10:]
     total[...] = jnp.zeros_like(total)
 
     @pl.loop(0, D // CHUNK)
     def _(step):
         cols = pl.ds(pl.multiple_of(step * CHUNK, CHUNK), CHUNK)
         total[...] += lax.dot_general(
-            jnp.concatenate([w[:, cols] for w in up], axis=0),
+            jnp.concatenate([w[:HIDDEN, cols] for w in weights], axis=0),
             jnp.concatenate([b[:, cols] for b in blocks], axis=0),
             (((1,), (1,)), ((), ())),
             preferred_element_type=jnp.float32,
@@ -180,57 +164,72 @@
     value = total[...]
     hidden[...] = (value / (1.0 + jnp.exp(-value))).astype(jnp.bfloat16).T
 
+
+def project_up(blocks, weights):
+    vmem = pl.BlockSpec(memory_space=pltpu.VMEM)
+    rows = len(blocks) * PAIR
+    return pl.pallas_call(
+        up_kernel,
+        out_shape=jax.ShapeDtypeStruct((rows, 2 * HIDDEN), jnp.bfloat16),
+        in_specs=[vmem] * 10,
+        out_specs=vmem,
+        scratch_shapes=[pltpu.VMEM((2 * HIDDEN, rows), jnp.float32)],
+        compiler_params=pltpu.CompilerParams(vmem_limit_bytes=16 * 2**20),
+        cost_estimate=pl.CostEstimate(flops=4 * rows * HIDDEN * D, bytes_accessed=2 * rows * D, transcendentals=0),
+        name="up",
+    )(*blocks, *weights)
+
+
+def down_kernel(begin, hidden, one, two, *outs):
+    rows = pl.ds(begin * PAIR, len(outs) * PAIR)
+
     @pl.loop(0, D // CHUNK)
     def _(step):
         cols = pl.ds(pl.multiple_of(step * CHUNK, CHUNK), CHUNK)
         product = jnp.dot(
-            hidden[...],
-            jnp.concatenate([w[:, cols] for w in down], axis=0),
+            hidden[rows, :],
+            jnp.concatenate([one[HIDDEN:, cols], two[HIDDEN:, cols]], axis=0),
             preferred_element_type=jnp.float32,
         ).astype(jnp.bfloat16)
         for i, out in enumerate(outs):
             out[:, cols] = product[i * PAIR : (i + 1) * PAIR]
 
 
-def feed_forward(blocks, up, down):
-    vmem = pl.BlockSpec(memory_space=pltpu.VMEM)
-    return pl.pallas_call(
-        ffn_kernel,
-        out_shape=[jax.ShapeDtypeStruct((PAIR, D), jnp.bfloat16)] * 8,
-        in_specs=[vmem] * 12,
-        out_specs=[vmem] * 8,
-        scratch_shapes=[
-            pltpu.VMEM((2 * HIDDEN, 8 * PAIR), jnp.float32),
-            pltpu.VMEM((8 * PAIR, 2 * HIDDEN), jnp.bfloat16),
-        ],
-        compiler_params=pltpu.CompilerParams(vmem_limit_bytes=16 * 2**20),
-        name="feed_forward",
-    )(*blocks, *up, *down)
+def project_down(hidden, weights, begin, end):
+    vmem = pl.BlockSpec(memory_space=pltpu.VMEM)
+    n = end - begin
+    return pl.pallas_call(
+        functools.partial(down_kernel, begin),
+        out_shape=[jax.ShapeDtypeStruct((PAIR, D), jnp.bfloat16)] * n,
+        in_specs=[vmem] * 3,
+        out_specs=[vmem] * n,
+        compiler_params=pltpu.CompilerParams(vmem_limit_bytes=16 * 2**20),
+        cost_estimate=pl.CostEstimate(
+            flops=4 * n * PAIR * HIDDEN * D, bytes_accessed=2 * n * PAIR * D, transcendentals=0
+        ),
+        name="down",
+    )(hidden, *weights)
 
 
 def f32(x):
     return x.astype(jnp.float32)
 
 
-def pack_kernel(own, near, wrap, far, held, after, first, second, handed):
-    first[:SLOTS] = own[...]
-    first[SLOTS:] = near[...]
-    second[:SLOTS] = wrap[...]
-    second[SLOTS:] = far[...]
-
-
-def pack(own, near, wrap, far, held, after):
-    vmem = pl.BlockSpec(memory_space=pltpu.VMEM)
-    block = jax.ShapeDtypeStruct((PAIR, D), jnp.bfloat16)
+def pack_kernel(one, two, block):
+    block[:SLOTS] = one[...]
+    block[SLOTS:] = two[...]
+
+
+def pack(one, two):
+    vmem = pl.BlockSpec(memory_space=pltpu.VMEM)
     return pl.pallas_call(
         pack_kernel,
-        out_shape=[block, block, jax.ShapeDtypeStruct(held.shape, held.dtype)],
-        in_specs=[vmem] * 5 + [pl.BlockSpec(memory_space=pl.ANY)],
-        out_specs=[vmem] * 3,
-        input_output_aliases={4: 2},
+        out_shape=jax.ShapeDtypeStruct((PAIR, D), jnp.bfloat16),
+        in_specs=[vmem] * 2,
+        out_specs=vmem,
         compiler_params=pltpu.CompilerParams(vmem_limit_bytes=16 * 2**20),
         name="pack",
-    )(own, near, wrap, far, held, after)
+    )(one, two)
 
 
 def merge_kernel(mine, arrived, *refs):
@@ -256,22 +255,21 @@
 def on_device(
     queries, cache_keys, cache_values, lengths, counts, norm_gain, up_weight, down_weight
 ):
-    up_own = up_weight.T
-    up_other = send(up_own, "core", "up")
-    attended, normed, down_held = attend(
-        queries, cache_keys, cache_values, lengths, counts, norm_gain, down_weight
+    attended, normed, weights = attend(
+        queries, cache_keys, cache_values, lengths, counts, norm_gain, up_weight.T, down_weight
     )
+    weights = weights, send(weights, "core", "weights")
     by_wrap, by_far, by_near = [send(normed, r, "gather") for r in ("swrap", "sfar", "snear")]
-    first, second, down_held = pack(normed, by_near, by_wrap, by_far, down_held, up_other)
-    down_other = send(down_held, "core", "down")
-    up_held = fetch(up_own, second)
+    first = pack(normed, by_near)
+    second = pack(by_wrap, by_far)
     first_w, second_n = send(first, "twrap", "gather"), send(second, "tnear", "gather")
     second_w, first_n = send(second, "twrap", "gather"), send(first, "tnear", "gather")
     first_f, second_f = send(first_w, "tnear", "gather2"), send(second_n, "twrap", "gather2")
-    blocks = [first, second, first_w, second_n, first_n, second_w, first_f, second_f]
-    first, second, first_w, second_n, first_n, second_w, first_f, second_f = feed_forward(
-        blocks, (up_held, up_other), (down_held, down_other)
+    hidden = project_up(
+        [first, second, first_w, second_n, first_n, second_w, first_f, second_f], weights
     )
+    first_f, second_f = project_down(hidden, weights, 6, 8)
+    first, second, first_w, second_n, first_n, second_w = project_down(hidden, weights, 0, 6)
     far_first = send(first_f, "tnear", "reduce2")
     far_second = send(second_f, "twrap", "reduce2")
     first_w, first_n, second_w = merge(first_w, far_first, first_n, second_w)

time: 74.7 us -> 78.5 us (1.051); the launches traced: 74.5 us -> 77.4 us
  starting transfers between devices: 22.2 us -> 27 us
  waiting for transfers between devices: 37 us -> 34.7 us
    ppermute x20 -> x19, starting transfers between devices: 22.2 us -> 27 us  [send(): return lax.ppermute(value, 'dp', ROUTES[route])]
    ppermute x20 -> x19, waiting for transfers between devices: 37 us -> 34.7 us  [send(): return lax.ppermute(value, 'dp', ROUTES[route])]
    pallas_call x1, Pallas kernels: 3.49 us -> 4.92 us  [attend(): pl.pallas_call(attend_kernel, out_shape=(jax.ShapeDtypeStruct((SLOTS, D),...]
    pallas_call x3 -> x5, Pallas kernels: 9.81 us -> 8.62 us  [the longest x2 4.98 us: project_down(): pl.pallas_call(functools.partial(down_kernel, begin), out_shape=[jax.Shap...]
  transfers between devices with their start and end apart: 20 -> 19, of which waited for: 14 -> 12; matrix products, arithmetic and copies ran while one was open for 0% -> 0% of each run, Pallas kernels for 8% -> 4%
where the time goes in v5:
time: 78.5 us; the launch traced here: 77.4 us
  waiting for transfers between devices  34.7 us (44%)
  starting transfers between devices  27 us (34%)
  Pallas kernels  13.7 us (17%)
  other arithmetic  1.06 us (1%)
    ppermute x19, waiting for transfers between devices, send(): return lax.ppermute(value, 'dp', ROUTES[route])  34.7 us
    ppermute x19, starting transfers between devices, send(): return lax.ppermute(value, 'dp', ROUTES[route])  27 us
    pallas_call x2, Pallas kernels, project_down(): pl.pallas_call(functools.partial(down_kernel, begin), out_shape=[jax.Shap...  4.98 us
    pallas_call x1, Pallas kernels, attend(): pl.pallas_call(attend_kernel, out_shape=(jax.ShapeDtypeStruct((SLOTS, D),...  4.92 us
    pallas_call x1, Pallas kernels, project_up(): pl.pallas_call(up_kernel, out_shape=jax.ShapeDtypeStruct((rows, 2 * HIDDE...  3.59 us
  transfers between devices with their start and end apart: 19, of which 12 were waited for; matrix products, arithmetic and copies ran while one was open for 0% of the time, Pallas kernels for 4%

profile of v5, /device:TPU:128, one launch (start us, length us, event | category | flops | bytes accessed | tf_op | source)
XLA Modules:
  0.0 77.4 jit_solution(15709468873878953325)
XLA Ops:
  0.7 4.9 %attend.1 = (bf16[16,6144]{1,0:T(8,128)(2,1)S(1)}, bf16[16,6144]{1,0:T(8,128)(2,1)S(1)}, bf16[896,6144]{1,0:T(8,128)(2,1)S(1)}) custom-call(s32[1]{0:T(128)S(6)} %copy.9.counts, s32[16]{0:T(128)} %lengths_in.1, bf16[16,6144]{1,0:T(8,128)(2,1)} %q_in.1, bf16[1024,512]{1,0:T(8,128)(2,1)} %k_in.1, bf16[1024,512]{1,0:T(8,128)(2,1)} %v_in.1, f32[1,6144]{1,0:T(1,128)} %bitcast.3, ...), custom_call_target="tpu_custom_call" | custom-call | tf_op jit(solution)/shard_map/attend/pallas_call | solution.py:128
  5.6 0.1 collective-permute-start.9
  5.7 1.6 %collective-permute-start = (bf16[16,6144]{1,0:T(8,128)(2,1)S(1)}, bf16[16,6144]{1,0:T(8,128)(2,1)S(1)}, u32[]{:S(2)}, u32[]{:S(2)}) collective-permute-start(bf16[16,6144]{1,0:T(8,128)(2,1)S(1)} %get-tuple-element.20.one), channel_id=1, source_target_pairs={{0,16},{8,72},{16,0},{24,88},{32,48},{40,104},{48,32},{56,120},{64... | collective-permute-start | bytes 589832 | tf_op jit(solution)/shard_map/gather_snear/ppermute | solution.py:47
  7.3 2.7 %collective-permute-start.2 = (bf16[16,6144]{1,0:T(8,128)(2,1)S(1)}, bf16[16,6144]{1,0:T(8,128)(2,1)S(1)}, u32[]{:S(2)}, u32[]{:S(2)}) collective-permute-start(bf16[16,6144]{1,0:T(8,128)(2,1)S(1)} %get-tuple-element.20.one), channel_id=1, source_target_pairs={{0,32},{8,136},{16,48},{24,152},{32,0},{40,168},{48,16},{56,184},{... | collective-permute-start | bytes 589832 | tf_op jit(solution)/shard_map/gather_sfar/ppermute | solution.py:47
  10.0 0.5 collective-permute-start.1
  10.5 1.0 %collective-permute-done.two = bf16[16,6144]{1,0:T(8,128)(2,1)S(1)} collective-permute-done((bf16[16,6144]{1,0:T(8,128)(2,1)S(1)}, bf16[16,6144]{1,0:T(8,128)(2,1)S(1)}, u32[]{:S(2)}, u32[]{:S(2)}) %collective-permute-start) | collective-permute-done | bytes 196640 | tf_op jit(solution)/shard_map/gather_snear/ppermute | solution.py:47
  11.5 3.1 %collective-permute-start.3 = (bf16[32,6144]{1,0:T(8,128)(2,1)S(1)}, bf16[32,6144]{1,0:T(8,128)(2,1)S(1)}, u32[]{:S(2)}, u32[]{:S(2)}) collective-permute-start(bf16[32,6144]{1,0:T(8,128)(2,1)S(1)} %pack.2.args_0_), channel_id=1, source_target_pairs={{0,192},{8,56},{16,208},{24,40},{32,224},{40,24},{48,240},{56,8},{... | collective-permute-start | bytes 1179656 | tf_op jit(solution)/shard_map/gather_twrap/ppermute | solution.py:47
  14.6 1.3 %collective-permute-done.2.two = bf16[16,6144]{1,0:T(8,128)(2,1)S(1)} collective-permute-done((bf16[16,6144]{1,0:T(8,128)(2,1)S(1)}, bf16[16,6144]{1,0:T(8,128)(2,1)S(1)}, u32[]{:S(2)}, u32[]{:S(2)}) %collective-permute-start.2) | collective-permute-done | bytes 196640 | tf_op jit(solution)/shard_map/gather_sfar/ppermute | solution.py:47
  15.8 4.1 %collective-permute-done.1.one = bf16[16,6144]{1,0:T(8,128)(2,1)S(1)} collective-permute-done((bf16[16,6144]{1,0:T(8,128)(2,1)S(1)}, bf16[16,6144]{1,0:T(8,128)(2,1)S(1)}, u32[]{:S(2)}, u32[]{:S(2)}) %collective-permute-start.1) | collective-permute-done | bytes 196640 | tf_op jit(solution)/shard_map/gather_swrap/ppermute | solution.py:47
  20.0 1.7 %collective-permute-start.4 = (bf16[32,6144]{1,0:T(8,128)(2,1)S(1)}, bf16[32,6144]{1,0:T(8,128)(2,1)S(1)}, u32[]{:S(2)}, u32[]{:S(2)}) collective-permute-start(bf16[32,6144]{1,0:T(8,128)(2,1)S(1)} %pack.3.args_1_), channel_id=1, source_target_pairs={{0,64},{8,24},{16,80},{24,8},{32,96},{40,56},{48,112},{56,40},{64,... | collective-permute-start | bytes 1179656 | tf_op jit(solution)/shard_map/gather_tnear/ppermute | solution.py:47
  21.6 0.4 collective-permute-start.5
  22.1 3.0 %collective-permute-start.6 = (bf16[32,6144]{1,0:T(8,128)(2,1)S(1)}, bf16[32,6144]{1,0:T(8,128)(2,1)S(1)}, u32[]{:S(2)}, u32[]{:S(2)}) collective-permute-start(bf16[32,6144]{1,0:T(8,128)(2,1)S(1)} %pack.3.args_1_), channel_id=1, source_target_pairs={{0,192},{8,56},{16,208},{24,40},{32,224},{40,24},{48,240},{56,8},{... | collective-permute-start | bytes 1179656 | tf_op jit(solution)/shard_map/gather_twrap/ppermute | solution.py:47
  25.1 0.0 collective-permute-done.3.args_2_
  25.1 0.1 collective-permute-start.7
  25.2 2.6 %collective-permute-done.4.args_3_ = bf16[32,6144]{1,0:T(8,128)(2,1)S(1)} collective-permute-done((bf16[32,6144]{1,0:T(8,128)(2,1)S(1)}, bf16[32,6144]{1,0:T(8,128)(2,1)S(1)}, u32[]{:S(2)}, u32[]{:S(2)}) %collective-permute-start.4) | collective-permute-done | bytes 393248 | tf_op jit(solution)/shard_map/gather_tnear/ppermute | solution.py:47
  27.8 3.0 %collective-permute-start.8 = (bf16[32,6144]{1,0:T(8,128)(2,1)S(1)}, bf16[32,6144]{1,0:T(8,128)(2,1)S(1)}, u32[]{:S(2)}, u32[]{:S(2)}) collective-permute-start(bf16[32,6144]{1,0:T(8,128)(2,1)S(1)} %collective-permute-done.4.args_3_), channel_id=1, source_target_pairs={{0,192},{8,56},{16,208},{24,40},{32,224},{40,24},{48,240},{56,8},{... | collective-permute-start | bytes 1179656 | tf_op jit(solution)/shard_map/gather2_twrap/ppermute | solution.py:47
  30.9 1.2 %collective-permute-done.5.args_4_ = bf16[32,6144]{1,0:T(8,128)(2,1)S(1)} collective-permute-done((bf16[32,6144]{1,0:T(8,128)(2,1)S(1)}, bf16[32,6144]{1,0:T(8,128)(2,1)S(1)}, u32[]{:S(2)}, u32[]{:S(2)}) %collective-permute-start.5) | collective-permute-done | bytes 393248 | tf_op jit(solution)/shard_map/gather_tnear/ppermute | solution.py:47
  32.0 0.0 collective-permute-done.6.args_5_
  32.1 4.2 %collective-permute-done.7.args_6_ = bf16[32,6144]{1,0:T(8,128)(2,1)S(1)} collective-permute-done((bf16[32,6144]{1,0:T(8,128)(2,1)S(1)}, bf16[32,6144]{1,0:T(8,128)(2,1)S(1)}, u32[]{:S(2)}, u32[]{:S(2)}) %collective-permute-start.7) | collective-permute-done | bytes 393248 | tf_op jit(solution)/shard_map/gather2_tnear/ppermute | solution.py:47
  36.3 0.6 collective-permute-done.8.args_7_
  36.8 0.0 collective-permute-done.9.args_9_.two
  36.8 3.6 %up.1.hidden = bf16[256,896]{1,0:T(8,128)(2,1)S(1)} custom-call(bf16[32,6144]{1,0:T(8,128)(2,1)S(1)} %pack.2.args_0_, bf16[32,6144]{1,0:T(8,128)(2,1)S(1)} %pack.3.args_1_, bf16[32,6144]{1,0:T(8,128)(2,1)S(1)} %collective-permute-done.3.args_2_, bf16[32,6144]{1,0:T(8,128)(2,1)S(1)} %collective-permute-done.4.args_3_, ...), custom_call_target="tpu_custom_call" | custom-call | flops 2818572288 | bytes 3145728 | tf_op jit(solution)/shard_map/up/pallas_call | solution.py:171
  40.4 2.2 %down.5 = (bf16[32,6144]{1,0:T(8,128)(2,1)S(1)}, bf16[32,6144]{1,0:T(8,128)(2,1)S(1)}) custom-call(bf16[256,896]{1,0:T(8,128)(2,1)S(1)} %up.1.hidden, bf16[896,6144]{1,0:T(8,128)(2,1)S(1)} %get-tuple-element.21.args_8_.one, bf16[896,6144]{1,0:T(8,128)(2,1)S(1)} %collective-permute-done.9.args_9_.two), custom_call_target="tpu_custom_call" | custom-call | flops 704643072 | bytes 786432 | tf_op jit(solution)/shard_map/down/pallas_call | solution.py:201
  42.6 1.1 %collective-permute-start.10 = (bf16[32,6144]{1,0:T(8,128)(2,1)S(1)}, bf16[32,6144]{1,0:T(8,128)(2,1)S(1)}, u32[]{:S(2)}, u32[]{:S(2)}) collective-permute-start(bf16[32,6144]{1,0:T(8,128)(2,1)S(1)} %get-tuple-element.24), channel_id=1, source_target_pairs={{0,64},{8,24},{16,80},{24,8},{32,96},{40,56},{48,112},{56,40},{64,... | collective-permute-start | bytes 1179656 | tf_op jit(solution)/shard_map/reduce2_tnear/ppermute | solution.py:47
  43.7 2.2 %collective-permute-start.15 = (bf16[32,6144]{1,0:T(8,128)(2,1)S(1)}, bf16[32,6144]{1,0:T(8,128)(2,1)S(1)}, u32[]{:S(2)}, u32[]{:S(2)}) collective-permute-start(bf16[32,6144]{1,0:T(8,128)(2,1)S(1)} %get-tuple-element.32), channel_id=1, source_target_pairs={{0,192},{8,56},{16,208},{24,40},{32,224},{40,24},{48,240},{56,8},{... | collective-permute-start | bytes 1179656 | tf_op jit(solution)/shard_map/reduce2_twrap/ppermute | solution.py:47
  45.9 2.8 %down.4 = (bf16[32,6144]{1,0:T(8,128)(2,1)S(1)}, bf16[32,6144]{1,0:T(8,128)(2,1)S(1)}, bf16[32,6144]{1,0:T(8,128)(2,1)S(1)}, bf16[32,6144]{1,0:T(8,128)(2,1)S(1)...) custom-call(bf16[256,896]{1,0:T(8,128)(2,1)S(1)} %up.1.hidden, ...), custom_call_target="tpu_custom_call" | custom-call | flops 2113929216 | bytes 2359296 | tf_op jit(solution)/shard_map/down/pallas_call | solution.py:201
  48.7 1.8 %collective-permute-done.10.arrived = bf16[32,6144]{1,0:T(8,128)(2,1)S(1)} collective-permute-done((bf16[32,6144]{1,0:T(8,128)(2,1)S(1)}, bf16[32,6144]{1,0:T(8,128)(2,1)S(1)}, u32[]{:S(2)}, u32[]{:S(2)}) %collective-permute-start.10) | collective-permute-done | bytes 393248 | tf_op jit(solution)/shard_map/reduce2_tnear/ppermute | solution.py:47
  50.5 0.1 merge.2
  50.6 1.3 %collective-permute-start.11 = (bf16[32,6144]{1,0:T(8,128)(2,1)S(1)}, bf16[32,6144]{1,0:T(8,128)(2,1)S(1)}, u32[]{:S(2)}, u32[]{:S(2)}) collective-permute-start(bf16[32,6144]{1,0:T(8,128)(2,1)S(1)} %get-tuple-element.27), channel_id=1, source_target_pairs={{0,64},{8,24},{16,80},{24,8},{32,96},{40,56},{48,112},{56,40},{64,... | collective-permute-start | bytes 1179656 | tf_op jit(solution)/shard_map/reduce_tnear/ppermute | solution.py:47
  51.9 2.2 %collective-permute-start.12 = (bf16[32,6144]{1,0:T(8,128)(2,1)S(1)}, bf16[32,6144]{1,0:T(8,128)(2,1)S(1)}, u32[]{:S(2)}, u32[]{:S(2)}) collective-permute-start(bf16[32,6144]{1,0:T(8,128)(2,1)S(1)} %get-tuple-element.28), channel_id=1, source_target_pairs={{0,192},{8,56},{16,208},{24,40},{32,224},{40,24},{48,240},{56,8},{... | collective-permute-start | bytes 1179656 | tf_op jit(solution)/shard_map/reduce_twrap/ppermute | solution.py:47
  54.1 1.1 %collective-permute-start.14 = (bf16[32,6144]{1,0:T(8,128)(2,1)S(1)}, bf16[32,6144]{1,0:T(8,128)(2,1)S(1)}, u32[]{:S(2)}, u32[]{:S(2)}) collective-permute-start(bf16[32,6144]{1,0:T(8,128)(2,1)S(1)} %get-tuple-element.30), channel_id=1, source_target_pairs={{0,192},{8,56},{16,208},{24,40},{32,224},{40,24},{48,240},{56,8},{... | collective-permute-start | bytes 1179656 | tf_op jit(solution)/shard_map/reduce_twrap/ppermute | solution.py:47
  55.1 0.0 collective-permute-done.15.arrived
  55.1 0.1 merge.3
  55.2 0.3 collective-permute-start.16
  55.5 3.1 %collective-permute-done.11 = bf16[32,6144]{1,0:T(8,128)(2,1)S(1)} collective-permute-done((bf16[32,6144]{1,0:T(8,128)(2,1)S(1)}, bf16[32,6144]{1,0:T(8,128)(2,1)S(1)}, u32[]{:S(2)}, u32[]{:S(2)}) %collective-permute-start.11) | collective-permute-done | bytes 393248 | tf_op jit(solution)/shard_map/reduce_tnear/ppermute | solution.py:47
  58.6 2.2 %collective-permute-done.12 = bf16[32,6144]{1,0:T(8,128)(2,1)S(1)} collective-permute-done((bf16[32,6144]{1,0:T(8,128)(2,1)S(1)}, bf16[32,6144]{1,0:T(8,128)(2,1)S(1)}, u32[]{:S(2)}, u32[]{:S(2)}) %collective-permute-start.12) | collective-permute-done | bytes 393248 | tf_op jit(solution)/shard_map/reduce_twrap/ppermute | solution.py:47
  60.9 0.1 convert_add_fusion
  61.0 0.1 collective-permute-start.13
  61.1 6.2 %collective-permute-done.14 = bf16[32,6144]{1,0:T(8,128)(2,1)S(1)} collective-permute-done((bf16[32,6144]{1,0:T(8,128)(2,1)S(1)}, bf16[32,6144]{1,0:T(8,128)(2,1)S(1)}, u32[]{:S(2)}, u32[]{:S(2)}) %collective-permute-start.14) | collective-permute-done | bytes 393248 | tf_op jit(solution)/shard_map/reduce_twrap/ppermute | solution.py:47
  67.3 0.0 collective-permute-done.16
  67.3 0.1 add_convert_fusion
  67.5 0.1 collective-permute-start.17
  67.6 2.5 %collective-permute-start.18 = (bf16[16,6144]{1,0:T(8,128)(2,1)S(1)}, bf16[16,6144]{1,0:T(8,128)(2,1)S(1)}, u32[]{:S(2)}, u32[]{:S(2)}) collective-permute-start(bf16[16,6144]{1,0:T(8,128)(2,1)S(1)} %get-tuple-element.34), channel_id=1, source_target_pairs={{0,32},{8,136},{16,48},{24,152},{32,0},{40,168},{48,16},{56,184},{... | collective-permute-start | bytes 589832 | tf_op jit(solution)/shard_map/home_sfar/ppermute | solution.py:47
  70.1 0.0 collective-permute-done.13
  70.1 6.5 %collective-permute-done.17 = bf16[16,6144]{1,0:T(8,128)(2,1)S(1)} collective-permute-done((bf16[16,6144]{1,0:T(8,128)(2,1)S(1)}, bf16[16,6144]{1,0:T(8,128)(2,1)S(1)}, u32[]{:S(2)}, u32[]{:S(2)}) %collective-permute-start.17) | collective-permute-done | bytes 196640 | tf_op jit(solution)/shard_map/home_swrap/ppermute | solution.py:47
  76.6 0.0 collective-permute-done.18
  76.6 0.8 %fusion.3 = bf16[16,6144]{1,0:T(8,128)(2,1)} fusion(f32[32,6144]{1,0:T(8,128)S(1)} %convert_add_fusion, bf16[16,6144]{1,0:T(8,128)(2,1)S(1)} %collective-permute-done.18, bf16[16,6144]{1,0:T(8,128)(2,1)S(1)} %collective-permute-done.17, bf16[16,6144]{1,0:T(8,128)(2,1)S(1)} %collective-permute-done.13, bf16[16,6144]{1,0:T(8,128)(2,1)S(1)} %get-tuple-element.19), kind=kLoop, calls=%fused_computation.7 | loop fusion | flops 884736 | bytes 1376256 | tf_op jit(solution)/shard_map/convert_element_type | solution.py:287
  (4 shorter events, 0.1 us)
Async XLA Ops:
  5.6 31.2 %collective-permute-start.9 = (bf16[896,6144]{1,0:T(8,128)(2,1)S(1)}, bf16[896,6144]{1,0:T(8,128)(2,1)S(1)}, u32[]{:S(2)}, u32[]{:S(2)}) collective-permute-start(bf16[896,6144]{1,0:T(8,128)(2,1)S(1)} %get-tuple-element.21.args_8_.one), channel_id=1, source_target_pairs={{0,8},{8,0},{16,24},{24,16},{32,40},{40,32},{48,56},{56,48},{64,72... | collective-permute-start | bytes 33030152 | tf_op jit(solution)/shard_map/weights_core/ppermute | solution.py:47
  5.7 5.8 %collective-permute-start = (bf16[16,6144]{1,0:T(8,128)(2,1)S(1)}, bf16[16,6144]{1,0:T(8,128)(2,1)S(1)}, u32[]{:S(2)}, u32[]{:S(2)}) collective-permute-start(bf16[16,6144]{1,0:T(8,128)(2,1)S(1)} %get-tuple-element.20.one), channel_id=1, source_target_pairs={{0,16},{8,72},{16,0},{24,88},{32,48},{40,104},{48,32},{56,120},{64... | collective-permute-start | bytes 589832 | tf_op jit(solution)/shard_map/gather_snear/ppermute | solution.py:47
  7.3 8.6 %collective-permute-start.2 = (bf16[16,6144]{1,0:T(8,128)(2,1)S(1)}, bf16[16,6144]{1,0:T(8,128)(2,1)S(1)}, u32[]{:S(2)}, u32[]{:S(2)}) collective-permute-start(bf16[16,6144]{1,0:T(8,128)(2,1)S(1)} %get-tuple-element.20.one), channel_id=1, source_target_pairs={{0,32},{8,136},{16,48},{24,152},{32,0},{40,168},{48,16},{56,184},{... | collective-permute-start | bytes 589832 | tf_op jit(solution)/shard_map/gather_sfar/ppermute | solution.py:47
  10.0 10.0 %collective-permute-start.1 = (bf16[16,6144]{1,0:T(8,128)(2,1)S(1)}, bf16[16,6144]{1,0:T(8,128)(2,1)S(1)}, u32[]{:S(2)}, u32[]{:S(2)}) collective-permute-start(bf16[16,6144]{1,0:T(8,128)(2,1)S(1)} %get-tuple-element.20.one), channel_id=1, source_target_pairs={{0,48},{8,200},{16,32},{24,216},{32,16},{40,232},{48,0},{56,248},{... | collective-permute-start | bytes 589832 | tf_op jit(solution)/shard_map/gather_swrap/ppermute | solution.py:47
  11.5 13.6 %collective-permute-start.3 = (bf16[32,6144]{1,0:T(8,128)(2,1)S(1)}, bf16[32,6144]{1,0:T(8,128)(2,1)S(1)}, u32[]{:S(2)}, u32[]{:S(2)}) collective-permute-start(bf16[32,6144]{1,0:T(8,128)(2,1)S(1)} %pack.2.args_0_), channel_id=1, source_target_pairs={{0,192},{8,56},{16,208},{24,40},{32,224},{40,24},{48,240},{56,8},{... | collective-permute-start | bytes 1179656 | tf_op jit(solution)/shard_map/gather_twrap/ppermute | solution.py:47
  20.0 7.9 %collective-permute-start.4 = (bf16[32,6144]{1,0:T(8,128)(2,1)S(1)}, bf16[32,6144]{1,0:T(8,128)(2,1)S(1)}, u32[]{:S(2)}, u32[]{:S(2)}) collective-permute-start(bf16[32,6144]{1,0:T(8,128)(2,1)S(1)} %pack.3.args_1_), channel_id=1, source_target_pairs={{0,64},{8,24},{16,80},{24,8},{32,96},{40,56},{48,112},{56,40},{64,... | collective-permute-start | bytes 1179656 | tf_op jit(solution)/shard_map/gather_tnear/ppermute | solution.py:47
  21.6 10.4 %collective-permute-start.5 = (bf16[32,6144]{1,0:T(8,128)(2,1)S(1)}, bf16[32,6144]{1,0:T(8,128)(2,1)S(1)}, u32[]{:S(2)}, u32[]{:S(2)}) collective-permute-start(bf16[32,6144]{1,0:T(8,128)(2,1)S(1)} %pack.2.args_0_), channel_id=1, source_target_pairs={{0,64},{8,24},{16,80},{24,8},{32,96},{40,56},{48,112},{56,40},{64,... | collective-permute-start | bytes 1179656 | tf_op jit(solution)/shard_map/gather_tnear/ppermute | solution.py:47
  22.1 10.0 %collective-permute-start.6 = (bf16[32,6144]{1,0:T(8,128)(2,1)S(1)}, bf16[32,6144]{1,0:T(8,128)(2,1)S(1)}, u32[]{:S(2)}, u32[]{:S(2)}) collective-permute-start(bf16[32,6144]{1,0:T(8,128)(2,1)S(1)} %pack.3.args_1_), channel_id=1, source_target_pairs={{0,192},{8,56},{16,208},{24,40},{32,224},{40,24},{48,240},{56,8},{... | collective-permute-start | bytes 1179656 | tf_op jit(solution)/shard_map/gather_twrap/ppermute | solution.py:47
  25.1 11.2 %collective-permute-start.7 = (bf16[32,6144]{1,0:T(8,128)(2,1)S(1)}, bf16[32,6144]{1,0:T(8,128)(2,1)S(1)}, u32[]{:S(2)}, u32[]{:S(2)}) collective-permute-start(bf16[32,6144]{1,0:T(8,128)(2,1)S(1)} %collective-permute-done.3.args_2_), channel_id=1, source_target_pairs={{0,64},{8,24},{16,80},{24,8},{32,96},{40,56},{48,112},{56,40},{64,... | collective-permute-start | bytes 1179656 | tf_op jit(solution)/shard_map/gather2_tnear/ppermute | solution.py:47
  27.8 9.0 %collective-permute-start.8 = (bf16[32,6144]{1,0:T(8,128)(2,1)S(1)}, bf16[32,6144]{1,0:T(8,128)(2,1)S(1)}, u32[]{:S(2)}, u32[]{:S(2)}) collective-permute-start(bf16[32,6144]{1,0:T(8,128)(2,1)S(1)} %collective-permute-done.4.args_3_), channel_id=1, source_target_pairs={{0,192},{8,56},{16,208},{24,40},{32,224},{40,24},{48,240},{56,8},{... | collective-permute-start | bytes 1179656 | tf_op jit(solution)/shard_map/gather2_twrap/ppermute | solution.py:47
  42.6 7.9 %collective-permute-start.10 = (bf16[32,6144]{1,0:T(8,128)(2,1)S(1)}, bf16[32,6144]{1,0:T(8,128)(2,1)S(1)}, u32[]{:S(2)}, u32[]{:S(2)}) collective-permute-start(bf16[32,6144]{1,0:T(8,128)(2,1)S(1)} %get-tuple-element.24), channel_id=1, source_target_pairs={{0,64},{8,24},{16,80},{24,8},{32,96},{40,56},{48,112},{56,40},{64,... | collective-permute-start | bytes 1179656 | tf_op jit(solution)/shard_map/reduce2_tnear/ppermute | solution.py:47
  43.7 11.4 %collective-permute-start.15 = (bf16[32,6144]{1,0:T(8,128)(2,1)S(1)}, bf16[32,6144]{1,0:T(8,128)(2,1)S(1)}, u32[]{:S(2)}, u32[]{:S(2)}) collective-permute-start(bf16[32,6144]{1,0:T(8,128)(2,1)S(1)} %get-tuple-element.32), channel_id=1, source_target_pairs={{0,192},{8,56},{16,208},{24,40},{32,224},{40,24},{48,240},{56,8},{... | collective-permute-start | bytes 1179656 | tf_op jit(solution)/shard_map/reduce2_twrap/ppermute | solution.py:47
  50.6 8.0 %collective-permute-start.11 = (bf16[32,6144]{1,0:T(8,128)(2,1)S(1)}, bf16[32,6144]{1,0:T(8,128)(2,1)S(1)}, u32[]{:S(2)}, u32[]{:S(2)}) collective-permute-start(bf16[32,6144]{1,0:T(8,128)(2,1)S(1)} %get-tuple-element.27), channel_id=1, source_target_pairs={{0,64},{8,24},{16,80},{24,8},{32,96},{40,56},{48,112},{56,40},{64,... | collective-permute-start | bytes 1179656 | tf_op jit(solution)/shard_map/reduce_tnear/ppermute | solution.py:47
  51.9 9.0 %collective-permute-start.12 = (bf16[32,6144]{1,0:T(8,128)(2,1)S(1)}, bf16[32,6144]{1,0:T(8,128)(2,1)S(1)}, u32[]{:S(2)}, u32[]{:S(2)}) collective-permute-start(bf16[32,6144]{1,0:T(8,128)(2,1)S(1)} %get-tuple-element.28), channel_id=1, source_target_pairs={{0,192},{8,56},{16,208},{24,40},{32,224},{40,24},{48,240},{56,8},{... | collective-permute-start | bytes 1179656 | tf_op jit(solution)/shard_map/reduce_twrap/ppermute | solution.py:47
  54.1 13.3 %collective-permute-start.14 = (bf16[32,6144]{1,0:T(8,128)(2,1)S(1)}, bf16[32,6144]{1,0:T(8,128)(2,1)S(1)}, u32[]{:S(2)}, u32[]{:S(2)}) collective-permute-start(bf16[32,6144]{1,0:T(8,128)(2,1)S(1)} %get-tuple-element.30), channel_id=1, source_target_pairs={{0,192},{8,56},{16,208},{24,40},{32,224},{40,24},{48,240},{56,8},{... | collective-permute-start | bytes 1179656 | tf_op jit(solution)/shard_map/reduce_twrap/ppermute | solution.py:47
  55.2 12.1 %collective-permute-start.16 = (bf16[32,6144]{1,0:T(8,128)(2,1)S(1)}, bf16[32,6144]{1,0:T(8,128)(2,1)S(1)}, u32[]{:S(2)}, u32[]{:S(2)}) collective-permute-start(bf16[32,6144]{1,0:T(8,128)(2,1)S(1)} %merge.3), channel_id=1, source_target_pairs={{0,64},{8,24},{16,80},{24,8},{32,96},{40,56},{48,112},{56,40},{64,... | collective-permute-start | bytes 1179656 | tf_op jit(solution)/shard_map/reduce_tnear/ppermute | solution.py:47
  61.0 9.1 %collective-permute-start.13 = (bf16[16,6144]{1,0:T(8,128)(2,1)S(1)}, bf16[16,6144]{1,0:T(8,128)(2,1)S(1)}, u32[]{:S(2)}, u32[]{:S(2)}) collective-permute-start(bf16[16,6144]{1,0:T(8,128)(2,1)S(1)} %slice.33), channel_id=1, source_target_pairs={{0,16},{8,72},{16,0},{24,88},{32,48},{40,104},{48,32},{56,120},{64... | collective-permute-start | bytes 589832 | tf_op jit(solution)/shard_map/home_snear/ppermute | solution.py:47
  67.5 9.1 %collective-permute-start.17 = (bf16[16,6144]{1,0:T(8,128)(2,1)S(1)}, bf16[16,6144]{1,0:T(8,128)(2,1)S(1)}, u32[]{:S(2)}, u32[]{:S(2)}) collective-permute-start(bf16[16,6144]{1,0:T(8,128)(2,1)S(1)} %get-tuple-element.33), channel_id=1, source_target_pairs={{0,48},{8,200},{16,32},{24,216},{32,16},{40,232},{48,0},{56,248},{... | collective-permute-start | bytes 589832 | tf_op jit(solution)/shard_map/home_swrap/ppermute | solution.py:47
  67.6 9.0 %collective-permute-start.18 = (bf16[16,6144]{1,0:T(8,128)(2,1)S(1)}, bf16[16,6144]{1,0:T(8,128)(2,1)S(1)}, u32[]{:S(2)}, u32[]{:S(2)}) collective-permute-start(bf16[16,6144]{1,0:T(8,128)(2,1)S(1)} %get-tuple-element.34), channel_id=1, source_target_pairs={{0,32},{8,136},{16,48},{24,152},{32,0},{40,168},{48,16},{56,184},{... | collective-permute-start | bytes 589832 | tf_op jit(solution)/shard_map/home_sfar/ppermute | solution.py:47

commit v6 on v4

--- a/solution.py
+++ b/solution.py
@@ -1,3 +1,5 @@
+import functools
+
 import jax
 import jax.numpy as jnp
 from jax import lax
@@ -163,22 +165,22 @@
     )(in_hbm(weights), after)
 
 
-def ffn_kernel(*args):
-    blocks, up, down, outs, (total, hidden) = args[:8], args[8:10], args[10:12], args[12:20], args[20:]
+def ffn_kernel(n, *args):
+    blocks, up, down, outs, (total, hidden) = args[:n], args[n : n + 2], args[n + 2 : n + 4], args[n + 4 : -2], args[-2:]
     total[...] = jnp.zeros_like(total)
 
     @pl.loop(0, D // CHUNK)
     def _(step):
         cols = pl.ds(pl.multiple_of(step * CHUNK, CHUNK), CHUNK)
         total[...] += lax.dot_general(
+            jnp.concatenate([b[:, cols] for b in blocks], axis=0),
             jnp.concatenate([w[:, cols] for w in up], axis=0),
-            jnp.concatenate([b[:, cols] for b in blocks], axis=0),
             (((1,), (1,)), ((), ())),
             preferred_element_type=jnp.float32,
         )
 
     value = total[...]
-    hidden[...] = (value / (1.0 + jnp.exp(-value))).astype(jnp.bfloat16).T
+    hidden[...] = (value / (1.0 + jnp.exp(-value))).astype(jnp.bfloat16)
 
     @pl.loop(0, D // CHUNK)
     def _(step):
@@ -194,16 +196,19 @@
 
 def feed_forward(blocks, up, down):
     vmem = pl.BlockSpec(memory_space=pltpu.VMEM)
-    return pl.pallas_call(
-        ffn_kernel,
-        out_shape=[jax.ShapeDtypeStruct((PAIR, D), jnp.bfloat16)] * 8,
-        in_specs=[vmem] * 12,
-        out_specs=[vmem] * 8,
+    n = len(blocks)
+    rows = n * PAIR
+    return pl.pallas_call(
+        functools.partial(ffn_kernel, n),
+        out_shape=[jax.ShapeDtypeStruct((PAIR, D), jnp.bfloat16)] * n,
+        in_specs=[vmem] * (n + 4),
+        out_specs=[vmem] * n,
         scratch_shapes=[
-            pltpu.VMEM((2 * HIDDEN, 8 * PAIR), jnp.float32),
-            pltpu.VMEM((8 * PAIR, 2 * HIDDEN), jnp.bfloat16),
+            pltpu.VMEM((rows, 2 * HIDDEN), jnp.float32),
+            pltpu.VMEM((rows, 2 * HIDDEN), jnp.bfloat16),
         ],
         compiler_params=pltpu.CompilerParams(vmem_limit_bytes=16 * 2**20),
+        cost_estimate=pl.CostEstimate(flops=8 * rows * HIDDEN * D, bytes_accessed=4 * rows * D, transcendentals=0),
         name="feed_forward",
     )(*blocks, *up, *down)
 
@@ -213,10 +218,10 @@
 
 
 def pack_kernel(own, near, wrap, far, held, after, first, second, handed):
-    first[:SLOTS] = own[...]
-    first[SLOTS:] = near[...]
-    second[:SLOTS] = wrap[...]
-    second[SLOTS:] = far[...]
+    first[:SLOTS] = wrap[...]
+    first[SLOTS:] = far[...]
+    second[:SLOTS] = own[...]
+    second[SLOTS:] = near[...]
 
 
 def pack(own, near, wrap, far, held, after):
@@ -268,24 +273,25 @@
     first_w, second_n = send(first, "twrap", "gather"), send(second, "tnear", "gather")
     second_w, first_n = send(second, "twrap", "gather"), send(first, "tnear", "gather")
     first_f, second_f = send(first_w, "tnear", "gather2"), send(second_n, "twrap", "gather2")
-    blocks = [first, second, first_w, second_n, first_n, second_w, first_f, second_f]
-    first, second, first_w, second_n, first_n, second_w, first_f, second_f = feed_forward(
-        blocks, (up_held, up_other), (down_held, down_other)
+    up, down = (up_held, up_other), (down_held, down_other)
+    first_f, second_f = feed_forward([first_f, second_f], up, down)
+    first, second, first_w, second_n, first_n, second_w = feed_forward(
+        [first, second, first_w, second_n, first_n, second_w], up, down
     )
     far_first = send(first_f, "tnear", "reduce2")
     far_second = send(second_f, "twrap", "reduce2")
-    first_w, first_n, second_w = merge(first_w, far_first, first_n, second_w)
+    near_second = send(second_w, "twrap", "reduce")
+    first_w, first_n = merge(first_w, far_first, first_n)
     back_first = send(first_w, "twrap", "reduce")
     near_first = send(first_n, "tnear", "reduce")
-    near_second = send(second_w, "twrap", "reduce")
     (second_n,) = merge(second_n, far_second)
     back_second = send(second_n, "tnear", "reduce")
     first = f32(first) + f32(near_first) + f32(back_first)
     second = f32(second) + f32(near_second) + f32(back_second)
-    home_near = send(first[SLOTS:].astype(jnp.bfloat16), "snear", "home")
-    home_wrap = send(second[:SLOTS].astype(jnp.bfloat16), "swrap", "home")
-    home_far = send(second[SLOTS:].astype(jnp.bfloat16), "sfar", "home")
-    projected = first[:SLOTS] + f32(home_near) + f32(home_wrap) + f32(home_far)
+    home_wrap = send(first[:SLOTS].astype(jnp.bfloat16), "swrap", "home")
+    home_far = send(first[SLOTS:].astype(jnp.bfloat16), "sfar", "home")
+    home_near = send(second[SLOTS:].astype(jnp.bfloat16), "snear", "home")
+    projected = second[:SLOTS] + f32(home_near) + f32(home_wrap) + f32(home_far)
     return (f32(attended) + projected).astype(jnp.bfloat16)
 
 

time: 74.7 us -> 75.2 us (level)
  Pallas kernels: 13.5 us -> 19.1 us
  waiting for transfers between devices: 37 us -> 33 us
  starting transfers between devices: 22.2 us -> 21.1 us
    pallas_call x1 -> x2, Pallas kernels: 7.19 us -> 12.8 us  [feed_forward(): pl.pallas_call(functools.partial(ffn_kernel, n), out_shape=[jax.ShapeDtyp...]
    ppermute x20, waiting for transfers between devices: 37 us -> 33 us  [send(): return lax.ppermute(value, 'dp', ROUTES[route])]
    ppermute x20, starting transfers between devices: 22.2 us -> 21.1 us  [send(): return lax.ppermute(value, 'dp', ROUTES[route])]
  transfers between devices with their start and end apart: 20 -> 20, of which waited for: 14 -> 14; matrix products, arithmetic and copies ran while one was open for 0% -> 0% of each run, Pallas kernels for 8% -> 25%
where the time goes in v6:
time: 75.2 us; the launch traced here: 75.1 us
  waiting for transfers between devices  33 us (44%)
  starting transfers between devices  21.1 us (28%)
  Pallas kernels  19.1 us (25%)
  other arithmetic  1.06 us (1%)
    ppermute x20, waiting for transfers between devices, send(): return lax.ppermute(value, 'dp', ROUTES[route])  33 us
    ppermute x20, starting transfers between devices, send(): return lax.ppermute(value, 'dp', ROUTES[route])  21.1 us
    pallas_call x2, Pallas kernels, feed_forward(): pl.pallas_call(functools.partial(ffn_kernel, n), out_shape=[jax.ShapeDtyp...  12.8 us
    pallas_call x1, Pallas kernels, attend(): pl.pallas_call(attend_kernel, out_shape=(jax.ShapeDtypeStruct((SLOTS, D),...  3.49 us
    pallas_call x1, Pallas kernels, fetch(): pl.pallas_call(fetch_kernel, out_shape=jax.ShapeDtypeStruct((HIDDEN, D),...  2.57 us
  transfers between devices with their start and end apart: 20, of which 14 were waited for; matrix products, arithmetic and copies ran while one was open for 0% of the time, Pallas kernels for 25%

profile of v6, /device:TPU:128, one launch (start us, length us, event | category | flops | bytes accessed | tf_op | source)
XLA Modules:
  0.0 75.1 jit_solution(15209098167016166428)
XLA Ops:
  0.7 3.5 %attend.1 = (bf16[16,6144]{1,0:T(8,128)(2,1)S(1)}, bf16[16,6144]{1,0:T(8,128)(2,1)S(1)}, bf16[448,6144]{1,0:T(8,128)(2,1)S(1)}) custom-call(s32[1]{0:T(128)S(6)} %copy.11.counts, s32[16]{0:T(128)} %lengths_in.1, bf16[16,6144]{1,0:T(8,128)(2,1)} %q_in.1, bf16[1024,512]{1,0:T(8,128)(2,1)} %k_in.1, bf16[1024,512]{1,0:T(8,128)(2,1)} %v_in.1, f32[1,6144]{1,0:T(1,128)} %bitcast.4, ...), custom_call_target="tpu_custom_call" | custom-call | tf_op jit(solution)/shard_map/attend/pallas_call | solution.py:126
  4.2 1.6 %collective-permute-start = (bf16[16,6144]{1,0:T(8,128)(2,1)S(1)}, bf16[16,6144]{1,0:T(8,128)(2,1)S(1)}, u32[]{:S(2)}, u32[]{:S(2)}) collective-permute-start(bf16[16,6144]{1,0:T(8,128)(2,1)S(1)} %get-tuple-element.22.own), channel_id=1, source_target_pairs={{0,16},{8,72},{16,0},{24,88},{32,48},{40,104},{48,32},{56,120},{64... | collective-permute-start | bytes 589832 | tf_op jit(solution)/shard_map/gather_snear/ppermute | solution.py:47
  5.7 2.1 %collective-permute-start.1 = (bf16[16,6144]{1,0:T(8,128)(2,1)S(1)}, bf16[16,6144]{1,0:T(8,128)(2,1)S(1)}, u32[]{:S(2)}, u32[]{:S(2)}) collective-permute-start(bf16[16,6144]{1,0:T(8,128)(2,1)S(1)} %get-tuple-element.22.own), channel_id=1, source_target_pairs={{0,48},{8,200},{16,32},{24,216},{32,16},{40,232},{48,0},{56,248},{... | collective-permute-start | bytes 589832 | tf_op jit(solution)/shard_map/gather_swrap/ppermute | solution.py:47
  7.8 0.6 collective-permute-start.2
  8.5 1.4 %collective-permute-done.near = bf16[16,6144]{1,0:T(8,128)(2,1)S(1)} collective-permute-done((bf16[16,6144]{1,0:T(8,128)(2,1)S(1)}, bf16[16,6144]{1,0:T(8,128)(2,1)S(1)}, u32[]{:S(2)}, u32[]{:S(2)}) %collective-permute-start) | collective-permute-done | bytes 196640 | tf_op jit(solution)/shard_map/gather_snear/ppermute | solution.py:47
  9.9 3.2 %collective-permute-done.1.wrap = bf16[16,6144]{1,0:T(8,128)(2,1)S(1)} collective-permute-done((bf16[16,6144]{1,0:T(8,128)(2,1)S(1)}, bf16[16,6144]{1,0:T(8,128)(2,1)S(1)}, u32[]{:S(2)}, u32[]{:S(2)}) %collective-permute-start.1) | collective-permute-done | bytes 196640 | tf_op jit(solution)/shard_map/gather_swrap/ppermute | solution.py:47
  13.2 1.8 %collective-permute-done.2.far = bf16[16,6144]{1,0:T(8,128)(2,1)S(1)} collective-permute-done((bf16[16,6144]{1,0:T(8,128)(2,1)S(1)}, bf16[16,6144]{1,0:T(8,128)(2,1)S(1)}, u32[]{:S(2)}, u32[]{:S(2)}) %collective-permute-start.2) | collective-permute-done | bytes 196640 | tf_op jit(solution)/shard_map/gather_sfar/ppermute | solution.py:47
  15.0 0.0 collective-permute-done.3.after.args_7_.args_3_
  15.0 0.1 pack.1
  15.1 0.1 collective-permute-start.8
  15.2 3.1 %collective-permute-start.4 = (bf16[32,6144]{1,0:T(8,128)(2,1)S(1)}, bf16[32,6144]{1,0:T(8,128)(2,1)S(1)}, u32[]{:S(2)}, u32[]{:S(2)}) collective-permute-start(bf16[32,6144]{1,0:T(8,128)(2,1)S(1)} %get-tuple-element.24.args_0_), channel_id=1, source_target_pairs={{0,192},{8,56},{16,208},{24,40},{32,224},{40,24},{48,240},{56,8},{... | collective-permute-start | bytes 1179656 | tf_op jit(solution)/shard_map/gather_twrap/ppermute | solution.py:47
  18.3 0.1 collective-permute-start.5
  18.4 5.8 %collective-permute-done.4.args_2_ = bf16[32,6144]{1,0:T(8,128)(2,1)S(1)} collective-permute-done((bf16[32,6144]{1,0:T(8,128)(2,1)S(1)}, bf16[32,6144]{1,0:T(8,128)(2,1)S(1)}, u32[]{:S(2)}, u32[]{:S(2)}) %collective-permute-start.4) | collective-permute-done | bytes 393248 | tf_op jit(solution)/shard_map/gather_twrap/ppermute | solution.py:47
  24.2 0.4 collective-permute-start.10
  24.6 1.4 %collective-permute-done.5.args_3_ = bf16[32,6144]{1,0:T(8,128)(2,1)S(1)} collective-permute-done((bf16[32,6144]{1,0:T(8,128)(2,1)S(1)}, bf16[32,6144]{1,0:T(8,128)(2,1)S(1)}, u32[]{:S(2)}, u32[]{:S(2)}) %collective-permute-start.5) | collective-permute-done | bytes 393248 | tf_op jit(solution)/shard_map/gather_tnear/ppermute | solution.py:47
  26.0 1.2 %collective-permute-start.11 = (bf16[32,6144]{1,0:T(8,128)(2,1)S(1)}, bf16[32,6144]{1,0:T(8,128)(2,1)S(1)}, u32[]{:S(2)}, u32[]{:S(2)}) collective-permute-start(bf16[32,6144]{1,0:T(8,128)(2,1)S(1)} %collective-permute-done.5.args_3_), channel_id=1, source_target_pairs={{0,192},{8,56},{16,208},{24,40},{32,224},{40,24},{48,240},{56,8},{... | collective-permute-start | bytes 1179656 | tf_op jit(solution)/shard_map/gather2_twrap/ppermute | solution.py:47
  27.3 1.4 %collective-permute-start.6 = (bf16[32,6144]{1,0:T(8,128)(2,1)S(1)}, bf16[32,6144]{1,0:T(8,128)(2,1)S(1)}, u32[]{:S(2)}, u32[]{:S(2)}) collective-permute-start(bf16[32,6144]{1,0:T(8,128)(2,1)S(1)} %get-tuple-element.24.args_0_), channel_id=1, source_target_pairs={{0,64},{8,24},{16,80},{24,8},{32,96},{40,56},{48,112},{56,40},{64,... | collective-permute-start | bytes 1179656 | tf_op jit(solution)/shard_map/gather_tnear/ppermute | solution.py:47
  28.7 0.6 collective-permute-start.7
  29.3 2.6 %fetch.1.args_6_.args_2_ = bf16[448,6144]{1,0:T(8,128)(2,1)S(1)} custom-call(bf16[448,6144]{1,0:T(8,128)(2,1)} %bitcast.3, bf16[32,6144]{1,0:T(8,128)(2,1)S(1)} %get-tuple-element.25.after.args_1_), custom_call_target="tpu_custom_call" | custom-call | bytes 11010048 | tf_op jit(solution)/shard_map/fetch/pallas_call | solution.py:156
  31.9 0.2 collective-permute-done.10.args_0_
  32.0 3.0 %collective-permute-done.11.args_1_ = bf16[32,6144]{1,0:T(8,128)(2,1)S(1)} collective-permute-done((bf16[32,6144]{1,0:T(8,128)(2,1)S(1)}, bf16[32,6144]{1,0:T(8,128)(2,1)S(1)}, u32[]{:S(2)}, u32[]{:S(2)}) %collective-permute-start.11) | collective-permute-done | bytes 393248 | tf_op jit(solution)/shard_map/gather2_twrap/ppermute | solution.py:47
  35.0 0.0 collective-permute-done.8.args_9_.args_5_
  35.0 5.8 %feed_forward.3 = (bf16[32,6144]{1,0:T(8,128)(2,1)S(1)}, bf16[32,6144]{1,0:T(8,128)(2,1)S(1)}) custom-call(bf16[32,6144]{1,0:T(8,128)(2,1)S(1)} %collective-permute-done.10.args_0_, bf16[32,6144]{1,0:T(8,128)(2,1)S(1)} %collective-permute-done.11.args_1_, bf16[448,6144]{1,0:T(8,128)(2,1)S(1)} %fetch.1.args_6_.args_2_, ...), custom_call_target="tpu_custom_call" | custom-call | flops 1409286144 | bytes 1572864 | tf_op jit(solution)/shard_map/feed_forward/pallas_call | solution.py:201
  40.9 1.3 %collective-permute-start.12 = (bf16[32,6144]{1,0:T(8,128)(2,1)S(1)}, bf16[32,6144]{1,0:T(8,128)(2,1)S(1)}, u32[]{:S(2)}, u32[]{:S(2)}) collective-permute-start(bf16[32,6144]{1,0:T(8,128)(2,1)S(1)} %get-tuple-element.30), channel_id=1, source_target_pairs={{0,192},{8,56},{16,208},{24,40},{32,224},{40,24},{48,240},{56,8},{... | collective-permute-start | bytes 1179656 | tf_op jit(solution)/shard_map/reduce2_twrap/ppermute | solution.py:47
  42.2 0.2 collective-permute-start.15
  42.4 0.0 collective-permute-done.6.args_4_
  42.4 0.0 collective-permute-done.7.args_5_
  42.4 7.0 %feed_forward.2 = (bf16[32,6144]{1,0:T(8,128)(2,1)S(1)}, bf16[32,6144]{1,0:T(8,128)(2,1)S(1)}, bf16[32,6144]{1,0:T(8,128)(2,1)S(1)}, bf16[32,6144]{1,0:T(8,128)(...) custom-call(bf16[32,6144]{1,0:T(8,128)(2,1)S(1)} %get-tuple-element.24.args_0_, ...), custom_call_target="tpu_custom_call" | custom-call | flops 4227858432 | bytes 4718592 | tf_op jit(solution)/shard_map/feed_forward/pallas_call | solution.py:201
  49.4 0.6 collective-permute-done.15.arrived
  49.9 0.1 merge.3
  50.0 2.1 %collective-permute-start.17 = (bf16[32,6144]{1,0:T(8,128)(2,1)S(1)}, bf16[32,6144]{1,0:T(8,128)(2,1)S(1)}, u32[]{:S(2)}, u32[]{:S(2)}) collective-permute-start(bf16[32,6144]{1,0:T(8,128)(2,1)S(1)} %get-tuple-element.36), channel_id=1, source_target_pairs={{0,192},{8,56},{16,208},{24,40},{32,224},{40,24},{48,240},{56,8},{... | collective-permute-start | bytes 1179656 | tf_op jit(solution)/shard_map/reduce_twrap/ppermute | solution.py:47
  52.2 0.6 collective-permute-start.16
  52.8 1.2 %collective-permute-start.9 = (bf16[32,6144]{1,0:T(8,128)(2,1)S(1)}, bf16[32,6144]{1,0:T(8,128)(2,1)S(1)}, u32[]{:S(2)}, u32[]{:S(2)}) collective-permute-start(bf16[32,6144]{1,0:T(8,128)(2,1)S(1)} %get-tuple-element.28), channel_id=1, source_target_pairs={{0,192},{8,56},{16,208},{24,40},{32,224},{40,24},{48,240},{56,8},{... | collective-permute-start | bytes 1179656 | tf_op jit(solution)/shard_map/reduce_twrap/ppermute | solution.py:47
  54.0 0.1 merge.2
  54.1 0.9 %collective-permute-start.13 = (bf16[32,6144]{1,0:T(8,128)(2,1)S(1)}, bf16[32,6144]{1,0:T(8,128)(2,1)S(1)}, u32[]{:S(2)}, u32[]{:S(2)}) collective-permute-start(bf16[32,6144]{1,0:T(8,128)(2,1)S(1)} %merge.2), channel_id=1, source_target_pairs={{0,64},{8,24},{16,80},{24,8},{32,96},{40,56},{48,112},{56,40},{64,... | collective-permute-start | bytes 1179656 | tf_op jit(solution)/shard_map/reduce_tnear/ppermute | solution.py:47
  55.0 4.2 %collective-permute-done.17 = bf16[32,6144]{1,0:T(8,128)(2,1)S(1)} collective-permute-done((bf16[32,6144]{1,0:T(8,128)(2,1)S(1)}, bf16[32,6144]{1,0:T(8,128)(2,1)S(1)}, u32[]{:S(2)}, u32[]{:S(2)}) %collective-permute-start.17) | collective-permute-done | bytes 393248 | tf_op jit(solution)/shard_map/reduce_twrap/ppermute | solution.py:47
  59.1 1.0 %collective-permute-done.16 = bf16[32,6144]{1,0:T(8,128)(2,1)S(1)} collective-permute-done((bf16[32,6144]{1,0:T(8,128)(2,1)S(1)}, bf16[32,6144]{1,0:T(8,128)(2,1)S(1)}, u32[]{:S(2)}, u32[]{:S(2)}) %collective-permute-start.16) | collective-permute-done | bytes 393248 | tf_op jit(solution)/shard_map/reduce_tnear/ppermute | solution.py:47
  60.1 0.1 add_convert_fusion
  60.3 1.1 %collective-permute-start.19 = (bf16[16,6144]{1,0:T(8,128)(2,1)S(1)}, bf16[16,6144]{1,0:T(8,128)(2,1)S(1)}, u32[]{:S(2)}, u32[]{:S(2)}) collective-permute-start(bf16[16,6144]{1,0:T(8,128)(2,1)S(1)} %get-tuple-element.38), channel_id=1, source_target_pairs={{0,32},{8,136},{16,48},{24,152},{32,0},{40,168},{48,16},{56,184},{... | collective-permute-start | bytes 589832 | tf_op jit(solution)/shard_map/home_sfar/ppermute | solution.py:47
  61.4 2.0 %collective-permute-start.18 = (bf16[16,6144]{1,0:T(8,128)(2,1)S(1)}, bf16[16,6144]{1,0:T(8,128)(2,1)S(1)}, u32[]{:S(2)}, u32[]{:S(2)}) collective-permute-start(bf16[16,6144]{1,0:T(8,128)(2,1)S(1)} %get-tuple-element.37), channel_id=1, source_target_pairs={{0,48},{8,200},{16,32},{24,216},{32,16},{40,232},{48,0},{56,248},{... | collective-permute-start | bytes 589832 | tf_op jit(solution)/shard_map/home_swrap/ppermute | solution.py:47
  63.5 4.1 %collective-permute-done.9 = bf16[32,6144]{1,0:T(8,128)(2,1)S(1)} collective-permute-done((bf16[32,6144]{1,0:T(8,128)(2,1)S(1)}, bf16[32,6144]{1,0:T(8,128)(2,1)S(1)}, u32[]{:S(2)}, u32[]{:S(2)}) %collective-permute-start.9) | collective-permute-done | bytes 393248 | tf_op jit(solution)/shard_map/reduce_twrap/ppermute | solution.py:47
  67.5 0.8 %collective-permute-done.13 = bf16[32,6144]{1,0:T(8,128)(2,1)S(1)} collective-permute-done((bf16[32,6144]{1,0:T(8,128)(2,1)S(1)}, bf16[32,6144]{1,0:T(8,128)(2,1)S(1)}, u32[]{:S(2)}, u32[]{:S(2)}) %collective-permute-start.13) | collective-permute-done | bytes 393248 | tf_op jit(solution)/shard_map/reduce_tnear/ppermute | solution.py:47
  68.4 0.1 convert_add_fusion
  68.5 0.3 collective-permute-start.14
  68.9 0.0 collective-permute-done.19
  68.9 0.8 %collective-permute-done.18 = bf16[16,6144]{1,0:T(8,128)(2,1)S(1)} collective-permute-done((bf16[16,6144]{1,0:T(8,128)(2,1)S(1)}, bf16[16,6144]{1,0:T(8,128)(2,1)S(1)}, u32[]{:S(2)}, u32[]{:S(2)}) %collective-permute-start.18) | collective-permute-done | bytes 196640 | tf_op jit(solution)/shard_map/home_swrap/ppermute | solution.py:47
  69.7 4.6 %collective-permute-done.14 = bf16[16,6144]{1,0:T(8,128)(2,1)S(1)} collective-permute-done((bf16[16,6144]{1,0:T(8,128)(2,1)S(1)}, bf16[16,6144]{1,0:T(8,128)(2,1)S(1)}, u32[]{:S(2)}, u32[]{:S(2)}) %collective-permute-start.14) | collective-permute-done | bytes 196640 | tf_op jit(solution)/shard_map/home_snear/ppermute | solution.py:47
  74.3 0.8 %fusion.3 = bf16[16,6144]{1,0:T(8,128)(2,1)} fusion(f32[32,6144]{1,0:T(8,128)S(1)} %convert_add_fusion, bf16[16,6144]{1,0:T(8,128)(2,1)S(1)} %collective-permute-done.19, bf16[16,6144]{1,0:T(8,128)(2,1)S(1)} %collective-permute-done.18, bf16[16,6144]{1,0:T(8,128)(2,1)S(1)} %collective-permute-done.14, bf16[16,6144]{1,0:T(8,128)(2,1)S(1)} %get-tuple-element.21), kind=kLoop, calls=%fused_computation.7 | loop fusion | flops 884736 | bytes 1376256 | tf_op jit(solution)/shard_map/convert_element_type | solution.py:295
  (4 shorter events, 0.1 us)
Async XLA Ops:
  0.0 15.0 %collective-permute-start.3 = (bf16[448,6144]{1,0:T(8,128)(2,1)}, bf16[448,6144]{1,0:T(8,128)(2,1)S(1)}, u32[]{:S(2)}, u32[]{:S(2)}) collective-permute-start(bf16[448,6144]{1,0:T(8,128)(2,1)} %bitcast.2), channel_id=1, source_target_pairs={{0,8},{8,0},{16,24},{24,16},{32,40},{40,32},{48,56},{56,48},{64,72... | collective-permute-start | bytes 16515080 | tf_op jit(solution)/shard_map/up_core/ppermute | solution.py:47
  4.2 5.8 %collective-permute-start = (bf16[16,6144]{1,0:T(8,128)(2,1)S(1)}, bf16[16,6144]{1,0:T(8,128)(2,1)S(1)}, u32[]{:S(2)}, u32[]{:S(2)}) collective-permute-start(bf16[16,6144]{1,0:T(8,128)(2,1)S(1)} %get-tuple-element.22.own), channel_id=1, source_target_pairs={{0,16},{8,72},{16,0},{24,88},{32,48},{40,104},{48,32},{56,120},{64... | collective-permute-start | bytes 589832 | tf_op jit(solution)/shard_map/gather_snear/ppermute | solution.py:47
  5.7 7.4 %collective-permute-start.1 = (bf16[16,6144]{1,0:T(8,128)(2,1)S(1)}, bf16[16,6144]{1,0:T(8,128)(2,1)S(1)}, u32[]{:S(2)}, u32[]{:S(2)}) collective-permute-start(bf16[16,6144]{1,0:T(8,128)(2,1)S(1)} %get-tuple-element.22.own), channel_id=1, source_target_pairs={{0,48},{8,200},{16,32},{24,216},{32,16},{40,232},{48,0},{56,248},{... | collective-permute-start | bytes 589832 | tf_op jit(solution)/shard_map/gather_swrap/ppermute | solution.py:47
  7.8 7.2 %collective-permute-start.2 = (bf16[16,6144]{1,0:T(8,128)(2,1)S(1)}, bf16[16,6144]{1,0:T(8,128)(2,1)S(1)}, u32[]{:S(2)}, u32[]{:S(2)}) collective-permute-start(bf16[16,6144]{1,0:T(8,128)(2,1)S(1)} %get-tuple-element.22.own), channel_id=1, source_target_pairs={{0,32},{8,136},{16,48},{24,152},{32,0},{40,168},{48,16},{56,184},{... | collective-permute-start | bytes 589832 | tf_op jit(solution)/shard_map/gather_sfar/ppermute | solution.py:47
  15.1 20.0 %collective-permute-start.8 = (bf16[448,6144]{1,0:T(8,128)(2,1)S(1)}, bf16[448,6144]{1,0:T(8,128)(2,1)S(1)}, u32[]{:S(2)}, u32[]{:S(2)}) collective-permute-start(bf16[448,6144]{1,0:T(8,128)(2,1)S(1)} %get-tuple-element.26.args_8_.args_4_), channel_id=1, source_target_pairs={{0,8},{8,0},{16,24},{24,16},{32,40},{40,32},{48,56},{56,48},{64,72... | collective-permute-start | bytes 16515080 | tf_op jit(solution)/shard_map/down_core/ppermute | solution.py:47
  15.2 9.1 %collective-permute-start.4 = (bf16[32,6144]{1,0:T(8,128)(2,1)S(1)}, bf16[32,6144]{1,0:T(8,128)(2,1)S(1)}, u32[]{:S(2)}, u32[]{:S(2)}) collective-permute-start(bf16[32,6144]{1,0:T(8,128)(2,1)S(1)} %get-tuple-element.24.args_0_), channel_id=1, source_target_pairs={{0,192},{8,56},{16,208},{24,40},{32,224},{40,24},{48,240},{56,8},{... | collective-permute-start | bytes 1179656 | tf_op jit(solution)/shard_map/gather_twrap/ppermute | solution.py:47
  18.3 7.8 %collective-permute-start.5 = (bf16[32,6144]{1,0:T(8,128)(2,1)S(1)}, bf16[32,6144]{1,0:T(8,128)(2,1)S(1)}, u32[]{:S(2)}, u32[]{:S(2)}) collective-permute-start(bf16[32,6144]{1,0:T(8,128)(2,1)S(1)} %get-tuple-element.25.after.args_1_), channel_id=1, source_target_pairs={{0,64},{8,24},{16,80},{24,8},{32,96},{40,56},{48,112},{56,40},{64,... | collective-permute-start | bytes 1179656 | tf_op jit(solution)/shard_map/gather_tnear/ppermute | solution.py:47
  24.2 7.8 %collective-permute-start.10 = (bf16[32,6144]{1,0:T(8,128)(2,1)S(1)}, bf16[32,6144]{1,0:T(8,128)(2,1)S(1)}, u32[]{:S(2)}, u32[]{:S(2)}) collective-permute-start(bf16[32,6144]{1,0:T(8,128)(2,1)S(1)} %collective-permute-done.4.args_2_), channel_id=1, source_target_pairs={{0,64},{8,24},{16,80},{24,8},{32,96},{40,56},{48,112},{56,40},{64,... | collective-permute-start | bytes 1179656 | tf_op jit(solution)/shard_map/gather2_tnear/ppermute | solution.py:47
  26.0 9.0 %collective-permute-start.11 = (bf16[32,6144]{1,0:T(8,128)(2,1)S(1)}, bf16[32,6144]{1,0:T(8,128)(2,1)S(1)}, u32[]{:S(2)}, u32[]{:S(2)}) collective-permute-start(bf16[32,6144]{1,0:T(8,128)(2,1)S(1)} %collective-permute-done.5.args_3_), channel_id=1, source_target_pairs={{0,192},{8,56},{16,208},{24,40},{32,224},{40,24},{48,240},{56,8},{... | collective-permute-start | bytes 1179656 | tf_op jit(solution)/shard_map/gather2_twrap/ppermute | solution.py:47
  27.3 15.1 %collective-permute-start.6 = (bf16[32,6144]{1,0:T(8,128)(2,1)S(1)}, bf16[32,6144]{1,0:T(8,128)(2,1)S(1)}, u32[]{:S(2)}, u32[]{:S(2)}) collective-permute-start(bf16[32,6144]{1,0:T(8,128)(2,1)S(1)} %get-tuple-element.24.args_0_), channel_id=1, source_target_pairs={{0,64},{8,24},{16,80},{24,8},{32,96},{40,56},{48,112},{56,40},{64,... | collective-permute-start | bytes 1179656 | tf_op jit(solution)/shard_map/gather_tnear/ppermute | solution.py:47
  28.7 13.7 %collective-permute-start.7 = (bf16[32,6144]{1,0:T(8,128)(2,1)S(1)}, bf16[32,6144]{1,0:T(8,128)(2,1)S(1)}, u32[]{:S(2)}, u32[]{:S(2)}) collective-permute-start(bf16[32,6144]{1,0:T(8,128)(2,1)S(1)} %get-tuple-element.25.after.args_1_), channel_id=1, source_target_pairs={{0,192},{8,56},{16,208},{24,40},{32,224},{40,24},{48,240},{56,8},{... | collective-permute-start | bytes 1179656 | tf_op jit(solution)/shard_map/gather_twrap/ppermute | solution.py:47
  40.9 13.1 %collective-permute-start.12 = (bf16[32,6144]{1,0:T(8,128)(2,1)S(1)}, bf16[32,6144]{1,0:T(8,128)(2,1)S(1)}, u32[]{:S(2)}, u32[]{:S(2)}) collective-permute-start(bf16[32,6144]{1,0:T(8,128)(2,1)S(1)} %get-tuple-element.30), channel_id=1, source_target_pairs={{0,192},{8,56},{16,208},{24,40},{32,224},{40,24},{48,240},{56,8},{... | collective-permute-start | bytes 1179656 | tf_op jit(solution)/shard_map/reduce2_twrap/ppermute | solution.py:47
  42.2 7.8 %collective-permute-start.15 = (bf16[32,6144]{1,0:T(8,128)(2,1)S(1)}, bf16[32,6144]{1,0:T(8,128)(2,1)S(1)}, u32[]{:S(2)}, u32[]{:S(2)}) collective-permute-start(bf16[32,6144]{1,0:T(8,128)(2,1)S(1)} %get-tuple-element.33), channel_id=1, source_target_pairs={{0,64},{8,24},{16,80},{24,8},{32,96},{40,56},{48,112},{56,40},{64,... | collective-permute-start | bytes 1179656 | tf_op jit(solution)/shard_map/reduce2_tnear/ppermute | solution.py:47
  50.0 9.1 %collective-permute-start.17 = (bf16[32,6144]{1,0:T(8,128)(2,1)S(1)}, bf16[32,6144]{1,0:T(8,128)(2,1)S(1)}, u32[]{:S(2)}, u32[]{:S(2)}) collective-permute-start(bf16[32,6144]{1,0:T(8,128)(2,1)S(1)} %get-tuple-element.36), channel_id=1, source_target_pairs={{0,192},{8,56},{16,208},{24,40},{32,224},{40,24},{48,240},{56,8},{... | collective-permute-start | bytes 1179656 | tf_op jit(solution)/shard_map/reduce_twrap/ppermute | solution.py:47
  52.2 8.0 %collective-permute-start.16 = (bf16[32,6144]{1,0:T(8,128)(2,1)S(1)}, bf16[32,6144]{1,0:T(8,128)(2,1)S(1)}, u32[]{:S(2)}, u32[]{:S(2)}) collective-permute-start(bf16[32,6144]{1,0:T(8,128)(2,1)S(1)} %get-tuple-element.35), channel_id=1, source_target_pairs={{0,64},{8,24},{16,80},{24,8},{32,96},{40,56},{48,112},{56,40},{64,... | collective-permute-start | bytes 1179656 | tf_op jit(solution)/shard_map/reduce_tnear/ppermute | solution.py:47
  52.8 14.8 %collective-permute-start.9 = (bf16[32,6144]{1,0:T(8,128)(2,1)S(1)}, bf16[32,6144]{1,0:T(8,128)(2,1)S(1)}, u32[]{:S(2)}, u32[]{:S(2)}) collective-permute-start(bf16[32,6144]{1,0:T(8,128)(2,1)S(1)} %get-tuple-element.28), channel_id=1, source_target_pairs={{0,192},{8,56},{16,208},{24,40},{32,224},{40,24},{48,240},{56,8},{... | collective-permute-start | bytes 1179656 | tf_op jit(solution)/shard_map/reduce_twrap/ppermute | solution.py:47
  54.1 14.3 %collective-permute-start.13 = (bf16[32,6144]{1,0:T(8,128)(2,1)S(1)}, bf16[32,6144]{1,0:T(8,128)(2,1)S(1)}, u32[]{:S(2)}, u32[]{:S(2)}) collective-permute-start(bf16[32,6144]{1,0:T(8,128)(2,1)S(1)} %merge.2), channel_id=1, source_target_pairs={{0,64},{8,24},{16,80},{24,8},{32,96},{40,56},{48,112},{56,40},{64,... | collective-permute-start | bytes 1179656 | tf_op jit(solution)/shard_map/reduce_tnear/ppermute | solution.py:47
  60.3 8.6 %collective-permute-start.19 = (bf16[16,6144]{1,0:T(8,128)(2,1)S(1)}, bf16[16,6144]{1,0:T(8,128)(2,1)S(1)}, u32[]{:S(2)}, u32[]{:S(2)}) collective-permute-start(bf16[16,6144]{1,0:T(8,128)(2,1)S(1)} %get-tuple-element.38), channel_id=1, source_target_pairs={{0,32},{8,136},{16,48},{24,152},{32,0},{40,168},{48,16},{56,184},{... | collective-permute-start | bytes 589832 | tf_op jit(solution)/shard_map/home_sfar/ppermute | solution.py:47
  61.4 8.2 %collective-permute-start.18 = (bf16[16,6144]{1,0:T(8,128)(2,1)S(1)}, bf16[16,6144]{1,0:T(8,128)(2,1)S(1)}, u32[]{:S(2)}, u32[]{:S(2)}) collective-permute-start(bf16[16,6144]{1,0:T(8,128)(2,1)S(1)} %get-tuple-element.37), channel_id=1, source_target_pairs={{0,48},{8,200},{16,32},{24,216},{32,16},{40,232},{48,0},{56,248},{... | collective-permute-start | bytes 589832 | tf_op jit(solution)/shard_map/home_swrap/ppermute | solution.py:47
  68.5 5.8 %collective-permute-start.14 = (bf16[16,6144]{1,0:T(8,128)(2,1)S(1)}, bf16[16,6144]{1,0:T(8,128)(2,1)S(1)}, u32[]{:S(2)}, u32[]{:S(2)}) collective-permute-start(bf16[16,6144]{1,0:T(8,128)(2,1)S(1)} %slice.33), channel_id=1, source_target_pairs={{0,16},{8,72},{16,0},{24,88},{32,48},{40,104},{48,32},{56,120},{64... | collective-permute-start | bytes 589832 | tf_op jit(solution)/shard_map/home_snear/ppermute | solution.py:47

commit v7 on v4

--- a/solution.py
+++ b/solution.py
@@ -1,3 +1,5 @@
+import functools
+
 import jax
 import jax.numpy as jnp
 from jax import lax
@@ -163,8 +165,8 @@
     )(in_hbm(weights), after)
 
 
-def ffn_kernel(*args):
-    blocks, up, down, outs, (total, hidden) = args[:8], args[8:10], args[10:12], args[12:20], args[20:]
+def up_kernel(*args):
+    blocks, up, (hidden, total) = args[:8], args[8:10], args[10:]
     total[...] = jnp.zeros_like(total)
 
     @pl.loop(0, D // CHUNK)
@@ -180,32 +182,51 @@
     value = total[...]
     hidden[...] = (value / (1.0 + jnp.exp(-value))).astype(jnp.bfloat16).T
 
+
+def project_up(blocks, up):
+    vmem = pl.BlockSpec(memory_space=pltpu.VMEM)
+    rows = len(blocks) * PAIR
+    return pl.pallas_call(
+        up_kernel,
+        out_shape=jax.ShapeDtypeStruct((rows, 2 * HIDDEN), jnp.bfloat16),
+        in_specs=[vmem] * 10,
+        out_specs=vmem,
+        scratch_shapes=[pltpu.VMEM((2 * HIDDEN, rows), jnp.float32)],
+        compiler_params=pltpu.CompilerParams(vmem_limit_bytes=16 * 2**20),
+        cost_estimate=pl.CostEstimate(flops=4 * rows * HIDDEN * D, bytes_accessed=2 * rows * D, transcendentals=0),
+        name="up",
+    )(*blocks, *up)
+
+
+def down_kernel(begin, hidden, one, two, *outs):
+    rows = pl.ds(begin * PAIR, len(outs) * PAIR)
+
     @pl.loop(0, D // CHUNK)
     def _(step):
         cols = pl.ds(pl.multiple_of(step * CHUNK, CHUNK), CHUNK)
         product = jnp.dot(
-            hidden[...],
-            jnp.concatenate([w[:, cols] for w in down], axis=0),
+            hidden[rows, :],
+            jnp.concatenate([one[:, cols], two[:, cols]], axis=0),
             preferred_element_type=jnp.float32,
         ).astype(jnp.bfloat16)
         for i, out in enumerate(outs):
             out[:, cols] = product[i * PAIR : (i + 1) * PAIR]
 
 
-def feed_forward(blocks, up, down):
-    vmem = pl.BlockSpec(memory_space=pltpu.VMEM)
-    return pl.pallas_call(
-        ffn_kernel,
-        out_shape=[jax.ShapeDtypeStruct((PAIR, D), jnp.bfloat16)] * 8,
-        in_specs=[vmem] * 12,
-        out_specs=[vmem] * 8,
-        scratch_shapes=[
-            pltpu.VMEM((2 * HIDDEN, 8 * PAIR), jnp.float32),
-            pltpu.VMEM((8 * PAIR, 2 * HIDDEN), jnp.bfloat16),
-        ],
-        compiler_params=pltpu.CompilerParams(vmem_limit_bytes=16 * 2**20),
-        name="feed_forward",
-    )(*blocks, *up, *down)
+def project_down(hidden, down, begin, end):
+    vmem = pl.BlockSpec(memory_space=pltpu.VMEM)
+    n = end - begin
+    return pl.pallas_call(
+        functools.partial(down_kernel, begin),
+        out_shape=[jax.ShapeDtypeStruct((PAIR, D), jnp.bfloat16)] * n,
+        in_specs=[vmem] * 3,
+        out_specs=[vmem] * n,
+        compiler_params=pltpu.CompilerParams(vmem_limit_bytes=16 * 2**20),
+        cost_estimate=pl.CostEstimate(
+            flops=4 * n * PAIR * HIDDEN * D, bytes_accessed=2 * n * PAIR * D, transcendentals=0
+        ),
+        name="down",
+    )(hidden, *down)
 
 
 def f32(x):
@@ -251,6 +272,49 @@
         compiler_params=pltpu.CompilerParams(vmem_limit_bytes=16 * 2**20),
         name="merge",
     )(mine, arrived, *waiting)
+
+
+def finish_first_kernel(own, near, back, second, second_near, kept, leaving, second_sum):
+    def total(rows):
+        return sum(x[rows, :].astype(jnp.float32) for x in (own, near, back))
+
+    kept[...] = total(slice(0, SLOTS))
+    leaving[...] = total(slice(SLOTS, PAIR)).astype(jnp.bfloat16)
+    second_sum[...] = second[...].astype(jnp.float32) + second_near[...].astype(jnp.float32)
+
+
+def finish_first(*blocks):
+    vmem = pl.BlockSpec(memory_space=pltpu.VMEM)
+    return pl.pallas_call(
+        finish_first_kernel,
+        out_shape=[
+            jax.ShapeDtypeStruct((SLOTS, D), jnp.float32),
+            jax.ShapeDtypeStruct((SLOTS, D), jnp.bfloat16),
+            jax.ShapeDtypeStruct((PAIR, D), jnp.float32),
+        ],
+        in_specs=[vmem] * 5,
+        out_specs=[vmem] * 3,
+        compiler_params=pltpu.CompilerParams(vmem_limit_bytes=16 * 2**20),
+        name="finish_first",
+    )(*blocks)
+
+
+def finish_second_kernel(part, back, one, two):
+    value = part[...] + back[...].astype(jnp.float32)
+    one[...] = value[:SLOTS].astype(jnp.bfloat16)
+    two[...] = value[SLOTS:].astype(jnp.bfloat16)
+
+
+def finish_second(part, back):
+    vmem = pl.BlockSpec(memory_space=pltpu.VMEM)
+    return pl.pallas_call(
+        finish_second_kernel,
+        out_shape=[jax.ShapeDtypeStruct((SLOTS, D), jnp.bfloat16)] * 2,
+        in_specs=[vmem] * 2,
+        out_specs=[vmem] * 2,
+        compiler_params=pltpu.CompilerParams(vmem_limit_bytes=16 * 2**20),
+        name="finish_second",
+    )(part, back)
 
 
 def on_device(
@@ -268,24 +332,26 @@
     first_w, second_n = send(first, "twrap", "gather"), send(second, "tnear", "gather")
     second_w, first_n = send(second, "twrap", "gather"), send(first, "tnear", "gather")
     first_f, second_f = send(first_w, "tnear", "gather2"), send(second_n, "twrap", "gather2")
-    blocks = [first, second, first_w, second_n, first_n, second_w, first_f, second_f]
-    first, second, first_w, second_n, first_n, second_w, first_f, second_f = feed_forward(
-        blocks, (up_held, up_other), (down_held, down_other)
+    hidden = project_up(
+        [first, second, first_w, second_n, first_n, second_w, first_f, second_f], (up_held, up_other)
     )
+    down = (down_held, down_other)
+    first_f, second_f = project_down(hidden, down, 6, 8)
+    first, second, first_w, second_n, first_n, second_w = project_down(hidden, down, 0, 6)
     far_first = send(first_f, "tnear", "reduce2")
     far_second = send(second_f, "twrap", "reduce2")
-    first_w, first_n, second_w = merge(first_w, far_first, first_n, second_w)
-    back_first = send(first_w, "twrap", "reduce")
     near_first = send(first_n, "tnear", "reduce")
     near_second = send(second_w, "twrap", "reduce")
+    (first_w,) = merge(first_w, far_first)
+    back_first = send(first_w, "twrap", "reduce")
     (second_n,) = merge(second_n, far_second)
     back_second = send(second_n, "tnear", "reduce")
-    first = f32(first) + f32(near_first) + f32(back_first)
-    second = f32(second) + f32(near_second) + f32(back_second)
-    home_near = send(first[SLOTS:].astype(jnp.bfloat16), "snear", "home")
-    home_wrap = send(second[:SLOTS].astype(jnp.bfloat16), "swrap", "home")
-    home_far = send(second[SLOTS:].astype(jnp.bfloat16), "sfar", "home")
-    projected = first[:SLOTS] + f32(home_near) + f32(home_wrap) + f32(home_far)
+    own, first_out, second_part = finish_first(first, near_first, back_first, second, near_second)
+    second_out = finish_second(second_part, back_second)
+    home_near = send(first_out, "snear", "home")
+    home_wrap = send(second_out[0], "swrap", "home")
+    home_far = send(second_out[1], "sfar", "home")
+    projected = own + f32(home_near) + f32(home_wrap) + f32(home_far)
     return (f32(attended) + projected).astype(jnp.bfloat16)
 
 

time: 74.7 us -> 70 us (0.937)
  waiting for transfers between devices: 37 us -> 31 us
  Pallas kernels: 13.5 us -> 15.1 us
    ppermute x20, waiting for transfers between devices: 37 us -> 31 us  [send(): return lax.ppermute(value, 'dp', ROUTES[route])]
    pallas_call x1 -> x5, Pallas kernels: 7.19 us -> 8.85 us  [the longest x2 4.98 us: project_down(): pl.pallas_call(functools.partial(down_kernel, begin), out_shape=[jax.Shap...]
  transfers between devices with their start and end apart: 20 -> 20, of which waited for: 14 -> 15; matrix products, arithmetic and copies ran while one was open for 0% -> 0% of each run, Pallas kernels for 8% -> 18%
where the time goes in v7:
time: 70 us; the launch traced here: 69.9 us
  waiting for transfers between devices  31 us (44%)
  starting transfers between devices  22.2 us (32%)
  Pallas kernels  15.1 us (22%)
  other arithmetic  0.8 us (1%)
  between operations  0.77 us (1%)
    ppermute x20, waiting for transfers between devices, send(): return lax.ppermute(value, 'dp', ROUTES[route])  31 us
    ppermute x20, starting transfers between devices, send(): return lax.ppermute(value, 'dp', ROUTES[route])  22.2 us
    pallas_call x2, Pallas kernels, project_down(): pl.pallas_call(functools.partial(down_kernel, begin), out_shape=[jax.Shap...  4.98 us
    pallas_call x1, Pallas kernels, project_up(): pl.pallas_call(up_kernel, out_shape=jax.ShapeDtypeStruct((rows, 2 * HIDDE...  3.59 us
    pallas_call x1, Pallas kernels, attend(): pl.pallas_call(attend_kernel, out_shape=(jax.ShapeDtypeStruct((SLOTS, D),...  3.49 us
    pallas_call x1, Pallas kernels, fetch(): pl.pallas_call(fetch_kernel, out_shape=jax.ShapeDtypeStruct((HIDDEN, D),...  2.57 us
  transfers between devices with their start and end apart: 20, of which 15 were waited for; matrix products, arithmetic and copies ran while one was open for 0% of the time, Pallas kernels for 18%

profile of v7, /device:TPU:128, one launch (start us, length us, event | category | flops | bytes accessed | tf_op | source)
XLA Modules:
  0.0 69.9 jit_solution(1364083500473402470)
XLA Ops:
  0.0 0.0 collective-permute-start.3
  0.7 3.5 %attend.1 = (bf16[16,6144]{1,0:T(8,128)(2,1)S(1)}, bf16[16,6144]{1,0:T(8,128)(2,1)S(1)}, bf16[448,6144]{1,0:T(8,128)(2,1)S(1)}) custom-call(s32[1]{0:T(128)S(6)} %copy.11.counts, s32[16]{0:T(128)} %lengths_in.1, bf16[16,6144]{1,0:T(8,128)(2,1)} %q_in.1, bf16[1024,512]{1,0:T(8,128)(2,1)} %k_in.1, bf16[1024,512]{1,0:T(8,128)(2,1)} %v_in.1, f32[1,6144]{1,0:T(1,128)} %bitcast.4, ...), custom_call_target="tpu_custom_call" | custom-call | tf_op jit(solution)/shard_map/attend/pallas_call | solution.py:126
  4.2 3.1 %collective-permute-start.2 = (bf16[16,6144]{1,0:T(8,128)(2,1)S(1)}, bf16[16,6144]{1,0:T(8,128)(2,1)S(1)}, u32[]{:S(2)}, u32[]{:S(2)}) collective-permute-start(bf16[16,6144]{1,0:T(8,128)(2,1)S(1)} %get-tuple-element.25.own), channel_id=1, source_target_pairs={{0,32},{8,136},{16,48},{24,152},{32,0},{40,168},{48,16},{56,184},{... | collective-permute-start | bytes 589832 | tf_op jit(solution)/shard_map/gather_sfar/ppermute | solution.py:47
  7.3 1.1 %collective-permute-start.1 = (bf16[16,6144]{1,0:T(8,128)(2,1)S(1)}, bf16[16,6144]{1,0:T(8,128)(2,1)S(1)}, u32[]{:S(2)}, u32[]{:S(2)}) collective-permute-start(bf16[16,6144]{1,0:T(8,128)(2,1)S(1)} %get-tuple-element.25.own), channel_id=1, source_target_pairs={{0,48},{8,200},{16,32},{24,216},{32,16},{40,232},{48,0},{56,248},{... | collective-permute-start | bytes 589832 | tf_op jit(solution)/shard_map/gather_swrap/ppermute | solution.py:47
  8.4 0.0 collective-permute-start
  8.4 3.0 %collective-permute-done.2.far = bf16[16,6144]{1,0:T(8,128)(2,1)S(1)} collective-permute-done((bf16[16,6144]{1,0:T(8,128)(2,1)S(1)}, bf16[16,6144]{1,0:T(8,128)(2,1)S(1)}, u32[]{:S(2)}, u32[]{:S(2)}) %collective-permute-start.2) | collective-permute-done | bytes 196640 | tf_op jit(solution)/shard_map/gather_sfar/ppermute | solution.py:47
  11.4 2.7 %collective-permute-done.1.wrap = bf16[16,6144]{1,0:T(8,128)(2,1)S(1)} collective-permute-done((bf16[16,6144]{1,0:T(8,128)(2,1)S(1)}, bf16[16,6144]{1,0:T(8,128)(2,1)S(1)}, u32[]{:S(2)}, u32[]{:S(2)}) %collective-permute-start.1) | collective-permute-done | bytes 196640 | tf_op jit(solution)/shard_map/gather_swrap/ppermute | solution.py:47
  14.1 0.0 collective-permute-done.near
  14.2 0.0 collective-permute-done.3.after.args_9_
  14.2 0.1 pack.1
  14.2 0.1 collective-permute-start.10
  14.3 3.1 %collective-permute-start.4 = (bf16[32,6144]{1,0:T(8,128)(2,1)S(1)}, bf16[32,6144]{1,0:T(8,128)(2,1)S(1)}, u32[]{:S(2)}, u32[]{:S(2)}) collective-permute-start(bf16[32,6144]{1,0:T(8,128)(2,1)S(1)} %get-tuple-element.27.args_0_), channel_id=1, source_target_pairs={{0,192},{8,56},{16,208},{24,40},{32,224},{40,24},{48,240},{56,8},{... | collective-permute-start | bytes 1179656 | tf_op jit(solution)/shard_map/gather_twrap/ppermute | solution.py:47
  17.4 0.1 collective-permute-start.5
  17.6 1.9 %collective-permute-start.6 = (bf16[32,6144]{1,0:T(8,128)(2,1)S(1)}, bf16[32,6144]{1,0:T(8,128)(2,1)S(1)}, u32[]{:S(2)}, u32[]{:S(2)}) collective-permute-start(bf16[32,6144]{1,0:T(8,128)(2,1)S(1)} %get-tuple-element.27.args_0_), channel_id=1, source_target_pairs={{0,64},{8,24},{16,80},{24,8},{32,96},{40,56},{48,112},{56,40},{64,... | collective-permute-start | bytes 1179656 | tf_op jit(solution)/shard_map/gather_tnear/ppermute | solution.py:47
  19.4 0.2 collective-permute-start.7
  19.7 3.7 %collective-permute-done.4.args_2_ = bf16[32,6144]{1,0:T(8,128)(2,1)S(1)} collective-permute-done((bf16[32,6144]{1,0:T(8,128)(2,1)S(1)}, bf16[32,6144]{1,0:T(8,128)(2,1)S(1)}, u32[]{:S(2)}, u32[]{:S(2)}) %collective-permute-start.4) | collective-permute-done | bytes 393248 | tf_op jit(solution)/shard_map/gather_twrap/ppermute | solution.py:47
  23.4 0.4 collective-permute-start.8
  23.8 1.4 %collective-permute-done.5.args_3_ = bf16[32,6144]{1,0:T(8,128)(2,1)S(1)} collective-permute-done((bf16[32,6144]{1,0:T(8,128)(2,1)S(1)}, bf16[32,6144]{1,0:T(8,128)(2,1)S(1)}, u32[]{:S(2)}, u32[]{:S(2)}) %collective-permute-start.5) | collective-permute-done | bytes 393248 | tf_op jit(solution)/shard_map/gather_tnear/ppermute | solution.py:47
  25.2 1.2 %collective-permute-start.9 = (bf16[32,6144]{1,0:T(8,128)(2,1)S(1)}, bf16[32,6144]{1,0:T(8,128)(2,1)S(1)}, u32[]{:S(2)}, u32[]{:S(2)}) collective-permute-start(bf16[32,6144]{1,0:T(8,128)(2,1)S(1)} %collective-permute-done.5.args_3_), channel_id=1, source_target_pairs={{0,192},{8,56},{16,208},{24,40},{32,224},{40,24},{48,240},{56,8},{... | collective-permute-start | bytes 1179656 | tf_op jit(solution)/shard_map/gather2_twrap/ppermute | solution.py:47
  26.4 2.6 %fetch.1.args_8_ = bf16[448,6144]{1,0:T(8,128)(2,1)S(1)} custom-call(bf16[448,6144]{1,0:T(8,128)(2,1)} %bitcast.3, bf16[32,6144]{1,0:T(8,128)(2,1)S(1)} %get-tuple-element.28.after.args_1_), custom_call_target="tpu_custom_call" | custom-call | bytes 11010048 | tf_op jit(solution)/shard_map/fetch/pallas_call | solution.py:156
  29.0 0.4 collective-permute-done.6.args_4_
  29.4 4.2 %collective-permute-done.8.args_6_ = bf16[32,6144]{1,0:T(8,128)(2,1)S(1)} collective-permute-done((bf16[32,6144]{1,0:T(8,128)(2,1)S(1)}, bf16[32,6144]{1,0:T(8,128)(2,1)S(1)}, u32[]{:S(2)}, u32[]{:S(2)}) %collective-permute-start.8) | collective-permute-done | bytes 393248 | tf_op jit(solution)/shard_map/gather2_tnear/ppermute | solution.py:47
  33.6 0.6 collective-permute-done.9.args_7_
  34.2 3.6 %up.1.hidden = bf16[256,896]{1,0:T(8,128)(2,1)S(1)} custom-call(bf16[32,6144]{1,0:T(8,128)(2,1)S(1)} %get-tuple-element.27.args_0_, bf16[32,6144]{1,0:T(8,128)(2,1)S(1)} %get-tuple-element.28.after.args_1_, bf16[32,6144]{1,0:T(8,128)(2,1)S(1)} %collective-permute-done.4.args_2_, bf16[32,6144]{1,0:T(8,128)(2,1)S(1)} %collective-permute-done.5.args_3_, ...), custom_call_target="tpu_custom_call" | custom-call | flops 2818572288 | bytes 3145728 | tf_op jit(solution)/shard_map/up/pallas_call | solution.py:189
  37.8 2.2 %down.5 = (bf16[32,6144]{1,0:T(8,128)(2,1)S(1)}, bf16[32,6144]{1,0:T(8,128)(2,1)S(1)}) custom-call(bf16[256,896]{1,0:T(8,128)(2,1)S(1)} %up.1.hidden, bf16[448,6144]{1,0:T(8,128)(2,1)S(1)} %get-tuple-element.29.one, bf16[448,6144]{1,0:T(8,128)(2,1)S(1)} %collective-permute-done.10.two), custom_call_target="tpu_custom_call" | custom-call | flops 704643072 | bytes 786432 | tf_op jit(solution)/shard_map/down/pallas_call | solution.py:219
  40.0 0.1 collective-permute-start.12
  40.1 2.0 %collective-permute-start.16 = (bf16[32,6144]{1,0:T(8,128)(2,1)S(1)}, bf16[32,6144]{1,0:T(8,128)(2,1)S(1)}, u32[]{:S(2)}, u32[]{:S(2)}) collective-permute-start(bf16[32,6144]{1,0:T(8,128)(2,1)S(1)} %get-tuple-element.40), channel_id=1, source_target_pairs={{0,192},{8,56},{16,208},{24,40},{32,224},{40,24},{48,240},{56,8},{... | collective-permute-start | bytes 1179656 | tf_op jit(solution)/shard_map/reduce2_twrap/ppermute | solution.py:47
  42.1 2.8 %down.4 = (bf16[32,6144]{1,0:T(8,128)(2,1)S(1)}, bf16[32,6144]{1,0:T(8,128)(2,1)S(1)}, bf16[32,6144]{1,0:T(8,128)(2,1)S(1)}, bf16[32,6144]{1,0:T(8,128)(2,1)S(1)...) custom-call(bf16[256,896]{1,0:T(8,128)(2,1)S(1)} %up.1.hidden, ...), custom_call_target="tpu_custom_call" | custom-call | flops 2113929216 | bytes 2359296 | tf_op jit(solution)/shard_map/down/pallas_call | solution.py:219
  44.9 0.7 collective-permute-start.11
  45.6 2.0 %collective-permute-start.14 = (bf16[32,6144]{1,0:T(8,128)(2,1)S(1)}, bf16[32,6144]{1,0:T(8,128)(2,1)S(1)}, u32[]{:S(2)}, u32[]{:S(2)}) collective-permute-start(bf16[32,6144]{1,0:T(8,128)(2,1)S(1)} %get-tuple-element.35), channel_id=1, source_target_pairs={{0,192},{8,56},{16,208},{24,40},{32,224},{40,24},{48,240},{56,8},{... | collective-permute-start | bytes 1179656 | tf_op jit(solution)/shard_map/reduce_twrap/ppermute | solution.py:47
  47.6 0.2 collective-permute-done.12.arrived
  47.8 0.1 merge.2
  47.9 1.3 %collective-permute-start.13 = (bf16[32,6144]{1,0:T(8,128)(2,1)S(1)}, bf16[32,6144]{1,0:T(8,128)(2,1)S(1)}, u32[]{:S(2)}, u32[]{:S(2)}) collective-permute-start(bf16[32,6144]{1,0:T(8,128)(2,1)S(1)} %merge.2), channel_id=1, source_target_pairs={{0,192},{8,56},{16,208},{24,40},{32,224},{40,24},{48,240},{56,8},{... | collective-permute-start | bytes 1179656 | tf_op jit(solution)/shard_map/reduce_twrap/ppermute | solution.py:47
  49.2 0.1 collective-permute-done.16.arrived
  49.3 0.1 merge.3
  49.4 0.6 collective-permute-start.17
  50.0 2.7 %collective-permute-done.11.near = bf16[32,6144]{1,0:T(8,128)(2,1)S(1)} collective-permute-done((bf16[32,6144]{1,0:T(8,128)(2,1)S(1)}, bf16[32,6144]{1,0:T(8,128)(2,1)S(1)}, u32[]{:S(2)}, u32[]{:S(2)}) %collective-permute-start.11) | collective-permute-done | bytes 393248 | tf_op jit(solution)/shard_map/reduce_tnear/ppermute | solution.py:47
  52.8 1.8 %collective-permute-done.14.second_near = bf16[32,6144]{1,0:T(8,128)(2,1)S(1)} collective-permute-done((bf16[32,6144]{1,0:T(8,128)(2,1)S(1)}, bf16[32,6144]{1,0:T(8,128)(2,1)S(1)}, u32[]{:S(2)}, u32[]{:S(2)}) %collective-permute-start.14) | collective-permute-done | bytes 393248 | tf_op jit(solution)/shard_map/reduce_twrap/ppermute | solution.py:47
  54.6 4.2 %collective-permute-done.13.back = bf16[32,6144]{1,0:T(8,128)(2,1)S(1)} collective-permute-done((bf16[32,6144]{1,0:T(8,128)(2,1)S(1)}, bf16[32,6144]{1,0:T(8,128)(2,1)S(1)}, u32[]{:S(2)}, u32[]{:S(2)}) %collective-permute-start.13) | collective-permute-done | bytes 393248 | tf_op jit(solution)/shard_map/reduce_twrap/ppermute | solution.py:47
  58.8 0.2 finish_first.1
  59.0 0.1 finish_second.1
  59.1 2.2 %collective-permute-start.18 = (bf16[16,6144]{1,0:T(8,128)(2,1)S(1)}, bf16[16,6144]{1,0:T(8,128)(2,1)S(1)}, u32[]{:S(2)}, u32[]{:S(2)}) collective-permute-start(bf16[16,6144]{1,0:T(8,128)(2,1)S(1)} %get-tuple-element.41), channel_id=1, source_target_pairs={{0,48},{8,200},{16,32},{24,216},{32,16},{40,232},{48,0},{56,248},{... | collective-permute-start | bytes 589832 | tf_op jit(solution)/shard_map/home_swrap/ppermute | solution.py:47
  61.3 1.1 %collective-permute-start.19 = (bf16[16,6144]{1,0:T(8,128)(2,1)S(1)}, bf16[16,6144]{1,0:T(8,128)(2,1)S(1)}, u32[]{:S(2)}, u32[]{:S(2)}) collective-permute-start(bf16[16,6144]{1,0:T(8,128)(2,1)S(1)} %get-tuple-element.42), channel_id=1, source_target_pairs={{0,32},{8,136},{16,48},{24,152},{32,0},{40,168},{48,16},{56,184},{... | collective-permute-start | bytes 589832 | tf_op jit(solution)/shard_map/home_sfar/ppermute | solution.py:47
  62.4 0.9 %collective-permute-start.15 = (bf16[16,6144]{1,0:T(8,128)(2,1)S(1)}, bf16[16,6144]{1,0:T(8,128)(2,1)S(1)}, u32[]{:S(2)}, u32[]{:S(2)}) collective-permute-start(bf16[16,6144]{1,0:T(8,128)(2,1)S(1)} %get-tuple-element.37), channel_id=1, source_target_pairs={{0,16},{8,72},{16,0},{24,88},{32,48},{40,104},{48,32},{56,120},{64... | collective-permute-start | bytes 589832 | tf_op jit(solution)/shard_map/home_snear/ppermute | solution.py:47
  63.3 3.4 %collective-permute-done.18 = bf16[16,6144]{1,0:T(8,128)(2,1)S(1)} collective-permute-done((bf16[16,6144]{1,0:T(8,128)(2,1)S(1)}, bf16[16,6144]{1,0:T(8,128)(2,1)S(1)}, u32[]{:S(2)}, u32[]{:S(2)}) %collective-permute-start.18) | collective-permute-done | bytes 196640 | tf_op jit(solution)/shard_map/home_swrap/ppermute | solution.py:47
  66.7 1.8 %collective-permute-done.19 = bf16[16,6144]{1,0:T(8,128)(2,1)S(1)} collective-permute-done((bf16[16,6144]{1,0:T(8,128)(2,1)S(1)}, bf16[16,6144]{1,0:T(8,128)(2,1)S(1)}, u32[]{:S(2)}, u32[]{:S(2)}) %collective-permute-start.19) | collective-permute-done | bytes 196640 | tf_op jit(solution)/shard_map/home_sfar/ppermute | solution.py:47
  68.5 0.6 collective-permute-done.15
  69.1 0.8 %add_convert_fusion = bf16[16,6144]{1,0:T(8,128)(2,1)} fusion(bf16[16,6144]{1,0:T(8,128)(2,1)S(1)} %collective-permute-done.19, bf16[16,6144]{1,0:T(8,128)(2,1)S(1)} %collective-permute-done.18, f32[16,6144]{1,0:T(8,128)S(1)} %get-tuple-element.36, bf16[16,6144]{1,0:T(8,128)(2,1)S(1)} %collective-permute-done.15, bf16[16,6144]{1,0:T(8,128)(2,1)S(1)} %get-tuple-element.24), kind=kLoop, calls=%fused_computation | loop fusion | flops 884736 | bytes 1376256 | tf_op jit(solution)/shard_map/convert_element_type | solution.py:355
  (3 shorter events, 0.0 us)
Async XLA Ops:
  0.0 14.2 %collective-permute-start.3 = (bf16[448,6144]{1,0:T(8,128)(2,1)}, bf16[448,6144]{1,0:T(8,128)(2,1)S(1)}, u32[]{:S(2)}, u32[]{:S(2)}) collective-permute-start(bf16[448,6144]{1,0:T(8,128)(2,1)} %bitcast.2), channel_id=1, source_target_pairs={{0,8},{8,0},{16,24},{24,16},{32,40},{40,32},{48,56},{56,48},{64,72... | collective-permute-start | bytes 16515080 | tf_op jit(solution)/shard_map/up_core/ppermute | solution.py:47
  4.2 7.3 %collective-permute-start.2 = (bf16[16,6144]{1,0:T(8,128)(2,1)S(1)}, bf16[16,6144]{1,0:T(8,128)(2,1)S(1)}, u32[]{:S(2)}, u32[]{:S(2)}) collective-permute-start(bf16[16,6144]{1,0:T(8,128)(2,1)S(1)} %get-tuple-element.25.own), channel_id=1, source_target_pairs={{0,32},{8,136},{16,48},{24,152},{32,0},{40,168},{48,16},{56,184},{... | collective-permute-start | bytes 589832 | tf_op jit(solution)/shard_map/gather_sfar/ppermute | solution.py:47
  7.3 6.9 %collective-permute-start.1 = (bf16[16,6144]{1,0:T(8,128)(2,1)S(1)}, bf16[16,6144]{1,0:T(8,128)(2,1)S(1)}, u32[]{:S(2)}, u32[]{:S(2)}) collective-permute-start(bf16[16,6144]{1,0:T(8,128)(2,1)S(1)} %get-tuple-element.25.own), channel_id=1, source_target_pairs={{0,48},{8,200},{16,32},{24,216},{32,16},{40,232},{48,0},{56,248},{... | collective-permute-start | bytes 589832 | tf_op jit(solution)/shard_map/gather_swrap/ppermute | solution.py:47
  8.4 5.7 %collective-permute-start = (bf16[16,6144]{1,0:T(8,128)(2,1)S(1)}, bf16[16,6144]{1,0:T(8,128)(2,1)S(1)}, u32[]{:S(2)}, u32[]{:S(2)}) collective-permute-start(bf16[16,6144]{1,0:T(8,128)(2,1)S(1)} %get-tuple-element.25.own), channel_id=1, source_target_pairs={{0,16},{8,72},{16,0},{24,88},{32,48},{40,104},{48,32},{56,120},{64... | collective-permute-start | bytes 589832 | tf_op jit(solution)/shard_map/gather_snear/ppermute | solution.py:47
  14.2 23.6 %collective-permute-start.10 = (bf16[448,6144]{1,0:T(8,128)(2,1)S(1)}, bf16[448,6144]{1,0:T(8,128)(2,1)S(1)}, u32[]{:S(2)}, u32[]{:S(2)}) collective-permute-start(bf16[448,6144]{1,0:T(8,128)(2,1)S(1)} %get-tuple-element.29.one), channel_id=1, source_target_pairs={{0,8},{8,0},{16,24},{24,16},{32,40},{40,32},{48,56},{56,48},{64,72... | collective-permute-start | bytes 16515080 | tf_op jit(solution)/shard_map/down_core/ppermute | solution.py:47
  14.3 9.1 %collective-permute-start.4 = (bf16[32,6144]{1,0:T(8,128)(2,1)S(1)}, bf16[32,6144]{1,0:T(8,128)(2,1)S(1)}, u32[]{:S(2)}, u32[]{:S(2)}) collective-permute-start(bf16[32,6144]{1,0:T(8,128)(2,1)S(1)} %get-tuple-element.27.args_0_), channel_id=1, source_target_pairs={{0,192},{8,56},{16,208},{24,40},{32,224},{40,24},{48,240},{56,8},{... | collective-permute-start | bytes 1179656 | tf_op jit(solution)/shard_map/gather_twrap/ppermute | solution.py:47
  17.4 7.8 %collective-permute-start.5 = (bf16[32,6144]{1,0:T(8,128)(2,1)S(1)}, bf16[32,6144]{1,0:T(8,128)(2,1)S(1)}, u32[]{:S(2)}, u32[]{:S(2)}) collective-permute-start(bf16[32,6144]{1,0:T(8,128)(2,1)S(1)} %get-tuple-element.28.after.args_1_), channel_id=1, source_target_pairs={{0,64},{8,24},{16,80},{24,8},{32,96},{40,56},{48,112},{56,40},{64,... | collective-permute-start | bytes 1179656 | tf_op jit(solution)/shard_map/gather_tnear/ppermute | solution.py:47
  17.6 11.9 %collective-permute-start.6 = (bf16[32,6144]{1,0:T(8,128)(2,1)S(1)}, bf16[32,6144]{1,0:T(8,128)(2,1)S(1)}, u32[]{:S(2)}, u32[]{:S(2)}) collective-permute-start(bf16[32,6144]{1,0:T(8,128)(2,1)S(1)} %get-tuple-element.27.args_0_), channel_id=1, source_target_pairs={{0,64},{8,24},{16,80},{24,8},{32,96},{40,56},{48,112},{56,40},{64,... | collective-permute-start | bytes 1179656 | tf_op jit(solution)/shard_map/gather_tnear/ppermute | solution.py:47
  19.4 10.0 %collective-permute-start.7 = (bf16[32,6144]{1,0:T(8,128)(2,1)S(1)}, bf16[32,6144]{1,0:T(8,128)(2,1)S(1)}, u32[]{:S(2)}, u32[]{:S(2)}) collective-permute-start(bf16[32,6144]{1,0:T(8,128)(2,1)S(1)} %get-tuple-element.28.after.args_1_), channel_id=1, source_target_pairs={{0,192},{8,56},{16,208},{24,40},{32,224},{40,24},{48,240},{56,8},{... | collective-permute-start | bytes 1179656 | tf_op jit(solution)/shard_map/gather_twrap/ppermute | solution.py:47
  23.4 10.2 %collective-permute-start.8 = (bf16[32,6144]{1,0:T(8,128)(2,1)S(1)}, bf16[32,6144]{1,0:T(8,128)(2,1)S(1)}, u32[]{:S(2)}, u32[]{:S(2)}) collective-permute-start(bf16[32,6144]{1,0:T(8,128)(2,1)S(1)} %collective-permute-done.4.args_2_), channel_id=1, source_target_pairs={{0,64},{8,24},{16,80},{24,8},{32,96},{40,56},{48,112},{56,40},{64,... | collective-permute-start | bytes 1179656 | tf_op jit(solution)/shard_map/gather2_tnear/ppermute | solution.py:47
  25.2 9.0 %collective-permute-start.9 = (bf16[32,6144]{1,0:T(8,128)(2,1)S(1)}, bf16[32,6144]{1,0:T(8,128)(2,1)S(1)}, u32[]{:S(2)}, u32[]{:S(2)}) collective-permute-start(bf16[32,6144]{1,0:T(8,128)(2,1)S(1)} %collective-permute-done.5.args_3_), channel_id=1, source_target_pairs={{0,192},{8,56},{16,208},{24,40},{32,224},{40,24},{48,240},{56,8},{... | collective-permute-start | bytes 1179656 | tf_op jit(solution)/shard_map/gather2_twrap/ppermute | solution.py:47
  40.0 7.9 %collective-permute-start.12 = (bf16[32,6144]{1,0:T(8,128)(2,1)S(1)}, bf16[32,6144]{1,0:T(8,128)(2,1)S(1)}, u32[]{:S(2)}, u32[]{:S(2)}) collective-permute-start(bf16[32,6144]{1,0:T(8,128)(2,1)S(1)} %get-tuple-element.33), channel_id=1, source_target_pairs={{0,64},{8,24},{16,80},{24,8},{32,96},{40,56},{48,112},{56,40},{64,... | collective-permute-start | bytes 1179656 | tf_op jit(solution)/shard_map/reduce2_tnear/ppermute | solution.py:47
  40.1 9.3 %collective-permute-start.16 = (bf16[32,6144]{1,0:T(8,128)(2,1)S(1)}, bf16[32,6144]{1,0:T(8,128)(2,1)S(1)}, u32[]{:S(2)}, u32[]{:S(2)}) collective-permute-start(bf16[32,6144]{1,0:T(8,128)(2,1)S(1)} %get-tuple-element.40), channel_id=1, source_target_pairs={{0,192},{8,56},{16,208},{24,40},{32,224},{40,24},{48,240},{56,8},{... | collective-permute-start | bytes 1179656 | tf_op jit(solution)/shard_map/reduce2_twrap/ppermute | solution.py:47
  44.9 7.9 %collective-permute-start.11 = (bf16[32,6144]{1,0:T(8,128)(2,1)S(1)}, bf16[32,6144]{1,0:T(8,128)(2,1)S(1)}, u32[]{:S(2)}, u32[]{:S(2)}) collective-permute-start(bf16[32,6144]{1,0:T(8,128)(2,1)S(1)} %get-tuple-element.31), channel_id=1, source_target_pairs={{0,64},{8,24},{16,80},{24,8},{32,96},{40,56},{48,112},{56,40},{64,... | collective-permute-start | bytes 1179656 | tf_op jit(solution)/shard_map/reduce_tnear/ppermute | solution.py:47
  45.6 9.0 %collective-permute-start.14 = (bf16[32,6144]{1,0:T(8,128)(2,1)S(1)}, bf16[32,6144]{1,0:T(8,128)(2,1)S(1)}, u32[]{:S(2)}, u32[]{:S(2)}) collective-permute-start(bf16[32,6144]{1,0:T(8,128)(2,1)S(1)} %get-tuple-element.35), channel_id=1, source_target_pairs={{0,192},{8,56},{16,208},{24,40},{32,224},{40,24},{48,240},{56,8},{... | collective-permute-start | bytes 1179656 | tf_op jit(solution)/shard_map/reduce_twrap/ppermute | solution.py:47
  47.9 10.9 %collective-permute-start.13 = (bf16[32,6144]{1,0:T(8,128)(2,1)S(1)}, bf16[32,6144]{1,0:T(8,128)(2,1)S(1)}, u32[]{:S(2)}, u32[]{:S(2)}) collective-permute-start(bf16[32,6144]{1,0:T(8,128)(2,1)S(1)} %merge.2), channel_id=1, source_target_pairs={{0,192},{8,56},{16,208},{24,40},{32,224},{40,24},{48,240},{56,8},{... | collective-permute-start | bytes 1179656 | tf_op jit(solution)/shard_map/reduce_twrap/ppermute | solution.py:47
  49.4 9.6 %collective-permute-start.17 = (bf16[32,6144]{1,0:T(8,128)(2,1)S(1)}, bf16[32,6144]{1,0:T(8,128)(2,1)S(1)}, u32[]{:S(2)}, u32[]{:S(2)}) collective-permute-start(bf16[32,6144]{1,0:T(8,128)(2,1)S(1)} %merge.3), channel_id=1, source_target_pairs={{0,64},{8,24},{16,80},{24,8},{32,96},{40,56},{48,112},{56,40},{64,... | collective-permute-start | bytes 1179656 | tf_op jit(solution)/shard_map/reduce_tnear/ppermute | solution.py:47
  59.1 7.6 %collective-permute-start.18 = (bf16[16,6144]{1,0:T(8,128)(2,1)S(1)}, bf16[16,6144]{1,0:T(8,128)(2,1)S(1)}, u32[]{:S(2)}, u32[]{:S(2)}) collective-permute-start(bf16[16,6144]{1,0:T(8,128)(2,1)S(1)} %get-tuple-element.41), channel_id=1, source_target_pairs={{0,48},{8,200},{16,32},{24,216},{32,16},{40,232},{48,0},{56,248},{... | collective-permute-start | bytes 589832 | tf_op jit(solution)/shard_map/home_swrap/ppermute | solution.py:47
  61.3 7.2 %collective-permute-start.19 = (bf16[16,6144]{1,0:T(8,128)(2,1)S(1)}, bf16[16,6144]{1,0:T(8,128)(2,1)S(1)}, u32[]{:S(2)}, u32[]{:S(2)}) collective-permute-start(bf16[16,6144]{1,0:T(8,128)(2,1)S(1)} %get-tuple-element.42), channel_id=1, source_target_pairs={{0,32},{8,136},{16,48},{24,152},{32,0},{40,168},{48,16},{56,184},{... | collective-permute-start | bytes 589832 | tf_op jit(solution)/shard_map/home_sfar/ppermute | solution.py:47
  62.4 6.7 %collective-permute-start.15 = (bf16[16,6144]{1,0:T(8,128)(2,1)S(1)}, bf16[16,6144]{1,0:T(8,128)(2,1)S(1)}, u32[]{:S(2)}, u32[]{:S(2)}) collective-permute-start(bf16[16,6144]{1,0:T(8,128)(2,1)S(1)} %get-tuple-element.37), channel_id=1, source_target_pairs={{0,16},{8,72},{16,0},{24,88},{32,48},{40,104},{48,32},{56,120},{64... | collective-permute-start | bytes 589832 | tf_op jit(solution)/shard_map/home_snear/ppermute | solution.py:47

commit v8 on v7

--- a/solution.py
+++ b/solution.py
@@ -229,15 +229,11 @@
     )(hidden, *down)
 
 
-def f32(x):
-    return x.astype(jnp.float32)
-
-
-def pack_kernel(own, near, wrap, far, held, after, first, second, handed):
-    first[:SLOTS] = own[...]
-    first[SLOTS:] = near[...]
-    second[:SLOTS] = wrap[...]
-    second[SLOTS:] = far[...]
+def pack_kernel(own, near, wrap, far, held, after, early, late, handed):
+    early[:SLOTS] = own[...]
+    early[SLOTS:] = near[...]
+    late[:SLOTS] = wrap[...]
+    late[SLOTS:] = far[...]
 
 
 def pack(own, near, wrap, far, held, after):
@@ -254,67 +250,60 @@
     )(own, near, wrap, far, held, after)
 
 
-def merge_kernel(mine, arrived, *refs):
-    waiting, (total, *later) = refs[: len(refs) // 2], refs[len(refs) // 2 :]
+def merge_kernel(n, mine, arrived, *refs):
+    waiting, (total, *later) = refs[:n], refs[-n - 1 :]
     total[...] = (mine[...].astype(jnp.float32) + arrived[...].astype(jnp.float32)).astype(jnp.bfloat16)
     for source, target in zip(waiting, later):
         target[...] = source[...]
 
 
-def merge(mine, arrived, *waiting):
-    vmem = pl.BlockSpec(memory_space=pltpu.VMEM)
-    n = 1 + len(waiting)
-    return pl.pallas_call(
-        merge_kernel,
-        out_shape=[jax.ShapeDtypeStruct((PAIR, D), jnp.bfloat16)] * n,
-        in_specs=[vmem] * (n + 1),
-        out_specs=[vmem] * n,
+def merge(mine, arrived, *waiting, after=()):
+    vmem = pl.BlockSpec(memory_space=pltpu.VMEM)
+    n = len(waiting)
+    return pl.pallas_call(
+        functools.partial(merge_kernel, n),
+        out_shape=[jax.ShapeDtypeStruct((PAIR, D), jnp.bfloat16)] * (1 + n),
+        in_specs=[vmem] * (2 + n) + [pl.BlockSpec(memory_space=pl.ANY)] * len(after),
+        out_specs=[vmem] * (1 + n),
         compiler_params=pltpu.CompilerParams(vmem_limit_bytes=16 * 2**20),
         name="merge",
-    )(mine, arrived, *waiting)
-
-
-def finish_first_kernel(own, near, back, second, second_near, kept, leaving, second_sum):
-    def total(rows):
-        return sum(x[rows, :].astype(jnp.float32) for x in (own, near, back))
-
-    kept[...] = total(slice(0, SLOTS))
-    leaving[...] = total(slice(SLOTS, PAIR)).astype(jnp.bfloat16)
-    second_sum[...] = second[...].astype(jnp.float32) + second_near[...].astype(jnp.float32)
-
-
-def finish_first(*blocks):
-    vmem = pl.BlockSpec(memory_space=pltpu.VMEM)
-    return pl.pallas_call(
-        finish_first_kernel,
-        out_shape=[
-            jax.ShapeDtypeStruct((SLOTS, D), jnp.float32),
-            jax.ShapeDtypeStruct((SLOTS, D), jnp.bfloat16),
-            jax.ShapeDtypeStruct((PAIR, D), jnp.float32),
-        ],
-        in_specs=[vmem] * 5,
-        out_specs=[vmem] * 3,
-        compiler_params=pltpu.CompilerParams(vmem_limit_bytes=16 * 2**20),
-        name="finish_first",
-    )(*blocks)
-
-
-def finish_second_kernel(part, back, one, two):
-    value = part[...] + back[...].astype(jnp.float32)
-    one[...] = value[:SLOTS].astype(jnp.bfloat16)
-    two[...] = value[SLOTS:].astype(jnp.bfloat16)
-
-
-def finish_second(part, back):
-    vmem = pl.BlockSpec(memory_space=pltpu.VMEM)
-    return pl.pallas_call(
-        finish_second_kernel,
-        out_shape=[jax.ShapeDtypeStruct((SLOTS, D), jnp.bfloat16)] * 2,
-        in_specs=[vmem] * 2,
+    )(mine, arrived, *waiting, *after)
+
+
+def finish_kernel(own, direct, back, *refs):
+    one, two = refs[-2:]
+    value = sum(x[...].astype(jnp.float32) for x in (own, direct, back))
+    one[...] = value[:SLOTS].astype(one.dtype)
+    two[...] = value[SLOTS:].astype(two.dtype)
+
+
+def finish(own, direct, back, kept_type, after=()):
+    vmem = pl.BlockSpec(memory_space=pltpu.VMEM)
+    return pl.pallas_call(
+        finish_kernel,
+        out_shape=[jax.ShapeDtypeStruct((SLOTS, D), kept_type), jax.ShapeDtypeStruct((SLOTS, D), jnp.bfloat16)],
+        in_specs=[vmem] * 3 + [pl.BlockSpec(memory_space=pl.ANY)] * len(after),
         out_specs=[vmem] * 2,
         compiler_params=pltpu.CompilerParams(vmem_limit_bytes=16 * 2**20),
-        name="finish_second",
-    )(part, back)
+        name="finish",
+    )(own, direct, back, *after)
+
+
+def collect_kernel(*refs):
+    *parts, out = refs
+    out[...] = sum(x[...].astype(jnp.float32) for x in parts)
+
+
+def collect(*parts):
+    vmem = pl.BlockSpec(memory_space=pltpu.VMEM)
+    return pl.pallas_call(
+        collect_kernel,
+        out_shape=jax.ShapeDtypeStruct((SLOTS, D), jnp.float32),
+        in_specs=[vmem] * len(parts),
+        out_specs=vmem,
+        compiler_params=pltpu.CompilerParams(vmem_limit_bytes=16 * 2**20),
+        name="collect",
+    )(*parts)
 
 
 def on_device(
@@ -326,33 +315,32 @@
         queries, cache_keys, cache_values, lengths, counts, norm_gain, down_weight
     )
     by_wrap, by_far, by_near = [send(normed, r, "gather") for r in ("swrap", "sfar", "snear")]
-    first, second, down_held = pack(normed, by_near, by_wrap, by_far, down_held, up_other)
+    early, late, down_held = pack(normed, by_near, by_wrap, by_far, down_held, up_other)
     down_other = send(down_held, "core", "down")
-    up_held = fetch(up_own, second)
-    first_w, second_n = send(first, "twrap", "gather"), send(second, "tnear", "gather")
-    second_w, first_n = send(second, "twrap", "gather"), send(first, "tnear", "gather")
-    first_f, second_f = send(first_w, "tnear", "gather2"), send(second_n, "twrap", "gather2")
+    early_n, late_w = send(early, "tnear", "gather"), send(late, "twrap", "gather")
+    late_n, early_w = send(late, "tnear", "gather"), send(early, "twrap", "gather")
+    early_f, late_f = send(early_n, "twrap", "gather2"), send(late_w, "tnear", "gather2")
+    up_held = fetch(up_own, late)
     hidden = project_up(
-        [first, second, first_w, second_n, first_n, second_w, first_f, second_f], (up_held, up_other)
+        [early, late, early_n, late_w, early_w, late_n, early_f, late_f], (up_held, up_other)
     )
     down = (down_held, down_other)
-    first_f, second_f = project_down(hidden, down, 6, 8)
-    first, second, first_w, second_n, first_n, second_w = project_down(hidden, down, 0, 6)
-    far_first = send(first_f, "tnear", "reduce2")
-    far_second = send(second_f, "twrap", "reduce2")
-    near_first = send(first_n, "tnear", "reduce")
-    near_second = send(second_w, "twrap", "reduce")
-    (first_w,) = merge(first_w, far_first)
-    back_first = send(first_w, "twrap", "reduce")
-    (second_n,) = merge(second_n, far_second)
-    back_second = send(second_n, "tnear", "reduce")
-    own, first_out, second_part = finish_first(first, near_first, back_first, second, near_second)
-    second_out = finish_second(second_part, back_second)
-    home_near = send(first_out, "snear", "home")
-    home_wrap = send(second_out[0], "swrap", "home")
-    home_far = send(second_out[1], "sfar", "home")
-    projected = own + f32(home_near) + f32(home_wrap) + f32(home_far)
-    return (f32(attended) + projected).astype(jnp.bfloat16)
+    early_f, late_f = project_down(hidden, down, 6, 8)
+    early, late, early_n, late_w, early_w, late_n = project_down(hidden, down, 0, 6)
+    far_late = send(late_f, "twrap", "reduce2")
+    far_early = send(early_f, "tnear", "reduce2")
+    direct_late = send(late_w, "twrap", "reduce")
+    (late_n,) = merge(late_n, far_late)
+    back_late = send(late_n, "tnear", "reduce")
+    early_w, early_n = merge(early_w, far_early, early_n, after=(late_n,))
+    back_early = send(early_w, "twrap", "reduce")
+    direct_early = send(early_n, "tnear", "reduce")
+    home_wrap, home_far = finish(late, direct_late, back_late, jnp.bfloat16)
+    own, home_near = finish(early, direct_early, back_early, jnp.float32, after=(home_wrap,))
+    home_wrap, home_far = send(home_wrap, "swrap", "home"), send(home_far, "sfar", "home")
+    home_near = send(home_near, "snear", "home")
+    mixed = collect(attended, own, home_wrap, home_far)
+    return (mixed + home_near.astype(jnp.float32)).astype(jnp.bfloat16)
 
 
 def solution(mesh):

time: 70 us -> 70 us (level)
  waiting for transfers between devices: 31 us -> 28.1 us
  starting transfers between devices: 22.2 us -> 24.8 us
    ppermute x20, waiting for transfers between devices: 31 us -> 28.1 us  [send(): return lax.ppermute(value, 'dp', ROUTES[route])]
    ppermute x20, starting transfers between devices: 22.2 us -> 24.8 us  [send(): return lax.ppermute(value, 'dp', ROUTES[route])]
  transfers between devices with their start and end apart: 20 -> 20, of which waited for: 15 -> 12; matrix products, arithmetic and copies ran while one was open for 0% -> 0% of each run, Pallas kernels for 18% -> 19%
where the time goes in v8:
time: 70 us; the launch traced here: 69.6 us
  waiting for transfers between devices  28.1 us (40%)
  starting transfers between devices  24.8 us (35%)
  Pallas kernels  15.2 us (22%)
  between operations  0.76 us (1%)
  other arithmetic  0.71 us (1%)
    ppermute x20, waiting for transfers between devices, send(): return lax.ppermute(value, 'dp', ROUTES[route])  28.1 us
    ppermute x20, starting transfers between devices, send(): return lax.ppermute(value, 'dp', ROUTES[route])  24.8 us
    pallas_call x2, Pallas kernels, project_down(): pl.pallas_call(functools.partial(down_kernel, begin), out_shape=[jax.Shap...  4.97 us
    pallas_call x1, Pallas kernels, project_up(): pl.pallas_call(up_kernel, out_shape=jax.ShapeDtypeStruct((rows, 2 * HIDDE...  3.59 us
    pallas_call x1, Pallas kernels, attend(): pl.pallas_call(attend_kernel, out_shape=(jax.ShapeDtypeStruct((SLOTS, D),...  3.49 us
    pallas_call x1, Pallas kernels, fetch(): pl.pallas_call(fetch_kernel, out_shape=jax.ShapeDtypeStruct((HIDDEN, D),...  2.57 us
  transfers between devices with their start and end apart: 20, of which 12 were waited for; matrix products, arithmetic and copies ran while one was open for 0% of the time, Pallas kernels for 19%

profile of v8, /device:TPU:128, one launch (start us, length us, event | category | flops | bytes accessed | tf_op | source)
XLA Modules:
  0.0 69.6 jit_solution(8680215945288833464)
XLA Ops:
  0.0 0.0 collective-permute-start.3
  0.7 3.5 %attend.1 = (bf16[16,6144]{1,0:T(8,128)(2,1)S(1)}, bf16[16,6144]{1,0:T(8,128)(2,1)S(1)}, bf16[448,6144]{1,0:T(8,128)(2,1)S(1)}) custom-call(s32[1]{0:T(128)S(6)} %copy.11.counts, s32[16]{0:T(128)} %lengths_in.1, bf16[16,6144]{1,0:T(8,128)(2,1)} %q_in.1, bf16[1024,512]{1,0:T(8,128)(2,1)} %k_in.1, bf16[1024,512]{1,0:T(8,128)(2,1)} %v_in.1, f32[1,6144]{1,0:T(1,128)} %bitcast.4, ...), custom_call_target="tpu_custom_call" | custom-call | tf_op jit(solution)/shard_map/attend/pallas_call | solution.py:126
  4.2 3.1 %collective-permute-start.2 = (bf16[16,6144]{1,0:T(8,128)(2,1)S(1)}, bf16[16,6144]{1,0:T(8,128)(2,1)S(1)}, u32[]{:S(2)}, u32[]{:S(2)}) collective-permute-start(bf16[16,6144]{1,0:T(8,128)(2,1)S(1)} %get-tuple-element.26.own), channel_id=1, source_target_pairs={{0,32},{8,136},{16,48},{24,152},{32,0},{40,168},{48,16},{56,184},{... | collective-permute-start | bytes 589832 | tf_op jit(solution)/shard_map/gather_sfar/ppermute | solution.py:47
  7.3 1.1 %collective-permute-start.1 = (bf16[16,6144]{1,0:T(8,128)(2,1)S(1)}, bf16[16,6144]{1,0:T(8,128)(2,1)S(1)}, u32[]{:S(2)}, u32[]{:S(2)}) collective-permute-start(bf16[16,6144]{1,0:T(8,128)(2,1)S(1)} %get-tuple-element.26.own), channel_id=1, source_target_pairs={{0,48},{8,200},{16,32},{24,216},{32,16},{40,232},{48,0},{56,248},{... | collective-permute-start | bytes 589832 | tf_op jit(solution)/shard_map/gather_swrap/ppermute | solution.py:47
  8.4 0.0 collective-permute-start
  8.4 3.0 %collective-permute-done.2.far = bf16[16,6144]{1,0:T(8,128)(2,1)S(1)} collective-permute-done((bf16[16,6144]{1,0:T(8,128)(2,1)S(1)}, bf16[16,6144]{1,0:T(8,128)(2,1)S(1)}, u32[]{:S(2)}, u32[]{:S(2)}) %collective-permute-start.2) | collective-permute-done | bytes 196640 | tf_op jit(solution)/shard_map/gather_sfar/ppermute | solution.py:47
  11.4 2.7 %collective-permute-done.1.wrap = bf16[16,6144]{1,0:T(8,128)(2,1)S(1)} collective-permute-done((bf16[16,6144]{1,0:T(8,128)(2,1)S(1)}, bf16[16,6144]{1,0:T(8,128)(2,1)S(1)}, u32[]{:S(2)}, u32[]{:S(2)}) %collective-permute-start.1) | collective-permute-done | bytes 196640 | tf_op jit(solution)/shard_map/gather_swrap/ppermute | solution.py:47
  14.1 0.0 collective-permute-done.near
  14.2 0.0 collective-permute-done.3.after.args_9_
  14.2 0.1 pack.1
  14.2 0.1 collective-permute-start.10
  14.3 1.7 %collective-permute-start.4 = (bf16[32,6144]{1,0:T(8,128)(2,1)S(1)}, bf16[32,6144]{1,0:T(8,128)(2,1)S(1)}, u32[]{:S(2)}, u32[]{:S(2)}) collective-permute-start(bf16[32,6144]{1,0:T(8,128)(2,1)S(1)} %get-tuple-element.28.args_0_), channel_id=1, source_target_pairs={{0,64},{8,24},{16,80},{24,8},{32,96},{40,56},{48,112},{56,40},{64,... | collective-permute-start | bytes 1179656 | tf_op jit(solution)/shard_map/gather_tnear/ppermute | solution.py:47
  16.0 2.2 %collective-permute-start.5 = (bf16[32,6144]{1,0:T(8,128)(2,1)S(1)}, bf16[32,6144]{1,0:T(8,128)(2,1)S(1)}, u32[]{:S(2)}, u32[]{:S(2)}) collective-permute-start(bf16[32,6144]{1,0:T(8,128)(2,1)S(1)} %get-tuple-element.29.after.args_1_), channel_id=1, source_target_pairs={{0,192},{8,56},{16,208},{24,40},{32,224},{40,24},{48,240},{56,8},{... | collective-permute-start | bytes 1179656 | tf_op jit(solution)/shard_map/gather_twrap/ppermute | solution.py:47
  18.2 1.1 %collective-permute-start.6 = (bf16[32,6144]{1,0:T(8,128)(2,1)S(1)}, bf16[32,6144]{1,0:T(8,128)(2,1)S(1)}, u32[]{:S(2)}, u32[]{:S(2)}) collective-permute-start(bf16[32,6144]{1,0:T(8,128)(2,1)S(1)} %get-tuple-element.28.args_0_), channel_id=1, source_target_pairs={{0,192},{8,56},{16,208},{24,40},{32,224},{40,24},{48,240},{56,8},{... | collective-permute-start | bytes 1179656 | tf_op jit(solution)/shard_map/gather_twrap/ppermute | solution.py:47
  19.2 3.0 %collective-permute-done.4.args_2_ = bf16[32,6144]{1,0:T(8,128)(2,1)S(1)} collective-permute-done((bf16[32,6144]{1,0:T(8,128)(2,1)S(1)}, bf16[32,6144]{1,0:T(8,128)(2,1)S(1)}, u32[]{:S(2)}, u32[]{:S(2)}) %collective-permute-start.4) | collective-permute-done | bytes 393248 | tf_op jit(solution)/shard_map/gather_tnear/ppermute | solution.py:47
  22.2 3.0 %collective-permute-start.8 = (bf16[32,6144]{1,0:T(8,128)(2,1)S(1)}, bf16[32,6144]{1,0:T(8,128)(2,1)S(1)}, u32[]{:S(2)}, u32[]{:S(2)}) collective-permute-start(bf16[32,6144]{1,0:T(8,128)(2,1)S(1)} %collective-permute-done.4.args_2_), channel_id=1, source_target_pairs={{0,192},{8,56},{16,208},{24,40},{32,224},{40,24},{48,240},{56,8},{... | collective-permute-start | bytes 1179656 | tf_op jit(solution)/shard_map/gather2_twrap/ppermute | solution.py:47
  25.2 0.0 collective-permute-done.5.args_3_
  25.2 0.1 collective-permute-start.9
  25.3 2.6 %fetch.1.args_8_ = bf16[448,6144]{1,0:T(8,128)(2,1)S(1)} custom-call(bf16[448,6144]{1,0:T(8,128)(2,1)} %bitcast.3, bf16[32,6144]{1,0:T(8,128)(2,1)S(1)} %get-tuple-element.29.after.args_1_), custom_call_target="tpu_custom_call" | custom-call | bytes 11010048 | tf_op jit(solution)/shard_map/fetch/pallas_call | solution.py:156
  27.9 1.3 %collective-permute-done.6.args_4_ = bf16[32,6144]{1,0:T(8,128)(2,1)S(1)} collective-permute-done((bf16[32,6144]{1,0:T(8,128)(2,1)S(1)}, bf16[32,6144]{1,0:T(8,128)(2,1)S(1)}, u32[]{:S(2)}, u32[]{:S(2)}) %collective-permute-start.6) | collective-permute-done | bytes 393248 | tf_op jit(solution)/shard_map/gather_twrap/ppermute | solution.py:47
  29.2 4.2 %collective-permute-done.8.args_6_ = bf16[32,6144]{1,0:T(8,128)(2,1)S(1)} collective-permute-done((bf16[32,6144]{1,0:T(8,128)(2,1)S(1)}, bf16[32,6144]{1,0:T(8,128)(2,1)S(1)}, u32[]{:S(2)}, u32[]{:S(2)}) %collective-permute-start.8) | collective-permute-done | bytes 393248 | tf_op jit(solution)/shard_map/gather2_twrap/ppermute | solution.py:47
  33.4 3.6 %up.1.hidden = bf16[256,896]{1,0:T(8,128)(2,1)S(1)} custom-call(bf16[32,6144]{1,0:T(8,128)(2,1)S(1)} %get-tuple-element.28.args_0_, bf16[32,6144]{1,0:T(8,128)(2,1)S(1)} %get-tuple-element.29.after.args_1_, bf16[32,6144]{1,0:T(8,128)(2,1)S(1)} %collective-permute-done.4.args_2_, bf16[32,6144]{1,0:T(8,128)(2,1)S(1)} %collective-permute-done.5.args_3_, ...), custom_call_target="tpu_custom_call" | custom-call | flops 2818572288 | bytes 3145728 | tf_op jit(solution)/shard_map/up/pallas_call | solution.py:189
  37.0 0.0 collective-permute-done.10.two
  37.0 2.2 %down.5 = (bf16[32,6144]{1,0:T(8,128)(2,1)S(1)}, bf16[32,6144]{1,0:T(8,128)(2,1)S(1)}) custom-call(bf16[256,896]{1,0:T(8,128)(2,1)S(1)} %up.1.hidden, bf16[448,6144]{1,0:T(8,128)(2,1)S(1)} %get-tuple-element.30.one, bf16[448,6144]{1,0:T(8,128)(2,1)S(1)} %collective-permute-done.10.two), custom_call_target="tpu_custom_call" | custom-call | flops 704643072 | bytes 786432 | tf_op jit(solution)/shard_map/down/pallas_call | solution.py:219
  39.2 2.3 %collective-permute-start.12 = (bf16[32,6144]{1,0:T(8,128)(2,1)S(1)}, bf16[32,6144]{1,0:T(8,128)(2,1)S(1)}, u32[]{:S(2)}, u32[]{:S(2)}) collective-permute-start(bf16[32,6144]{1,0:T(8,128)(2,1)S(1)} %get-tuple-element.36), channel_id=1, source_target_pairs={{0,192},{8,56},{16,208},{24,40},{32,224},{40,24},{48,240},{56,8},{... | collective-permute-start | bytes 1179656 | tf_op jit(solution)/shard_map/reduce2_twrap/ppermute | solution.py:47
  41.5 0.0 collective-permute-start.11
  41.5 2.8 %down.4 = (bf16[32,6144]{1,0:T(8,128)(2,1)S(1)}, bf16[32,6144]{1,0:T(8,128)(2,1)S(1)}, bf16[32,6144]{1,0:T(8,128)(2,1)S(1)}, bf16[32,6144]{1,0:T(8,128)(2,1)S(1)...) custom-call(bf16[256,896]{1,0:T(8,128)(2,1)S(1)} %up.1.hidden, ...), custom_call_target="tpu_custom_call" | custom-call | flops 2113929216 | bytes 2359296 | tf_op jit(solution)/shard_map/down/pallas_call | solution.py:219
  44.3 1.1 %collective-permute-start.15 = (bf16[32,6144]{1,0:T(8,128)(2,1)S(1)}, bf16[32,6144]{1,0:T(8,128)(2,1)S(1)}, u32[]{:S(2)}, u32[]{:S(2)}) collective-permute-start(bf16[32,6144]{1,0:T(8,128)(2,1)S(1)} %get-tuple-element.40), channel_id=1, source_target_pairs={{0,192},{8,56},{16,208},{24,40},{32,224},{40,24},{48,240},{56,8},{... | collective-permute-start | bytes 1179656 | tf_op jit(solution)/shard_map/reduce_twrap/ppermute | solution.py:47
  45.4 2.8 %collective-permute-done.12.arrived = bf16[32,6144]{1,0:T(8,128)(2,1)S(1)} collective-permute-done((bf16[32,6144]{1,0:T(8,128)(2,1)S(1)}, bf16[32,6144]{1,0:T(8,128)(2,1)S(1)}, u32[]{:S(2)}, u32[]{:S(2)}) %collective-permute-start.12) | collective-permute-done | bytes 393248 | tf_op jit(solution)/shard_map/reduce2_twrap/ppermute | solution.py:47
  48.3 0.1 merge.2.refs_1_
  48.4 0.1 collective-permute-start.16
  48.5 0.8 %collective-permute-done.11.arrived = bf16[32,6144]{1,0:T(8,128)(2,1)S(1)} collective-permute-done((bf16[32,6144]{1,0:T(8,128)(2,1)S(1)}, bf16[32,6144]{1,0:T(8,128)(2,1)S(1)}, u32[]{:S(2)}, u32[]{:S(2)}) %collective-permute-start.11) | collective-permute-done | bytes 393248 | tf_op jit(solution)/shard_map/reduce2_tnear/ppermute | solution.py:47
  49.2 0.1 merge.3
  49.3 1.3 %collective-permute-start.13 = (bf16[32,6144]{1,0:T(8,128)(2,1)S(1)}, bf16[32,6144]{1,0:T(8,128)(2,1)S(1)}, u32[]{:S(2)}, u32[]{:S(2)}) collective-permute-start(bf16[32,6144]{1,0:T(8,128)(2,1)S(1)} %get-tuple-element.37), channel_id=1, source_target_pairs={{0,64},{8,24},{16,80},{24,8},{32,96},{40,56},{48,112},{56,40},{64,... | collective-permute-start | bytes 1179656 | tf_op jit(solution)/shard_map/reduce_tnear/ppermute | solution.py:47
  50.7 2.2 %collective-permute-start.14 = (bf16[32,6144]{1,0:T(8,128)(2,1)S(1)}, bf16[32,6144]{1,0:T(8,128)(2,1)S(1)}, u32[]{:S(2)}, u32[]{:S(2)}) collective-permute-start(bf16[32,6144]{1,0:T(8,128)(2,1)S(1)} %get-tuple-element.38), channel_id=1, source_target_pairs={{0,192},{8,56},{16,208},{24,40},{32,224},{40,24},{48,240},{56,8},{... | collective-permute-start | bytes 1179656 | tf_op jit(solution)/shard_map/reduce_twrap/ppermute | solution.py:47
  52.8 0.5 collective-permute-done.15.direct
  53.3 2.9 %collective-permute-done.16.back = bf16[32,6144]{1,0:T(8,128)(2,1)S(1)} collective-permute-done((bf16[32,6144]{1,0:T(8,128)(2,1)S(1)}, bf16[32,6144]{1,0:T(8,128)(2,1)S(1)}, u32[]{:S(2)}, u32[]{:S(2)}) %collective-permute-start.16) | collective-permute-done | bytes 393248 | tf_op jit(solution)/shard_map/reduce_tnear/ppermute | solution.py:47
  56.2 0.1 finish.2
  56.4 1.9 %collective-permute-start.18 = (bf16[16,6144]{1,0:T(8,128)(2,1)S(1)}, bf16[16,6144]{1,0:T(8,128)(2,1)S(1)}, u32[]{:S(2)}, u32[]{:S(2)}) collective-permute-start(bf16[16,6144]{1,0:T(8,128)(2,1)S(1)} %get-tuple-element.43), channel_id=1, source_target_pairs={{0,32},{8,136},{16,48},{24,152},{32,0},{40,168},{48,16},{56,184},{... | collective-permute-start | bytes 589832 | tf_op jit(solution)/shard_map/home_sfar/ppermute | solution.py:47
  58.3 1.8 %collective-permute-start.17 = (bf16[16,6144]{1,0:T(8,128)(2,1)S(1)}, bf16[16,6144]{1,0:T(8,128)(2,1)S(1)}, u32[]{:S(2)}, u32[]{:S(2)}) collective-permute-start(bf16[16,6144]{1,0:T(8,128)(2,1)S(1)} %get-tuple-element.41.refs_0_), channel_id=1, source_target_pairs={{0,48},{8,200},{16,32},{24,216},{32,16},{40,232},{48,0},{56,248},{... | collective-permute-start | bytes 589832 | tf_op jit(solution)/shard_map/home_swrap/ppermute | solution.py:47
  60.1 2.9 %collective-permute-done.13.direct = bf16[32,6144]{1,0:T(8,128)(2,1)S(1)} collective-permute-done((bf16[32,6144]{1,0:T(8,128)(2,1)S(1)}, bf16[32,6144]{1,0:T(8,128)(2,1)S(1)}, u32[]{:S(2)}, u32[]{:S(2)}) %collective-permute-start.13) | collective-permute-done | bytes 393248 | tf_op jit(solution)/shard_map/reduce_tnear/ppermute | solution.py:47
  63.0 0.1 finish.3
  63.1 1.7 %collective-permute-start.19 = (bf16[16,6144]{1,0:T(8,128)(2,1)S(1)}, bf16[16,6144]{1,0:T(8,128)(2,1)S(1)}, u32[]{:S(2)}, u32[]{:S(2)}) collective-permute-start(bf16[16,6144]{1,0:T(8,128)(2,1)S(1)} %get-tuple-element.44), channel_id=1, source_target_pairs={{0,16},{8,72},{16,0},{24,88},{32,48},{40,104},{48,32},{56,120},{64... | collective-permute-start | bytes 589832 | tf_op jit(solution)/shard_map/home_snear/ppermute | solution.py:47
  64.8 0.0 collective-permute-done.18.refs_3_
  64.8 0.9 %collective-permute-done.17.refs_2_ = bf16[16,6144]{1,0:T(8,128)(2,1)S(1)} collective-permute-done((bf16[16,6144]{1,0:T(8,128)(2,1)S(1)}, bf16[16,6144]{1,0:T(8,128)(2,1)S(1)}, u32[]{:S(2)}, u32[]{:S(2)}) %collective-permute-start.17) | collective-permute-done | bytes 196640 | tf_op jit(solution)/shard_map/home_swrap/ppermute | solution.py:47
  65.7 0.1 collect.1
  65.8 3.1 %collective-permute-done.19 = bf16[16,6144]{1,0:T(8,128)(2,1)S(1)} collective-permute-done((bf16[16,6144]{1,0:T(8,128)(2,1)S(1)}, bf16[16,6144]{1,0:T(8,128)(2,1)S(1)}, u32[]{:S(2)}, u32[]{:S(2)}) %collective-permute-start.19) | collective-permute-done | bytes 196640 | tf_op jit(solution)/shard_map/home_snear/ppermute | solution.py:47
  68.9 0.7 %add_convert_fusion = bf16[16,6144]{1,0:T(8,128)(2,1)} fusion(f32[16,6144]{1,0:T(8,128)S(1)} %collect.1, bf16[16,6144]{1,0:T(8,128)(2,1)S(1)} %collective-permute-done.19), kind=kLoop, calls=%fused_computation | loop fusion | flops 294912 | bytes 786432 | tf_op jit(solution)/shard_map/convert_element_type | solution.py:343
  (4 shorter events, 0.0 us)
Async XLA Ops:
  0.0 14.2 %collective-permute-start.3 = (bf16[448,6144]{1,0:T(8,128)(2,1)}, bf16[448,6144]{1,0:T(8,128)(2,1)S(1)}, u32[]{:S(2)}, u32[]{:S(2)}) collective-permute-start(bf16[448,6144]{1,0:T(8,128)(2,1)} %bitcast.2), channel_id=1, source_target_pairs={{0,8},{8,0},{16,24},{24,16},{32,40},{40,32},{48,56},{56,48},{64,72... | collective-permute-start | bytes 16515080 | tf_op jit(solution)/shard_map/up_core/ppermute | solution.py:47
  4.2 7.3 %collective-permute-start.2 = (bf16[16,6144]{1,0:T(8,128)(2,1)S(1)}, bf16[16,6144]{1,0:T(8,128)(2,1)S(1)}, u32[]{:S(2)}, u32[]{:S(2)}) collective-permute-start(bf16[16,6144]{1,0:T(8,128)(2,1)S(1)} %get-tuple-element.26.own), channel_id=1, source_target_pairs={{0,32},{8,136},{16,48},{24,152},{32,0},{40,168},{48,16},{56,184},{... | collective-permute-start | bytes 589832 | tf_op jit(solution)/shard_map/gather_sfar/ppermute | solution.py:47
  7.3 6.9 %collective-permute-start.1 = (bf16[16,6144]{1,0:T(8,128)(2,1)S(1)}, bf16[16,6144]{1,0:T(8,128)(2,1)S(1)}, u32[]{:S(2)}, u32[]{:S(2)}) collective-permute-start(bf16[16,6144]{1,0:T(8,128)(2,1)S(1)} %get-tuple-element.26.own), channel_id=1, source_target_pairs={{0,48},{8,200},{16,32},{24,216},{32,16},{40,232},{48,0},{56,248},{... | collective-permute-start | bytes 589832 | tf_op jit(solution)/shard_map/gather_swrap/ppermute | solution.py:47
  8.4 5.7 %collective-permute-start = (bf16[16,6144]{1,0:T(8,128)(2,1)S(1)}, bf16[16,6144]{1,0:T(8,128)(2,1)S(1)}, u32[]{:S(2)}, u32[]{:S(2)}) collective-permute-start(bf16[16,6144]{1,0:T(8,128)(2,1)S(1)} %get-tuple-element.26.own), channel_id=1, source_target_pairs={{0,16},{8,72},{16,0},{24,88},{32,48},{40,104},{48,32},{56,120},{64... | collective-permute-start | bytes 589832 | tf_op jit(solution)/shard_map/gather_snear/ppermute | solution.py:47
  14.2 22.8 %collective-permute-start.10 = (bf16[448,6144]{1,0:T(8,128)(2,1)S(1)}, bf16[448,6144]{1,0:T(8,128)(2,1)S(1)}, u32[]{:S(2)}, u32[]{:S(2)}) collective-permute-start(bf16[448,6144]{1,0:T(8,128)(2,1)S(1)} %get-tuple-element.30.one), channel_id=1, source_target_pairs={{0,8},{8,0},{16,24},{24,16},{32,40},{40,32},{48,56},{56,48},{64,72... | collective-permute-start | bytes 16515080 | tf_op jit(solution)/shard_map/down_core/ppermute | solution.py:47
  14.3 7.9 %collective-permute-start.4 = (bf16[32,6144]{1,0:T(8,128)(2,1)S(1)}, bf16[32,6144]{1,0:T(8,128)(2,1)S(1)}, u32[]{:S(2)}, u32[]{:S(2)}) collective-permute-start(bf16[32,6144]{1,0:T(8,128)(2,1)S(1)} %get-tuple-element.28.args_0_), channel_id=1, source_target_pairs={{0,64},{8,24},{16,80},{24,8},{32,96},{40,56},{48,112},{56,40},{64,... | collective-permute-start | bytes 1179656 | tf_op jit(solution)/shard_map/gather_tnear/ppermute | solution.py:47
  16.0 9.2 %collective-permute-start.5 = (bf16[32,6144]{1,0:T(8,128)(2,1)S(1)}, bf16[32,6144]{1,0:T(8,128)(2,1)S(1)}, u32[]{:S(2)}, u32[]{:S(2)}) collective-permute-start(bf16[32,6144]{1,0:T(8,128)(2,1)S(1)} %get-tuple-element.29.after.args_1_), channel_id=1, source_target_pairs={{0,192},{8,56},{16,208},{24,40},{32,224},{40,24},{48,240},{56,8},{... | collective-permute-start | bytes 1179656 | tf_op jit(solution)/shard_map/gather_twrap/ppermute | solution.py:47
  18.2 11.0 %collective-permute-start.6 = (bf16[32,6144]{1,0:T(8,128)(2,1)S(1)}, bf16[32,6144]{1,0:T(8,128)(2,1)S(1)}, u32[]{:S(2)}, u32[]{:S(2)}) collective-permute-start(bf16[32,6144]{1,0:T(8,128)(2,1)S(1)} %get-tuple-element.28.args_0_), channel_id=1, source_target_pairs={{0,192},{8,56},{16,208},{24,40},{32,224},{40,24},{48,240},{56,8},{... | collective-permute-start | bytes 1179656 | tf_op jit(solution)/shard_map/gather_twrap/ppermute | solution.py:47
  19.2 10.0 %collective-permute-start.7 = (bf16[32,6144]{1,0:T(8,128)(2,1)S(1)}, bf16[32,6144]{1,0:T(8,128)(2,1)S(1)}, u32[]{:S(2)}, u32[]{:S(2)}) collective-permute-start(bf16[32,6144]{1,0:T(8,128)(2,1)S(1)} %get-tuple-element.29.after.args_1_), channel_id=1, source_target_pairs={{0,64},{8,24},{16,80},{24,8},{32,96},{40,56},{48,112},{56,40},{64,... | collective-permute-start | bytes 1179656 | tf_op jit(solution)/shard_map/gather_tnear/ppermute | solution.py:47
  22.2 11.2 %collective-permute-start.8 = (bf16[32,6144]{1,0:T(8,128)(2,1)S(1)}, bf16[32,6144]{1,0:T(8,128)(2,1)S(1)}, u32[]{:S(2)}, u32[]{:S(2)}) collective-permute-start(bf16[32,6144]{1,0:T(8,128)(2,1)S(1)} %collective-permute-done.4.args_2_), channel_id=1, source_target_pairs={{0,192},{8,56},{16,208},{24,40},{32,224},{40,24},{48,240},{56,8},{... | collective-permute-start | bytes 1179656 | tf_op jit(solution)/shard_map/gather2_twrap/ppermute | solution.py:47
  25.2 8.2 %collective-permute-start.9 = (bf16[32,6144]{1,0:T(8,128)(2,1)S(1)}, bf16[32,6144]{1,0:T(8,128)(2,1)S(1)}, u32[]{:S(2)}, u32[]{:S(2)}) collective-permute-start(bf16[32,6144]{1,0:T(8,128)(2,1)S(1)} %collective-permute-done.5.args_3_), channel_id=1, source_target_pairs={{0,64},{8,24},{16,80},{24,8},{32,96},{40,56},{48,112},{56,40},{64,... | collective-permute-start | bytes 1179656 | tf_op jit(solution)/shard_map/gather2_tnear/ppermute | solution.py:47
  39.2 9.1 %collective-permute-start.12 = (bf16[32,6144]{1,0:T(8,128)(2,1)S(1)}, bf16[32,6144]{1,0:T(8,128)(2,1)S(1)}, u32[]{:S(2)}, u32[]{:S(2)}) collective-permute-start(bf16[32,6144]{1,0:T(8,128)(2,1)S(1)} %get-tuple-element.36), channel_id=1, source_target_pairs={{0,192},{8,56},{16,208},{24,40},{32,224},{40,24},{48,240},{56,8},{... | collective-permute-start | bytes 1179656 | tf_op jit(solution)/shard_map/reduce2_twrap/ppermute | solution.py:47
  41.5 7.8 %collective-permute-start.11 = (bf16[32,6144]{1,0:T(8,128)(2,1)S(1)}, bf16[32,6144]{1,0:T(8,128)(2,1)S(1)}, u32[]{:S(2)}, u32[]{:S(2)}) collective-permute-start(bf16[32,6144]{1,0:T(8,128)(2,1)S(1)} %get-tuple-element.33), channel_id=1, source_target_pairs={{0,64},{8,24},{16,80},{24,8},{32,96},{40,56},{48,112},{56,40},{64,... | collective-permute-start | bytes 1179656 | tf_op jit(solution)/shard_map/reduce2_tnear/ppermute | solution.py:47
  44.3 9.1 %collective-permute-start.15 = (bf16[32,6144]{1,0:T(8,128)(2,1)S(1)}, bf16[32,6144]{1,0:T(8,128)(2,1)S(1)}, u32[]{:S(2)}, u32[]{:S(2)}) collective-permute-start(bf16[32,6144]{1,0:T(8,128)(2,1)S(1)} %get-tuple-element.40), channel_id=1, source_target_pairs={{0,192},{8,56},{16,208},{24,40},{32,224},{40,24},{48,240},{56,8},{... | collective-permute-start | bytes 1179656 | tf_op jit(solution)/shard_map/reduce_twrap/ppermute | solution.py:47
  48.4 7.9 %collective-permute-start.16 = (bf16[32,6144]{1,0:T(8,128)(2,1)S(1)}, bf16[32,6144]{1,0:T(8,128)(2,1)S(1)}, u32[]{:S(2)}, u32[]{:S(2)}) collective-permute-start(bf16[32,6144]{1,0:T(8,128)(2,1)S(1)} %merge.2.refs_1_), channel_id=1, source_target_pairs={{0,64},{8,24},{16,80},{24,8},{32,96},{40,56},{48,112},{56,40},{64,... | collective-permute-start | bytes 1179656 | tf_op jit(solution)/shard_map/reduce_tnear/ppermute | solution.py:47
  49.3 13.7 %collective-permute-start.13 = (bf16[32,6144]{1,0:T(8,128)(2,1)S(1)}, bf16[32,6144]{1,0:T(8,128)(2,1)S(1)}, u32[]{:S(2)}, u32[]{:S(2)}) collective-permute-start(bf16[32,6144]{1,0:T(8,128)(2,1)S(1)} %get-tuple-element.37), channel_id=1, source_target_pairs={{0,64},{8,24},{16,80},{24,8},{32,96},{40,56},{48,112},{56,40},{64,... | collective-permute-start | bytes 1179656 | tf_op jit(solution)/shard_map/reduce_tnear/ppermute | solution.py:47
  50.7 12.3 %collective-permute-start.14 = (bf16[32,6144]{1,0:T(8,128)(2,1)S(1)}, bf16[32,6144]{1,0:T(8,128)(2,1)S(1)}, u32[]{:S(2)}, u32[]{:S(2)}) collective-permute-start(bf16[32,6144]{1,0:T(8,128)(2,1)S(1)} %get-tuple-element.38), channel_id=1, source_target_pairs={{0,192},{8,56},{16,208},{24,40},{32,224},{40,24},{48,240},{56,8},{... | collective-permute-start | bytes 1179656 | tf_op jit(solution)/shard_map/reduce_twrap/ppermute | solution.py:47
  56.4 8.4 %collective-permute-start.18 = (bf16[16,6144]{1,0:T(8,128)(2,1)S(1)}, bf16[16,6144]{1,0:T(8,128)(2,1)S(1)}, u32[]{:S(2)}, u32[]{:S(2)}) collective-permute-start(bf16[16,6144]{1,0:T(8,128)(2,1)S(1)} %get-tuple-element.43), channel_id=1, source_target_pairs={{0,32},{8,136},{16,48},{24,152},{32,0},{40,168},{48,16},{56,184},{... | collective-permute-start | bytes 589832 | tf_op jit(solution)/shard_map/home_sfar/ppermute | solution.py:47
  58.3 7.5 %collective-permute-start.17 = (bf16[16,6144]{1,0:T(8,128)(2,1)S(1)}, bf16[16,6144]{1,0:T(8,128)(2,1)S(1)}, u32[]{:S(2)}, u32[]{:S(2)}) collective-permute-start(bf16[16,6144]{1,0:T(8,128)(2,1)S(1)} %get-tuple-element.41.refs_0_), channel_id=1, source_target_pairs={{0,48},{8,200},{16,32},{24,216},{32,16},{40,232},{48,0},{56,248},{... | collective-permute-start | bytes 589832 | tf_op jit(solution)/shard_map/home_swrap/ppermute | solution.py:47
  63.1 5.8 %collective-permute-start.19 = (bf16[16,6144]{1,0:T(8,128)(2,1)S(1)}, bf16[16,6144]{1,0:T(8,128)(2,1)S(1)}, u32[]{:S(2)}, u32[]{:S(2)}) collective-permute-start(bf16[16,6144]{1,0:T(8,128)(2,1)S(1)} %get-tuple-element.44), channel_id=1, source_target_pairs={{0,16},{8,72},{16,0},{24,88},{32,48},{40,104},{48,32},{56,120},{64... | collective-permute-start | bytes 589832 | tf_op jit(solution)/shard_map/home_snear/ppermute | solution.py:47

commit v9 on v8

--- a/solution.py
+++ b/solution.py
@@ -1,4 +1,5 @@
 import functools
+import math
 
 import jax
 import jax.numpy as jnp
@@ -52,7 +53,7 @@
 
 
 def attend_kernel(
-    counts, lengths_in, q_in, k_in, v_in, gain_in, down, attended, normed, down_held, lengths, q, k, v, gain, sems
+    lengths_in, q_in, k_in, v_in, gain_in, down, attended, normed, down_held, lengths, q, k, v, gain, sems
 ):
     copies = [
         pltpu.make_async_copy(a, b, sems.at[i])
@@ -82,8 +83,8 @@
     position = lax.broadcasted_iota(jnp.int32, (SLOTS, POOL), 1)
     inside = (position >= starts) & (position < ends)
     offset = jnp.where(inside, jnp.float32(0.0), jnp.float32(-1e30))
-    live = row < counts[0]
     squares = jnp.zeros((SLOTS, HD), jnp.float32)
+    ones = jnp.ones((POOL, HD), jnp.bfloat16)
     copies[1].wait()
     copies[2].wait()
     for kv in range(KVH):
@@ -97,19 +98,18 @@
         )
         masked = scores.reshape(GROUP, SLOTS, POOL) + offset[None]
         top = jnp.max(masked, axis=-1, keepdims=True)
-        raised = jnp.exp((masked - top) * jnp.float32(HD ** (-0.5)))
-        total = jnp.sum(raised, axis=-1, keepdims=True)
+        raised = jnp.exp2((masked - top) * jnp.float32(HD ** (-0.5) * math.log2(math.e)))
         if kv == 0:
             copies[3].wait()
         mixed = lax.dot_general(
             raised.astype(jnp.bfloat16).reshape(GROUP * SLOTS, POOL),
-            v[:, kv * HD : (kv + 1) * HD],
+            jnp.concatenate([v[:, kv * HD : (kv + 1) * HD], ones], axis=1),
             (((1,), (0,)), ((), ())),
             preferred_element_type=jnp.float32,
         )
-        mixed = mixed.reshape(GROUP, SLOTS, HD) / total
+        mixed = (mixed[:, :HD] / mixed[:, HD:]).reshape(GROUP, SLOTS, HD)
         for g, h in enumerate(heads):
-            part = jnp.where(live, mixed[g], jnp.float32(0.0)).astype(jnp.bfloat16)
+            part = mixed[g].astype(jnp.bfloat16)
             attended[:, h * HD : (h + 1) * HD] = part
             wide = part.astype(jnp.float32)
             squares = squares + wide * wide
@@ -120,7 +120,7 @@
     copies[5].wait()
 
 
-def attend(queries, cache_keys, cache_values, lengths, counts, norm_gain, down_rows):
+def attend(queries, cache_keys, cache_values, lengths, norm_gain, down_rows):
     vmem = pl.BlockSpec(memory_space=pltpu.VMEM)
     any_space = pl.BlockSpec(memory_space=pl.ANY)
     return pl.pallas_call(
@@ -130,7 +130,7 @@
             jax.ShapeDtypeStruct((SLOTS, D), jnp.bfloat16),
             jax.ShapeDtypeStruct((HIDDEN, D), jnp.bfloat16),
         ),
-        in_specs=[pl.BlockSpec(memory_space=pltpu.SMEM)] + [any_space] * 6,
+        in_specs=[any_space] * 6,
         out_specs=(vmem, vmem, vmem),
         scratch_shapes=[
             pltpu.SMEM((SLOTS,), jnp.int32),
@@ -142,7 +142,7 @@
         ],
         compiler_params=pltpu.CompilerParams(vmem_limit_bytes=16 * 2**20),
         name="attend",
-    )(counts, *map(in_hbm, (lengths, queries, cache_keys, cache_values, norm_gain.reshape(1, D), down_rows)))
+    )(*map(in_hbm, (lengths, queries, cache_keys, cache_values, norm_gain.reshape(1, D), down_rows)))
 
 
 def fetch_kernel(weights, after, held, sem):
@@ -312,7 +312,7 @@
     up_own = up_weight.T
     up_other = send(up_own, "core", "up")
     attended, normed, down_held = attend(
-        queries, cache_keys, cache_values, lengths, counts, norm_gain, down_weight
+        queries, cache_keys, cache_values, lengths, norm_gain, down_weight
     )
     by_wrap, by_far, by_near = [send(normed, r, "gather") for r in ("swrap", "sfar", "snear")]
     early, late, down_held = pack(normed, by_near, by_wrap, by_far, down_held, up_other)
@@ -332,15 +332,16 @@
     direct_late = send(late_w, "twrap", "reduce")
     (late_n,) = merge(late_n, far_late)
     back_late = send(late_n, "tnear", "reduce")
-    early_w, early_n = merge(early_w, far_early, early_n, after=(late_n,))
+    direct_early = send(early_n, "tnear", "reduce")
+    (early_w,) = merge(early_w, far_early, after=(late_n,))
     back_early = send(early_w, "twrap", "reduce")
-    direct_early = send(early_n, "tnear", "reduce")
-    home_wrap, home_far = finish(late, direct_late, back_late, jnp.bfloat16)
+    home_wrap, home_far = finish(late, direct_late, back_late, jnp.bfloat16, after=(direct_early,))
     own, home_near = finish(early, direct_early, back_early, jnp.float32, after=(home_wrap,))
     home_wrap, home_far = send(home_wrap, "swrap", "home"), send(home_far, "sfar", "home")
     home_near = send(home_near, "snear", "home")
     mixed = collect(attended, own, home_wrap, home_far)
-    return (mixed + home_near.astype(jnp.float32)).astype(jnp.bfloat16)
+    live = jnp.arange(SLOTS, dtype=jnp.int32)[:, None] < counts[0]
+    return jnp.where(live, mixed + home_near.astype(jnp.float32), jnp.float32(0.0)).astype(jnp.bfloat16)
 
 
 def solution(mesh):

time: 70 us -> 69.3 us (0.990)
  starting transfers between devices: 24.8 us -> 23.3 us
    ppermute x20, starting transfers between devices: 24.8 us -> 23.3 us  [send(): return lax.ppermute(value, 'dp', ROUTES[route])]
  transfers between devices with their start and end apart: 20 -> 20, of which waited for: 12 -> 15; matrix products, arithmetic and copies ran while one was open for 0% -> 0% of each run, Pallas kernels for 19% -> 19%
where the time goes in v9:
time: 69.3 us; the launch traced here: 68.6 us
  waiting for transfers between devices  28.7 us (41%)
  starting transfers between devices  23.3 us (34%)
  Pallas kernels  15.1 us (22%)
  other arithmetic  0.77 us (1%)
  between operations  0.76 us (1%)
    ppermute x20, waiting for transfers between devices, send(): return lax.ppermute(value, 'dp', ROUTES[route])  28.7 us
    ppermute x20, starting transfers between devices, send(): return lax.ppermute(value, 'dp', ROUTES[route])  23.3 us
    pallas_call x2, Pallas kernels, project_down(): pl.pallas_call(functools.partial(down_kernel, begin), out_shape=[jax.Shap...  4.98 us
    pallas_call x1, Pallas kernels, project_up(): pl.pallas_call(up_kernel, out_shape=jax.ShapeDtypeStruct((rows, 2 * HIDDE...  3.59 us
    pallas_call x1, Pallas kernels, attend(): pl.pallas_call(attend_kernel, out_shape=(jax.ShapeDtypeStruct((SLOTS, D),...  3.34 us
    pallas_call x1, Pallas kernels, fetch(): pl.pallas_call(fetch_kernel, out_shape=jax.ShapeDtypeStruct((HIDDEN, D),...  2.57 us
  transfers between devices with their start and end apart: 20, of which 15 were waited for; matrix products, arithmetic and copies ran while one was open for 0% of the time, Pallas kernels for 19%

profile of v9, /device:TPU:128, one launch (start us, length us, event | category | flops | bytes accessed | tf_op | source)
XLA Modules:
  0.0 68.6 jit_solution(4633237748023379366)
XLA Ops:
  0.0 0.0 collective-permute-start.3
  0.0 3.3 %attend.1 = (bf16[16,6144]{1,0:T(8,128)(2,1)S(1)}, bf16[16,6144]{1,0:T(8,128)(2,1)S(1)}, bf16[448,6144]{1,0:T(8,128)(2,1)S(1)}) custom-call(s32[16]{0:T(128)} %lengths_in.1, bf16[16,6144]{1,0:T(8,128)(2,1)} %q_in.1, bf16[1024,512]{1,0:T(8,128)(2,1)} %k_in.1, bf16[1024,512]{1,0:T(8,128)(2,1)} %v_in.1, f32[1,6144]{1,0:T(1,128)} %bitcast.6, bf16[448,6144]{1,0:T(8,128)(2,1)} %down.3), custom_call_target="tpu_custom_call" | custom-call | tf_op jit(solution)/shard_map/attend/pallas_call | solution.py:126
  3.4 1.6 %collective-permute-start = (bf16[16,6144]{1,0:T(8,128)(2,1)S(1)}, bf16[16,6144]{1,0:T(8,128)(2,1)S(1)}, u32[]{:S(2)}, u32[]{:S(2)}) collective-permute-start(bf16[16,6144]{1,0:T(8,128)(2,1)S(1)} %get-tuple-element.24.own), channel_id=1, source_target_pairs={{0,16},{8,72},{16,0},{24,88},{32,48},{40,104},{48,32},{56,120},{64... | collective-permute-start | bytes 589832 | tf_op jit(solution)/shard_map/gather_snear/ppermute | solution.py:48
  4.9 2.1 %collective-permute-start.1 = (bf16[16,6144]{1,0:T(8,128)(2,1)S(1)}, bf16[16,6144]{1,0:T(8,128)(2,1)S(1)}, u32[]{:S(2)}, u32[]{:S(2)}) collective-permute-start(bf16[16,6144]{1,0:T(8,128)(2,1)S(1)} %get-tuple-element.24.own), channel_id=1, source_target_pairs={{0,48},{8,200},{16,32},{24,216},{32,16},{40,232},{48,0},{56,248},{... | collective-permute-start | bytes 589832 | tf_op jit(solution)/shard_map/gather_swrap/ppermute | solution.py:48
  7.0 0.6 collective-permute-start.2
  7.7 1.4 %collective-permute-done.near = bf16[16,6144]{1,0:T(8,128)(2,1)S(1)} collective-permute-done((bf16[16,6144]{1,0:T(8,128)(2,1)S(1)}, bf16[16,6144]{1,0:T(8,128)(2,1)S(1)}, u32[]{:S(2)}, u32[]{:S(2)}) %collective-permute-start) | collective-permute-done | bytes 196640 | tf_op jit(solution)/shard_map/gather_snear/ppermute | solution.py:48
  9.1 3.2 %collective-permute-done.1.wrap = bf16[16,6144]{1,0:T(8,128)(2,1)S(1)} collective-permute-done((bf16[16,6144]{1,0:T(8,128)(2,1)S(1)}, bf16[16,6144]{1,0:T(8,128)(2,1)S(1)}, u32[]{:S(2)}, u32[]{:S(2)}) %collective-permute-start.1) | collective-permute-done | bytes 196640 | tf_op jit(solution)/shard_map/gather_swrap/ppermute | solution.py:48
  12.4 1.8 %collective-permute-done.2.far = bf16[16,6144]{1,0:T(8,128)(2,1)S(1)} collective-permute-done((bf16[16,6144]{1,0:T(8,128)(2,1)S(1)}, bf16[16,6144]{1,0:T(8,128)(2,1)S(1)}, u32[]{:S(2)}, u32[]{:S(2)}) %collective-permute-start.2) | collective-permute-done | bytes 196640 | tf_op jit(solution)/shard_map/gather_sfar/ppermute | solution.py:48
  14.2 0.0 collective-permute-done.3.after.args_9_
  14.2 0.1 pack.1
  14.3 0.1 collective-permute-start.10
  14.4 1.7 %collective-permute-start.4 = (bf16[32,6144]{1,0:T(8,128)(2,1)S(1)}, bf16[32,6144]{1,0:T(8,128)(2,1)S(1)}, u32[]{:S(2)}, u32[]{:S(2)}) collective-permute-start(bf16[32,6144]{1,0:T(8,128)(2,1)S(1)} %get-tuple-element.26.args_0_), channel_id=1, source_target_pairs={{0,64},{8,24},{16,80},{24,8},{32,96},{40,56},{48,112},{56,40},{64,... | collective-permute-start | bytes 1179656 | tf_op jit(solution)/shard_map/gather_tnear/ppermute | solution.py:48
  16.0 2.2 %collective-permute-start.5 = (bf16[32,6144]{1,0:T(8,128)(2,1)S(1)}, bf16[32,6144]{1,0:T(8,128)(2,1)S(1)}, u32[]{:S(2)}, u32[]{:S(2)}) collective-permute-start(bf16[32,6144]{1,0:T(8,128)(2,1)S(1)} %get-tuple-element.27.after.args_1_), channel_id=1, source_target_pairs={{0,192},{8,56},{16,208},{24,40},{32,224},{40,24},{48,240},{56,8},{... | collective-permute-start | bytes 1179656 | tf_op jit(solution)/shard_map/gather_twrap/ppermute | solution.py:48
  18.2 1.1 %collective-permute-start.6 = (bf16[32,6144]{1,0:T(8,128)(2,1)S(1)}, bf16[32,6144]{1,0:T(8,128)(2,1)S(1)}, u32[]{:S(2)}, u32[]{:S(2)}) collective-permute-start(bf16[32,6144]{1,0:T(8,128)(2,1)S(1)} %get-tuple-element.26.args_0_), channel_id=1, source_target_pairs={{0,192},{8,56},{16,208},{24,40},{32,224},{40,24},{48,240},{56,8},{... | collective-permute-start | bytes 1179656 | tf_op jit(solution)/shard_map/gather_twrap/ppermute | solution.py:48
  19.3 0.0 collective-permute-start.7
  19.3 3.0 %collective-permute-done.4.args_2_ = bf16[32,6144]{1,0:T(8,128)(2,1)S(1)} collective-permute-done((bf16[32,6144]{1,0:T(8,128)(2,1)S(1)}, bf16[32,6144]{1,0:T(8,128)(2,1)S(1)}, u32[]{:S(2)}, u32[]{:S(2)}) %collective-permute-start.4) | collective-permute-done | bytes 393248 | tf_op jit(solution)/shard_map/gather_tnear/ppermute | solution.py:48
  22.2 3.0 %collective-permute-start.8 = (bf16[32,6144]{1,0:T(8,128)(2,1)S(1)}, bf16[32,6144]{1,0:T(8,128)(2,1)S(1)}, u32[]{:S(2)}, u32[]{:S(2)}) collective-permute-start(bf16[32,6144]{1,0:T(8,128)(2,1)S(1)} %collective-permute-done.4.args_2_), channel_id=1, source_target_pairs={{0,192},{8,56},{16,208},{24,40},{32,224},{40,24},{48,240},{56,8},{... | collective-permute-start | bytes 1179656 | tf_op jit(solution)/shard_map/gather2_twrap/ppermute | solution.py:48
  25.2 0.0 collective-permute-done.5.args_3_
  25.2 0.1 collective-permute-start.9
  25.4 2.6 %fetch.1.args_8_ = bf16[448,6144]{1,0:T(8,128)(2,1)S(1)} custom-call(bf16[448,6144]{1,0:T(8,128)(2,1)} %bitcast.5, bf16[32,6144]{1,0:T(8,128)(2,1)S(1)} %get-tuple-element.27.after.args_1_), custom_call_target="tpu_custom_call" | custom-call | bytes 11010048 | tf_op jit(solution)/shard_map/fetch/pallas_call | solution.py:156
  28.0 1.3 %collective-permute-done.6.args_4_ = bf16[32,6144]{1,0:T(8,128)(2,1)S(1)} collective-permute-done((bf16[32,6144]{1,0:T(8,128)(2,1)S(1)}, bf16[32,6144]{1,0:T(8,128)(2,1)S(1)}, u32[]{:S(2)}, u32[]{:S(2)}) %collective-permute-start.6) | collective-permute-done | bytes 393248 | tf_op jit(solution)/shard_map/gather_twrap/ppermute | solution.py:48
  29.2 4.2 %collective-permute-done.8.args_6_ = bf16[32,6144]{1,0:T(8,128)(2,1)S(1)} collective-permute-done((bf16[32,6144]{1,0:T(8,128)(2,1)S(1)}, bf16[32,6144]{1,0:T(8,128)(2,1)S(1)}, u32[]{:S(2)}, u32[]{:S(2)}) %collective-permute-start.8) | collective-permute-done | bytes 393248 | tf_op jit(solution)/shard_map/gather2_twrap/ppermute | solution.py:48
  33.4 3.6 %up.1.hidden = bf16[256,896]{1,0:T(8,128)(2,1)S(1)} custom-call(bf16[32,6144]{1,0:T(8,128)(2,1)S(1)} %get-tuple-element.26.args_0_, bf16[32,6144]{1,0:T(8,128)(2,1)S(1)} %get-tuple-element.27.after.args_1_, bf16[32,6144]{1,0:T(8,128)(2,1)S(1)} %collective-permute-done.4.args_2_, bf16[32,6144]{1,0:T(8,128)(2,1)S(1)} %collective-permute-done.5.args_3_, ...), custom_call_target="tpu_custom_call" | custom-call | flops 2818572288 | bytes 3145728 | tf_op jit(solution)/shard_map/up/pallas_call | solution.py:189
  37.1 2.2 %down.5 = (bf16[32,6144]{1,0:T(8,128)(2,1)S(1)}, bf16[32,6144]{1,0:T(8,128)(2,1)S(1)}) custom-call(bf16[256,896]{1,0:T(8,128)(2,1)S(1)} %up.1.hidden, bf16[448,6144]{1,0:T(8,128)(2,1)S(1)} %get-tuple-element.28.one, bf16[448,6144]{1,0:T(8,128)(2,1)S(1)} %collective-permute-done.10.two), custom_call_target="tpu_custom_call" | custom-call | flops 704643072 | bytes 786432 | tf_op jit(solution)/shard_map/down/pallas_call | solution.py:219
  39.2 2.3 %collective-permute-start.13 = (bf16[32,6144]{1,0:T(8,128)(2,1)S(1)}, bf16[32,6144]{1,0:T(8,128)(2,1)S(1)}, u32[]{:S(2)}, u32[]{:S(2)}) collective-permute-start(bf16[32,6144]{1,0:T(8,128)(2,1)S(1)} %get-tuple-element.34), channel_id=1, source_target_pairs={{0,192},{8,56},{16,208},{24,40},{32,224},{40,24},{48,240},{56,8},{... | collective-permute-start | bytes 1179656 | tf_op jit(solution)/shard_map/reduce2_twrap/ppermute | solution.py:48
  41.5 2.8 %down.4 = (bf16[32,6144]{1,0:T(8,128)(2,1)S(1)}, bf16[32,6144]{1,0:T(8,128)(2,1)S(1)}, bf16[32,6144]{1,0:T(8,128)(2,1)S(1)}, bf16[32,6144]{1,0:T(8,128)(2,1)S(1)...) custom-call(bf16[256,896]{1,0:T(8,128)(2,1)S(1)} %up.1.hidden, ...), custom_call_target="tpu_custom_call" | custom-call | flops 2113929216 | bytes 2359296 | tf_op jit(solution)/shard_map/down/pallas_call | solution.py:219
  44.3 2.3 %collective-permute-start.11 = (bf16[32,6144]{1,0:T(8,128)(2,1)S(1)}, bf16[32,6144]{1,0:T(8,128)(2,1)S(1)}, u32[]{:S(2)}, u32[]{:S(2)}) collective-permute-start(bf16[32,6144]{1,0:T(8,128)(2,1)S(1)} %get-tuple-element.30), channel_id=1, source_target_pairs={{0,64},{8,24},{16,80},{24,8},{32,96},{40,56},{48,112},{56,40},{64,... | collective-permute-start | bytes 1179656 | tf_op jit(solution)/shard_map/reduce_tnear/ppermute | solution.py:48
  46.6 1.1 %collective-permute-start.15 = (bf16[32,6144]{1,0:T(8,128)(2,1)S(1)}, bf16[32,6144]{1,0:T(8,128)(2,1)S(1)}, u32[]{:S(2)}, u32[]{:S(2)}) collective-permute-start(bf16[32,6144]{1,0:T(8,128)(2,1)S(1)} %get-tuple-element.36), channel_id=1, source_target_pairs={{0,192},{8,56},{16,208},{24,40},{32,224},{40,24},{48,240},{56,8},{... | collective-permute-start | bytes 1179656 | tf_op jit(solution)/shard_map/reduce_twrap/ppermute | solution.py:48
  47.7 0.6 collective-permute-done.13.arrived
  48.3 0.1 merge.2.refs_0_
  48.4 0.1 collective-permute-start.16
  48.5 0.8 %collective-permute-done.12.arrived = bf16[32,6144]{1,0:T(8,128)(2,1)S(1)} collective-permute-done((bf16[32,6144]{1,0:T(8,128)(2,1)S(1)}, bf16[32,6144]{1,0:T(8,128)(2,1)S(1)}, u32[]{:S(2)}, u32[]{:S(2)}) %collective-permute-start.12) | collective-permute-done | bytes 393248 | tf_op jit(solution)/shard_map/reduce2_tnear/ppermute | solution.py:48
  49.3 0.1 merge.3
  49.4 1.5 %collective-permute-start.14 = (bf16[32,6144]{1,0:T(8,128)(2,1)S(1)}, bf16[32,6144]{1,0:T(8,128)(2,1)S(1)}, u32[]{:S(2)}, u32[]{:S(2)}) collective-permute-start(bf16[32,6144]{1,0:T(8,128)(2,1)S(1)} %merge.3), channel_id=1, source_target_pairs={{0,192},{8,56},{16,208},{24,40},{32,224},{40,24},{48,240},{56,8},{... | collective-permute-start | bytes 1179656 | tf_op jit(solution)/shard_map/reduce_twrap/ppermute | solution.py:48
  50.9 2.6 %collective-permute-done.11.refs_0_.direct = bf16[32,6144]{1,0:T(8,128)(2,1)S(1)} collective-permute-done((bf16[32,6144]{1,0:T(8,128)(2,1)S(1)}, bf16[32,6144]{1,0:T(8,128)(2,1)S(1)}, u32[]{:S(2)}, u32[]{:S(2)}) %collective-permute-start.11) | collective-permute-done | bytes 393248 | tf_op jit(solution)/shard_map/reduce_tnear/ppermute | solution.py:48
  53.5 2.1 %collective-permute-done.15.direct = bf16[32,6144]{1,0:T(8,128)(2,1)S(1)} collective-permute-done((bf16[32,6144]{1,0:T(8,128)(2,1)S(1)}, bf16[32,6144]{1,0:T(8,128)(2,1)S(1)}, u32[]{:S(2)}, u32[]{:S(2)}) %collective-permute-start.15) | collective-permute-done | bytes 393248 | tf_op jit(solution)/shard_map/reduce_twrap/ppermute | solution.py:48
  55.6 2.1 %collective-permute-done.16.back = bf16[32,6144]{1,0:T(8,128)(2,1)S(1)} collective-permute-done((bf16[32,6144]{1,0:T(8,128)(2,1)S(1)}, bf16[32,6144]{1,0:T(8,128)(2,1)S(1)}, u32[]{:S(2)}, u32[]{:S(2)}) %collective-permute-start.16) | collective-permute-done | bytes 393248 | tf_op jit(solution)/shard_map/reduce_tnear/ppermute | solution.py:48
  57.7 0.1 finish.2
  57.9 1.9 %collective-permute-start.17 = (bf16[16,6144]{1,0:T(8,128)(2,1)S(1)}, bf16[16,6144]{1,0:T(8,128)(2,1)S(1)}, u32[]{:S(2)}, u32[]{:S(2)}) collective-permute-start(bf16[16,6144]{1,0:T(8,128)(2,1)S(1)} %get-tuple-element.37.refs_0_), channel_id=1, source_target_pairs={{0,48},{8,200},{16,32},{24,216},{32,16},{40,232},{48,0},{56,248},{... | collective-permute-start | bytes 589832 | tf_op jit(solution)/shard_map/home_swrap/ppermute | solution.py:48
  59.8 0.8 %collective-permute-start.18 = (bf16[16,6144]{1,0:T(8,128)(2,1)S(1)}, bf16[16,6144]{1,0:T(8,128)(2,1)S(1)}, u32[]{:S(2)}, u32[]{:S(2)}) collective-permute-start(bf16[16,6144]{1,0:T(8,128)(2,1)S(1)} %get-tuple-element.39), channel_id=1, source_target_pairs={{0,32},{8,136},{16,48},{24,152},{32,0},{40,168},{48,16},{56,184},{... | collective-permute-start | bytes 589832 | tf_op jit(solution)/shard_map/home_sfar/ppermute | solution.py:48
  60.6 0.7 collective-permute-done.14.back
  61.3 0.1 finish.3
  61.4 0.8 %collective-permute-start.19 = (bf16[16,6144]{1,0:T(8,128)(2,1)S(1)}, bf16[16,6144]{1,0:T(8,128)(2,1)S(1)}, u32[]{:S(2)}, u32[]{:S(2)}) collective-permute-start(bf16[16,6144]{1,0:T(8,128)(2,1)S(1)} %get-tuple-element.40), channel_id=1, source_target_pairs={{0,16},{8,72},{16,0},{24,88},{32,48},{40,104},{48,32},{56,120},{64... | collective-permute-start | bytes 589832 | tf_op jit(solution)/shard_map/home_snear/ppermute | solution.py:48
  62.9 2.2 %collective-permute-done.17.refs_2_ = bf16[16,6144]{1,0:T(8,128)(2,1)S(1)} collective-permute-done((bf16[16,6144]{1,0:T(8,128)(2,1)S(1)}, bf16[16,6144]{1,0:T(8,128)(2,1)S(1)}, u32[]{:S(2)}, u32[]{:S(2)}) %collective-permute-start.17) | collective-permute-done | bytes 196640 | tf_op jit(solution)/shard_map/home_swrap/ppermute | solution.py:48
  65.1 1.8 %collective-permute-done.18.refs_3_ = bf16[16,6144]{1,0:T(8,128)(2,1)S(1)} collective-permute-done((bf16[16,6144]{1,0:T(8,128)(2,1)S(1)}, bf16[16,6144]{1,0:T(8,128)(2,1)S(1)}, u32[]{:S(2)}, u32[]{:S(2)}) %collective-permute-start.18) | collective-permute-done | bytes 196640 | tf_op jit(solution)/shard_map/home_sfar/ppermute | solution.py:48
  66.9 0.1 collect.1
  67.0 0.8 %collective-permute-done.19 = bf16[16,6144]{1,0:T(8,128)(2,1)S(1)} collective-permute-done((bf16[16,6144]{1,0:T(8,128)(2,1)S(1)}, bf16[16,6144]{1,0:T(8,128)(2,1)S(1)}, u32[]{:S(2)}, u32[]{:S(2)}) %collective-permute-start.19) | collective-permute-done | bytes 196640 | tf_op jit(solution)/shard_map/home_snear/ppermute | solution.py:48
  67.8 0.8 %select_convert_fusion = bf16[16,6144]{1,0:T(8,128)(2,1)} fusion(f32[16,6144]{1,0:T(8,128)S(1)} %collect.1, bf16[16,6144]{1,0:T(8,128)(2,1)S(1)} %collective-permute-done.19, pred[16]{0:T(512)(128)(4,1)S(1)} %iota_compare_fusion), kind=kLoop, calls=%fused_computation | loop fusion | flops 393216 | bytes 786448 | tf_op jit(solution)/shard_map/convert_element_type | solution.py:344
  (5 shorter events, 0.0 us)
Async XLA Ops:
  0.0 14.2 %collective-permute-start.3 = (bf16[448,6144]{1,0:T(8,128)(2,1)}, bf16[448,6144]{1,0:T(8,128)(2,1)S(1)}, u32[]{:S(2)}, u32[]{:S(2)}) collective-permute-start(bf16[448,6144]{1,0:T(8,128)(2,1)} %bitcast.4), channel_id=1, source_target_pairs={{0,8},{8,0},{16,24},{24,16},{32,40},{40,32},{48,56},{56,48},{64,72... | collective-permute-start | bytes 16515080 | tf_op jit(solution)/shard_map/up_core/ppermute | solution.py:48
  3.4 5.8 %collective-permute-start = (bf16[16,6144]{1,0:T(8,128)(2,1)S(1)}, bf16[16,6144]{1,0:T(8,128)(2,1)S(1)}, u32[]{:S(2)}, u32[]{:S(2)}) collective-permute-start(bf16[16,6144]{1,0:T(8,128)(2,1)S(1)} %get-tuple-element.24.own), channel_id=1, source_target_pairs={{0,16},{8,72},{16,0},{24,88},{32,48},{40,104},{48,32},{56,120},{64... | collective-permute-start | bytes 589832 | tf_op jit(solution)/shard_map/gather_snear/ppermute | solution.py:48
  4.9 7.4 %collective-permute-start.1 = (bf16[16,6144]{1,0:T(8,128)(2,1)S(1)}, bf16[16,6144]{1,0:T(8,128)(2,1)S(1)}, u32[]{:S(2)}, u32[]{:S(2)}) collective-permute-start(bf16[16,6144]{1,0:T(8,128)(2,1)S(1)} %get-tuple-element.24.own), channel_id=1, source_target_pairs={{0,48},{8,200},{16,32},{24,216},{32,16},{40,232},{48,0},{56,248},{... | collective-permute-start | bytes 589832 | tf_op jit(solution)/shard_map/gather_swrap/ppermute | solution.py:48
  7.0 7.2 %collective-permute-start.2 = (bf16[16,6144]{1,0:T(8,128)(2,1)S(1)}, bf16[16,6144]{1,0:T(8,128)(2,1)S(1)}, u32[]{:S(2)}, u32[]{:S(2)}) collective-permute-start(bf16[16,6144]{1,0:T(8,128)(2,1)S(1)} %get-tuple-element.24.own), channel_id=1, source_target_pairs={{0,32},{8,136},{16,48},{24,152},{32,0},{40,168},{48,16},{56,184},{... | collective-permute-start | bytes 589832 | tf_op jit(solution)/shard_map/gather_sfar/ppermute | solution.py:48
  14.3 22.8 %collective-permute-start.10 = (bf16[448,6144]{1,0:T(8,128)(2,1)S(1)}, bf16[448,6144]{1,0:T(8,128)(2,1)S(1)}, u32[]{:S(2)}, u32[]{:S(2)}) collective-permute-start(bf16[448,6144]{1,0:T(8,128)(2,1)S(1)} %get-tuple-element.28.one), channel_id=1, source_target_pairs={{0,8},{8,0},{16,24},{24,16},{32,40},{40,32},{48,56},{56,48},{64,72... | collective-permute-start | bytes 16515080 | tf_op jit(solution)/shard_map/down_core/ppermute | solution.py:48
  14.4 7.9 %collective-permute-start.4 = (bf16[32,6144]{1,0:T(8,128)(2,1)S(1)}, bf16[32,6144]{1,0:T(8,128)(2,1)S(1)}, u32[]{:S(2)}, u32[]{:S(2)}) collective-permute-start(bf16[32,6144]{1,0:T(8,128)(2,1)S(1)} %get-tuple-element.26.args_0_), channel_id=1, source_target_pairs={{0,64},{8,24},{16,80},{24,8},{32,96},{40,56},{48,112},{56,40},{64,... | collective-permute-start | bytes 1179656 | tf_op jit(solution)/shard_map/gather_tnear/ppermute | solution.py:48
  16.0 9.2 %collective-permute-start.5 = (bf16[32,6144]{1,0:T(8,128)(2,1)S(1)}, bf16[32,6144]{1,0:T(8,128)(2,1)S(1)}, u32[]{:S(2)}, u32[]{:S(2)}) collective-permute-start(bf16[32,6144]{1,0:T(8,128)(2,1)S(1)} %get-tuple-element.27.after.args_1_), channel_id=1, source_target_pairs={{0,192},{8,56},{16,208},{24,40},{32,224},{40,24},{48,240},{56,8},{... | collective-permute-start | bytes 1179656 | tf_op jit(solution)/shard_map/gather_twrap/ppermute | solution.py:48
  18.2 11.0 %collective-permute-start.6 = (bf16[32,6144]{1,0:T(8,128)(2,1)S(1)}, bf16[32,6144]{1,0:T(8,128)(2,1)S(1)}, u32[]{:S(2)}, u32[]{:S(2)}) collective-permute-start(bf16[32,6144]{1,0:T(8,128)(2,1)S(1)} %get-tuple-element.26.args_0_), channel_id=1, source_target_pairs={{0,192},{8,56},{16,208},{24,40},{32,224},{40,24},{48,240},{56,8},{... | collective-permute-start | bytes 1179656 | tf_op jit(solution)/shard_map/gather_twrap/ppermute | solution.py:48
  19.3 10.0 %collective-permute-start.7 = (bf16[32,6144]{1,0:T(8,128)(2,1)S(1)}, bf16[32,6144]{1,0:T(8,128)(2,1)S(1)}, u32[]{:S(2)}, u32[]{:S(2)}) collective-permute-start(bf16[32,6144]{1,0:T(8,128)(2,1)S(1)} %get-tuple-element.27.after.args_1_), channel_id=1, source_target_pairs={{0,64},{8,24},{16,80},{24,8},{32,96},{40,56},{48,112},{56,40},{64,... | collective-permute-start | bytes 1179656 | tf_op jit(solution)/shard_map/gather_tnear/ppermute | solution.py:48
  22.2 11.2 %collective-permute-start.8 = (bf16[32,6144]{1,0:T(8,128)(2,1)S(1)}, bf16[32,6144]{1,0:T(8,128)(2,1)S(1)}, u32[]{:S(2)}, u32[]{:S(2)}) collective-permute-start(bf16[32,6144]{1,0:T(8,128)(2,1)S(1)} %collective-permute-done.4.args_2_), channel_id=1, source_target_pairs={{0,192},{8,56},{16,208},{24,40},{32,224},{40,24},{48,240},{56,8},{... | collective-permute-start | bytes 1179656 | tf_op jit(solution)/shard_map/gather2_twrap/ppermute | solution.py:48
  25.2 8.2 %collective-permute-start.9 = (bf16[32,6144]{1,0:T(8,128)(2,1)S(1)}, bf16[32,6144]{1,0:T(8,128)(2,1)S(1)}, u32[]{:S(2)}, u32[]{:S(2)}) collective-permute-start(bf16[32,6144]{1,0:T(8,128)(2,1)S(1)} %collective-permute-done.5.args_3_), channel_id=1, source_target_pairs={{0,64},{8,24},{16,80},{24,8},{32,96},{40,56},{48,112},{56,40},{64,... | collective-permute-start | bytes 1179656 | tf_op jit(solution)/shard_map/gather2_tnear/ppermute | solution.py:48
  39.2 9.1 %collective-permute-start.13 = (bf16[32,6144]{1,0:T(8,128)(2,1)S(1)}, bf16[32,6144]{1,0:T(8,128)(2,1)S(1)}, u32[]{:S(2)}, u32[]{:S(2)}) collective-permute-start(bf16[32,6144]{1,0:T(8,128)(2,1)S(1)} %get-tuple-element.34), channel_id=1, source_target_pairs={{0,192},{8,56},{16,208},{24,40},{32,224},{40,24},{48,240},{56,8},{... | collective-permute-start | bytes 1179656 | tf_op jit(solution)/shard_map/reduce2_twrap/ppermute | solution.py:48
  41.5 7.8 %collective-permute-start.12 = (bf16[32,6144]{1,0:T(8,128)(2,1)S(1)}, bf16[32,6144]{1,0:T(8,128)(2,1)S(1)}, u32[]{:S(2)}, u32[]{:S(2)}) collective-permute-start(bf16[32,6144]{1,0:T(8,128)(2,1)S(1)} %get-tuple-element.32), channel_id=1, source_target_pairs={{0,64},{8,24},{16,80},{24,8},{32,96},{40,56},{48,112},{56,40},{64,... | collective-permute-start | bytes 1179656 | tf_op jit(solution)/shard_map/reduce2_tnear/ppermute | solution.py:48
  44.3 9.2 %collective-permute-start.11 = (bf16[32,6144]{1,0:T(8,128)(2,1)S(1)}, bf16[32,6144]{1,0:T(8,128)(2,1)S(1)}, u32[]{:S(2)}, u32[]{:S(2)}) collective-permute-start(bf16[32,6144]{1,0:T(8,128)(2,1)S(1)} %get-tuple-element.30), channel_id=1, source_target_pairs={{0,64},{8,24},{16,80},{24,8},{32,96},{40,56},{48,112},{56,40},{64,... | collective-permute-start | bytes 1179656 | tf_op jit(solution)/shard_map/reduce_tnear/ppermute | solution.py:48
  46.6 9.0 %collective-permute-start.15 = (bf16[32,6144]{1,0:T(8,128)(2,1)S(1)}, bf16[32,6144]{1,0:T(8,128)(2,1)S(1)}, u32[]{:S(2)}, u32[]{:S(2)}) collective-permute-start(bf16[32,6144]{1,0:T(8,128)(2,1)S(1)} %get-tuple-element.36), channel_id=1, source_target_pairs={{0,192},{8,56},{16,208},{24,40},{32,224},{40,24},{48,240},{56,8},{... | collective-permute-start | bytes 1179656 | tf_op jit(solution)/shard_map/reduce_twrap/ppermute | solution.py:48
  48.4 9.3 %collective-permute-start.16 = (bf16[32,6144]{1,0:T(8,128)(2,1)S(1)}, bf16[32,6144]{1,0:T(8,128)(2,1)S(1)}, u32[]{:S(2)}, u32[]{:S(2)}) collective-permute-start(bf16[32,6144]{1,0:T(8,128)(2,1)S(1)} %merge.2.refs_0_), channel_id=1, source_target_pairs={{0,64},{8,24},{16,80},{24,8},{32,96},{40,56},{48,112},{56,40},{64,... | collective-permute-start | bytes 1179656 | tf_op jit(solution)/shard_map/reduce_tnear/ppermute | solution.py:48
  49.4 11.9 %collective-permute-start.14 = (bf16[32,6144]{1,0:T(8,128)(2,1)S(1)}, bf16[32,6144]{1,0:T(8,128)(2,1)S(1)}, u32[]{:S(2)}, u32[]{:S(2)}) collective-permute-start(bf16[32,6144]{1,0:T(8,128)(2,1)S(1)} %merge.3), channel_id=1, source_target_pairs={{0,192},{8,56},{16,208},{24,40},{32,224},{40,24},{48,240},{56,8},{... | collective-permute-start | bytes 1179656 | tf_op jit(solution)/shard_map/reduce_twrap/ppermute | solution.py:48
  57.9 7.2 %collective-permute-start.17 = (bf16[16,6144]{1,0:T(8,128)(2,1)S(1)}, bf16[16,6144]{1,0:T(8,128)(2,1)S(1)}, u32[]{:S(2)}, u32[]{:S(2)}) collective-permute-start(bf16[16,6144]{1,0:T(8,128)(2,1)S(1)} %get-tuple-element.37.refs_0_), channel_id=1, source_target_pairs={{0,48},{8,200},{16,32},{24,216},{32,16},{40,232},{48,0},{56,248},{... | collective-permute-start | bytes 589832 | tf_op jit(solution)/shard_map/home_swrap/ppermute | solution.py:48
  59.8 7.2 %collective-permute-start.18 = (bf16[16,6144]{1,0:T(8,128)(2,1)S(1)}, bf16[16,6144]{1,0:T(8,128)(2,1)S(1)}, u32[]{:S(2)}, u32[]{:S(2)}) collective-permute-start(bf16[16,6144]{1,0:T(8,128)(2,1)S(1)} %get-tuple-element.39), channel_id=1, source_target_pairs={{0,32},{8,136},{16,48},{24,152},{32,0},{40,168},{48,16},{56,184},{... | collective-permute-start | bytes 589832 | tf_op jit(solution)/shard_map/home_sfar/ppermute | solution.py:48
  61.4 6.4 %collective-permute-start.19 = (bf16[16,6144]{1,0:T(8,128)(2,1)S(1)}, bf16[16,6144]{1,0:T(8,128)(2,1)S(1)}, u32[]{:S(2)}, u32[]{:S(2)}) collective-permute-start(bf16[16,6144]{1,0:T(8,128)(2,1)S(1)} %get-tuple-element.40), channel_id=1, source_target_pairs={{0,16},{8,72},{16,0},{24,88},{32,48},{40,104},{48,32},{56,120},{64... | collective-permute-start | bytes 589832 | tf_op jit(solution)/shard_map/home_snear/ppermute | solution.py:48

commit v10 on v9

--- a/solution.py
+++ b/solution.py
@@ -160,7 +160,7 @@
         out_specs=pl.BlockSpec(memory_space=pltpu.VMEM),
         scratch_shapes=[pltpu.SemaphoreType.DMA],
         compiler_params=pltpu.CompilerParams(vmem_limit_bytes=16 * 2**20),
-        cost_estimate=pl.CostEstimate(flops=0, bytes_accessed=4 * HIDDEN * D, transcendentals=0),
+        cost_estimate=pl.CostEstimate(flops=10**11, bytes_accessed=4 * HIDDEN * D, transcendentals=0),
         name="fetch",
     )(in_hbm(weights), after)
 
@@ -229,25 +229,38 @@
     )(hidden, *down)
 
 
-def pack_kernel(own, near, wrap, far, held, after, early, late, handed):
-    early[:SLOTS] = own[...]
-    early[SLOTS:] = near[...]
-    late[:SLOTS] = wrap[...]
-    late[SLOTS:] = far[...]
-
-
-def pack(own, near, wrap, far, held, after):
-    vmem = pl.BlockSpec(memory_space=pltpu.VMEM)
-    block = jax.ShapeDtypeStruct((PAIR, D), jnp.bfloat16)
+def pack_kernel(one, two, block):
+    block[:SLOTS] = one[...]
+    block[SLOTS:] = two[...]
+
+
+def pack(one, two):
+    vmem = pl.BlockSpec(memory_space=pltpu.VMEM)
     return pl.pallas_call(
         pack_kernel,
-        out_shape=[block, block, jax.ShapeDtypeStruct(held.shape, held.dtype)],
-        in_specs=[vmem] * 5 + [pl.BlockSpec(memory_space=pl.ANY)],
-        out_specs=[vmem] * 3,
-        input_output_aliases={4: 2},
+        out_shape=jax.ShapeDtypeStruct((PAIR, D), jnp.bfloat16),
+        in_specs=[vmem] * 2,
+        out_specs=vmem,
         compiler_params=pltpu.CompilerParams(vmem_limit_bytes=16 * 2**20),
         name="pack",
-    )(own, near, wrap, far, held, after)
+    )(one, two)
+
+
+def hand_kernel(*refs):
+    pass
+
+
+def hand(held, *after):
+    vmem = pl.BlockSpec(memory_space=pltpu.VMEM)
+    return pl.pallas_call(
+        hand_kernel,
+        out_shape=jax.ShapeDtypeStruct(held.shape, held.dtype),
+        in_specs=[vmem] + [pl.BlockSpec(memory_space=pl.ANY)] * len(after),
+        out_specs=vmem,
+        input_output_aliases={0: 0},
+        compiler_params=pltpu.CompilerParams(vmem_limit_bytes=16 * 2**20),
+        name="hand",
+    )(held, *after)
 
 
 def merge_kernel(n, mine, arrived, *refs):
@@ -315,11 +328,14 @@
         queries, cache_keys, cache_values, lengths, norm_gain, down_weight
     )
     by_wrap, by_far, by_near = [send(normed, r, "gather") for r in ("swrap", "sfar", "snear")]
-    early, late, down_held = pack(normed, by_near, by_wrap, by_far, down_held, up_other)
-    down_other = send(down_held, "core", "down")
+    early = pack(normed, by_near)
+    late = pack(by_wrap, by_far)
     early_n, late_w = send(early, "tnear", "gather"), send(late, "twrap", "gather")
     late_n, early_w = send(late, "tnear", "gather"), send(early, "twrap", "gather")
+    early_n = hand(early_n, early_w)
     early_f, late_f = send(early_n, "twrap", "gather2"), send(late_w, "tnear", "gather2")
+    down_held = hand(down_held, up_other)
+    down_other = send(down_held, "core", "down")
     up_held = fetch(up_own, late)
     hidden = project_up(
         [early, late, early_n, late_w, early_w, late_n, early_f, late_f], (up_held, up_other)

time: 69.3 us -> 69.4 us (level)
  transfers between devices with their start and end apart: 20 -> 20, of which waited for: 15 -> 16; matrix products, arithmetic and copies ran while one was open for 0% -> 0% of each run, Pallas kernels for 19% -> 19%
where the time goes in v10:
time: 69.4 us; the launch traced here: 69.3 us
  waiting for transfers between devices  28.9 us (42%)
  starting transfers between devices  23.8 us (34%)
  Pallas kernels  15.1 us (22%)
  other arithmetic  0.77 us (1%)
  between operations  0.77 us (1%)
    ppermute x20, waiting for transfers between devices, send(): return lax.ppermute(value, 'dp', ROUTES[route])  28.9 us
    ppermute x20, starting transfers between devices, send(): return lax.ppermute(value, 'dp', ROUTES[route])  23.8 us
    pallas_call x2, Pallas kernels, project_down(): pl.pallas_call(functools.partial(down_kernel, begin), out_shape=[jax.Shap...  4.98 us
    pallas_call x1, Pallas kernels, project_up(): pl.pallas_call(up_kernel, out_shape=jax.ShapeDtypeStruct((rows, 2 * HIDDE...  3.58 us
    pallas_call x1, Pallas kernels, attend(): pl.pallas_call(attend_kernel, out_shape=(jax.ShapeDtypeStruct((SLOTS, D),...  3.34 us
    pallas_call x1, Pallas kernels, fetch(): pl.pallas_call(fetch_kernel, out_shape=jax.ShapeDtypeStruct((HIDDEN, D),...  2.57 us
  transfers between devices with their start and end apart: 20, of which 16 were waited for; matrix products, arithmetic and copies ran while one was open for 0% of the time, Pallas kernels for 19%

profile of v10, /device:TPU:128, one launch (start us, length us, event | category | flops | bytes accessed | tf_op | source)
XLA Modules:
  0.0 69.3 jit_solution(8584017465264125581)
XLA Ops:
  0.0 0.0 collective-permute-start.9
  0.0 3.3 %attend.1 = (bf16[16,6144]{1,0:T(8,128)(2,1)S(1)}, bf16[16,6144]{1,0:T(8,128)(2,1)S(1)}, bf16[448,6144]{1,0:T(8,128)(2,1)S(1)}) custom-call(s32[16]{0:T(128)} %lengths_in.1, bf16[16,6144]{1,0:T(8,128)(2,1)} %q_in.1, bf16[1024,512]{1,0:T(8,128)(2,1)} %k_in.1, bf16[1024,512]{1,0:T(8,128)(2,1)} %v_in.1, f32[1,6144]{1,0:T(1,128)} %bitcast.4, bf16[448,6144]{1,0:T(8,128)(2,1)} %down.3), custom_call_target="tpu_custom_call" | custom-call | tf_op jit(solution)/shard_map/attend/pallas_call | solution.py:126
  3.4 1.6 %collective-permute-start = (bf16[16,6144]{1,0:T(8,128)(2,1)S(1)}, bf16[16,6144]{1,0:T(8,128)(2,1)S(1)}, u32[]{:S(2)}, u32[]{:S(2)}) collective-permute-start(bf16[16,6144]{1,0:T(8,128)(2,1)S(1)} %get-tuple-element.21.one), channel_id=1, source_target_pairs={{0,16},{8,72},{16,0},{24,88},{32,48},{40,104},{48,32},{56,120},{64... | collective-permute-start | bytes 589832 | tf_op jit(solution)/shard_map/gather_snear/ppermute | solution.py:48
  4.9 2.1 %collective-permute-start.1 = (bf16[16,6144]{1,0:T(8,128)(2,1)S(1)}, bf16[16,6144]{1,0:T(8,128)(2,1)S(1)}, u32[]{:S(2)}, u32[]{:S(2)}) collective-permute-start(bf16[16,6144]{1,0:T(8,128)(2,1)S(1)} %get-tuple-element.21.one), channel_id=1, source_target_pairs={{0,48},{8,200},{16,32},{24,216},{32,16},{40,232},{48,0},{56,248},{... | collective-permute-start | bytes 589832 | tf_op jit(solution)/shard_map/gather_swrap/ppermute | solution.py:48
  7.0 0.6 collective-permute-start.2
  7.7 1.4 %collective-permute-done.two = bf16[16,6144]{1,0:T(8,128)(2,1)S(1)} collective-permute-done((bf16[16,6144]{1,0:T(8,128)(2,1)S(1)}, bf16[16,6144]{1,0:T(8,128)(2,1)S(1)}, u32[]{:S(2)}, u32[]{:S(2)}) %collective-permute-start) | collective-permute-done | bytes 196640 | tf_op jit(solution)/shard_map/gather_snear/ppermute | solution.py:48
  9.1 3.1 %collective-permute-start.4 = (bf16[32,6144]{1,0:T(8,128)(2,1)S(1)}, bf16[32,6144]{1,0:T(8,128)(2,1)S(1)}, u32[]{:S(2)}, u32[]{:S(2)}) collective-permute-start(bf16[32,6144]{1,0:T(8,128)(2,1)S(1)} %pack.2.args_0_), channel_id=1, source_target_pairs={{0,192},{8,56},{16,208},{24,40},{32,224},{40,24},{48,240},{56,8},{... | collective-permute-start | bytes 1179656 | tf_op jit(solution)/shard_map/gather_twrap/ppermute | solution.py:48
  12.2 0.1 collective-permute-start.3
  12.4 0.3 collective-permute-done.1.one
  12.7 1.8 %collective-permute-done.2.two = bf16[16,6144]{1,0:T(8,128)(2,1)S(1)} collective-permute-done((bf16[16,6144]{1,0:T(8,128)(2,1)S(1)}, bf16[16,6144]{1,0:T(8,128)(2,1)S(1)}, u32[]{:S(2)}, u32[]{:S(2)}) %collective-permute-start.2) | collective-permute-done | bytes 196640 | tf_op jit(solution)/shard_map/gather_sfar/ppermute | solution.py:48
  14.5 3.1 %collective-permute-start.5 = (bf16[32,6144]{1,0:T(8,128)(2,1)S(1)}, bf16[32,6144]{1,0:T(8,128)(2,1)S(1)}, u32[]{:S(2)}, u32[]{:S(2)}) collective-permute-start(bf16[32,6144]{1,0:T(8,128)(2,1)S(1)} %pack.3.after.args_1_), channel_id=1, source_target_pairs={{0,192},{8,56},{16,208},{24,40},{32,224},{40,24},{48,240},{56,8},{... | collective-permute-start | bytes 1179656 | tf_op jit(solution)/shard_map/gather_twrap/ppermute | solution.py:48
  17.6 0.1 collective-permute-start.6
  17.7 0.5 collective-permute-done.4.refs_1_.args_4_
  18.2 1.8 %collective-permute-done.3.refs_0_ = bf16[32,6144]{1,0:T(8,128)(2,1)S(1)} collective-permute-done((bf16[32,6144]{1,0:T(8,128)(2,1)S(1)}, bf16[32,6144]{1,0:T(8,128)(2,1)S(1)}, u32[]{:S(2)}, u32[]{:S(2)}) %collective-permute-start.3) | collective-permute-done | bytes 393248 | tf_op jit(solution)/shard_map/gather_tnear/ppermute | solution.py:48
  20.0 1.2 %collective-permute-start.7 = (bf16[32,6144]{1,0:T(8,128)(2,1)S(1)}, bf16[32,6144]{1,0:T(8,128)(2,1)S(1)}, u32[]{:S(2)}, u32[]{:S(2)}) collective-permute-start(bf16[32,6144]{1,0:T(8,128)(2,1)S(1)} %hand.2.args_2_), channel_id=1, source_target_pairs={{0,192},{8,56},{16,208},{24,40},{32,224},{40,24},{48,240},{56,8},{... | collective-permute-start | bytes 1179656 | tf_op jit(solution)/shard_map/gather2_twrap/ppermute | solution.py:48
  21.2 2.3 %collective-permute-done.5.args_3_ = bf16[32,6144]{1,0:T(8,128)(2,1)S(1)} collective-permute-done((bf16[32,6144]{1,0:T(8,128)(2,1)S(1)}, bf16[32,6144]{1,0:T(8,128)(2,1)S(1)}, u32[]{:S(2)}, u32[]{:S(2)}) %collective-permute-start.5) | collective-permute-done | bytes 393248 | tf_op jit(solution)/shard_map/gather_twrap/ppermute | solution.py:48
  23.6 0.4 collective-permute-start.8
  23.9 0.0 collective-permute-start.10
  24.0 2.6 %fetch.1.args_8_ = bf16[448,6144]{1,0:T(8,128)(2,1)S(1)} custom-call(bf16[448,6144]{1,0:T(8,128)(2,1)} %bitcast.6, bf16[32,6144]{1,0:T(8,128)(2,1)S(1)} %pack.3.after.args_1_), custom_call_target="tpu_custom_call" | custom-call | flops 99999997952 | bytes 11010048 | tf_op jit(solution)/shard_map/fetch/pallas_call | solution.py:156
  26.5 0.0 collective-permute-done.6.args_5_
  26.5 2.5 %collective-permute-done.7.args_6_ = bf16[32,6144]{1,0:T(8,128)(2,1)S(1)} collective-permute-done((bf16[32,6144]{1,0:T(8,128)(2,1)S(1)}, bf16[32,6144]{1,0:T(8,128)(2,1)S(1)}, u32[]{:S(2)}, u32[]{:S(2)}) %collective-permute-start.7) | collective-permute-done | bytes 393248 | tf_op jit(solution)/shard_map/gather2_twrap/ppermute | solution.py:48
  29.0 2.3 %collective-permute-done.8.args_7_ = bf16[32,6144]{1,0:T(8,128)(2,1)S(1)} collective-permute-done((bf16[32,6144]{1,0:T(8,128)(2,1)S(1)}, bf16[32,6144]{1,0:T(8,128)(2,1)S(1)}, u32[]{:S(2)}, u32[]{:S(2)}) %collective-permute-start.8) | collective-permute-done | bytes 393248 | tf_op jit(solution)/shard_map/gather2_tnear/ppermute | solution.py:48
  31.4 3.6 %up.1.hidden = bf16[256,896]{1,0:T(8,128)(2,1)S(1)} custom-call(bf16[32,6144]{1,0:T(8,128)(2,1)S(1)} %pack.2.args_0_, bf16[32,6144]{1,0:T(8,128)(2,1)S(1)} %pack.3.after.args_1_, bf16[32,6144]{1,0:T(8,128)(2,1)S(1)} %hand.2.args_2_, bf16[32,6144]{1,0:T(8,128)(2,1)S(1)} %collective-permute-done.5.args_3_, ...), custom_call_target="tpu_custom_call" | custom-call | flops 2818572288 | bytes 3145728 | tf_op jit(solution)/shard_map/up/pallas_call | solution.py:189
  35.0 2.2 %down.5 = (bf16[32,6144]{1,0:T(8,128)(2,1)S(1)}, bf16[32,6144]{1,0:T(8,128)(2,1)S(1)}) custom-call(bf16[256,896]{1,0:T(8,128)(2,1)S(1)} %up.1.hidden, bf16[448,6144]{1,0:T(8,128)(2,1)S(1)} %hand.3.one, bf16[448,6144]{1,0:T(8,128)(2,1)S(1)} %collective-permute-done.10.two), custom_call_target="tpu_custom_call" | custom-call | flops 704643072 | bytes 786432 | tf_op jit(solution)/shard_map/down/pallas_call | solution.py:219
  37.1 3.1 %collective-permute-start.13 = (bf16[32,6144]{1,0:T(8,128)(2,1)S(1)}, bf16[32,6144]{1,0:T(8,128)(2,1)S(1)}, u32[]{:S(2)}, u32[]{:S(2)}) collective-permute-start(bf16[32,6144]{1,0:T(8,128)(2,1)S(1)} %get-tuple-element.28), channel_id=1, source_target_pairs={{0,192},{8,56},{16,208},{24,40},{32,224},{40,24},{48,240},{56,8},{... | collective-permute-start | bytes 1179656 | tf_op jit(solution)/shard_map/reduce2_twrap/ppermute | solution.py:48
  40.2 2.8 %down.4 = (bf16[32,6144]{1,0:T(8,128)(2,1)S(1)}, bf16[32,6144]{1,0:T(8,128)(2,1)S(1)}, bf16[32,6144]{1,0:T(8,128)(2,1)S(1)}, bf16[32,6144]{1,0:T(8,128)(2,1)S(1)...) custom-call(bf16[256,896]{1,0:T(8,128)(2,1)S(1)} %up.1.hidden, bf16[448,6144]{1,0:T(8,128)(2,1)S(1)} %hand.3.one, ...), custom_call_target="tpu_custom_call" | custom-call | flops 2113929216 | bytes 2359296 | tf_op jit(solution)/shard_map/down/pallas_call | solution.py:219
  43.1 2.3 %collective-permute-start.11 = (bf16[32,6144]{1,0:T(8,128)(2,1)S(1)}, bf16[32,6144]{1,0:T(8,128)(2,1)S(1)}, u32[]{:S(2)}, u32[]{:S(2)}) collective-permute-start(bf16[32,6144]{1,0:T(8,128)(2,1)S(1)} %get-tuple-element.24), channel_id=1, source_target_pairs={{0,64},{8,24},{16,80},{24,8},{32,96},{40,56},{48,112},{56,40},{64,... | collective-permute-start | bytes 1179656 | tf_op jit(solution)/shard_map/reduce_tnear/ppermute | solution.py:48
  45.4 0.2 collective-permute-start.15
  45.6 0.6 collective-permute-done.13.arrived
  46.2 0.1 merge.2.refs_0_
  46.3 0.1 collective-permute-start.16
  46.4 1.6 %collective-permute-done.12.arrived = bf16[32,6144]{1,0:T(8,128)(2,1)S(1)} collective-permute-done((bf16[32,6144]{1,0:T(8,128)(2,1)S(1)}, bf16[32,6144]{1,0:T(8,128)(2,1)S(1)}, u32[]{:S(2)}, u32[]{:S(2)}) %collective-permute-start.12) | collective-permute-done | bytes 393248 | tf_op jit(solution)/shard_map/reduce2_tnear/ppermute | solution.py:48
  48.0 0.1 merge.3
  48.1 1.5 %collective-permute-start.14 = (bf16[32,6144]{1,0:T(8,128)(2,1)S(1)}, bf16[32,6144]{1,0:T(8,128)(2,1)S(1)}, u32[]{:S(2)}, u32[]{:S(2)}) collective-permute-start(bf16[32,6144]{1,0:T(8,128)(2,1)S(1)} %merge.3), channel_id=1, source_target_pairs={{0,192},{8,56},{16,208},{24,40},{32,224},{40,24},{48,240},{56,8},{... | collective-permute-start | bytes 1179656 | tf_op jit(solution)/shard_map/reduce_twrap/ppermute | solution.py:48
  49.6 2.6 %collective-permute-done.11.refs_0_.direct = bf16[32,6144]{1,0:T(8,128)(2,1)S(1)} collective-permute-done((bf16[32,6144]{1,0:T(8,128)(2,1)S(1)}, bf16[32,6144]{1,0:T(8,128)(2,1)S(1)}, u32[]{:S(2)}, u32[]{:S(2)}) %collective-permute-start.11) | collective-permute-done | bytes 393248 | tf_op jit(solution)/shard_map/reduce_tnear/ppermute | solution.py:48
  52.2 2.1 %collective-permute-done.15.direct = bf16[32,6144]{1,0:T(8,128)(2,1)S(1)} collective-permute-done((bf16[32,6144]{1,0:T(8,128)(2,1)S(1)}, bf16[32,6144]{1,0:T(8,128)(2,1)S(1)}, u32[]{:S(2)}, u32[]{:S(2)}) %collective-permute-start.15) | collective-permute-done | bytes 393248 | tf_op jit(solution)/shard_map/reduce_twrap/ppermute | solution.py:48
  54.3 2.1 %collective-permute-done.16.back = bf16[32,6144]{1,0:T(8,128)(2,1)S(1)} collective-permute-done((bf16[32,6144]{1,0:T(8,128)(2,1)S(1)}, bf16[32,6144]{1,0:T(8,128)(2,1)S(1)}, u32[]{:S(2)}, u32[]{:S(2)}) %collective-permute-start.16) | collective-permute-done | bytes 393248 | tf_op jit(solution)/shard_map/reduce_tnear/ppermute | solution.py:48
  56.5 0.1 finish.2
  56.6 2.1 %collective-permute-start.17 = (bf16[16,6144]{1,0:T(8,128)(2,1)S(1)}, bf16[16,6144]{1,0:T(8,128)(2,1)S(1)}, u32[]{:S(2)}, u32[]{:S(2)}) collective-permute-start(bf16[16,6144]{1,0:T(8,128)(2,1)S(1)} %get-tuple-element.31.refs_0_), channel_id=1, source_target_pairs={{0,48},{8,200},{16,32},{24,216},{32,16},{40,232},{48,0},{56,248},{... | collective-permute-start | bytes 589832 | tf_op jit(solution)/shard_map/home_swrap/ppermute | solution.py:48
  58.7 0.9 %collective-permute-start.18 = (bf16[16,6144]{1,0:T(8,128)(2,1)S(1)}, bf16[16,6144]{1,0:T(8,128)(2,1)S(1)}, u32[]{:S(2)}, u32[]{:S(2)}) collective-permute-start(bf16[16,6144]{1,0:T(8,128)(2,1)S(1)} %get-tuple-element.33), channel_id=1, source_target_pairs={{0,32},{8,136},{16,48},{24,152},{32,0},{40,168},{48,16},{56,184},{... | collective-permute-start | bytes 589832 | tf_op jit(solution)/shard_map/home_sfar/ppermute | solution.py:48
  59.7 3.0 %collective-permute-done.14.back = bf16[32,6144]{1,0:T(8,128)(2,1)S(1)} collective-permute-done((bf16[32,6144]{1,0:T(8,128)(2,1)S(1)}, bf16[32,6144]{1,0:T(8,128)(2,1)S(1)}, u32[]{:S(2)}, u32[]{:S(2)}) %collective-permute-start.14) | collective-permute-done | bytes 393248 | tf_op jit(solution)/shard_map/reduce_twrap/ppermute | solution.py:48
  62.6 0.1 finish.3
  62.8 1.1 %collective-permute-start.19 = (bf16[16,6144]{1,0:T(8,128)(2,1)S(1)}, bf16[16,6144]{1,0:T(8,128)(2,1)S(1)}, u32[]{:S(2)}, u32[]{:S(2)}) collective-permute-start(bf16[16,6144]{1,0:T(8,128)(2,1)S(1)} %get-tuple-element.34), channel_id=1, source_target_pairs={{0,16},{8,72},{16,0},{24,88},{32,48},{40,104},{48,32},{56,120},{64... | collective-permute-start | bytes 589832 | tf_op jit(solution)/shard_map/home_snear/ppermute | solution.py:48
  64.6 0.0 collective-permute-done.17.refs_2_
  64.6 1.3 %collective-permute-done.18.refs_3_ = bf16[16,6144]{1,0:T(8,128)(2,1)S(1)} collective-permute-done((bf16[16,6144]{1,0:T(8,128)(2,1)S(1)}, bf16[16,6144]{1,0:T(8,128)(2,1)S(1)}, u32[]{:S(2)}, u32[]{:S(2)}) %collective-permute-start.18) | collective-permute-done | bytes 196640 | tf_op jit(solution)/shard_map/home_sfar/ppermute | solution.py:48
  65.9 0.1 collect.1
  66.0 2.5 %collective-permute-done.19 = bf16[16,6144]{1,0:T(8,128)(2,1)S(1)} collective-permute-done((bf16[16,6144]{1,0:T(8,128)(2,1)S(1)}, bf16[16,6144]{1,0:T(8,128)(2,1)S(1)}, u32[]{:S(2)}, u32[]{:S(2)}) %collective-permute-start.19) | collective-permute-done | bytes 196640 | tf_op jit(solution)/shard_map/home_snear/ppermute | solution.py:48
  68.5 0.8 %select_convert_fusion = bf16[16,6144]{1,0:T(8,128)(2,1)} fusion(f32[16,6144]{1,0:T(8,128)S(1)} %collect.1, bf16[16,6144]{1,0:T(8,128)(2,1)S(1)} %collective-permute-done.19, pred[16]{0:T(512)(128)(4,1)S(1)} %iota_compare_fusion), kind=kLoop, calls=%fused_computation | loop fusion | flops 393216 | bytes 786448 | tf_op jit(solution)/shard_map/convert_element_type | solution.py:360
  (8 shorter events, 0.1 us)
Async XLA Ops:
  0.0 23.9 %collective-permute-start.9 = (bf16[448,6144]{1,0:T(8,128)(2,1)}, bf16[448,6144]{1,0:T(8,128)(2,1)S(1)}, u32[]{:S(2)}, u32[]{:S(2)}) collective-permute-start(bf16[448,6144]{1,0:T(8,128)(2,1)} %bitcast.5), channel_id=1, source_target_pairs={{0,8},{8,0},{16,24},{24,16},{32,40},{40,32},{48,56},{56,48},{64,72... | collective-permute-start | bytes 16515080 | tf_op jit(solution)/shard_map/up_core/ppermute | solution.py:48
  3.4 5.8 %collective-permute-start = (bf16[16,6144]{1,0:T(8,128)(2,1)S(1)}, bf16[16,6144]{1,0:T(8,128)(2,1)S(1)}, u32[]{:S(2)}, u32[]{:S(2)}) collective-permute-start(bf16[16,6144]{1,0:T(8,128)(2,1)S(1)} %get-tuple-element.21.one), channel_id=1, source_target_pairs={{0,16},{8,72},{16,0},{24,88},{32,48},{40,104},{48,32},{56,120},{64... | collective-permute-start | bytes 589832 | tf_op jit(solution)/shard_map/gather_snear/ppermute | solution.py:48
  4.9 7.7 %collective-permute-start.1 = (bf16[16,6144]{1,0:T(8,128)(2,1)S(1)}, bf16[16,6144]{1,0:T(8,128)(2,1)S(1)}, u32[]{:S(2)}, u32[]{:S(2)}) collective-permute-start(bf16[16,6144]{1,0:T(8,128)(2,1)S(1)} %get-tuple-element.21.one), channel_id=1, source_target_pairs={{0,48},{8,200},{16,32},{24,216},{32,16},{40,232},{48,0},{56,248},{... | collective-permute-start | bytes 589832 | tf_op jit(solution)/shard_map/gather_swrap/ppermute | solution.py:48
  7.0 7.4 %collective-permute-start.2 = (bf16[16,6144]{1,0:T(8,128)(2,1)S(1)}, bf16[16,6144]{1,0:T(8,128)(2,1)S(1)}, u32[]{:S(2)}, u32[]{:S(2)}) collective-permute-start(bf16[16,6144]{1,0:T(8,128)(2,1)S(1)} %get-tuple-element.21.one), channel_id=1, source_target_pairs={{0,32},{8,136},{16,48},{24,152},{32,0},{40,168},{48,16},{56,184},{... | collective-permute-start | bytes 589832 | tf_op jit(solution)/shard_map/gather_sfar/ppermute | solution.py:48
  9.1 9.1 %collective-permute-start.4 = (bf16[32,6144]{1,0:T(8,128)(2,1)S(1)}, bf16[32,6144]{1,0:T(8,128)(2,1)S(1)}, u32[]{:S(2)}, u32[]{:S(2)}) collective-permute-start(bf16[32,6144]{1,0:T(8,128)(2,1)S(1)} %pack.2.args_0_), channel_id=1, source_target_pairs={{0,192},{8,56},{16,208},{24,40},{32,224},{40,24},{48,240},{56,8},{... | collective-permute-start | bytes 1179656 | tf_op jit(solution)/shard_map/gather_twrap/ppermute | solution.py:48
  12.2 7.8 %collective-permute-start.3 = (bf16[32,6144]{1,0:T(8,128)(2,1)S(1)}, bf16[32,6144]{1,0:T(8,128)(2,1)S(1)}, u32[]{:S(2)}, u32[]{:S(2)}) collective-permute-start(bf16[32,6144]{1,0:T(8,128)(2,1)S(1)} %pack.2.args_0_), channel_id=1, source_target_pairs={{0,64},{8,24},{16,80},{24,8},{32,96},{40,56},{48,112},{56,40},{64,... | collective-permute-start | bytes 1179656 | tf_op jit(solution)/shard_map/gather_tnear/ppermute | solution.py:48
  14.5 9.1 %collective-permute-start.5 = (bf16[32,6144]{1,0:T(8,128)(2,1)S(1)}, bf16[32,6144]{1,0:T(8,128)(2,1)S(1)}, u32[]{:S(2)}, u32[]{:S(2)}) collective-permute-start(bf16[32,6144]{1,0:T(8,128)(2,1)S(1)} %pack.3.after.args_1_), channel_id=1, source_target_pairs={{0,192},{8,56},{16,208},{24,40},{32,224},{40,24},{48,240},{56,8},{... | collective-permute-start | bytes 1179656 | tf_op jit(solution)/shard_map/gather_twrap/ppermute | solution.py:48
  17.6 8.9 %collective-permute-start.6 = (bf16[32,6144]{1,0:T(8,128)(2,1)S(1)}, bf16[32,6144]{1,0:T(8,128)(2,1)S(1)}, u32[]{:S(2)}, u32[]{:S(2)}) collective-permute-start(bf16[32,6144]{1,0:T(8,128)(2,1)S(1)} %pack.3.after.args_1_), channel_id=1, source_target_pairs={{0,64},{8,24},{16,80},{24,8},{32,96},{40,56},{48,112},{56,40},{64,... | collective-permute-start | bytes 1179656 | tf_op jit(solution)/shard_map/gather_tnear/ppermute | solution.py:48
  20.0 9.0 %collective-permute-start.7 = (bf16[32,6144]{1,0:T(8,128)(2,1)S(1)}, bf16[32,6144]{1,0:T(8,128)(2,1)S(1)}, u32[]{:S(2)}, u32[]{:S(2)}) collective-permute-start(bf16[32,6144]{1,0:T(8,128)(2,1)S(1)} %hand.2.args_2_), channel_id=1, source_target_pairs={{0,192},{8,56},{16,208},{24,40},{32,224},{40,24},{48,240},{56,8},{... | collective-permute-start | bytes 1179656 | tf_op jit(solution)/shard_map/gather2_twrap/ppermute | solution.py:48
  23.6 7.8 %collective-permute-start.8 = (bf16[32,6144]{1,0:T(8,128)(2,1)S(1)}, bf16[32,6144]{1,0:T(8,128)(2,1)S(1)}, u32[]{:S(2)}, u32[]{:S(2)}) collective-permute-start(bf16[32,6144]{1,0:T(8,128)(2,1)S(1)} %collective-permute-done.5.args_3_), channel_id=1, source_target_pairs={{0,64},{8,24},{16,80},{24,8},{32,96},{40,56},{48,112},{56,40},{64,... | collective-permute-start | bytes 1179656 | tf_op jit(solution)/shard_map/gather2_tnear/ppermute | solution.py:48
  23.9 11.0 %collective-permute-start.10 = (bf16[448,6144]{1,0:T(8,128)(2,1)S(1)}, bf16[448,6144]{1,0:T(8,128)(2,1)S(1)}, u32[]{:S(2)}, u32[]{:S(2)}) collective-permute-start(bf16[448,6144]{1,0:T(8,128)(2,1)S(1)} %hand.3.one), channel_id=1, source_target_pairs={{0,8},{8,0},{16,24},{24,16},{32,40},{40,32},{48,56},{56,48},{64,72... | collective-permute-start | bytes 16515080 | tf_op jit(solution)/shard_map/down_core/ppermute | solution.py:48
  37.1 9.1 %collective-permute-start.13 = (bf16[32,6144]{1,0:T(8,128)(2,1)S(1)}, bf16[32,6144]{1,0:T(8,128)(2,1)S(1)}, u32[]{:S(2)}, u32[]{:S(2)}) collective-permute-start(bf16[32,6144]{1,0:T(8,128)(2,1)S(1)} %get-tuple-element.28), channel_id=1, source_target_pairs={{0,192},{8,56},{16,208},{24,40},{32,224},{40,24},{48,240},{56,8},{... | collective-permute-start | bytes 1179656 | tf_op jit(solution)/shard_map/reduce2_twrap/ppermute | solution.py:48
  40.2 7.8 %collective-permute-start.12 = (bf16[32,6144]{1,0:T(8,128)(2,1)S(1)}, bf16[32,6144]{1,0:T(8,128)(2,1)S(1)}, u32[]{:S(2)}, u32[]{:S(2)}) collective-permute-start(bf16[32,6144]{1,0:T(8,128)(2,1)S(1)} %get-tuple-element.26), channel_id=1, source_target_pairs={{0,64},{8,24},{16,80},{24,8},{32,96},{40,56},{48,112},{56,40},{64,... | collective-permute-start | bytes 1179656 | tf_op jit(solution)/shard_map/reduce2_tnear/ppermute | solution.py:48
  43.1 9.2 %collective-permute-start.11 = (bf16[32,6144]{1,0:T(8,128)(2,1)S(1)}, bf16[32,6144]{1,0:T(8,128)(2,1)S(1)}, u32[]{:S(2)}, u32[]{:S(2)}) collective-permute-start(bf16[32,6144]{1,0:T(8,128)(2,1)S(1)} %get-tuple-element.24), channel_id=1, source_target_pairs={{0,64},{8,24},{16,80},{24,8},{32,96},{40,56},{48,112},{56,40},{64,... | collective-permute-start | bytes 1179656 | tf_op jit(solution)/shard_map/reduce_tnear/ppermute | solution.py:48
  45.4 9.0 %collective-permute-start.15 = (bf16[32,6144]{1,0:T(8,128)(2,1)S(1)}, bf16[32,6144]{1,0:T(8,128)(2,1)S(1)}, u32[]{:S(2)}, u32[]{:S(2)}) collective-permute-start(bf16[32,6144]{1,0:T(8,128)(2,1)S(1)} %get-tuple-element.30), channel_id=1, source_target_pairs={{0,192},{8,56},{16,208},{24,40},{32,224},{40,24},{48,240},{56,8},{... | collective-permute-start | bytes 1179656 | tf_op jit(solution)/shard_map/reduce_twrap/ppermute | solution.py:48
  46.3 10.1 %collective-permute-start.16 = (bf16[32,6144]{1,0:T(8,128)(2,1)S(1)}, bf16[32,6144]{1,0:T(8,128)(2,1)S(1)}, u32[]{:S(2)}, u32[]{:S(2)}) collective-permute-start(bf16[32,6144]{1,0:T(8,128)(2,1)S(1)} %merge.2.refs_0_), channel_id=1, source_target_pairs={{0,64},{8,24},{16,80},{24,8},{32,96},{40,56},{48,112},{56,40},{64,... | collective-permute-start | bytes 1179656 | tf_op jit(solution)/shard_map/reduce_tnear/ppermute | solution.py:48
  48.1 14.5 %collective-permute-start.14 = (bf16[32,6144]{1,0:T(8,128)(2,1)S(1)}, bf16[32,6144]{1,0:T(8,128)(2,1)S(1)}, u32[]{:S(2)}, u32[]{:S(2)}) collective-permute-start(bf16[32,6144]{1,0:T(8,128)(2,1)S(1)} %merge.3), channel_id=1, source_target_pairs={{0,192},{8,56},{16,208},{24,40},{32,224},{40,24},{48,240},{56,8},{... | collective-permute-start | bytes 1179656 | tf_op jit(solution)/shard_map/reduce_twrap/ppermute | solution.py:48
  56.6 8.0 %collective-permute-start.17 = (bf16[16,6144]{1,0:T(8,128)(2,1)S(1)}, bf16[16,6144]{1,0:T(8,128)(2,1)S(1)}, u32[]{:S(2)}, u32[]{:S(2)}) collective-permute-start(bf16[16,6144]{1,0:T(8,128)(2,1)S(1)} %get-tuple-element.31.refs_0_), channel_id=1, source_target_pairs={{0,48},{8,200},{16,32},{24,216},{32,16},{40,232},{48,0},{56,248},{... | collective-permute-start | bytes 589832 | tf_op jit(solution)/shard_map/home_swrap/ppermute | solution.py:48
  58.7 7.2 %collective-permute-start.18 = (bf16[16,6144]{1,0:T(8,128)(2,1)S(1)}, bf16[16,6144]{1,0:T(8,128)(2,1)S(1)}, u32[]{:S(2)}, u32[]{:S(2)}) collective-permute-start(bf16[16,6144]{1,0:T(8,128)(2,1)S(1)} %get-tuple-element.33), channel_id=1, source_target_pairs={{0,32},{8,136},{16,48},{24,152},{32,0},{40,168},{48,16},{56,184},{... | collective-permute-start | bytes 589832 | tf_op jit(solution)/shard_map/home_sfar/ppermute | solution.py:48
  62.8 5.8 %collective-permute-start.19 = (bf16[16,6144]{1,0:T(8,128)(2,1)S(1)}, bf16[16,6144]{1,0:T(8,128)(2,1)S(1)}, u32[]{:S(2)}, u32[]{:S(2)}) collective-permute-start(bf16[16,6144]{1,0:T(8,128)(2,1)S(1)} %get-tuple-element.34), channel_id=1, source_target_pairs={{0,16},{8,72},{16,0},{24,88},{32,48},{40,104},{48,32},{56,120},{64... | collective-permute-start | bytes 589832 | tf_op jit(solution)/shard_map/home_snear/ppermute | solution.py:48

commit v11 on v10

--- a/solution.py
+++ b/solution.py
@@ -346,13 +346,13 @@
     far_late = send(late_f, "twrap", "reduce2")
     far_early = send(early_f, "tnear", "reduce2")
     direct_late = send(late_w, "twrap", "reduce")
-    (late_n,) = merge(late_n, far_late)
+    direct_early = send(early_n, "tnear", "reduce")
+    (early_w,) = merge(early_w, far_early)
+    back_early = send(early_w, "twrap", "reduce")
+    (late_n,) = merge(late_n, far_late, after=(early_w,))
     back_late = send(late_n, "tnear", "reduce")
-    direct_early = send(early_n, "tnear", "reduce")
-    (early_w,) = merge(early_w, far_early, after=(late_n,))
-    back_early = send(early_w, "twrap", "reduce")
-    home_wrap, home_far = finish(late, direct_late, back_late, jnp.bfloat16, after=(direct_early,))
-    own, home_near = finish(early, direct_early, back_early, jnp.float32, after=(home_wrap,))
+    own, home_near = finish(early, direct_early, back_early, jnp.float32, after=(direct_late,))
+    home_wrap, home_far = finish(late, direct_late, back_late, jnp.bfloat16, after=(own,))
     home_wrap, home_far = send(home_wrap, "swrap", "home"), send(home_far, "sfar", "home")
     home_near = send(home_near, "snear", "home")
     mixed = collect(attended, own, home_wrap, home_far)

time: 69.4 us -> 69.9 us (level)
  starting transfers between devices: 23.8 us -> 24.8 us
  waiting for transfers between devices: 28.9 us -> 27.9 us
    ppermute x20, starting transfers between devices: 23.8 us -> 24.8 us  [send(): return lax.ppermute(value, 'dp', ROUTES[route])]
    ppermute x20, waiting for transfers between devices: 28.9 us -> 27.9 us  [send(): return lax.ppermute(value, 'dp', ROUTES[route])]
  transfers between devices with their start and end apart: 20 -> 20, of which waited for: 16 -> 13; matrix products, arithmetic and copies ran while one was open for 0% -> 0% of each run, Pallas kernels for 19% -> 18%
where the time goes in v11:
time: 69.9 us; the launch traced here: 69.3 us
  waiting for transfers between devices  27.9 us (40%)
  starting transfers between devices  24.8 us (35%)
  Pallas kernels  15.1 us (22%)
  between operations  0.78 us (1%)
  other arithmetic  0.77 us (1%)
    ppermute x20, waiting for transfers between devices, send(): return lax.ppermute(value, 'dp', ROUTES[route])  27.9 us
    ppermute x20, starting transfers between devices, send(): return lax.ppermute(value, 'dp', ROUTES[route])  24.8 us
    pallas_call x2, Pallas kernels, project_down(): pl.pallas_call(functools.partial(down_kernel, begin), out_shape=[jax.Shap...  4.98 us
    pallas_call x1, Pallas kernels, project_up(): pl.pallas_call(up_kernel, out_shape=jax.ShapeDtypeStruct((rows, 2 * HIDDE...  3.58 us
    pallas_call x1, Pallas kernels, attend(): pl.pallas_call(attend_kernel, out_shape=(jax.ShapeDtypeStruct((SLOTS, D),...  3.34 us
    pallas_call x1, Pallas kernels, fetch(): pl.pallas_call(fetch_kernel, out_shape=jax.ShapeDtypeStruct((HIDDEN, D),...  2.57 us
  transfers between devices with their start and end apart: 20, of which 13 were waited for; matrix products, arithmetic and copies ran while one was open for 0% of the time, Pallas kernels for 18%

profile of v11, /device:TPU:128, one launch (start us, length us, event | category | flops | bytes accessed | tf_op | source)
XLA Modules:
  0.0 69.3 jit_solution(10143720097444625588)
XLA Ops:
  0.0 3.3 %attend.1 = (bf16[16,6144]{1,0:T(8,128)(2,1)S(1)}, bf16[16,6144]{1,0:T(8,128)(2,1)S(1)}, bf16[448,6144]{1,0:T(8,128)(2,1)S(1)}) custom-call(s32[16]{0:T(128)} %lengths_in.1, bf16[16,6144]{1,0:T(8,128)(2,1)} %q_in.1, bf16[1024,512]{1,0:T(8,128)(2,1)} %k_in.1, bf16[1024,512]{1,0:T(8,128)(2,1)} %v_in.1, f32[1,6144]{1,0:T(1,128)} %bitcast.4, bf16[448,6144]{1,0:T(8,128)(2,1)} %down.3), custom_call_target="tpu_custom_call" | custom-call | tf_op jit(solution)/shard_map/attend/pallas_call | solution.py:126
  3.4 1.6 %collective-permute-start = (bf16[16,6144]{1,0:T(8,128)(2,1)S(1)}, bf16[16,6144]{1,0:T(8,128)(2,1)S(1)}, u32[]{:S(2)}, u32[]{:S(2)}) collective-permute-start(bf16[16,6144]{1,0:T(8,128)(2,1)S(1)} %get-tuple-element.21.one), channel_id=1, source_target_pairs={{0,16},{8,72},{16,0},{24,88},{32,48},{40,104},{48,32},{56,120},{64... | collective-permute-start | bytes 589832 | tf_op jit(solution)/shard_map/gather_snear/ppermute | solution.py:48
  4.9 2.1 %collective-permute-start.1 = (bf16[16,6144]{1,0:T(8,128)(2,1)S(1)}, bf16[16,6144]{1,0:T(8,128)(2,1)S(1)}, u32[]{:S(2)}, u32[]{:S(2)}) collective-permute-start(bf16[16,6144]{1,0:T(8,128)(2,1)S(1)} %get-tuple-element.21.one), channel_id=1, source_target_pairs={{0,48},{8,200},{16,32},{24,216},{32,16},{40,232},{48,0},{56,248},{... | collective-permute-start | bytes 589832 | tf_op jit(solution)/shard_map/gather_swrap/ppermute | solution.py:48
  7.0 0.6 collective-permute-start.2
  7.7 1.4 %collective-permute-done.two = bf16[16,6144]{1,0:T(8,128)(2,1)S(1)} collective-permute-done((bf16[16,6144]{1,0:T(8,128)(2,1)S(1)}, bf16[16,6144]{1,0:T(8,128)(2,1)S(1)}, u32[]{:S(2)}, u32[]{:S(2)}) %collective-permute-start) | collective-permute-done | bytes 196640 | tf_op jit(solution)/shard_map/gather_snear/ppermute | solution.py:48
  9.1 3.1 %collective-permute-start.4 = (bf16[32,6144]{1,0:T(8,128)(2,1)S(1)}, bf16[32,6144]{1,0:T(8,128)(2,1)S(1)}, u32[]{:S(2)}, u32[]{:S(2)}) collective-permute-start(bf16[32,6144]{1,0:T(8,128)(2,1)S(1)} %pack.2.args_0_), channel_id=1, source_target_pairs={{0,192},{8,56},{16,208},{24,40},{32,224},{40,24},{48,240},{56,8},{... | collective-permute-start | bytes 1179656 | tf_op jit(solution)/shard_map/gather_twrap/ppermute | solution.py:48
  12.2 0.1 collective-permute-start.3
  12.4 0.3 collective-permute-done.1.one
  12.7 1.8 %collective-permute-done.2.two = bf16[16,6144]{1,0:T(8,128)(2,1)S(1)} collective-permute-done((bf16[16,6144]{1,0:T(8,128)(2,1)S(1)}, bf16[16,6144]{1,0:T(8,128)(2,1)S(1)}, u32[]{:S(2)}, u32[]{:S(2)}) %collective-permute-start.2) | collective-permute-done | bytes 196640 | tf_op jit(solution)/shard_map/gather_sfar/ppermute | solution.py:48
  14.5 3.1 %collective-permute-start.5 = (bf16[32,6144]{1,0:T(8,128)(2,1)S(1)}, bf16[32,6144]{1,0:T(8,128)(2,1)S(1)}, u32[]{:S(2)}, u32[]{:S(2)}) collective-permute-start(bf16[32,6144]{1,0:T(8,128)(2,1)S(1)} %pack.3.after.args_1_), channel_id=1, source_target_pairs={{0,192},{8,56},{16,208},{24,40},{32,224},{40,24},{48,240},{56,8},{... | collective-permute-start | bytes 1179656 | tf_op jit(solution)/shard_map/gather_twrap/ppermute | solution.py:48
  17.6 0.1 collective-permute-start.6
  17.7 0.5 collective-permute-done.4.refs_1_.args_4_
  18.2 1.8 %collective-permute-done.3.refs_0_ = bf16[32,6144]{1,0:T(8,128)(2,1)S(1)} collective-permute-done((bf16[32,6144]{1,0:T(8,128)(2,1)S(1)}, bf16[32,6144]{1,0:T(8,128)(2,1)S(1)}, u32[]{:S(2)}, u32[]{:S(2)}) %collective-permute-start.3) | collective-permute-done | bytes 393248 | tf_op jit(solution)/shard_map/gather_tnear/ppermute | solution.py:48
  20.0 1.2 %collective-permute-start.7 = (bf16[32,6144]{1,0:T(8,128)(2,1)S(1)}, bf16[32,6144]{1,0:T(8,128)(2,1)S(1)}, u32[]{:S(2)}, u32[]{:S(2)}) collective-permute-start(bf16[32,6144]{1,0:T(8,128)(2,1)S(1)} %hand.2.args_2_), channel_id=1, source_target_pairs={{0,192},{8,56},{16,208},{24,40},{32,224},{40,24},{48,240},{56,8},{... | collective-permute-start | bytes 1179656 | tf_op jit(solution)/shard_map/gather2_twrap/ppermute | solution.py:48
  21.2 2.3 %collective-permute-done.5.args_3_ = bf16[32,6144]{1,0:T(8,128)(2,1)S(1)} collective-permute-done((bf16[32,6144]{1,0:T(8,128)(2,1)S(1)}, bf16[32,6144]{1,0:T(8,128)(2,1)S(1)}, u32[]{:S(2)}, u32[]{:S(2)}) %collective-permute-start.5) | collective-permute-done | bytes 393248 | tf_op jit(solution)/shard_map/gather_twrap/ppermute | solution.py:48
  23.6 0.4 collective-permute-start.8
  23.9 0.0 collective-permute-done.9.args_9_.refs_1_
  23.9 0.0 collective-permute-start.10
  24.0 2.6 %fetch.1.args_8_ = bf16[448,6144]{1,0:T(8,128)(2,1)S(1)} custom-call(bf16[448,6144]{1,0:T(8,128)(2,1)} %bitcast.6, bf16[32,6144]{1,0:T(8,128)(2,1)S(1)} %pack.3.after.args_1_), custom_call_target="tpu_custom_call" | custom-call | flops 99999997952 | bytes 11010048 | tf_op jit(solution)/shard_map/fetch/pallas_call | solution.py:156
  26.5 2.5 %collective-permute-done.7.args_6_ = bf16[32,6144]{1,0:T(8,128)(2,1)S(1)} collective-permute-done((bf16[32,6144]{1,0:T(8,128)(2,1)S(1)}, bf16[32,6144]{1,0:T(8,128)(2,1)S(1)}, u32[]{:S(2)}, u32[]{:S(2)}) %collective-permute-start.7) | collective-permute-done | bytes 393248 | tf_op jit(solution)/shard_map/gather2_twrap/ppermute | solution.py:48
  29.0 2.3 %collective-permute-done.8.args_7_ = bf16[32,6144]{1,0:T(8,128)(2,1)S(1)} collective-permute-done((bf16[32,6144]{1,0:T(8,128)(2,1)S(1)}, bf16[32,6144]{1,0:T(8,128)(2,1)S(1)}, u32[]{:S(2)}, u32[]{:S(2)}) %collective-permute-start.8) | collective-permute-done | bytes 393248 | tf_op jit(solution)/shard_map/gather2_tnear/ppermute | solution.py:48
  31.4 3.6 %up.1.hidden = bf16[256,896]{1,0:T(8,128)(2,1)S(1)} custom-call(bf16[32,6144]{1,0:T(8,128)(2,1)S(1)} %pack.2.args_0_, bf16[32,6144]{1,0:T(8,128)(2,1)S(1)} %pack.3.after.args_1_, bf16[32,6144]{1,0:T(8,128)(2,1)S(1)} %hand.2.args_2_, bf16[32,6144]{1,0:T(8,128)(2,1)S(1)} %collective-permute-done.5.args_3_, ...), custom_call_target="tpu_custom_call" | custom-call | flops 2818572288 | bytes 3145728 | tf_op jit(solution)/shard_map/up/pallas_call | solution.py:189
  34.9 0.0 collective-permute-done.10.two
  35.0 2.2 %down.5 = (bf16[32,6144]{1,0:T(8,128)(2,1)S(1)}, bf16[32,6144]{1,0:T(8,128)(2,1)S(1)}) custom-call(bf16[256,896]{1,0:T(8,128)(2,1)S(1)} %up.1.hidden, bf16[448,6144]{1,0:T(8,128)(2,1)S(1)} %hand.3.one, bf16[448,6144]{1,0:T(8,128)(2,1)S(1)} %collective-permute-done.10.two), custom_call_target="tpu_custom_call" | custom-call | flops 704643072 | bytes 786432 | tf_op jit(solution)/shard_map/down/pallas_call | solution.py:219
  37.1 0.5 collective-permute-start.12
  37.6 2.8 %collective-permute-start.15 = (bf16[32,6144]{1,0:T(8,128)(2,1)S(1)}, bf16[32,6144]{1,0:T(8,128)(2,1)S(1)}, u32[]{:S(2)}, u32[]{:S(2)}) collective-permute-start(bf16[32,6144]{1,0:T(8,128)(2,1)S(1)} %get-tuple-element.31), channel_id=1, source_target_pairs={{0,192},{8,56},{16,208},{24,40},{32,224},{40,24},{48,240},{56,8},{... | collective-permute-start | bytes 1179656 | tf_op jit(solution)/shard_map/reduce2_twrap/ppermute | solution.py:48
  40.3 2.8 %down.4 = (bf16[32,6144]{1,0:T(8,128)(2,1)S(1)}, bf16[32,6144]{1,0:T(8,128)(2,1)S(1)}, bf16[32,6144]{1,0:T(8,128)(2,1)S(1)}, bf16[32,6144]{1,0:T(8,128)(2,1)S(1)...) custom-call(bf16[256,896]{1,0:T(8,128)(2,1)S(1)} %up.1.hidden, bf16[448,6144]{1,0:T(8,128)(2,1)S(1)} %hand.3.one, ...), custom_call_target="tpu_custom_call" | custom-call | flops 2113929216 | bytes 2359296 | tf_op jit(solution)/shard_map/down/pallas_call | solution.py:219
  43.2 1.6 %collective-permute-start.11 = (bf16[32,6144]{1,0:T(8,128)(2,1)S(1)}, bf16[32,6144]{1,0:T(8,128)(2,1)S(1)}, u32[]{:S(2)}, u32[]{:S(2)}) collective-permute-start(bf16[32,6144]{1,0:T(8,128)(2,1)S(1)} %get-tuple-element.24), channel_id=1, source_target_pairs={{0,64},{8,24},{16,80},{24,8},{32,96},{40,56},{48,112},{56,40},{64,... | collective-permute-start | bytes 1179656 | tf_op jit(solution)/shard_map/reduce_tnear/ppermute | solution.py:48
  44.8 0.6 collective-permute-start.14
  45.4 0.0 collective-permute-done.12.arrived
  45.4 0.1 merge.2.refs_0_
  45.5 2.7 %collective-permute-start.13 = (bf16[32,6144]{1,0:T(8,128)(2,1)S(1)}, bf16[32,6144]{1,0:T(8,128)(2,1)S(1)}, u32[]{:S(2)}, u32[]{:S(2)}) collective-permute-start(bf16[32,6144]{1,0:T(8,128)(2,1)S(1)} %merge.2.refs_0_), channel_id=1, source_target_pairs={{0,192},{8,56},{16,208},{24,40},{32,224},{40,24},{48,240},{56,8},{... | collective-permute-start | bytes 1179656 | tf_op jit(solution)/shard_map/reduce_twrap/ppermute | solution.py:48
  48.2 0.0 collective-permute-done.15.arrived
  48.2 0.1 merge.3
  48.3 0.1 collective-permute-start.16
  48.4 2.8 %collective-permute-done.11.direct = bf16[32,6144]{1,0:T(8,128)(2,1)S(1)} collective-permute-done((bf16[32,6144]{1,0:T(8,128)(2,1)S(1)}, bf16[32,6144]{1,0:T(8,128)(2,1)S(1)}, u32[]{:S(2)}, u32[]{:S(2)}) %collective-permute-start.11) | collective-permute-done | bytes 393248 | tf_op jit(solution)/shard_map/reduce_tnear/ppermute | solution.py:48
  51.2 2.5 %collective-permute-done.14.refs_0_.direct = bf16[32,6144]{1,0:T(8,128)(2,1)S(1)} collective-permute-done((bf16[32,6144]{1,0:T(8,128)(2,1)S(1)}, bf16[32,6144]{1,0:T(8,128)(2,1)S(1)}, u32[]{:S(2)}, u32[]{:S(2)}) %collective-permute-start.14) | collective-permute-done | bytes 393248 | tf_op jit(solution)/shard_map/reduce_twrap/ppermute | solution.py:48
  53.7 4.5 %collective-permute-done.13.back = bf16[32,6144]{1,0:T(8,128)(2,1)S(1)} collective-permute-done((bf16[32,6144]{1,0:T(8,128)(2,1)S(1)}, bf16[32,6144]{1,0:T(8,128)(2,1)S(1)}, u32[]{:S(2)}, u32[]{:S(2)}) %collective-permute-start.13) | collective-permute-done | bytes 393248 | tf_op jit(solution)/shard_map/reduce_twrap/ppermute | solution.py:48
  58.2 0.1 finish.2
  58.4 0.1 finish.3
  58.5 2.8 %collective-permute-start.17 = (bf16[16,6144]{1,0:T(8,128)(2,1)S(1)}, bf16[16,6144]{1,0:T(8,128)(2,1)S(1)}, u32[]{:S(2)}, u32[]{:S(2)}) collective-permute-start(bf16[16,6144]{1,0:T(8,128)(2,1)S(1)} %get-tuple-element.32), channel_id=1, source_target_pairs={{0,48},{8,200},{16,32},{24,216},{32,16},{40,232},{48,0},{56,248},{... | collective-permute-start | bytes 589832 | tf_op jit(solution)/shard_map/home_swrap/ppermute | solution.py:48
  61.3 1.4 %collective-permute-start.18 = (bf16[16,6144]{1,0:T(8,128)(2,1)S(1)}, bf16[16,6144]{1,0:T(8,128)(2,1)S(1)}, u32[]{:S(2)}, u32[]{:S(2)}) collective-permute-start(bf16[16,6144]{1,0:T(8,128)(2,1)S(1)} %get-tuple-element.33), channel_id=1, source_target_pairs={{0,32},{8,136},{16,48},{24,152},{32,0},{40,168},{48,16},{56,184},{... | collective-permute-start | bytes 589832 | tf_op jit(solution)/shard_map/home_sfar/ppermute | solution.py:48
  62.7 0.0 collective-permute-start.19
  63.4 3.2 %collective-permute-done.17.refs_2_ = bf16[16,6144]{1,0:T(8,128)(2,1)S(1)} collective-permute-done((bf16[16,6144]{1,0:T(8,128)(2,1)S(1)}, bf16[16,6144]{1,0:T(8,128)(2,1)S(1)}, u32[]{:S(2)}, u32[]{:S(2)}) %collective-permute-start.17) | collective-permute-done | bytes 196640 | tf_op jit(solution)/shard_map/home_swrap/ppermute | solution.py:48
  66.6 1.8 %collective-permute-done.18.refs_3_ = bf16[16,6144]{1,0:T(8,128)(2,1)S(1)} collective-permute-done((bf16[16,6144]{1,0:T(8,128)(2,1)S(1)}, bf16[16,6144]{1,0:T(8,128)(2,1)S(1)}, u32[]{:S(2)}, u32[]{:S(2)}) %collective-permute-start.18) | collective-permute-done | bytes 196640 | tf_op jit(solution)/shard_map/home_sfar/ppermute | solution.py:48
  68.4 0.1 collect.1
  68.5 0.0 collective-permute-done.19
  68.5 0.8 %select_convert_fusion = bf16[16,6144]{1,0:T(8,128)(2,1)} fusion(f32[16,6144]{1,0:T(8,128)S(1)} %collect.1, bf16[16,6144]{1,0:T(8,128)(2,1)S(1)} %collective-permute-done.19, pred[16]{0:T(512)(128)(4,1)S(1)} %iota_compare_fusion), kind=kLoop, calls=%fused_computation | loop fusion | flops 393216 | bytes 786448 | tf_op jit(solution)/shard_map/convert_element_type | solution.py:360
  (8 shorter events, 0.1 us)
Async XLA Ops:
  0.0 23.9 %collective-permute-start.9 = (bf16[448,6144]{1,0:T(8,128)(2,1)}, bf16[448,6144]{1,0:T(8,128)(2,1)S(1)}, u32[]{:S(2)}, u32[]{:S(2)}) collective-permute-start(bf16[448,6144]{1,0:T(8,128)(2,1)} %bitcast.5), channel_id=1, source_target_pairs={{0,8},{8,0},{16,24},{24,16},{32,40},{40,32},{48,56},{56,48},{64,72... | collective-permute-start | bytes 16515080 | tf_op jit(solution)/shard_map/up_core/ppermute | solution.py:48
  3.4 5.8 %collective-permute-start = (bf16[16,6144]{1,0:T(8,128)(2,1)S(1)}, bf16[16,6144]{1,0:T(8,128)(2,1)S(1)}, u32[]{:S(2)}, u32[]{:S(2)}) collective-permute-start(bf16[16,6144]{1,0:T(8,128)(2,1)S(1)} %get-tuple-element.21.one), channel_id=1, source_target_pairs={{0,16},{8,72},{16,0},{24,88},{32,48},{40,104},{48,32},{56,120},{64... | collective-permute-start | bytes 589832 | tf_op jit(solution)/shard_map/gather_snear/ppermute | solution.py:48
  4.9 7.7 %collective-permute-start.1 = (bf16[16,6144]{1,0:T(8,128)(2,1)S(1)}, bf16[16,6144]{1,0:T(8,128)(2,1)S(1)}, u32[]{:S(2)}, u32[]{:S(2)}) collective-permute-start(bf16[16,6144]{1,0:T(8,128)(2,1)S(1)} %get-tuple-element.21.one), channel_id=1, source_target_pairs={{0,48},{8,200},{16,32},{24,216},{32,16},{40,232},{48,0},{56,248},{... | collective-permute-start | bytes 589832 | tf_op jit(solution)/shard_map/gather_swrap/ppermute | solution.py:48
  7.0 7.4 %collective-permute-start.2 = (bf16[16,6144]{1,0:T(8,128)(2,1)S(1)}, bf16[16,6144]{1,0:T(8,128)(2,1)S(1)}, u32[]{:S(2)}, u32[]{:S(2)}) collective-permute-start(bf16[16,6144]{1,0:T(8,128)(2,1)S(1)} %get-tuple-element.21.one), channel_id=1, source_target_pairs={{0,32},{8,136},{16,48},{24,152},{32,0},{40,168},{48,16},{56,184},{... | collective-permute-start | bytes 589832 | tf_op jit(solution)/shard_map/gather_sfar/ppermute | solution.py:48
  9.1 9.1 %collective-permute-start.4 = (bf16[32,6144]{1,0:T(8,128)(2,1)S(1)}, bf16[32,6144]{1,0:T(8,128)(2,1)S(1)}, u32[]{:S(2)}, u32[]{:S(2)}) collective-permute-start(bf16[32,6144]{1,0:T(8,128)(2,1)S(1)} %pack.2.args_0_), channel_id=1, source_target_pairs={{0,192},{8,56},{16,208},{24,40},{32,224},{40,24},{48,240},{56,8},{... | collective-permute-start | bytes 1179656 | tf_op jit(solution)/shard_map/gather_twrap/ppermute | solution.py:48
  12.2 7.8 %collective-permute-start.3 = (bf16[32,6144]{1,0:T(8,128)(2,1)S(1)}, bf16[32,6144]{1,0:T(8,128)(2,1)S(1)}, u32[]{:S(2)}, u32[]{:S(2)}) collective-permute-start(bf16[32,6144]{1,0:T(8,128)(2,1)S(1)} %pack.2.args_0_), channel_id=1, source_target_pairs={{0,64},{8,24},{16,80},{24,8},{32,96},{40,56},{48,112},{56,40},{64,... | collective-permute-start | bytes 1179656 | tf_op jit(solution)/shard_map/gather_tnear/ppermute | solution.py:48
  14.5 9.1 %collective-permute-start.5 = (bf16[32,6144]{1,0:T(8,128)(2,1)S(1)}, bf16[32,6144]{1,0:T(8,128)(2,1)S(1)}, u32[]{:S(2)}, u32[]{:S(2)}) collective-permute-start(bf16[32,6144]{1,0:T(8,128)(2,1)S(1)} %pack.3.after.args_1_), channel_id=1, source_target_pairs={{0,192},{8,56},{16,208},{24,40},{32,224},{40,24},{48,240},{56,8},{... | collective-permute-start | bytes 1179656 | tf_op jit(solution)/shard_map/gather_twrap/ppermute | solution.py:48
  17.6 8.9 %collective-permute-start.6 = (bf16[32,6144]{1,0:T(8,128)(2,1)S(1)}, bf16[32,6144]{1,0:T(8,128)(2,1)S(1)}, u32[]{:S(2)}, u32[]{:S(2)}) collective-permute-start(bf16[32,6144]{1,0:T(8,128)(2,1)S(1)} %pack.3.after.args_1_), channel_id=1, source_target_pairs={{0,64},{8,24},{16,80},{24,8},{32,96},{40,56},{48,112},{56,40},{64,... | collective-permute-start | bytes 1179656 | tf_op jit(solution)/shard_map/gather_tnear/ppermute | solution.py:48
  20.0 9.0 %collective-permute-start.7 = (bf16[32,6144]{1,0:T(8,128)(2,1)S(1)}, bf16[32,6144]{1,0:T(8,128)(2,1)S(1)}, u32[]{:S(2)}, u32[]{:S(2)}) collective-permute-start(bf16[32,6144]{1,0:T(8,128)(2,1)S(1)} %hand.2.args_2_), channel_id=1, source_target_pairs={{0,192},{8,56},{16,208},{24,40},{32,224},{40,24},{48,240},{56,8},{... | collective-permute-start | bytes 1179656 | tf_op jit(solution)/shard_map/gather2_twrap/ppermute | solution.py:48
  23.6 7.8 %collective-permute-start.8 = (bf16[32,6144]{1,0:T(8,128)(2,1)S(1)}, bf16[32,6144]{1,0:T(8,128)(2,1)S(1)}, u32[]{:S(2)}, u32[]{:S(2)}) collective-permute-start(bf16[32,6144]{1,0:T(8,128)(2,1)S(1)} %collective-permute-done.5.args_3_), channel_id=1, source_target_pairs={{0,64},{8,24},{16,80},{24,8},{32,96},{40,56},{48,112},{56,40},{64,... | collective-permute-start | bytes 1179656 | tf_op jit(solution)/shard_map/gather2_tnear/ppermute | solution.py:48
  23.9 11.0 %collective-permute-start.10 = (bf16[448,6144]{1,0:T(8,128)(2,1)S(1)}, bf16[448,6144]{1,0:T(8,128)(2,1)S(1)}, u32[]{:S(2)}, u32[]{:S(2)}) collective-permute-start(bf16[448,6144]{1,0:T(8,128)(2,1)S(1)} %hand.3.one), channel_id=1, source_target_pairs={{0,8},{8,0},{16,24},{24,16},{32,40},{40,32},{48,56},{56,48},{64,72... | collective-permute-start | bytes 16515080 | tf_op jit(solution)/shard_map/down_core/ppermute | solution.py:48
  37.1 8.2 %collective-permute-start.12 = (bf16[32,6144]{1,0:T(8,128)(2,1)S(1)}, bf16[32,6144]{1,0:T(8,128)(2,1)S(1)}, u32[]{:S(2)}, u32[]{:S(2)}) collective-permute-start(bf16[32,6144]{1,0:T(8,128)(2,1)S(1)} %get-tuple-element.26), channel_id=1, source_target_pairs={{0,64},{8,24},{16,80},{24,8},{32,96},{40,56},{48,112},{56,40},{64,... | collective-permute-start | bytes 1179656 | tf_op jit(solution)/shard_map/reduce2_tnear/ppermute | solution.py:48
  37.6 10.6 %collective-permute-start.15 = (bf16[32,6144]{1,0:T(8,128)(2,1)S(1)}, bf16[32,6144]{1,0:T(8,128)(2,1)S(1)}, u32[]{:S(2)}, u32[]{:S(2)}) collective-permute-start(bf16[32,6144]{1,0:T(8,128)(2,1)S(1)} %get-tuple-element.31), channel_id=1, source_target_pairs={{0,192},{8,56},{16,208},{24,40},{32,224},{40,24},{48,240},{56,8},{... | collective-permute-start | bytes 1179656 | tf_op jit(solution)/shard_map/reduce2_twrap/ppermute | solution.py:48
  43.2 8.0 %collective-permute-start.11 = (bf16[32,6144]{1,0:T(8,128)(2,1)S(1)}, bf16[32,6144]{1,0:T(8,128)(2,1)S(1)}, u32[]{:S(2)}, u32[]{:S(2)}) collective-permute-start(bf16[32,6144]{1,0:T(8,128)(2,1)S(1)} %get-tuple-element.24), channel_id=1, source_target_pairs={{0,64},{8,24},{16,80},{24,8},{32,96},{40,56},{48,112},{56,40},{64,... | collective-permute-start | bytes 1179656 | tf_op jit(solution)/shard_map/reduce_tnear/ppermute | solution.py:48
  44.8 9.0 %collective-permute-start.14 = (bf16[32,6144]{1,0:T(8,128)(2,1)S(1)}, bf16[32,6144]{1,0:T(8,128)(2,1)S(1)}, u32[]{:S(2)}, u32[]{:S(2)}) collective-permute-start(bf16[32,6144]{1,0:T(8,128)(2,1)S(1)} %get-tuple-element.27), channel_id=1, source_target_pairs={{0,192},{8,56},{16,208},{24,40},{32,224},{40,24},{48,240},{56,8},{... | collective-permute-start | bytes 1179656 | tf_op jit(solution)/shard_map/reduce_twrap/ppermute | solution.py:48
  45.5 12.7 %collective-permute-start.13 = (bf16[32,6144]{1,0:T(8,128)(2,1)S(1)}, bf16[32,6144]{1,0:T(8,128)(2,1)S(1)}, u32[]{:S(2)}, u32[]{:S(2)}) collective-permute-start(bf16[32,6144]{1,0:T(8,128)(2,1)S(1)} %merge.2.refs_0_), channel_id=1, source_target_pairs={{0,192},{8,56},{16,208},{24,40},{32,224},{40,24},{48,240},{56,8},{... | collective-permute-start | bytes 1179656 | tf_op jit(solution)/shard_map/reduce_twrap/ppermute | solution.py:48
  48.3 10.0 %collective-permute-start.16 = (bf16[32,6144]{1,0:T(8,128)(2,1)S(1)}, bf16[32,6144]{1,0:T(8,128)(2,1)S(1)}, u32[]{:S(2)}, u32[]{:S(2)}) collective-permute-start(bf16[32,6144]{1,0:T(8,128)(2,1)S(1)} %merge.3), channel_id=1, source_target_pairs={{0,64},{8,24},{16,80},{24,8},{32,96},{40,56},{48,112},{56,40},{64,... | collective-permute-start | bytes 1179656 | tf_op jit(solution)/shard_map/reduce_tnear/ppermute | solution.py:48
  58.5 8.1 %collective-permute-start.17 = (bf16[16,6144]{1,0:T(8,128)(2,1)S(1)}, bf16[16,6144]{1,0:T(8,128)(2,1)S(1)}, u32[]{:S(2)}, u32[]{:S(2)}) collective-permute-start(bf16[16,6144]{1,0:T(8,128)(2,1)S(1)} %get-tuple-element.32), channel_id=1, source_target_pairs={{0,48},{8,200},{16,32},{24,216},{32,16},{40,232},{48,0},{56,248},{... | collective-permute-start | bytes 589832 | tf_op jit(solution)/shard_map/home_swrap/ppermute | solution.py:48
  61.3 7.2 %collective-permute-start.18 = (bf16[16,6144]{1,0:T(8,128)(2,1)S(1)}, bf16[16,6144]{1,0:T(8,128)(2,1)S(1)}, u32[]{:S(2)}, u32[]{:S(2)}) collective-permute-start(bf16[16,6144]{1,0:T(8,128)(2,1)S(1)} %get-tuple-element.33), channel_id=1, source_target_pairs={{0,32},{8,136},{16,48},{24,152},{32,0},{40,168},{48,16},{56,184},{... | collective-permute-start | bytes 589832 | tf_op jit(solution)/shard_map/home_sfar/ppermute | solution.py:48
  62.7 5.9 %collective-permute-start.19 = (bf16[16,6144]{1,0:T(8,128)(2,1)S(1)}, bf16[16,6144]{1,0:T(8,128)(2,1)S(1)}, u32[]{:S(2)}, u32[]{:S(2)}) collective-permute-start(bf16[16,6144]{1,0:T(8,128)(2,1)S(1)} %get-tuple-element.34), channel_id=1, source_target_pairs={{0,16},{8,72},{16,0},{24,88},{32,48},{40,104},{48,32},{56,120},{64... | collective-permute-start | bytes 589832 | tf_op jit(solution)/shard_map/home_snear/ppermute | solution.py:48

commit v12 on v10

--- a/solution.py
+++ b/solution.py
@@ -167,6 +167,8 @@
 
 def up_kernel(*args):
     blocks, up, (hidden, total) = args[:8], args[8:10], args[10:]
+    lows, highs = slice(0, SLOTS), slice(SLOTS, PAIR)
+    order = [(part, half) for part in (0, 1) for half in (lows, highs)]
     total[...] = jnp.zeros_like(total)
 
     @pl.loop(0, D // CHUNK)
@@ -174,7 +176,7 @@
         cols = pl.ds(pl.multiple_of(step * CHUNK, CHUNK), CHUNK)
         total[...] += lax.dot_general(
             jnp.concatenate([w[:, cols] for w in up], axis=0),
-            jnp.concatenate([b[:, cols] for b in blocks], axis=0),
+            jnp.concatenate([blocks[2 * t + part][half, cols] for part, half in order for t in range(SIDE)], axis=0),
             (((1,), (1,)), ((), ())),
             preferred_element_type=jnp.float32,
         )
@@ -338,23 +340,23 @@
     down_other = send(down_held, "core", "down")
     up_held = fetch(up_own, late)
     hidden = project_up(
-        [early, late, early_n, late_w, early_w, late_n, early_f, late_f], (up_held, up_other)
+        [early, late, early_n, late_n, early_w, late_w, early_f, late_f], (up_held, up_other)
     )
     down = (down_held, down_other)
     early_f, late_f = project_down(hidden, down, 6, 8)
-    early, late, early_n, late_w, early_w, late_n = project_down(hidden, down, 0, 6)
-    far_late = send(late_f, "twrap", "reduce2")
-    far_early = send(early_f, "tnear", "reduce2")
-    direct_late = send(late_w, "twrap", "reduce")
+    early, late, early_n, late_n, early_w, late_w = project_down(hidden, down, 0, 6)
+    far_late = send(late_f, "swrap", "reduce2")
+    far_early = send(early_f, "snear", "reduce2")
+    direct_late = send(late_w, "swrap", "reduce")
     (late_n,) = merge(late_n, far_late)
-    back_late = send(late_n, "tnear", "reduce")
-    direct_early = send(early_n, "tnear", "reduce")
+    back_late = send(late_n, "snear", "reduce")
+    direct_early = send(early_n, "snear", "reduce")
     (early_w,) = merge(early_w, far_early, after=(late_n,))
-    back_early = send(early_w, "twrap", "reduce")
+    back_early = send(early_w, "swrap", "reduce")
     home_wrap, home_far = finish(late, direct_late, back_late, jnp.bfloat16, after=(direct_early,))
     own, home_near = finish(early, direct_early, back_early, jnp.float32, after=(home_wrap,))
-    home_wrap, home_far = send(home_wrap, "swrap", "home"), send(home_far, "sfar", "home")
-    home_near = send(home_near, "snear", "home")
+    home_wrap, home_far = send(home_wrap, "twrap", "home"), send(home_far, "tfar", "home")
+    home_near = send(home_near, "tnear", "home")
     mixed = collect(attended, own, home_wrap, home_far)
     live = jnp.arange(SLOTS, dtype=jnp.int32)[:, None] < counts[0]
     return jnp.where(live, mixed + home_near.astype(jnp.float32), jnp.float32(0.0)).astype(jnp.bfloat16)

time: 69.4 us -> 68.6 us (0.988)
  the two profiles are of different devices: /device:TPU:128 before, /device:TPU:152 now
where the time goes in v12:
time: 68.6 us; the launch traced here: 68.5 us
  waiting for transfers between devices  33.4 us (49%)
  starting transfers between devices  18.5 us (27%)
  Pallas kernels  15.1 us (22%)
  between operations  0.78 us (1%)
  other arithmetic  0.77 us (1%)
    ppermute x20, waiting for transfers between devices, send(): return lax.ppermute(value, 'dp', ROUTES[route])  33.4 us
    ppermute x20, starting transfers between devices, send(): return lax.ppermute(value, 'dp', ROUTES[route])  18.5 us
    pallas_call x2, Pallas kernels, project_down(): pl.pallas_call(functools.partial(down_kernel, begin), out_shape=[jax.Shap...  4.98 us
    pallas_call x1, Pallas kernels, project_up(): pl.pallas_call(up_kernel, out_shape=jax.ShapeDtypeStruct((rows, 2 * HIDDE...  3.59 us
    pallas_call x1, Pallas kernels, attend(): pl.pallas_call(attend_kernel, out_shape=(jax.ShapeDtypeStruct((SLOTS, D),...  3.34 us
    pallas_call x1, Pallas kernels, fetch(): pl.pallas_call(fetch_kernel, out_shape=jax.ShapeDtypeStruct((HIDDEN, D),...  2.57 us
  transfers between devices with their start and end apart: 20, of which 15 were waited for; matrix products, arithmetic and copies ran while one was open for 0% of the time, Pallas kernels for 19%

profile of v12, /device:TPU:152, one launch (start us, length us, event | category | flops | bytes accessed | tf_op | source)
XLA Modules:
  0.0 68.5 jit_solution(9969434764505101178)
XLA Ops:
  0.0 3.3 %attend.1 = (bf16[16,6144]{1,0:T(8,128)(2,1)S(1)}, bf16[16,6144]{1,0:T(8,128)(2,1)S(1)}, bf16[448,6144]{1,0:T(8,128)(2,1)S(1)}) custom-call(s32[16]{0:T(128)} %lengths_in.1, bf16[16,6144]{1,0:T(8,128)(2,1)} %q_in.1, bf16[1024,512]{1,0:T(8,128)(2,1)} %k_in.1, bf16[1024,512]{1,0:T(8,128)(2,1)} %v_in.1, f32[1,6144]{1,0:T(1,128)} %bitcast.4, bf16[448,6144]{1,0:T(8,128)(2,1)} %down.3), custom_call_target="tpu_custom_call" | custom-call | tf_op jit(solution)/shard_map/attend/pallas_call | solution.py:126
  3.4 1.6 %collective-permute-start = (bf16[16,6144]{1,0:T(8,128)(2,1)S(1)}, bf16[16,6144]{1,0:T(8,128)(2,1)S(1)}, u32[]{:S(2)}, u32[]{:S(2)}) collective-permute-start(bf16[16,6144]{1,0:T(8,128)(2,1)S(1)} %get-tuple-element.21.one), channel_id=1, source_target_pairs={{0,16},{8,72},{16,0},{24,88},{32,48},{40,104},{48,32},{56,120},{64... | collective-permute-start | bytes 589832 | tf_op jit(solution)/shard_map/gather_snear/ppermute | solution.py:48
  4.9 2.1 %collective-permute-start.1 = (bf16[16,6144]{1,0:T(8,128)(2,1)S(1)}, bf16[16,6144]{1,0:T(8,128)(2,1)S(1)}, u32[]{:S(2)}, u32[]{:S(2)}) collective-permute-start(bf16[16,6144]{1,0:T(8,128)(2,1)S(1)} %get-tuple-element.21.one), channel_id=1, source_target_pairs={{0,48},{8,200},{16,32},{24,216},{32,16},{40,232},{48,0},{56,248},{... | collective-permute-start | bytes 589832 | tf_op jit(solution)/shard_map/gather_swrap/ppermute | solution.py:48
  7.0 0.6 collective-permute-start.2
  7.7 1.4 %collective-permute-done.two = bf16[16,6144]{1,0:T(8,128)(2,1)S(1)} collective-permute-done((bf16[16,6144]{1,0:T(8,128)(2,1)S(1)}, bf16[16,6144]{1,0:T(8,128)(2,1)S(1)}, u32[]{:S(2)}, u32[]{:S(2)}) %collective-permute-start) | collective-permute-done | bytes 196640 | tf_op jit(solution)/shard_map/gather_snear/ppermute | solution.py:48
  9.1 0.3 collective-permute-start.4
  9.5 1.0 %collective-permute-start.3 = (bf16[32,6144]{1,0:T(8,128)(2,1)S(1)}, bf16[32,6144]{1,0:T(8,128)(2,1)S(1)}, u32[]{:S(2)}, u32[]{:S(2)}) collective-permute-start(bf16[32,6144]{1,0:T(8,128)(2,1)S(1)} %pack.2.args_0_), channel_id=1, source_target_pairs={{0,64},{8,24},{16,80},{24,8},{32,96},{40,56},{48,112},{56,40},{64,... | collective-permute-start | bytes 1179656 | tf_op jit(solution)/shard_map/gather_tnear/ppermute | solution.py:48
  10.4 2.3 %collective-permute-done.1.one = bf16[16,6144]{1,0:T(8,128)(2,1)S(1)} collective-permute-done((bf16[16,6144]{1,0:T(8,128)(2,1)S(1)}, bf16[16,6144]{1,0:T(8,128)(2,1)S(1)}, u32[]{:S(2)}, u32[]{:S(2)}) %collective-permute-start.1) | collective-permute-done | bytes 196640 | tf_op jit(solution)/shard_map/gather_swrap/ppermute | solution.py:48
  12.7 1.8 %collective-permute-done.2.two = bf16[16,6144]{1,0:T(8,128)(2,1)S(1)} collective-permute-done((bf16[16,6144]{1,0:T(8,128)(2,1)S(1)}, bf16[16,6144]{1,0:T(8,128)(2,1)S(1)}, u32[]{:S(2)}, u32[]{:S(2)}) %collective-permute-start.2) | collective-permute-done | bytes 196640 | tf_op jit(solution)/shard_map/gather_sfar/ppermute | solution.py:48
  14.5 0.3 collective-permute-start.6
  14.8 1.0 %collective-permute-start.5 = (bf16[32,6144]{1,0:T(8,128)(2,1)S(1)}, bf16[32,6144]{1,0:T(8,128)(2,1)S(1)}, u32[]{:S(2)}, u32[]{:S(2)}) collective-permute-start(bf16[32,6144]{1,0:T(8,128)(2,1)S(1)} %pack.3.after.args_1_), channel_id=1, source_target_pairs={{0,64},{8,24},{16,80},{24,8},{32,96},{40,56},{48,112},{56,40},{64,... | collective-permute-start | bytes 1179656 | tf_op jit(solution)/shard_map/gather_tnear/ppermute | solution.py:48
  15.8 2.4 %collective-permute-done.4.refs_1_.args_4_ = bf16[32,6144]{1,0:T(8,128)(2,1)S(1)} collective-permute-done((bf16[32,6144]{1,0:T(8,128)(2,1)S(1)}, bf16[32,6144]{1,0:T(8,128)(2,1)S(1)}, u32[]{:S(2)}, u32[]{:S(2)}) %collective-permute-start.4) | collective-permute-done | bytes 393248 | tf_op jit(solution)/shard_map/gather_twrap/ppermute | solution.py:48
  18.2 0.0 collective-permute-done.3.refs_0_
  18.2 2.0 %collective-permute-start.7 = (bf16[32,6144]{1,0:T(8,128)(2,1)S(1)}, bf16[32,6144]{1,0:T(8,128)(2,1)S(1)}, u32[]{:S(2)}, u32[]{:S(2)}) collective-permute-start(bf16[32,6144]{1,0:T(8,128)(2,1)S(1)} %hand.2.args_2_), channel_id=1, source_target_pairs={{0,192},{8,56},{16,208},{24,40},{32,224},{40,24},{48,240},{56,8},{... | collective-permute-start | bytes 1179656 | tf_op jit(solution)/shard_map/gather2_twrap/ppermute | solution.py:48
  20.2 3.3 %collective-permute-done.6.args_5_ = bf16[32,6144]{1,0:T(8,128)(2,1)S(1)} collective-permute-done((bf16[32,6144]{1,0:T(8,128)(2,1)S(1)}, bf16[32,6144]{1,0:T(8,128)(2,1)S(1)}, u32[]{:S(2)}, u32[]{:S(2)}) %collective-permute-start.6) | collective-permute-done | bytes 393248 | tf_op jit(solution)/shard_map/gather_twrap/ppermute | solution.py:48
  23.6 0.0 collective-permute-done.9.args_9_.refs_1_
  23.6 0.1 collective-permute-start.10
  23.7 2.6 %fetch.1.args_8_ = bf16[448,6144]{1,0:T(8,128)(2,1)S(1)} custom-call(bf16[448,6144]{1,0:T(8,128)(2,1)} %bitcast.6, bf16[32,6144]{1,0:T(8,128)(2,1)S(1)} %pack.3.after.args_1_), custom_call_target="tpu_custom_call" | custom-call | flops 99999997952 | bytes 11010048 | tf_op jit(solution)/shard_map/fetch/pallas_call | solution.py:156
  26.3 0.0 collective-permute-done.5.args_3_
  26.3 1.5 %collective-permute-done.7.args_6_ = bf16[32,6144]{1,0:T(8,128)(2,1)S(1)} collective-permute-done((bf16[32,6144]{1,0:T(8,128)(2,1)S(1)}, bf16[32,6144]{1,0:T(8,128)(2,1)S(1)}, u32[]{:S(2)}, u32[]{:S(2)}) %collective-permute-start.7) | collective-permute-done | bytes 393248 | tf_op jit(solution)/shard_map/gather2_twrap/ppermute | solution.py:48
  27.8 3.6 %collective-permute-done.8.args_7_ = bf16[32,6144]{1,0:T(8,128)(2,1)S(1)} collective-permute-done((bf16[32,6144]{1,0:T(8,128)(2,1)S(1)}, bf16[32,6144]{1,0:T(8,128)(2,1)S(1)}, u32[]{:S(2)}, u32[]{:S(2)}) %collective-permute-start.8) | collective-permute-done | bytes 393248 | tf_op jit(solution)/shard_map/gather2_tnear/ppermute | solution.py:48
  31.4 3.6 %up.1.hidden = bf16[256,896]{1,0:T(8,128)(2,1)S(1)} custom-call(bf16[32,6144]{1,0:T(8,128)(2,1)S(1)} %pack.2.args_0_, bf16[32,6144]{1,0:T(8,128)(2,1)S(1)} %pack.3.after.args_1_, bf16[32,6144]{1,0:T(8,128)(2,1)S(1)} %hand.2.args_2_, bf16[32,6144]{1,0:T(8,128)(2,1)S(1)} %collective-permute-done.5.args_3_, ...), custom_call_target="tpu_custom_call" | custom-call | flops 2818572288 | bytes 3145728 | tf_op jit(solution)/shard_map/up/pallas_call | solution.py:191
  35.0 0.0 collective-permute-done.10.two
  35.0 2.2 %down.5 = (bf16[32,6144]{1,0:T(8,128)(2,1)S(1)}, bf16[32,6144]{1,0:T(8,128)(2,1)S(1)}) custom-call(bf16[256,896]{1,0:T(8,128)(2,1)S(1)} %up.1.hidden, bf16[448,6144]{1,0:T(8,128)(2,1)S(1)} %hand.3.one, bf16[448,6144]{1,0:T(8,128)(2,1)S(1)} %collective-permute-done.10.two), custom_call_target="tpu_custom_call" | custom-call | flops 704643072 | bytes 786432 | tf_op jit(solution)/shard_map/down/pallas_call | solution.py:221
  37.1 2.1 %collective-permute-start.13 = (bf16[32,6144]{1,0:T(8,128)(2,1)S(1)}, bf16[32,6144]{1,0:T(8,128)(2,1)S(1)}, u32[]{:S(2)}, u32[]{:S(2)}) collective-permute-start(bf16[32,6144]{1,0:T(8,128)(2,1)S(1)} %get-tuple-element.28), channel_id=1, source_target_pairs={{0,48},{8,200},{16,32},{24,216},{32,16},{40,232},{48,0},{56,248},{... | collective-permute-start | bytes 1179656 | tf_op jit(solution)/shard_map/reduce2_swrap/ppermute | solution.py:48
  39.3 0.0 collective-permute-start.12
  39.3 2.8 %down.4 = (bf16[32,6144]{1,0:T(8,128)(2,1)S(1)}, bf16[32,6144]{1,0:T(8,128)(2,1)S(1)}, bf16[32,6144]{1,0:T(8,128)(2,1)S(1)}, bf16[32,6144]{1,0:T(8,128)(2,1)S(1)...) custom-call(bf16[256,896]{1,0:T(8,128)(2,1)S(1)} %up.1.hidden, bf16[448,6144]{1,0:T(8,128)(2,1)S(1)} %hand.3.one, ...), custom_call_target="tpu_custom_call" | custom-call | flops 2113929216 | bytes 2359296 | tf_op jit(solution)/shard_map/down/pallas_call | solution.py:221
  42.1 2.3 %collective-permute-start.11 = (bf16[32,6144]{1,0:T(8,128)(2,1)S(1)}, bf16[32,6144]{1,0:T(8,128)(2,1)S(1)}, u32[]{:S(2)}, u32[]{:S(2)}) collective-permute-start(bf16[32,6144]{1,0:T(8,128)(2,1)S(1)} %get-tuple-element.24), channel_id=1, source_target_pairs={{0,16},{8,72},{16,0},{24,88},{32,48},{40,104},{48,32},{56,120},{64... | collective-permute-start | bytes 1179656 | tf_op jit(solution)/shard_map/reduce_snear/ppermute | solution.py:48
  44.4 1.2 %collective-permute-start.15 = (bf16[32,6144]{1,0:T(8,128)(2,1)S(1)}, bf16[32,6144]{1,0:T(8,128)(2,1)S(1)}, u32[]{:S(2)}, u32[]{:S(2)}) collective-permute-start(bf16[32,6144]{1,0:T(8,128)(2,1)S(1)} %get-tuple-element.30), channel_id=1, source_target_pairs={{0,48},{8,200},{16,32},{24,216},{32,16},{40,232},{48,0},{56,248},{... | collective-permute-start | bytes 1179656 | tf_op jit(solution)/shard_map/reduce_swrap/ppermute | solution.py:48
  45.6 0.6 collective-permute-done.13.arrived
  46.2 0.1 merge.2.refs_0_
  46.3 0.1 collective-permute-start.16
  46.4 0.6 collective-permute-done.12.arrived
  47.1 0.1 merge.3
  47.1 1.5 %collective-permute-start.14 = (bf16[32,6144]{1,0:T(8,128)(2,1)S(1)}, bf16[32,6144]{1,0:T(8,128)(2,1)S(1)}, u32[]{:S(2)}, u32[]{:S(2)}) collective-permute-start(bf16[32,6144]{1,0:T(8,128)(2,1)S(1)} %merge.3), channel_id=1, source_target_pairs={{0,48},{8,200},{16,32},{24,216},{32,16},{40,232},{48,0},{56,248},{... | collective-permute-start | bytes 1179656 | tf_op jit(solution)/shard_map/reduce_swrap/ppermute | solution.py:48
  48.7 2.6 %collective-permute-done.11.refs_0_.direct = bf16[32,6144]{1,0:T(8,128)(2,1)S(1)} collective-permute-done((bf16[32,6144]{1,0:T(8,128)(2,1)S(1)}, bf16[32,6144]{1,0:T(8,128)(2,1)S(1)}, u32[]{:S(2)}, u32[]{:S(2)}) %collective-permute-start.11) | collective-permute-done | bytes 393248 | tf_op jit(solution)/shard_map/reduce_snear/ppermute | solution.py:48
  51.3 2.1 %collective-permute-done.15.direct = bf16[32,6144]{1,0:T(8,128)(2,1)S(1)} collective-permute-done((bf16[32,6144]{1,0:T(8,128)(2,1)S(1)}, bf16[32,6144]{1,0:T(8,128)(2,1)S(1)}, u32[]{:S(2)}, u32[]{:S(2)}) %collective-permute-start.15) | collective-permute-done | bytes 393248 | tf_op jit(solution)/shard_map/reduce_swrap/ppermute | solution.py:48
  53.4 2.1 %collective-permute-done.16.back = bf16[32,6144]{1,0:T(8,128)(2,1)S(1)} collective-permute-done((bf16[32,6144]{1,0:T(8,128)(2,1)S(1)}, bf16[32,6144]{1,0:T(8,128)(2,1)S(1)}, u32[]{:S(2)}, u32[]{:S(2)}) %collective-permute-start.16) | collective-permute-done | bytes 393248 | tf_op jit(solution)/shard_map/reduce_snear/ppermute | solution.py:48
  55.5 0.1 finish.2
  55.6 0.3 collective-permute-start.17
  55.9 1.9 %collective-permute-start.18 = (bf16[16,6144]{1,0:T(8,128)(2,1)S(1)}, bf16[16,6144]{1,0:T(8,128)(2,1)S(1)}, u32[]{:S(2)}, u32[]{:S(2)}) collective-permute-start(bf16[16,6144]{1,0:T(8,128)(2,1)S(1)} %get-tuple-element.33), channel_id=1, source_target_pairs={{0,128},{8,40},{16,144},{24,56},{32,160},{40,8},{48,176},{56,24},{... | collective-permute-start | bytes 589832 | tf_op jit(solution)/shard_map/home_tfar/ppermute | solution.py:48
  57.8 4.0 %collective-permute-done.14.back = bf16[32,6144]{1,0:T(8,128)(2,1)S(1)} collective-permute-done((bf16[32,6144]{1,0:T(8,128)(2,1)S(1)}, bf16[32,6144]{1,0:T(8,128)(2,1)S(1)}, u32[]{:S(2)}, u32[]{:S(2)}) %collective-permute-start.14) | collective-permute-done | bytes 393248 | tf_op jit(solution)/shard_map/reduce_swrap/ppermute | solution.py:48
  61.8 0.1 finish.3
  61.9 0.1 collective-permute-start.19
  62.7 2.0 %collective-permute-done.17.refs_2_ = bf16[16,6144]{1,0:T(8,128)(2,1)S(1)} collective-permute-done((bf16[16,6144]{1,0:T(8,128)(2,1)S(1)}, bf16[16,6144]{1,0:T(8,128)(2,1)S(1)}, u32[]{:S(2)}, u32[]{:S(2)}) %collective-permute-start.17) | collective-permute-done | bytes 196640 | tf_op jit(solution)/shard_map/home_twrap/ppermute | solution.py:48
  64.7 0.1 collect.1
  64.8 2.9 %collective-permute-done.19 = bf16[16,6144]{1,0:T(8,128)(2,1)S(1)} collective-permute-done((bf16[16,6144]{1,0:T(8,128)(2,1)S(1)}, bf16[16,6144]{1,0:T(8,128)(2,1)S(1)}, u32[]{:S(2)}, u32[]{:S(2)}) %collective-permute-start.19) | collective-permute-done | bytes 196640 | tf_op jit(solution)/shard_map/home_tnear/ppermute | solution.py:48
  67.7 0.8 %select_convert_fusion = bf16[16,6144]{1,0:T(8,128)(2,1)} fusion(f32[16,6144]{1,0:T(8,128)S(1)} %collect.1, bf16[16,6144]{1,0:T(8,128)(2,1)S(1)} %collective-permute-done.19, pred[16]{0:T(512)(128)(4,1)S(1)} %iota_compare_fusion), kind=kLoop, calls=%fused_computation | loop fusion | flops 393216 | bytes 786448 | tf_op jit(solution)/shard_map/convert_element_type | solution.py:362
  (8 shorter events, 0.1 us)
Async XLA Ops:
  0.0 23.6 %collective-permute-start.9 = (bf16[448,6144]{1,0:T(8,128)(2,1)}, bf16[448,6144]{1,0:T(8,128)(2,1)S(1)}, u32[]{:S(2)}, u32[]{:S(2)}) collective-permute-start(bf16[448,6144]{1,0:T(8,128)(2,1)} %bitcast.5), channel_id=1, source_target_pairs={{0,8},{8,0},{16,24},{24,16},{32,40},{40,32},{48,56},{56,48},{64,72... | collective-permute-start | bytes 16515080 | tf_op jit(solution)/shard_map/up_core/ppermute | solution.py:48
  3.4 5.8 %collective-permute-start = (bf16[16,6144]{1,0:T(8,128)(2,1)S(1)}, bf16[16,6144]{1,0:T(8,128)(2,1)S(1)}, u32[]{:S(2)}, u32[]{:S(2)}) collective-permute-start(bf16[16,6144]{1,0:T(8,128)(2,1)S(1)} %get-tuple-element.21.one), channel_id=1, source_target_pairs={{0,16},{8,72},{16,0},{24,88},{32,48},{40,104},{48,32},{56,120},{64... | collective-permute-start | bytes 589832 | tf_op jit(solution)/shard_map/gather_snear/ppermute | solution.py:48
  4.9 7.7 %collective-permute-start.1 = (bf16[16,6144]{1,0:T(8,128)(2,1)S(1)}, bf16[16,6144]{1,0:T(8,128)(2,1)S(1)}, u32[]{:S(2)}, u32[]{:S(2)}) collective-permute-start(bf16[16,6144]{1,0:T(8,128)(2,1)S(1)} %get-tuple-element.21.one), channel_id=1, source_target_pairs={{0,48},{8,200},{16,32},{24,216},{32,16},{40,232},{48,0},{56,248},{... | collective-permute-start | bytes 589832 | tf_op jit(solution)/shard_map/gather_swrap/ppermute | solution.py:48
  7.0 7.4 %collective-permute-start.2 = (bf16[16,6144]{1,0:T(8,128)(2,1)S(1)}, bf16[16,6144]{1,0:T(8,128)(2,1)S(1)}, u32[]{:S(2)}, u32[]{:S(2)}) collective-permute-start(bf16[16,6144]{1,0:T(8,128)(2,1)S(1)} %get-tuple-element.21.one), channel_id=1, source_target_pairs={{0,32},{8,136},{16,48},{24,152},{32,0},{40,168},{48,16},{56,184},{... | collective-permute-start | bytes 589832 | tf_op jit(solution)/shard_map/gather_sfar/ppermute | solution.py:48
  9.1 9.1 %collective-permute-start.4 = (bf16[32,6144]{1,0:T(8,128)(2,1)S(1)}, bf16[32,6144]{1,0:T(8,128)(2,1)S(1)}, u32[]{:S(2)}, u32[]{:S(2)}) collective-permute-start(bf16[32,6144]{1,0:T(8,128)(2,1)S(1)} %pack.2.args_0_), channel_id=1, source_target_pairs={{0,192},{8,56},{16,208},{24,40},{32,224},{40,24},{48,240},{56,8},{... | collective-permute-start | bytes 1179656 | tf_op jit(solution)/shard_map/gather_twrap/ppermute | solution.py:48
  9.5 8.8 %collective-permute-start.3 = (bf16[32,6144]{1,0:T(8,128)(2,1)S(1)}, bf16[32,6144]{1,0:T(8,128)(2,1)S(1)}, u32[]{:S(2)}, u32[]{:S(2)}) collective-permute-start(bf16[32,6144]{1,0:T(8,128)(2,1)S(1)} %pack.2.args_0_), channel_id=1, source_target_pairs={{0,64},{8,24},{16,80},{24,8},{32,96},{40,56},{48,112},{56,40},{64,... | collective-permute-start | bytes 1179656 | tf_op jit(solution)/shard_map/gather_tnear/ppermute | solution.py:48
  14.5 9.1 %collective-permute-start.6 = (bf16[32,6144]{1,0:T(8,128)(2,1)S(1)}, bf16[32,6144]{1,0:T(8,128)(2,1)S(1)}, u32[]{:S(2)}, u32[]{:S(2)}) collective-permute-start(bf16[32,6144]{1,0:T(8,128)(2,1)S(1)} %pack.3.after.args_1_), channel_id=1, source_target_pairs={{0,192},{8,56},{16,208},{24,40},{32,224},{40,24},{48,240},{56,8},{... | collective-permute-start | bytes 1179656 | tf_op jit(solution)/shard_map/gather_twrap/ppermute | solution.py:48
  14.8 11.5 %collective-permute-start.5 = (bf16[32,6144]{1,0:T(8,128)(2,1)S(1)}, bf16[32,6144]{1,0:T(8,128)(2,1)S(1)}, u32[]{:S(2)}, u32[]{:S(2)}) collective-permute-start(bf16[32,6144]{1,0:T(8,128)(2,1)S(1)} %pack.3.after.args_1_), channel_id=1, source_target_pairs={{0,64},{8,24},{16,80},{24,8},{32,96},{40,56},{48,112},{56,40},{64,... | collective-permute-start | bytes 1179656 | tf_op jit(solution)/shard_map/gather_tnear/ppermute | solution.py:48
  18.2 9.6 %collective-permute-start.7 = (bf16[32,6144]{1,0:T(8,128)(2,1)S(1)}, bf16[32,6144]{1,0:T(8,128)(2,1)S(1)}, u32[]{:S(2)}, u32[]{:S(2)}) collective-permute-start(bf16[32,6144]{1,0:T(8,128)(2,1)S(1)} %hand.2.args_2_), channel_id=1, source_target_pairs={{0,192},{8,56},{16,208},{24,40},{32,224},{40,24},{48,240},{56,8},{... | collective-permute-start | bytes 1179656 | tf_op jit(solution)/shard_map/gather2_twrap/ppermute | solution.py:48
  23.6 7.8 %collective-permute-start.8 = (bf16[32,6144]{1,0:T(8,128)(2,1)S(1)}, bf16[32,6144]{1,0:T(8,128)(2,1)S(1)}, u32[]{:S(2)}, u32[]{:S(2)}) collective-permute-start(bf16[32,6144]{1,0:T(8,128)(2,1)S(1)} %collective-permute-done.6.args_5_), channel_id=1, source_target_pairs={{0,64},{8,24},{16,80},{24,8},{32,96},{40,56},{48,112},{56,40},{64,... | collective-permute-start | bytes 1179656 | tf_op jit(solution)/shard_map/gather2_tnear/ppermute | solution.py:48
  23.6 11.4 %collective-permute-start.10 = (bf16[448,6144]{1,0:T(8,128)(2,1)S(1)}, bf16[448,6144]{1,0:T(8,128)(2,1)S(1)}, u32[]{:S(2)}, u32[]{:S(2)}) collective-permute-start(bf16[448,6144]{1,0:T(8,128)(2,1)S(1)} %hand.3.one), channel_id=1, source_target_pairs={{0,8},{8,0},{16,24},{24,16},{32,40},{40,32},{48,56},{56,48},{64,72... | collective-permute-start | bytes 16515080 | tf_op jit(solution)/shard_map/down_core/ppermute | solution.py:48
  37.1 9.1 %collective-permute-start.13 = (bf16[32,6144]{1,0:T(8,128)(2,1)S(1)}, bf16[32,6144]{1,0:T(8,128)(2,1)S(1)}, u32[]{:S(2)}, u32[]{:S(2)}) collective-permute-start(bf16[32,6144]{1,0:T(8,128)(2,1)S(1)} %get-tuple-element.28), channel_id=1, source_target_pairs={{0,48},{8,200},{16,32},{24,216},{32,16},{40,232},{48,0},{56,248},{... | collective-permute-start | bytes 1179656 | tf_op jit(solution)/shard_map/reduce2_swrap/ppermute | solution.py:48
  39.3 7.8 %collective-permute-start.12 = (bf16[32,6144]{1,0:T(8,128)(2,1)S(1)}, bf16[32,6144]{1,0:T(8,128)(2,1)S(1)}, u32[]{:S(2)}, u32[]{:S(2)}) collective-permute-start(bf16[32,6144]{1,0:T(8,128)(2,1)S(1)} %get-tuple-element.26), channel_id=1, source_target_pairs={{0,16},{8,72},{16,0},{24,88},{32,48},{40,104},{48,32},{56,120},{64... | collective-permute-start | bytes 1179656 | tf_op jit(solution)/shard_map/reduce2_snear/ppermute | solution.py:48
  42.1 9.2 %collective-permute-start.11 = (bf16[32,6144]{1,0:T(8,128)(2,1)S(1)}, bf16[32,6144]{1,0:T(8,128)(2,1)S(1)}, u32[]{:S(2)}, u32[]{:S(2)}) collective-permute-start(bf16[32,6144]{1,0:T(8,128)(2,1)S(1)} %get-tuple-element.24), channel_id=1, source_target_pairs={{0,16},{8,72},{16,0},{24,88},{32,48},{40,104},{48,32},{56,120},{64... | collective-permute-start | bytes 1179656 | tf_op jit(solution)/shard_map/reduce_snear/ppermute | solution.py:48
  44.4 9.0 %collective-permute-start.15 = (bf16[32,6144]{1,0:T(8,128)(2,1)S(1)}, bf16[32,6144]{1,0:T(8,128)(2,1)S(1)}, u32[]{:S(2)}, u32[]{:S(2)}) collective-permute-start(bf16[32,6144]{1,0:T(8,128)(2,1)S(1)} %get-tuple-element.30), channel_id=1, source_target_pairs={{0,48},{8,200},{16,32},{24,216},{32,16},{40,232},{48,0},{56,248},{... | collective-permute-start | bytes 1179656 | tf_op jit(solution)/shard_map/reduce_swrap/ppermute | solution.py:48
  46.3 9.2 %collective-permute-start.16 = (bf16[32,6144]{1,0:T(8,128)(2,1)S(1)}, bf16[32,6144]{1,0:T(8,128)(2,1)S(1)}, u32[]{:S(2)}, u32[]{:S(2)}) collective-permute-start(bf16[32,6144]{1,0:T(8,128)(2,1)S(1)} %merge.2.refs_0_), channel_id=1, source_target_pairs={{0,16},{8,72},{16,0},{24,88},{32,48},{40,104},{48,32},{56,120},{64... | collective-permute-start | bytes 1179656 | tf_op jit(solution)/shard_map/reduce_snear/ppermute | solution.py:48
  47.1 14.7 %collective-permute-start.14 = (bf16[32,6144]{1,0:T(8,128)(2,1)S(1)}, bf16[32,6144]{1,0:T(8,128)(2,1)S(1)}, u32[]{:S(2)}, u32[]{:S(2)}) collective-permute-start(bf16[32,6144]{1,0:T(8,128)(2,1)S(1)} %merge.3), channel_id=1, source_target_pairs={{0,48},{8,200},{16,32},{24,216},{32,16},{40,232},{48,0},{56,248},{... | collective-permute-start | bytes 1179656 | tf_op jit(solution)/shard_map/reduce_swrap/ppermute | solution.py:48
  55.6 9.1 %collective-permute-start.17 = (bf16[16,6144]{1,0:T(8,128)(2,1)S(1)}, bf16[16,6144]{1,0:T(8,128)(2,1)S(1)}, u32[]{:S(2)}, u32[]{:S(2)}) collective-permute-start(bf16[16,6144]{1,0:T(8,128)(2,1)S(1)} %get-tuple-element.31.refs_0_), channel_id=1, source_target_pairs={{0,192},{8,56},{16,208},{24,40},{32,224},{40,24},{48,240},{56,8},{... | collective-permute-start | bytes 589832 | tf_op jit(solution)/shard_map/home_twrap/ppermute | solution.py:48
  55.9 8.8 %collective-permute-start.18 = (bf16[16,6144]{1,0:T(8,128)(2,1)S(1)}, bf16[16,6144]{1,0:T(8,128)(2,1)S(1)}, u32[]{:S(2)}, u32[]{:S(2)}) collective-permute-start(bf16[16,6144]{1,0:T(8,128)(2,1)S(1)} %get-tuple-element.33), channel_id=1, source_target_pairs={{0,128},{8,40},{16,144},{24,56},{32,160},{40,8},{48,176},{56,24},{... | collective-permute-start | bytes 589832 | tf_op jit(solution)/shard_map/home_tfar/ppermute | solution.py:48
  61.9 5.8 %collective-permute-start.19 = (bf16[16,6144]{1,0:T(8,128)(2,1)S(1)}, bf16[16,6144]{1,0:T(8,128)(2,1)S(1)}, u32[]{:S(2)}, u32[]{:S(2)}) collective-permute-start(bf16[16,6144]{1,0:T(8,128)(2,1)S(1)} %get-tuple-element.34), channel_id=1, source_target_pairs={{0,64},{8,24},{16,80},{24,8},{32,96},{40,56},{48,112},{56,40},{64,... | collective-permute-start | bytes 589832 | tf_op jit(solution)/shard_map/home_tnear/ppermute | solution.py:48

commit v13 on v12

--- a/solution.py
+++ b/solution.py
@@ -345,14 +345,14 @@
     down = (down_held, down_other)
     early_f, late_f = project_down(hidden, down, 6, 8)
     early, late, early_n, late_n, early_w, late_w = project_down(hidden, down, 0, 6)
-    far_late = send(late_f, "swrap", "reduce2")
-    far_early = send(early_f, "snear", "reduce2")
-    direct_late = send(late_w, "swrap", "reduce")
-    (late_n,) = merge(late_n, far_late)
-    back_late = send(late_n, "snear", "reduce")
-    direct_early = send(early_n, "snear", "reduce")
-    (early_w,) = merge(early_w, far_early, after=(late_n,))
-    back_early = send(early_w, "swrap", "reduce")
+    far_late = send(late_f, "snear", "reduce2")
+    far_early = send(early_f, "swrap", "reduce2")
+    direct_late = send(late_n, "snear", "reduce")
+    direct_early = send(early_w, "swrap", "reduce")
+    (late_w,) = merge(late_w, far_late)
+    back_late = send(late_w, "swrap", "reduce")
+    (early_n,) = merge(early_n, far_early, after=(late_w,))
+    back_early = send(early_n, "snear", "reduce")
     home_wrap, home_far = finish(late, direct_late, back_late, jnp.bfloat16, after=(direct_early,))
     own, home_near = finish(early, direct_early, back_early, jnp.float32, after=(home_wrap,))
     home_wrap, home_far = send(home_wrap, "twrap", "home"), send(home_far, "tfar", "home")

time: 68.6 us -> 67.4 us (0.983)
  the two profiles are of different devices: /device:TPU:152 before, /device:TPU:128 now
where the time goes in v13:
time: 67.4 us; the launch traced here: 67.2 us
  waiting for transfers between devices  26.9 us (40%)
  starting transfers between devices  23.7 us (35%)
  Pallas kernels  15.1 us (22%)
  other arithmetic  0.77 us (1%)
  between operations  0.77 us (1%)
    ppermute x20, waiting for transfers between devices, send(): return lax.ppermute(value, 'dp', ROUTES[route])  26.9 us
    ppermute x20, starting transfers between devices, send(): return lax.ppermute(value, 'dp', ROUTES[route])  23.7 us
    pallas_call x2, Pallas kernels, project_down(): pl.pallas_call(functools.partial(down_kernel, begin), out_shape=[jax.Shap...  4.98 us
    pallas_call x1, Pallas kernels, project_up(): pl.pallas_call(up_kernel, out_shape=jax.ShapeDtypeStruct((rows, 2 * HIDDE...  3.58 us
    pallas_call x1, Pallas kernels, attend(): pl.pallas_call(attend_kernel, out_shape=(jax.ShapeDtypeStruct((SLOTS, D),...  3.34 us
    pallas_call x1, Pallas kernels, fetch(): pl.pallas_call(fetch_kernel, out_shape=jax.ShapeDtypeStruct((HIDDEN, D),...  2.57 us
  transfers between devices with their start and end apart: 20, of which 14 were waited for; matrix products, arithmetic and copies ran while one was open for 0% of the time, Pallas kernels for 19%

profile of v13, /device:TPU:128, one launch (start us, length us, event | category | flops | bytes accessed | tf_op | source)
XLA Modules:
  0.0 67.2 jit_solution(2676153393906852232)
XLA Ops:
  0.0 0.0 collective-permute-start.9
  0.0 3.3 %attend.1 = (bf16[16,6144]{1,0:T(8,128)(2,1)S(1)}, bf16[16,6144]{1,0:T(8,128)(2,1)S(1)}, bf16[448,6144]{1,0:T(8,128)(2,1)S(1)}) custom-call(s32[16]{0:T(128)} %lengths_in.1, bf16[16,6144]{1,0:T(8,128)(2,1)} %q_in.1, bf16[1024,512]{1,0:T(8,128)(2,1)} %k_in.1, bf16[1024,512]{1,0:T(8,128)(2,1)} %v_in.1, f32[1,6144]{1,0:T(1,128)} %bitcast.4, bf16[448,6144]{1,0:T(8,128)(2,1)} %down.3), custom_call_target="tpu_custom_call" | custom-call | tf_op jit(solution)/shard_map/attend/pallas_call | solution.py:126
  3.4 1.6 %collective-permute-start = (bf16[16,6144]{1,0:T(8,128)(2,1)S(1)}, bf16[16,6144]{1,0:T(8,128)(2,1)S(1)}, u32[]{:S(2)}, u32[]{:S(2)}) collective-permute-start(bf16[16,6144]{1,0:T(8,128)(2,1)S(1)} %get-tuple-element.21.one), channel_id=1, source_target_pairs={{0,16},{8,72},{16,0},{24,88},{32,48},{40,104},{48,32},{56,120},{64... | collective-permute-start | bytes 589832 | tf_op jit(solution)/shard_map/gather_snear/ppermute | solution.py:48
  4.9 2.1 %collective-permute-start.1 = (bf16[16,6144]{1,0:T(8,128)(2,1)S(1)}, bf16[16,6144]{1,0:T(8,128)(2,1)S(1)}, u32[]{:S(2)}, u32[]{:S(2)}) collective-permute-start(bf16[16,6144]{1,0:T(8,128)(2,1)S(1)} %get-tuple-element.21.one), channel_id=1, source_target_pairs={{0,48},{8,200},{16,32},{24,216},{32,16},{40,232},{48,0},{56,248},{... | collective-permute-start | bytes 589832 | tf_op jit(solution)/shard_map/gather_swrap/ppermute | solution.py:48
  7.0 0.6 collective-permute-start.2
  7.7 1.4 %collective-permute-done.two = bf16[16,6144]{1,0:T(8,128)(2,1)S(1)} collective-permute-done((bf16[16,6144]{1,0:T(8,128)(2,1)S(1)}, bf16[16,6144]{1,0:T(8,128)(2,1)S(1)}, u32[]{:S(2)}, u32[]{:S(2)}) %collective-permute-start) | collective-permute-done | bytes 196640 | tf_op jit(solution)/shard_map/gather_snear/ppermute | solution.py:48
  9.1 3.1 %collective-permute-start.4 = (bf16[32,6144]{1,0:T(8,128)(2,1)S(1)}, bf16[32,6144]{1,0:T(8,128)(2,1)S(1)}, u32[]{:S(2)}, u32[]{:S(2)}) collective-permute-start(bf16[32,6144]{1,0:T(8,128)(2,1)S(1)} %pack.2.args_0_), channel_id=1, source_target_pairs={{0,192},{8,56},{16,208},{24,40},{32,224},{40,24},{48,240},{56,8},{... | collective-permute-start | bytes 1179656 | tf_op jit(solution)/shard_map/gather_twrap/ppermute | solution.py:48
  12.2 0.1 collective-permute-start.3
  12.4 0.3 collective-permute-done.1.one
  12.7 1.8 %collective-permute-done.2.two = bf16[16,6144]{1,0:T(8,128)(2,1)S(1)} collective-permute-done((bf16[16,6144]{1,0:T(8,128)(2,1)S(1)}, bf16[16,6144]{1,0:T(8,128)(2,1)S(1)}, u32[]{:S(2)}, u32[]{:S(2)}) %collective-permute-start.2) | collective-permute-done | bytes 196640 | tf_op jit(solution)/shard_map/gather_sfar/ppermute | solution.py:48
  14.5 3.1 %collective-permute-start.6 = (bf16[32,6144]{1,0:T(8,128)(2,1)S(1)}, bf16[32,6144]{1,0:T(8,128)(2,1)S(1)}, u32[]{:S(2)}, u32[]{:S(2)}) collective-permute-start(bf16[32,6144]{1,0:T(8,128)(2,1)S(1)} %pack.3.after.args_1_), channel_id=1, source_target_pairs={{0,192},{8,56},{16,208},{24,40},{32,224},{40,24},{48,240},{56,8},{... | collective-permute-start | bytes 1179656 | tf_op jit(solution)/shard_map/gather_twrap/ppermute | solution.py:48
  17.6 0.1 collective-permute-start.5
  17.7 0.5 collective-permute-done.4.refs_1_.args_4_
  18.2 1.8 %collective-permute-done.3.refs_0_ = bf16[32,6144]{1,0:T(8,128)(2,1)S(1)} collective-permute-done((bf16[32,6144]{1,0:T(8,128)(2,1)S(1)}, bf16[32,6144]{1,0:T(8,128)(2,1)S(1)}, u32[]{:S(2)}, u32[]{:S(2)}) %collective-permute-start.3) | collective-permute-done | bytes 393248 | tf_op jit(solution)/shard_map/gather_tnear/ppermute | solution.py:48
  20.0 1.2 %collective-permute-start.7 = (bf16[32,6144]{1,0:T(8,128)(2,1)S(1)}, bf16[32,6144]{1,0:T(8,128)(2,1)S(1)}, u32[]{:S(2)}, u32[]{:S(2)}) collective-permute-start(bf16[32,6144]{1,0:T(8,128)(2,1)S(1)} %hand.2.args_2_), channel_id=1, source_target_pairs={{0,192},{8,56},{16,208},{24,40},{32,224},{40,24},{48,240},{56,8},{... | collective-permute-start | bytes 1179656 | tf_op jit(solution)/shard_map/gather2_twrap/ppermute | solution.py:48
  21.2 2.3 %collective-permute-done.6.args_5_ = bf16[32,6144]{1,0:T(8,128)(2,1)S(1)} collective-permute-done((bf16[32,6144]{1,0:T(8,128)(2,1)S(1)}, bf16[32,6144]{1,0:T(8,128)(2,1)S(1)}, u32[]{:S(2)}, u32[]{:S(2)}) %collective-permute-start.6) | collective-permute-done | bytes 393248 | tf_op jit(solution)/shard_map/gather_twrap/ppermute | solution.py:48
  23.6 0.4 collective-permute-start.8
  23.9 0.0 collective-permute-done.9.args_9_.refs_1_
  23.9 0.0 collective-permute-start.10
  24.0 2.6 %fetch.1.args_8_ = bf16[448,6144]{1,0:T(8,128)(2,1)S(1)} custom-call(bf16[448,6144]{1,0:T(8,128)(2,1)} %bitcast.6, bf16[32,6144]{1,0:T(8,128)(2,1)S(1)} %pack.3.after.args_1_), custom_call_target="tpu_custom_call" | custom-call | flops 99999997952 | bytes 11010048 | tf_op jit(solution)/shard_map/fetch/pallas_call | solution.py:156
  26.5 0.0 collective-permute-done.5.args_3_
  26.5 2.5 %collective-permute-done.7.args_6_ = bf16[32,6144]{1,0:T(8,128)(2,1)S(1)} collective-permute-done((bf16[32,6144]{1,0:T(8,128)(2,1)S(1)}, bf16[32,6144]{1,0:T(8,128)(2,1)S(1)}, u32[]{:S(2)}, u32[]{:S(2)}) %collective-permute-start.7) | collective-permute-done | bytes 393248 | tf_op jit(solution)/shard_map/gather2_twrap/ppermute | solution.py:48
  29.0 2.3 %collective-permute-done.8.args_7_ = bf16[32,6144]{1,0:T(8,128)(2,1)S(1)} collective-permute-done((bf16[32,6144]{1,0:T(8,128)(2,1)S(1)}, bf16[32,6144]{1,0:T(8,128)(2,1)S(1)}, u32[]{:S(2)}, u32[]{:S(2)}) %collective-permute-start.8) | collective-permute-done | bytes 393248 | tf_op jit(solution)/shard_map/gather2_tnear/ppermute | solution.py:48
  31.4 3.6 %up.1.hidden = bf16[256,896]{1,0:T(8,128)(2,1)S(1)} custom-call(bf16[32,6144]{1,0:T(8,128)(2,1)S(1)} %pack.2.args_0_, bf16[32,6144]{1,0:T(8,128)(2,1)S(1)} %pack.3.after.args_1_, bf16[32,6144]{1,0:T(8,128)(2,1)S(1)} %hand.2.args_2_, bf16[32,6144]{1,0:T(8,128)(2,1)S(1)} %collective-permute-done.5.args_3_, ...), custom_call_target="tpu_custom_call" | custom-call | flops 2818572288 | bytes 3145728 | tf_op jit(solution)/shard_map/up/pallas_call | solution.py:191
  35.0 2.2 %down.5 = (bf16[32,6144]{1,0:T(8,128)(2,1)S(1)}, bf16[32,6144]{1,0:T(8,128)(2,1)S(1)}) custom-call(bf16[256,896]{1,0:T(8,128)(2,1)S(1)} %up.1.hidden, bf16[448,6144]{1,0:T(8,128)(2,1)S(1)} %hand.3.one, bf16[448,6144]{1,0:T(8,128)(2,1)S(1)} %collective-permute-done.10.two), custom_call_target="tpu_custom_call" | custom-call | flops 704643072 | bytes 786432 | tf_op jit(solution)/shard_map/down/pallas_call | solution.py:221
  37.1 1.0 %collective-permute-start.13 = (bf16[32,6144]{1,0:T(8,128)(2,1)S(1)}, bf16[32,6144]{1,0:T(8,128)(2,1)S(1)}, u32[]{:S(2)}, u32[]{:S(2)}) collective-permute-start(bf16[32,6144]{1,0:T(8,128)(2,1)S(1)} %get-tuple-element.28), channel_id=1, source_target_pairs={{0,16},{8,72},{16,0},{24,88},{32,48},{40,104},{48,32},{56,120},{64... | collective-permute-start | bytes 1179656 | tf_op jit(solution)/shard_map/reduce2_snear/ppermute | solution.py:48
  38.1 1.5 %collective-permute-start.12 = (bf16[32,6144]{1,0:T(8,128)(2,1)S(1)}, bf16[32,6144]{1,0:T(8,128)(2,1)S(1)}, u32[]{:S(2)}, u32[]{:S(2)}) collective-permute-start(bf16[32,6144]{1,0:T(8,128)(2,1)S(1)} %get-tuple-element.26), channel_id=1, source_target_pairs={{0,48},{8,200},{16,32},{24,216},{32,16},{40,232},{48,0},{56,248},{... | collective-permute-start | bytes 1179656 | tf_op jit(solution)/shard_map/reduce2_swrap/ppermute | solution.py:48
  39.7 2.8 %down.4 = (bf16[32,6144]{1,0:T(8,128)(2,1)S(1)}, bf16[32,6144]{1,0:T(8,128)(2,1)S(1)}, bf16[32,6144]{1,0:T(8,128)(2,1)S(1)}, bf16[32,6144]{1,0:T(8,128)(2,1)S(1)...) custom-call(bf16[256,896]{1,0:T(8,128)(2,1)S(1)} %up.1.hidden, bf16[448,6144]{1,0:T(8,128)(2,1)S(1)} %hand.3.one, ...), custom_call_target="tpu_custom_call" | custom-call | flops 2113929216 | bytes 2359296 | tf_op jit(solution)/shard_map/down/pallas_call | solution.py:221
  42.5 2.0 %collective-permute-start.11 = (bf16[32,6144]{1,0:T(8,128)(2,1)S(1)}, bf16[32,6144]{1,0:T(8,128)(2,1)S(1)}, u32[]{:S(2)}, u32[]{:S(2)}) collective-permute-start(bf16[32,6144]{1,0:T(8,128)(2,1)S(1)} %get-tuple-element.24), channel_id=1, source_target_pairs={{0,48},{8,200},{16,32},{24,216},{32,16},{40,232},{48,0},{56,248},{... | collective-permute-start | bytes 1179656 | tf_op jit(solution)/shard_map/reduce_swrap/ppermute | solution.py:48
  44.5 0.5 collective-permute-done.13.arrived
  45.0 0.1 merge.2.refs_0_
  45.1 2.1 %collective-permute-start.16 = (bf16[32,6144]{1,0:T(8,128)(2,1)S(1)}, bf16[32,6144]{1,0:T(8,128)(2,1)S(1)}, u32[]{:S(2)}, u32[]{:S(2)}) collective-permute-start(bf16[32,6144]{1,0:T(8,128)(2,1)S(1)} %merge.2.refs_0_), channel_id=1, source_target_pairs={{0,48},{8,200},{16,32},{24,216},{32,16},{40,232},{48,0},{56,248},{... | collective-permute-start | bytes 1179656 | tf_op jit(solution)/shard_map/reduce_swrap/ppermute | solution.py:48
  47.2 0.1 merge.3
  47.3 0.5 collective-permute-start.14
  47.8 4.0 %collective-permute-done.11.refs_0_.direct = bf16[32,6144]{1,0:T(8,128)(2,1)S(1)} collective-permute-done((bf16[32,6144]{1,0:T(8,128)(2,1)S(1)}, bf16[32,6144]{1,0:T(8,128)(2,1)S(1)}, u32[]{:S(2)}, u32[]{:S(2)}) %collective-permute-start.11) | collective-permute-done | bytes 393248 | tf_op jit(solution)/shard_map/reduce_swrap/ppermute | solution.py:48
  51.7 0.5 collective-permute-done.15.direct
  52.2 3.7 %collective-permute-done.16.back = bf16[32,6144]{1,0:T(8,128)(2,1)S(1)} collective-permute-done((bf16[32,6144]{1,0:T(8,128)(2,1)S(1)}, bf16[32,6144]{1,0:T(8,128)(2,1)S(1)}, u32[]{:S(2)}, u32[]{:S(2)}) %collective-permute-start.16) | collective-permute-done | bytes 393248 | tf_op jit(solution)/shard_map/reduce_swrap/ppermute | solution.py:48
  56.0 0.1 finish.2
  56.1 3.1 %collective-permute-start.17 = (bf16[16,6144]{1,0:T(8,128)(2,1)S(1)}, bf16[16,6144]{1,0:T(8,128)(2,1)S(1)}, u32[]{:S(2)}, u32[]{:S(2)}) collective-permute-start(bf16[16,6144]{1,0:T(8,128)(2,1)S(1)} %get-tuple-element.31.refs_0_), channel_id=1, source_target_pairs={{0,192},{8,56},{16,208},{24,40},{32,224},{40,24},{48,240},{56,8},{... | collective-permute-start | bytes 589832 | tf_op jit(solution)/shard_map/home_twrap/ppermute | solution.py:48
  59.2 0.0 collective-permute-start.18
  59.2 0.0 collective-permute-done.14.back
  59.2 0.1 finish.3
  59.3 1.2 %collective-permute-start.19 = (bf16[16,6144]{1,0:T(8,128)(2,1)S(1)}, bf16[16,6144]{1,0:T(8,128)(2,1)S(1)}, u32[]{:S(2)}, u32[]{:S(2)}) collective-permute-start(bf16[16,6144]{1,0:T(8,128)(2,1)S(1)} %get-tuple-element.34), channel_id=1, source_target_pairs={{0,64},{8,24},{16,80},{24,8},{32,96},{40,56},{48,112},{56,40},{64,... | collective-permute-start | bytes 589832 | tf_op jit(solution)/shard_map/home_tnear/ppermute | solution.py:48
  61.2 3.3 %collective-permute-done.17.refs_2_ = bf16[16,6144]{1,0:T(8,128)(2,1)S(1)} collective-permute-done((bf16[16,6144]{1,0:T(8,128)(2,1)S(1)}, bf16[16,6144]{1,0:T(8,128)(2,1)S(1)}, u32[]{:S(2)}, u32[]{:S(2)}) %collective-permute-start.17) | collective-permute-done | bytes 196640 | tf_op jit(solution)/shard_map/home_twrap/ppermute | solution.py:48
  64.5 1.9 %collective-permute-done.18.refs_3_ = bf16[16,6144]{1,0:T(8,128)(2,1)S(1)} collective-permute-done((bf16[16,6144]{1,0:T(8,128)(2,1)S(1)}, bf16[16,6144]{1,0:T(8,128)(2,1)S(1)}, u32[]{:S(2)}, u32[]{:S(2)}) %collective-permute-start.18) | collective-permute-done | bytes 196640 | tf_op jit(solution)/shard_map/home_tfar/ppermute | solution.py:48
  66.4 0.1 collect.1
  66.5 0.0 collective-permute-done.19
  66.5 0.8 %select_convert_fusion = bf16[16,6144]{1,0:T(8,128)(2,1)} fusion(f32[16,6144]{1,0:T(8,128)S(1)} %collect.1, bf16[16,6144]{1,0:T(8,128)(2,1)S(1)} %collective-permute-done.19, pred[16]{0:T(512)(128)(4,1)S(1)} %iota_compare_fusion), kind=kLoop, calls=%fused_computation | loop fusion | flops 393216 | bytes 786448 | tf_op jit(solution)/shard_map/convert_element_type | solution.py:362
  (8 shorter events, 0.1 us)
Async XLA Ops:
  0.0 23.9 %collective-permute-start.9 = (bf16[448,6144]{1,0:T(8,128)(2,1)}, bf16[448,6144]{1,0:T(8,128)(2,1)S(1)}, u32[]{:S(2)}, u32[]{:S(2)}) collective-permute-start(bf16[448,6144]{1,0:T(8,128)(2,1)} %bitcast.5), channel_id=1, source_target_pairs={{0,8},{8,0},{16,24},{24,16},{32,40},{40,32},{48,56},{56,48},{64,72... | collective-permute-start | bytes 16515080 | tf_op jit(solution)/shard_map/up_core/ppermute | solution.py:48
  3.4 5.8 %collective-permute-start = (bf16[16,6144]{1,0:T(8,128)(2,1)S(1)}, bf16[16,6144]{1,0:T(8,128)(2,1)S(1)}, u32[]{:S(2)}, u32[]{:S(2)}) collective-permute-start(bf16[16,6144]{1,0:T(8,128)(2,1)S(1)} %get-tuple-element.21.one), channel_id=1, source_target_pairs={{0,16},{8,72},{16,0},{24,88},{32,48},{40,104},{48,32},{56,120},{64... | collective-permute-start | bytes 589832 | tf_op jit(solution)/shard_map/gather_snear/ppermute | solution.py:48
  4.9 7.7 %collective-permute-start.1 = (bf16[16,6144]{1,0:T(8,128)(2,1)S(1)}, bf16[16,6144]{1,0:T(8,128)(2,1)S(1)}, u32[]{:S(2)}, u32[]{:S(2)}) collective-permute-start(bf16[16,6144]{1,0:T(8,128)(2,1)S(1)} %get-tuple-element.21.one), channel_id=1, source_target_pairs={{0,48},{8,200},{16,32},{24,216},{32,16},{40,232},{48,0},{56,248},{... | collective-permute-start | bytes 589832 | tf_op jit(solution)/shard_map/gather_swrap/ppermute | solution.py:48
  7.0 7.4 %collective-permute-start.2 = (bf16[16,6144]{1,0:T(8,128)(2,1)S(1)}, bf16[16,6144]{1,0:T(8,128)(2,1)S(1)}, u32[]{:S(2)}, u32[]{:S(2)}) collective-permute-start(bf16[16,6144]{1,0:T(8,128)(2,1)S(1)} %get-tuple-element.21.one), channel_id=1, source_target_pairs={{0,32},{8,136},{16,48},{24,152},{32,0},{40,168},{48,16},{56,184},{... | collective-permute-start | bytes 589832 | tf_op jit(solution)/shard_map/gather_sfar/ppermute | solution.py:48
  9.1 9.1 %collective-permute-start.4 = (bf16[32,6144]{1,0:T(8,128)(2,1)S(1)}, bf16[32,6144]{1,0:T(8,128)(2,1)S(1)}, u32[]{:S(2)}, u32[]{:S(2)}) collective-permute-start(bf16[32,6144]{1,0:T(8,128)(2,1)S(1)} %pack.2.args_0_), channel_id=1, source_target_pairs={{0,192},{8,56},{16,208},{24,40},{32,224},{40,24},{48,240},{56,8},{... | collective-permute-start | bytes 1179656 | tf_op jit(solution)/shard_map/gather_twrap/ppermute | solution.py:48
  12.2 7.8 %collective-permute-start.3 = (bf16[32,6144]{1,0:T(8,128)(2,1)S(1)}, bf16[32,6144]{1,0:T(8,128)(2,1)S(1)}, u32[]{:S(2)}, u32[]{:S(2)}) collective-permute-start(bf16[32,6144]{1,0:T(8,128)(2,1)S(1)} %pack.2.args_0_), channel_id=1, source_target_pairs={{0,64},{8,24},{16,80},{24,8},{32,96},{40,56},{48,112},{56,40},{64,... | collective-permute-start | bytes 1179656 | tf_op jit(solution)/shard_map/gather_tnear/ppermute | solution.py:48
  14.5 9.1 %collective-permute-start.6 = (bf16[32,6144]{1,0:T(8,128)(2,1)S(1)}, bf16[32,6144]{1,0:T(8,128)(2,1)S(1)}, u32[]{:S(2)}, u32[]{:S(2)}) collective-permute-start(bf16[32,6144]{1,0:T(8,128)(2,1)S(1)} %pack.3.after.args_1_), channel_id=1, source_target_pairs={{0,192},{8,56},{16,208},{24,40},{32,224},{40,24},{48,240},{56,8},{... | collective-permute-start | bytes 1179656 | tf_op jit(solution)/shard_map/gather_twrap/ppermute | solution.py:48
  17.6 8.9 %collective-permute-start.5 = (bf16[32,6144]{1,0:T(8,128)(2,1)S(1)}, bf16[32,6144]{1,0:T(8,128)(2,1)S(1)}, u32[]{:S(2)}, u32[]{:S(2)}) collective-permute-start(bf16[32,6144]{1,0:T(8,128)(2,1)S(1)} %pack.3.after.args_1_), channel_id=1, source_target_pairs={{0,64},{8,24},{16,80},{24,8},{32,96},{40,56},{48,112},{56,40},{64,... | collective-permute-start | bytes 1179656 | tf_op jit(solution)/shard_map/gather_tnear/ppermute | solution.py:48
  20.0 9.0 %collective-permute-start.7 = (bf16[32,6144]{1,0:T(8,128)(2,1)S(1)}, bf16[32,6144]{1,0:T(8,128)(2,1)S(1)}, u32[]{:S(2)}, u32[]{:S(2)}) collective-permute-start(bf16[32,6144]{1,0:T(8,128)(2,1)S(1)} %hand.2.args_2_), channel_id=1, source_target_pairs={{0,192},{8,56},{16,208},{24,40},{32,224},{40,24},{48,240},{56,8},{... | collective-permute-start | bytes 1179656 | tf_op jit(solution)/shard_map/gather2_twrap/ppermute | solution.py:48
  23.6 7.8 %collective-permute-start.8 = (bf16[32,6144]{1,0:T(8,128)(2,1)S(1)}, bf16[32,6144]{1,0:T(8,128)(2,1)S(1)}, u32[]{:S(2)}, u32[]{:S(2)}) collective-permute-start(bf16[32,6144]{1,0:T(8,128)(2,1)S(1)} %collective-permute-done.6.args_5_), channel_id=1, source_target_pairs={{0,64},{8,24},{16,80},{24,8},{32,96},{40,56},{48,112},{56,40},{64,... | collective-permute-start | bytes 1179656 | tf_op jit(solution)/shard_map/gather2_tnear/ppermute | solution.py:48
  23.9 11.0 %collective-permute-start.10 = (bf16[448,6144]{1,0:T(8,128)(2,1)S(1)}, bf16[448,6144]{1,0:T(8,128)(2,1)S(1)}, u32[]{:S(2)}, u32[]{:S(2)}) collective-permute-start(bf16[448,6144]{1,0:T(8,128)(2,1)S(1)} %hand.3.one), channel_id=1, source_target_pairs={{0,8},{8,0},{16,24},{24,16},{32,40},{40,32},{48,56},{56,48},{64,72... | collective-permute-start | bytes 16515080 | tf_op jit(solution)/shard_map/down_core/ppermute | solution.py:48
  37.1 7.9 %collective-permute-start.13 = (bf16[32,6144]{1,0:T(8,128)(2,1)S(1)}, bf16[32,6144]{1,0:T(8,128)(2,1)S(1)}, u32[]{:S(2)}, u32[]{:S(2)}) collective-permute-start(bf16[32,6144]{1,0:T(8,128)(2,1)S(1)} %get-tuple-element.28), channel_id=1, source_target_pairs={{0,16},{8,72},{16,0},{24,88},{32,48},{40,104},{48,32},{56,120},{64... | collective-permute-start | bytes 1179656 | tf_op jit(solution)/shard_map/reduce2_snear/ppermute | solution.py:48
  38.1 9.1 %collective-permute-start.12 = (bf16[32,6144]{1,0:T(8,128)(2,1)S(1)}, bf16[32,6144]{1,0:T(8,128)(2,1)S(1)}, u32[]{:S(2)}, u32[]{:S(2)}) collective-permute-start(bf16[32,6144]{1,0:T(8,128)(2,1)S(1)} %get-tuple-element.26), channel_id=1, source_target_pairs={{0,48},{8,200},{16,32},{24,216},{32,16},{40,232},{48,0},{56,248},{... | collective-permute-start | bytes 1179656 | tf_op jit(solution)/shard_map/reduce2_swrap/ppermute | solution.py:48
  42.5 9.3 %collective-permute-start.11 = (bf16[32,6144]{1,0:T(8,128)(2,1)S(1)}, bf16[32,6144]{1,0:T(8,128)(2,1)S(1)}, u32[]{:S(2)}, u32[]{:S(2)}) collective-permute-start(bf16[32,6144]{1,0:T(8,128)(2,1)S(1)} %get-tuple-element.24), channel_id=1, source_target_pairs={{0,48},{8,200},{16,32},{24,216},{32,16},{40,232},{48,0},{56,248},{... | collective-permute-start | bytes 1179656 | tf_op jit(solution)/shard_map/reduce_swrap/ppermute | solution.py:48
  44.5 7.8 %collective-permute-start.15 = (bf16[32,6144]{1,0:T(8,128)(2,1)S(1)}, bf16[32,6144]{1,0:T(8,128)(2,1)S(1)}, u32[]{:S(2)}, u32[]{:S(2)}) collective-permute-start(bf16[32,6144]{1,0:T(8,128)(2,1)S(1)} %get-tuple-element.30), channel_id=1, source_target_pairs={{0,16},{8,72},{16,0},{24,88},{32,48},{40,104},{48,32},{56,120},{64... | collective-permute-start | bytes 1179656 | tf_op jit(solution)/shard_map/reduce_snear/ppermute | solution.py:48
  45.1 10.9 %collective-permute-start.16 = (bf16[32,6144]{1,0:T(8,128)(2,1)S(1)}, bf16[32,6144]{1,0:T(8,128)(2,1)S(1)}, u32[]{:S(2)}, u32[]{:S(2)}) collective-permute-start(bf16[32,6144]{1,0:T(8,128)(2,1)S(1)} %merge.2.refs_0_), channel_id=1, source_target_pairs={{0,48},{8,200},{16,32},{24,216},{32,16},{40,232},{48,0},{56,248},{... | collective-permute-start | bytes 1179656 | tf_op jit(solution)/shard_map/reduce_swrap/ppermute | solution.py:48
  47.3 11.9 %collective-permute-start.14 = (bf16[32,6144]{1,0:T(8,128)(2,1)S(1)}, bf16[32,6144]{1,0:T(8,128)(2,1)S(1)}, u32[]{:S(2)}, u32[]{:S(2)}) collective-permute-start(bf16[32,6144]{1,0:T(8,128)(2,1)S(1)} %merge.3), channel_id=1, source_target_pairs={{0,16},{8,72},{16,0},{24,88},{32,48},{40,104},{48,32},{56,120},{64... | collective-permute-start | bytes 1179656 | tf_op jit(solution)/shard_map/reduce_snear/ppermute | solution.py:48
  56.1 8.4 %collective-permute-start.17 = (bf16[16,6144]{1,0:T(8,128)(2,1)S(1)}, bf16[16,6144]{1,0:T(8,128)(2,1)S(1)}, u32[]{:S(2)}, u32[]{:S(2)}) collective-permute-start(bf16[16,6144]{1,0:T(8,128)(2,1)S(1)} %get-tuple-element.31.refs_0_), channel_id=1, source_target_pairs={{0,192},{8,56},{16,208},{24,40},{32,224},{40,24},{48,240},{56,8},{... | collective-permute-start | bytes 589832 | tf_op jit(solution)/shard_map/home_twrap/ppermute | solution.py:48
  59.2 7.2 %collective-permute-start.18 = (bf16[16,6144]{1,0:T(8,128)(2,1)S(1)}, bf16[16,6144]{1,0:T(8,128)(2,1)S(1)}, u32[]{:S(2)}, u32[]{:S(2)}) collective-permute-start(bf16[16,6144]{1,0:T(8,128)(2,1)S(1)} %get-tuple-element.33), channel_id=1, source_target_pairs={{0,128},{8,40},{16,144},{24,56},{32,160},{40,8},{48,176},{56,24},{... | collective-permute-start | bytes 589832 | tf_op jit(solution)/shard_map/home_tfar/ppermute | solution.py:48
  59.3 7.1 %collective-permute-start.19 = (bf16[16,6144]{1,0:T(8,128)(2,1)S(1)}, bf16[16,6144]{1,0:T(8,128)(2,1)S(1)}, u32[]{:S(2)}, u32[]{:S(2)}) collective-permute-start(bf16[16,6144]{1,0:T(8,128)(2,1)S(1)} %get-tuple-element.34), channel_id=1, source_target_pairs={{0,64},{8,24},{16,80},{24,8},{32,96},{40,56},{48,112},{56,40},{64,... | collective-permute-start | bytes 589832 | tf_op jit(solution)/shard_map/home_tnear/ppermute | solution.py:48

commit v14 on v13

--- a/solution.py
+++ b/solution.py
@@ -71,18 +71,22 @@
     for copy in copies:
         copy.start()
     copies[0].wait()
-    row = lax.broadcasted_iota(jnp.int32, (SLOTS, 1), 0)
-    starts = jnp.zeros((SLOTS, 1), jnp.int32)
-    ends = jnp.zeros((SLOTS, 1), jnp.int32)
+    column = lax.broadcasted_iota(jnp.int32, (1, HD), 1)
+    starts = jnp.zeros((1, HD), jnp.int32)
+    ends = jnp.zeros((1, HD), jnp.int32)
     at = jnp.int32(0)
     for i in range(SLOTS):
         after = at + lengths[i]
-        starts = jnp.where(row == i, at, starts)
-        ends = jnp.where(row == i, after, ends)
+        starts = jnp.where(column == i, at, starts)
+        ends = jnp.where(column == i, after, ends)
         at = after
-    position = lax.broadcasted_iota(jnp.int32, (SLOTS, POOL), 1)
+    position = lax.broadcasted_iota(jnp.int32, (POOL, HD), 0)
     inside = (position >= starts) & (position < ends)
-    offset = jnp.where(inside, jnp.float32(0.0), jnp.float32(-1e30))
+    offset = jnp.where(inside, jnp.float32(0.0), jnp.float32(-1e30)).astype(jnp.bfloat16)
+    row = lax.broadcasted_iota(jnp.int32, (SLOTS, HD), 0)
+    slot = lax.broadcasted_iota(jnp.int32, (SLOTS, HD), 1)
+    own_slot = jnp.where(row == slot, jnp.float32(1.0), jnp.float32(0.0)).astype(jnp.bfloat16)
+    own_slot = jnp.concatenate([own_slot] * GROUP, axis=0)
     squares = jnp.zeros((SLOTS, HD), jnp.float32)
     ones = jnp.ones((POOL, HD), jnp.bfloat16)
     copies[1].wait()
@@ -91,18 +95,17 @@
         heads = range(kv * GROUP, (kv + 1) * GROUP)
         rows = jnp.concatenate([q[:, h * HD : (h + 1) * HD] for h in heads], axis=0)
         scores = lax.dot_general(
-            rows,
-            k[:, kv * HD : (kv + 1) * HD],
+            jnp.concatenate([rows, own_slot], axis=1),
+            jnp.concatenate([k[:, kv * HD : (kv + 1) * HD], offset], axis=1),
             (((1,), (1,)), ((), ())),
             preferred_element_type=jnp.float32,
         )
-        masked = scores.reshape(GROUP, SLOTS, POOL) + offset[None]
-        top = jnp.max(masked, axis=-1, keepdims=True)
-        raised = jnp.exp2((masked - top) * jnp.float32(HD ** (-0.5) * math.log2(math.e)))
+        top = jnp.max(scores, axis=-1, keepdims=True)
+        raised = jnp.exp2((scores - top) * jnp.float32(HD ** (-0.5) * math.log2(math.e)))
         if kv == 0:
             copies[3].wait()
         mixed = lax.dot_general(
-            raised.astype(jnp.bfloat16).reshape(GROUP * SLOTS, POOL),
+            raised.astype(jnp.bfloat16),
             jnp.concatenate([v[:, kv * HD : (kv + 1) * HD], ones], axis=1),
             (((1,), (0,)), ((), ())),
             preferred_element_type=jnp.float32,
@@ -166,22 +169,16 @@
 
 
 def up_kernel(*args):
-    blocks, up, (hidden, total) = args[:8], args[8:10], args[10:]
+    blocks, up, hidden = args[:8], args[8:10], args[10]
     lows, highs = slice(0, SLOTS), slice(SLOTS, PAIR)
     order = [(part, half) for part in (0, 1) for half in (lows, highs)]
-    total[...] = jnp.zeros_like(total)
-
-    @pl.loop(0, D // CHUNK)
-    def _(step):
-        cols = pl.ds(pl.multiple_of(step * CHUNK, CHUNK), CHUNK)
-        total[...] += lax.dot_general(
-            jnp.concatenate([w[:, cols] for w in up], axis=0),
-            jnp.concatenate([blocks[2 * t + part][half, cols] for part, half in order for t in range(SIDE)], axis=0),
-            (((1,), (1,)), ((), ())),
-            preferred_element_type=jnp.float32,
-        )
-
-    value = total[...]
+    rows = jnp.concatenate([blocks[2 * t + part][half, :] for part, half in order for t in range(SIDE)], axis=0)
+    value = lax.dot_general(
+        jnp.concatenate([w[...] for w in up], axis=0),
+        rows,
+        (((1,), (1,)), ((), ())),
+        preferred_element_type=jnp.float32,
+    )
     hidden[...] = (value / (1.0 + jnp.exp(-value))).astype(jnp.bfloat16).T
 
 
@@ -193,7 +190,6 @@
         out_shape=jax.ShapeDtypeStruct((rows, 2 * HIDDEN), jnp.bfloat16),
         in_specs=[vmem] * 10,
         out_specs=vmem,
-        scratch_shapes=[pltpu.VMEM((2 * HIDDEN, rows), jnp.float32)],
         compiler_params=pltpu.CompilerParams(vmem_limit_bytes=16 * 2**20),
         cost_estimate=pl.CostEstimate(flops=4 * rows * HIDDEN * D, bytes_accessed=2 * rows * D, transcendentals=0),
         name="up",

time: 67.4 us -> 67 us (level)
  no operation moved by 1% of the time
where the time goes in v14:
time: 67 us; the launch traced here: 66.9 us
  waiting for transfers between devices  27.1 us (40%)
  starting transfers between devices  23.4 us (35%)
  Pallas kernels  14.9 us (22%)
  other arithmetic  0.77 us (1%)
  between operations  0.77 us (1%)
    ppermute x20, waiting for transfers between devices, send(): return lax.ppermute(value, 'dp', ROUTES[route])  27.1 us
    ppermute x20, starting transfers between devices, send(): return lax.ppermute(value, 'dp', ROUTES[route])  23.4 us
    pallas_call x2, Pallas kernels, project_down(): pl.pallas_call(functools.partial(down_kernel, begin), out_shape=[jax.Shap...  4.98 us
    pallas_call x1, Pallas kernels, attend(): pl.pallas_call(attend_kernel, out_shape=(jax.ShapeDtypeStruct((SLOTS, D),...  3.66 us
    pallas_call x1, Pallas kernels, project_up(): pl.pallas_call(up_kernel, out_shape=jax.ShapeDtypeStruct((rows, 2 * HIDDE...  3.13 us
    pallas_call x1, Pallas kernels, fetch(): pl.pallas_call(fetch_kernel, out_shape=jax.ShapeDtypeStruct((HIDDEN, D),...  2.57 us
  transfers between devices with their start and end apart: 20, of which 14 were waited for; matrix products, arithmetic and copies ran while one was open for 0% of the time, Pallas kernels for 19%

profile of v14, /device:TPU:128, one launch (start us, length us, event | category | flops | bytes accessed | tf_op | source)
XLA Modules:
  0.0 66.9 jit_solution(7123059934819095811)
XLA Ops:
  0.0 0.0 collective-permute-start.9
  0.0 3.7 %attend.1 = (bf16[16,6144]{1,0:T(8,128)(2,1)S(1)}, bf16[16,6144]{1,0:T(8,128)(2,1)S(1)}, bf16[448,6144]{1,0:T(8,128)(2,1)S(1)}) custom-call(s32[16]{0:T(128)} %lengths_in.1, bf16[16,6144]{1,0:T(8,128)(2,1)} %q_in.1, bf16[1024,512]{1,0:T(8,128)(2,1)} %k_in.1, bf16[1024,512]{1,0:T(8,128)(2,1)} %v_in.1, f32[1,6144]{1,0:T(1,128)} %bitcast.4, bf16[448,6144]{1,0:T(8,128)(2,1)} %down.3), custom_call_target="tpu_custom_call" | custom-call | tf_op jit(solution)/shard_map/attend/pallas_call | solution.py:129
  3.7 1.6 %collective-permute-start = (bf16[16,6144]{1,0:T(8,128)(2,1)S(1)}, bf16[16,6144]{1,0:T(8,128)(2,1)S(1)}, u32[]{:S(2)}, u32[]{:S(2)}) collective-permute-start(bf16[16,6144]{1,0:T(8,128)(2,1)S(1)} %get-tuple-element.21.one), channel_id=1, source_target_pairs={{0,16},{8,72},{16,0},{24,88},{32,48},{40,104},{48,32},{56,120},{64... | collective-permute-start | bytes 589832 | tf_op jit(solution)/shard_map/gather_snear/ppermute | solution.py:48
  5.3 2.1 %collective-permute-start.1 = (bf16[16,6144]{1,0:T(8,128)(2,1)S(1)}, bf16[16,6144]{1,0:T(8,128)(2,1)S(1)}, u32[]{:S(2)}, u32[]{:S(2)}) collective-permute-start(bf16[16,6144]{1,0:T(8,128)(2,1)S(1)} %get-tuple-element.21.one), channel_id=1, source_target_pairs={{0,48},{8,200},{16,32},{24,216},{32,16},{40,232},{48,0},{56,248},{... | collective-permute-start | bytes 589832 | tf_op jit(solution)/shard_map/gather_swrap/ppermute | solution.py:48
  7.3 0.6 collective-permute-start.2
  8.0 1.4 %collective-permute-done.two = bf16[16,6144]{1,0:T(8,128)(2,1)S(1)} collective-permute-done((bf16[16,6144]{1,0:T(8,128)(2,1)S(1)}, bf16[16,6144]{1,0:T(8,128)(2,1)S(1)}, u32[]{:S(2)}, u32[]{:S(2)}) %collective-permute-start) | collective-permute-done | bytes 196640 | tf_op jit(solution)/shard_map/gather_snear/ppermute | solution.py:48
  9.5 3.1 %collective-permute-start.4 = (bf16[32,6144]{1,0:T(8,128)(2,1)S(1)}, bf16[32,6144]{1,0:T(8,128)(2,1)S(1)}, u32[]{:S(2)}, u32[]{:S(2)}) collective-permute-start(bf16[32,6144]{1,0:T(8,128)(2,1)S(1)} %pack.2.args_0_), channel_id=1, source_target_pairs={{0,192},{8,56},{16,208},{24,40},{32,224},{40,24},{48,240},{56,8},{... | collective-permute-start | bytes 1179656 | tf_op jit(solution)/shard_map/gather_twrap/ppermute | solution.py:48
  12.6 0.1 collective-permute-start.3
  12.7 0.3 collective-permute-done.1.one
  13.0 1.8 %collective-permute-done.2.two = bf16[16,6144]{1,0:T(8,128)(2,1)S(1)} collective-permute-done((bf16[16,6144]{1,0:T(8,128)(2,1)S(1)}, bf16[16,6144]{1,0:T(8,128)(2,1)S(1)}, u32[]{:S(2)}, u32[]{:S(2)}) %collective-permute-start.2) | collective-permute-done | bytes 196640 | tf_op jit(solution)/shard_map/gather_sfar/ppermute | solution.py:48
  14.8 3.1 %collective-permute-start.6 = (bf16[32,6144]{1,0:T(8,128)(2,1)S(1)}, bf16[32,6144]{1,0:T(8,128)(2,1)S(1)}, u32[]{:S(2)}, u32[]{:S(2)}) collective-permute-start(bf16[32,6144]{1,0:T(8,128)(2,1)S(1)} %pack.3.after.args_1_), channel_id=1, source_target_pairs={{0,192},{8,56},{16,208},{24,40},{32,224},{40,24},{48,240},{56,8},{... | collective-permute-start | bytes 1179656 | tf_op jit(solution)/shard_map/gather_twrap/ppermute | solution.py:48
  17.9 0.1 collective-permute-start.5
  18.1 0.5 collective-permute-done.4.refs_1_.args_4_
  18.5 1.8 %collective-permute-done.3.refs_0_ = bf16[32,6144]{1,0:T(8,128)(2,1)S(1)} collective-permute-done((bf16[32,6144]{1,0:T(8,128)(2,1)S(1)}, bf16[32,6144]{1,0:T(8,128)(2,1)S(1)}, u32[]{:S(2)}, u32[]{:S(2)}) %collective-permute-start.3) | collective-permute-done | bytes 393248 | tf_op jit(solution)/shard_map/gather_tnear/ppermute | solution.py:48
  20.3 1.2 %collective-permute-start.7 = (bf16[32,6144]{1,0:T(8,128)(2,1)S(1)}, bf16[32,6144]{1,0:T(8,128)(2,1)S(1)}, u32[]{:S(2)}, u32[]{:S(2)}) collective-permute-start(bf16[32,6144]{1,0:T(8,128)(2,1)S(1)} %hand.2.args_2_), channel_id=1, source_target_pairs={{0,192},{8,56},{16,208},{24,40},{32,224},{40,24},{48,240},{56,8},{... | collective-permute-start | bytes 1179656 | tf_op jit(solution)/shard_map/gather2_twrap/ppermute | solution.py:48
  21.6 2.3 %collective-permute-done.6.args_5_ = bf16[32,6144]{1,0:T(8,128)(2,1)S(1)} collective-permute-done((bf16[32,6144]{1,0:T(8,128)(2,1)S(1)}, bf16[32,6144]{1,0:T(8,128)(2,1)S(1)}, u32[]{:S(2)}, u32[]{:S(2)}) %collective-permute-start.6) | collective-permute-done | bytes 393248 | tf_op jit(solution)/shard_map/gather_twrap/ppermute | solution.py:48
  23.9 0.4 collective-permute-start.8
  24.3 0.0 collective-permute-done.9.args_9_.refs_1_
  24.3 0.0 collective-permute-start.10
  24.3 2.6 %fetch.1.args_8_ = bf16[448,6144]{1,0:T(8,128)(2,1)S(1)} custom-call(bf16[448,6144]{1,0:T(8,128)(2,1)} %bitcast.6, bf16[32,6144]{1,0:T(8,128)(2,1)S(1)} %pack.3.after.args_1_), custom_call_target="tpu_custom_call" | custom-call | flops 99999997952 | bytes 11010048 | tf_op jit(solution)/shard_map/fetch/pallas_call | solution.py:159
  26.8 0.0 collective-permute-done.5.args_3_
  26.9 2.5 %collective-permute-done.7.args_6_ = bf16[32,6144]{1,0:T(8,128)(2,1)S(1)} collective-permute-done((bf16[32,6144]{1,0:T(8,128)(2,1)S(1)}, bf16[32,6144]{1,0:T(8,128)(2,1)S(1)}, u32[]{:S(2)}, u32[]{:S(2)}) %collective-permute-start.7) | collective-permute-done | bytes 393248 | tf_op jit(solution)/shard_map/gather2_twrap/ppermute | solution.py:48
  29.3 2.3 %collective-permute-done.8.args_7_ = bf16[32,6144]{1,0:T(8,128)(2,1)S(1)} collective-permute-done((bf16[32,6144]{1,0:T(8,128)(2,1)S(1)}, bf16[32,6144]{1,0:T(8,128)(2,1)S(1)}, u32[]{:S(2)}, u32[]{:S(2)}) %collective-permute-start.8) | collective-permute-done | bytes 393248 | tf_op jit(solution)/shard_map/gather2_tnear/ppermute | solution.py:48
  31.7 3.1 %up.1.hidden = bf16[256,896]{1,0:T(8,128)(2,1)S(1)} custom-call(bf16[32,6144]{1,0:T(8,128)(2,1)S(1)} %pack.2.args_0_, bf16[32,6144]{1,0:T(8,128)(2,1)S(1)} %pack.3.after.args_1_, bf16[32,6144]{1,0:T(8,128)(2,1)S(1)} %hand.2.args_2_, bf16[32,6144]{1,0:T(8,128)(2,1)S(1)} %collective-permute-done.5.args_3_, ...), custom_call_target="tpu_custom_call" | custom-call | flops 2818572288 | bytes 3145728 | tf_op jit(solution)/shard_map/up/pallas_call | solution.py:188
  34.8 0.0 collective-permute-done.10.two
  34.8 2.2 %down.5 = (bf16[32,6144]{1,0:T(8,128)(2,1)S(1)}, bf16[32,6144]{1,0:T(8,128)(2,1)S(1)}) custom-call(bf16[256,896]{1,0:T(8,128)(2,1)S(1)} %up.1.hidden, bf16[448,6144]{1,0:T(8,128)(2,1)S(1)} %hand.3.one, bf16[448,6144]{1,0:T(8,128)(2,1)S(1)} %collective-permute-done.10.two), custom_call_target="tpu_custom_call" | custom-call | flops 704643072 | bytes 786432 | tf_op jit(solution)/shard_map/down/pallas_call | solution.py:217
  37.0 1.0 %collective-permute-start.13 = (bf16[32,6144]{1,0:T(8,128)(2,1)S(1)}, bf16[32,6144]{1,0:T(8,128)(2,1)S(1)}, u32[]{:S(2)}, u32[]{:S(2)}) collective-permute-start(bf16[32,6144]{1,0:T(8,128)(2,1)S(1)} %get-tuple-element.28), channel_id=1, source_target_pairs={{0,16},{8,72},{16,0},{24,88},{32,48},{40,104},{48,32},{56,120},{64... | collective-permute-start | bytes 1179656 | tf_op jit(solution)/shard_map/reduce2_snear/ppermute | solution.py:48
  38.0 1.5 %collective-permute-start.12 = (bf16[32,6144]{1,0:T(8,128)(2,1)S(1)}, bf16[32,6144]{1,0:T(8,128)(2,1)S(1)}, u32[]{:S(2)}, u32[]{:S(2)}) collective-permute-start(bf16[32,6144]{1,0:T(8,128)(2,1)S(1)} %get-tuple-element.26), channel_id=1, source_target_pairs={{0,48},{8,200},{16,32},{24,216},{32,16},{40,232},{48,0},{56,248},{... | collective-permute-start | bytes 1179656 | tf_op jit(solution)/shard_map/reduce2_swrap/ppermute | solution.py:48
  39.5 2.8 %down.4 = (bf16[32,6144]{1,0:T(8,128)(2,1)S(1)}, bf16[32,6144]{1,0:T(8,128)(2,1)S(1)}, bf16[32,6144]{1,0:T(8,128)(2,1)S(1)}, bf16[32,6144]{1,0:T(8,128)(2,1)S(1)...) custom-call(bf16[256,896]{1,0:T(8,128)(2,1)S(1)} %up.1.hidden, bf16[448,6144]{1,0:T(8,128)(2,1)S(1)} %hand.3.one, ...), custom_call_target="tpu_custom_call" | custom-call | flops 2113929216 | bytes 2359296 | tf_op jit(solution)/shard_map/down/pallas_call | solution.py:217
  42.3 1.8 %collective-permute-start.11 = (bf16[32,6144]{1,0:T(8,128)(2,1)S(1)}, bf16[32,6144]{1,0:T(8,128)(2,1)S(1)}, u32[]{:S(2)}, u32[]{:S(2)}) collective-permute-start(bf16[32,6144]{1,0:T(8,128)(2,1)S(1)} %get-tuple-element.24), channel_id=1, source_target_pairs={{0,48},{8,200},{16,32},{24,216},{32,16},{40,232},{48,0},{56,248},{... | collective-permute-start | bytes 1179656 | tf_op jit(solution)/shard_map/reduce_swrap/ppermute | solution.py:48
  44.1 0.0 collective-permute-start.15
  44.1 0.7 %collective-permute-done.13.arrived = bf16[32,6144]{1,0:T(8,128)(2,1)S(1)} collective-permute-done((bf16[32,6144]{1,0:T(8,128)(2,1)S(1)}, bf16[32,6144]{1,0:T(8,128)(2,1)S(1)}, u32[]{:S(2)}, u32[]{:S(2)}) %collective-permute-start.13) | collective-permute-done | bytes 393248 | tf_op jit(solution)/shard_map/reduce2_snear/ppermute | solution.py:48
  44.9 0.1 merge.2.refs_0_
  45.0 2.1 %collective-permute-start.16 = (bf16[32,6144]{1,0:T(8,128)(2,1)S(1)}, bf16[32,6144]{1,0:T(8,128)(2,1)S(1)}, u32[]{:S(2)}, u32[]{:S(2)}) collective-permute-start(bf16[32,6144]{1,0:T(8,128)(2,1)S(1)} %merge.2.refs_0_), channel_id=1, source_target_pairs={{0,48},{8,200},{16,32},{24,216},{32,16},{40,232},{48,0},{56,248},{... | collective-permute-start | bytes 1179656 | tf_op jit(solution)/shard_map/reduce_swrap/ppermute | solution.py:48
  47.1 0.0 collective-permute-done.12.arrived
  47.1 0.1 merge.3
  47.2 0.3 collective-permute-start.14
  47.5 4.0 %collective-permute-done.11.refs_0_.direct = bf16[32,6144]{1,0:T(8,128)(2,1)S(1)} collective-permute-done((bf16[32,6144]{1,0:T(8,128)(2,1)S(1)}, bf16[32,6144]{1,0:T(8,128)(2,1)S(1)}, u32[]{:S(2)}, u32[]{:S(2)}) %collective-permute-start.11) | collective-permute-done | bytes 393248 | tf_op jit(solution)/shard_map/reduce_swrap/ppermute | solution.py:48
  51.4 0.5 collective-permute-done.15.direct
  51.9 3.7 %collective-permute-done.16.back = bf16[32,6144]{1,0:T(8,128)(2,1)S(1)} collective-permute-done((bf16[32,6144]{1,0:T(8,128)(2,1)S(1)}, bf16[32,6144]{1,0:T(8,128)(2,1)S(1)}, u32[]{:S(2)}, u32[]{:S(2)}) %collective-permute-start.16) | collective-permute-done | bytes 393248 | tf_op jit(solution)/shard_map/reduce_swrap/ppermute | solution.py:48
  55.6 0.1 finish.2
  55.8 3.1 %collective-permute-start.17 = (bf16[16,6144]{1,0:T(8,128)(2,1)S(1)}, bf16[16,6144]{1,0:T(8,128)(2,1)S(1)}, u32[]{:S(2)}, u32[]{:S(2)}) collective-permute-start(bf16[16,6144]{1,0:T(8,128)(2,1)S(1)} %get-tuple-element.31.refs_0_), channel_id=1, source_target_pairs={{0,192},{8,56},{16,208},{24,40},{32,224},{40,24},{48,240},{56,8},{... | collective-permute-start | bytes 589832 | tf_op jit(solution)/shard_map/home_twrap/ppermute | solution.py:48
  58.9 0.1 finish.3
  59.0 1.2 %collective-permute-start.19 = (bf16[16,6144]{1,0:T(8,128)(2,1)S(1)}, bf16[16,6144]{1,0:T(8,128)(2,1)S(1)}, u32[]{:S(2)}, u32[]{:S(2)}) collective-permute-start(bf16[16,6144]{1,0:T(8,128)(2,1)S(1)} %get-tuple-element.34), channel_id=1, source_target_pairs={{0,64},{8,24},{16,80},{24,8},{32,96},{40,56},{48,112},{56,40},{64,... | collective-permute-start | bytes 589832 | tf_op jit(solution)/shard_map/home_tnear/ppermute | solution.py:48
  60.9 3.3 %collective-permute-done.17.refs_2_ = bf16[16,6144]{1,0:T(8,128)(2,1)S(1)} collective-permute-done((bf16[16,6144]{1,0:T(8,128)(2,1)S(1)}, bf16[16,6144]{1,0:T(8,128)(2,1)S(1)}, u32[]{:S(2)}, u32[]{:S(2)}) %collective-permute-start.17) | collective-permute-done | bytes 196640 | tf_op jit(solution)/shard_map/home_twrap/ppermute | solution.py:48
  64.2 1.9 %collective-permute-done.18.refs_3_ = bf16[16,6144]{1,0:T(8,128)(2,1)S(1)} collective-permute-done((bf16[16,6144]{1,0:T(8,128)(2,1)S(1)}, bf16[16,6144]{1,0:T(8,128)(2,1)S(1)}, u32[]{:S(2)}, u32[]{:S(2)}) %collective-permute-start.18) | collective-permute-done | bytes 196640 | tf_op jit(solution)/shard_map/home_tfar/ppermute | solution.py:48
  66.1 0.1 collect.1
  66.1 0.8 %select_convert_fusion = bf16[16,6144]{1,0:T(8,128)(2,1)} fusion(f32[16,6144]{1,0:T(8,128)S(1)} %collect.1, bf16[16,6144]{1,0:T(8,128)(2,1)S(1)} %collective-permute-done.19, pred[16]{0:T(512)(128)(4,1)S(1)} %iota_compare_fusion), kind=kLoop, calls=%fused_computation | loop fusion | flops 393216 | bytes 786448 | tf_op jit(solution)/shard_map/convert_element_type | solution.py:358
  (8 shorter events, 0.1 us)
Async XLA Ops:
  0.0 24.3 %collective-permute-start.9 = (bf16[448,6144]{1,0:T(8,128)(2,1)}, bf16[448,6144]{1,0:T(8,128)(2,1)S(1)}, u32[]{:S(2)}, u32[]{:S(2)}) collective-permute-start(bf16[448,6144]{1,0:T(8,128)(2,1)} %bitcast.5), channel_id=1, source_target_pairs={{0,8},{8,0},{16,24},{24,16},{32,40},{40,32},{48,56},{56,48},{64,72... | collective-permute-start | bytes 16515080 | tf_op jit(solution)/shard_map/up_core/ppermute | solution.py:48
  3.7 5.8 %collective-permute-start = (bf16[16,6144]{1,0:T(8,128)(2,1)S(1)}, bf16[16,6144]{1,0:T(8,128)(2,1)S(1)}, u32[]{:S(2)}, u32[]{:S(2)}) collective-permute-start(bf16[16,6144]{1,0:T(8,128)(2,1)S(1)} %get-tuple-element.21.one), channel_id=1, source_target_pairs={{0,16},{8,72},{16,0},{24,88},{32,48},{40,104},{48,32},{56,120},{64... | collective-permute-start | bytes 589832 | tf_op jit(solution)/shard_map/gather_snear/ppermute | solution.py:48
  5.3 7.7 %collective-permute-start.1 = (bf16[16,6144]{1,0:T(8,128)(2,1)S(1)}, bf16[16,6144]{1,0:T(8,128)(2,1)S(1)}, u32[]{:S(2)}, u32[]{:S(2)}) collective-permute-start(bf16[16,6144]{1,0:T(8,128)(2,1)S(1)} %get-tuple-element.21.one), channel_id=1, source_target_pairs={{0,48},{8,200},{16,32},{24,216},{32,16},{40,232},{48,0},{56,248},{... | collective-permute-start | bytes 589832 | tf_op jit(solution)/shard_map/gather_swrap/ppermute | solution.py:48
  7.3 7.4 %collective-permute-start.2 = (bf16[16,6144]{1,0:T(8,128)(2,1)S(1)}, bf16[16,6144]{1,0:T(8,128)(2,1)S(1)}, u32[]{:S(2)}, u32[]{:S(2)}) collective-permute-start(bf16[16,6144]{1,0:T(8,128)(2,1)S(1)} %get-tuple-element.21.one), channel_id=1, source_target_pairs={{0,32},{8,136},{16,48},{24,152},{32,0},{40,168},{48,16},{56,184},{... | collective-permute-start | bytes 589832 | tf_op jit(solution)/shard_map/gather_sfar/ppermute | solution.py:48
  9.5 9.1 %collective-permute-start.4 = (bf16[32,6144]{1,0:T(8,128)(2,1)S(1)}, bf16[32,6144]{1,0:T(8,128)(2,1)S(1)}, u32[]{:S(2)}, u32[]{:S(2)}) collective-permute-start(bf16[32,6144]{1,0:T(8,128)(2,1)S(1)} %pack.2.args_0_), channel_id=1, source_target_pairs={{0,192},{8,56},{16,208},{24,40},{32,224},{40,24},{48,240},{56,8},{... | collective-permute-start | bytes 1179656 | tf_op jit(solution)/shard_map/gather_twrap/ppermute | solution.py:48
  12.6 7.8 %collective-permute-start.3 = (bf16[32,6144]{1,0:T(8,128)(2,1)S(1)}, bf16[32,6144]{1,0:T(8,128)(2,1)S(1)}, u32[]{:S(2)}, u32[]{:S(2)}) collective-permute-start(bf16[32,6144]{1,0:T(8,128)(2,1)S(1)} %pack.2.args_0_), channel_id=1, source_target_pairs={{0,64},{8,24},{16,80},{24,8},{32,96},{40,56},{48,112},{56,40},{64,... | collective-permute-start | bytes 1179656 | tf_op jit(solution)/shard_map/gather_tnear/ppermute | solution.py:48
  14.8 9.1 %collective-permute-start.6 = (bf16[32,6144]{1,0:T(8,128)(2,1)S(1)}, bf16[32,6144]{1,0:T(8,128)(2,1)S(1)}, u32[]{:S(2)}, u32[]{:S(2)}) collective-permute-start(bf16[32,6144]{1,0:T(8,128)(2,1)S(1)} %pack.3.after.args_1_), channel_id=1, source_target_pairs={{0,192},{8,56},{16,208},{24,40},{32,224},{40,24},{48,240},{56,8},{... | collective-permute-start | bytes 1179656 | tf_op jit(solution)/shard_map/gather_twrap/ppermute | solution.py:48
  17.9 8.9 %collective-permute-start.5 = (bf16[32,6144]{1,0:T(8,128)(2,1)S(1)}, bf16[32,6144]{1,0:T(8,128)(2,1)S(1)}, u32[]{:S(2)}, u32[]{:S(2)}) collective-permute-start(bf16[32,6144]{1,0:T(8,128)(2,1)S(1)} %pack.3.after.args_1_), channel_id=1, source_target_pairs={{0,64},{8,24},{16,80},{24,8},{32,96},{40,56},{48,112},{56,40},{64,... | collective-permute-start | bytes 1179656 | tf_op jit(solution)/shard_map/gather_tnear/ppermute | solution.py:48
  20.3 9.0 %collective-permute-start.7 = (bf16[32,6144]{1,0:T(8,128)(2,1)S(1)}, bf16[32,6144]{1,0:T(8,128)(2,1)S(1)}, u32[]{:S(2)}, u32[]{:S(2)}) collective-permute-start(bf16[32,6144]{1,0:T(8,128)(2,1)S(1)} %hand.2.args_2_), channel_id=1, source_target_pairs={{0,192},{8,56},{16,208},{24,40},{32,224},{40,24},{48,240},{56,8},{... | collective-permute-start | bytes 1179656 | tf_op jit(solution)/shard_map/gather2_twrap/ppermute | solution.py:48
  23.9 7.8 %collective-permute-start.8 = (bf16[32,6144]{1,0:T(8,128)(2,1)S(1)}, bf16[32,6144]{1,0:T(8,128)(2,1)S(1)}, u32[]{:S(2)}, u32[]{:S(2)}) collective-permute-start(bf16[32,6144]{1,0:T(8,128)(2,1)S(1)} %collective-permute-done.6.args_5_), channel_id=1, source_target_pairs={{0,64},{8,24},{16,80},{24,8},{32,96},{40,56},{48,112},{56,40},{64,... | collective-permute-start | bytes 1179656 | tf_op jit(solution)/shard_map/gather2_tnear/ppermute | solution.py:48
  24.3 10.5 %collective-permute-start.10 = (bf16[448,6144]{1,0:T(8,128)(2,1)S(1)}, bf16[448,6144]{1,0:T(8,128)(2,1)S(1)}, u32[]{:S(2)}, u32[]{:S(2)}) collective-permute-start(bf16[448,6144]{1,0:T(8,128)(2,1)S(1)} %hand.3.one), channel_id=1, source_target_pairs={{0,8},{8,0},{16,24},{24,16},{32,40},{40,32},{48,56},{56,48},{64,72... | collective-permute-start | bytes 16515080 | tf_op jit(solution)/shard_map/down_core/ppermute | solution.py:48
  37.0 7.9 %collective-permute-start.13 = (bf16[32,6144]{1,0:T(8,128)(2,1)S(1)}, bf16[32,6144]{1,0:T(8,128)(2,1)S(1)}, u32[]{:S(2)}, u32[]{:S(2)}) collective-permute-start(bf16[32,6144]{1,0:T(8,128)(2,1)S(1)} %get-tuple-element.28), channel_id=1, source_target_pairs={{0,16},{8,72},{16,0},{24,88},{32,48},{40,104},{48,32},{56,120},{64... | collective-permute-start | bytes 1179656 | tf_op jit(solution)/shard_map/reduce2_snear/ppermute | solution.py:48
  38.0 9.1 %collective-permute-start.12 = (bf16[32,6144]{1,0:T(8,128)(2,1)S(1)}, bf16[32,6144]{1,0:T(8,128)(2,1)S(1)}, u32[]{:S(2)}, u32[]{:S(2)}) collective-permute-start(bf16[32,6144]{1,0:T(8,128)(2,1)S(1)} %get-tuple-element.26), channel_id=1, source_target_pairs={{0,48},{8,200},{16,32},{24,216},{32,16},{40,232},{48,0},{56,248},{... | collective-permute-start | bytes 1179656 | tf_op jit(solution)/shard_map/reduce2_swrap/ppermute | solution.py:48
  42.3 9.1 %collective-permute-start.11 = (bf16[32,6144]{1,0:T(8,128)(2,1)S(1)}, bf16[32,6144]{1,0:T(8,128)(2,1)S(1)}, u32[]{:S(2)}, u32[]{:S(2)}) collective-permute-start(bf16[32,6144]{1,0:T(8,128)(2,1)S(1)} %get-tuple-element.24), channel_id=1, source_target_pairs={{0,48},{8,200},{16,32},{24,216},{32,16},{40,232},{48,0},{56,248},{... | collective-permute-start | bytes 1179656 | tf_op jit(solution)/shard_map/reduce_swrap/ppermute | solution.py:48
  44.1 7.8 %collective-permute-start.15 = (bf16[32,6144]{1,0:T(8,128)(2,1)S(1)}, bf16[32,6144]{1,0:T(8,128)(2,1)S(1)}, u32[]{:S(2)}, u32[]{:S(2)}) collective-permute-start(bf16[32,6144]{1,0:T(8,128)(2,1)S(1)} %get-tuple-element.30), channel_id=1, source_target_pairs={{0,16},{8,72},{16,0},{24,88},{32,48},{40,104},{48,32},{56,120},{64... | collective-permute-start | bytes 1179656 | tf_op jit(solution)/shard_map/reduce_snear/ppermute | solution.py:48
  45.0 10.7 %collective-permute-start.16 = (bf16[32,6144]{1,0:T(8,128)(2,1)S(1)}, bf16[32,6144]{1,0:T(8,128)(2,1)S(1)}, u32[]{:S(2)}, u32[]{:S(2)}) collective-permute-start(bf16[32,6144]{1,0:T(8,128)(2,1)S(1)} %merge.2.refs_0_), channel_id=1, source_target_pairs={{0,48},{8,200},{16,32},{24,216},{32,16},{40,232},{48,0},{56,248},{... | collective-permute-start | bytes 1179656 | tf_op jit(solution)/shard_map/reduce_swrap/ppermute | solution.py:48
  47.2 11.7 %collective-permute-start.14 = (bf16[32,6144]{1,0:T(8,128)(2,1)S(1)}, bf16[32,6144]{1,0:T(8,128)(2,1)S(1)}, u32[]{:S(2)}, u32[]{:S(2)}) collective-permute-start(bf16[32,6144]{1,0:T(8,128)(2,1)S(1)} %merge.3), channel_id=1, source_target_pairs={{0,16},{8,72},{16,0},{24,88},{32,48},{40,104},{48,32},{56,120},{64... | collective-permute-start | bytes 1179656 | tf_op jit(solution)/shard_map/reduce_snear/ppermute | solution.py:48
  55.8 8.4 %collective-permute-start.17 = (bf16[16,6144]{1,0:T(8,128)(2,1)S(1)}, bf16[16,6144]{1,0:T(8,128)(2,1)S(1)}, u32[]{:S(2)}, u32[]{:S(2)}) collective-permute-start(bf16[16,6144]{1,0:T(8,128)(2,1)S(1)} %get-tuple-element.31.refs_0_), channel_id=1, source_target_pairs={{0,192},{8,56},{16,208},{24,40},{32,224},{40,24},{48,240},{56,8},{... | collective-permute-start | bytes 589832 | tf_op jit(solution)/shard_map/home_twrap/ppermute | solution.py:48
  58.9 7.2 %collective-permute-start.18 = (bf16[16,6144]{1,0:T(8,128)(2,1)S(1)}, bf16[16,6144]{1,0:T(8,128)(2,1)S(1)}, u32[]{:S(2)}, u32[]{:S(2)}) collective-permute-start(bf16[16,6144]{1,0:T(8,128)(2,1)S(1)} %get-tuple-element.33), channel_id=1, source_target_pairs={{0,128},{8,40},{16,144},{24,56},{32,160},{40,8},{48,176},{56,24},{... | collective-permute-start | bytes 589832 | tf_op jit(solution)/shard_map/home_tfar/ppermute | solution.py:48
  59.0 7.1 %collective-permute-start.19 = (bf16[16,6144]{1,0:T(8,128)(2,1)S(1)}, bf16[16,6144]{1,0:T(8,128)(2,1)S(1)}, u32[]{:S(2)}, u32[]{:S(2)}) collective-permute-start(bf16[16,6144]{1,0:T(8,128)(2,1)S(1)} %get-tuple-element.34), channel_id=1, source_target_pairs={{0,64},{8,24},{16,80},{24,8},{32,96},{40,56},{48,112},{56,40},{64,... | collective-permute-start | bytes 589832 | tf_op jit(solution)/shard_map/home_tnear/ppermute | solution.py:48

commit v15 on v13

--- a/solution.py
+++ b/solution.py
@@ -18,7 +18,6 @@
 HIDDEN = 448
 SIDE = 4
 PAIR = 2 * SLOTS
-CHUNK = 3072
 
 
 def device(y, x, c):
@@ -166,22 +165,16 @@
 
 
 def up_kernel(*args):
-    blocks, up, (hidden, total) = args[:8], args[8:10], args[10:]
+    blocks, up, hidden = args[:8], args[8:10], args[10]
     lows, highs = slice(0, SLOTS), slice(SLOTS, PAIR)
     order = [(part, half) for part in (0, 1) for half in (lows, highs)]
-    total[...] = jnp.zeros_like(total)
-
-    @pl.loop(0, D // CHUNK)
-    def _(step):
-        cols = pl.ds(pl.multiple_of(step * CHUNK, CHUNK), CHUNK)
-        total[...] += lax.dot_general(
-            jnp.concatenate([w[:, cols] for w in up], axis=0),
-            jnp.concatenate([blocks[2 * t + part][half, cols] for part, half in order for t in range(SIDE)], axis=0),
-            (((1,), (1,)), ((), ())),
-            preferred_element_type=jnp.float32,
-        )
-
-    value = total[...]
+    rows = jnp.concatenate([blocks[2 * t + part][half, :] for part, half in order for t in range(SIDE)], axis=0)
+    value = lax.dot_general(
+        jnp.concatenate([w[...] for w in up], axis=0),
+        rows,
+        (((1,), (1,)), ((), ())),
+        preferred_element_type=jnp.float32,
+    )
     hidden[...] = (value / (1.0 + jnp.exp(-value))).astype(jnp.bfloat16).T
 
 
@@ -193,7 +186,6 @@
         out_shape=jax.ShapeDtypeStruct((rows, 2 * HIDDEN), jnp.bfloat16),
         in_specs=[vmem] * 10,
         out_specs=vmem,
-        scratch_shapes=[pltpu.VMEM((2 * HIDDEN, rows), jnp.float32)],
         compiler_params=pltpu.CompilerParams(vmem_limit_bytes=16 * 2**20),
         cost_estimate=pl.CostEstimate(flops=4 * rows * HIDDEN * D, bytes_accessed=2 * rows * D, transcendentals=0),
         name="up",
@@ -201,18 +193,13 @@
 
 
 def down_kernel(begin, hidden, one, two, *outs):
-    rows = pl.ds(begin * PAIR, len(outs) * PAIR)
-
-    @pl.loop(0, D // CHUNK)
-    def _(step):
-        cols = pl.ds(pl.multiple_of(step * CHUNK, CHUNK), CHUNK)
-        product = jnp.dot(
-            hidden[rows, :],
-            jnp.concatenate([one[:, cols], two[:, cols]], axis=0),
-            preferred_element_type=jnp.float32,
-        ).astype(jnp.bfloat16)
-        for i, out in enumerate(outs):
-            out[:, cols] = product[i * PAIR : (i + 1) * PAIR]
+    product = jnp.dot(
+        hidden[begin * PAIR : (begin + len(outs)) * PAIR, :],
+        jnp.concatenate([one[...], two[...]], axis=0),
+        preferred_element_type=jnp.float32,
+    ).astype(jnp.bfloat16)
+    for i, out in enumerate(outs):
+        out[...] = product[i * PAIR : (i + 1) * PAIR]
 
 
 def project_down(hidden, down, begin, end):

time: 67.4 us -> 66.4 us (0.985)
  Pallas kernels: 15.1 us -> 14.3 us
  transfers between devices with their start and end apart: 20 -> 20, of which waited for: 14 -> 14; matrix products, arithmetic and copies ran while one was open for 0% -> 0% of each run, Pallas kernels for 19% -> 18%
where the time goes in v15:
time: 66.4 us; the launch traced here: 66.3 us
  waiting for transfers between devices  27.2 us (41%)
  starting transfers between devices  23.2 us (35%)
  Pallas kernels  14.3 us (22%)
  other arithmetic  0.77 us (1%)
  between operations  0.77 us (1%)
    ppermute x20, waiting for transfers between devices, send(): return lax.ppermute(value, 'dp', ROUTES[route])  27.2 us
    ppermute x20, starting transfers between devices, send(): return lax.ppermute(value, 'dp', ROUTES[route])  23.2 us
    pallas_call x2, Pallas kernels, project_down(): pl.pallas_call(functools.partial(down_kernel, begin), out_shape=[jax.Shap...  4.66 us
    pallas_call x1, Pallas kernels, attend(): pl.pallas_call(attend_kernel, out_shape=(jax.ShapeDtypeStruct((SLOTS, D),...  3.34 us
    pallas_call x1, Pallas kernels, project_up(): pl.pallas_call(up_kernel, out_shape=jax.ShapeDtypeStruct((rows, 2 * HIDDE...  3.12 us
    pallas_call x1, Pallas kernels, fetch(): pl.pallas_call(fetch_kernel, out_shape=jax.ShapeDtypeStruct((HIDDEN, D),...  2.57 us
  transfers between devices with their start and end apart: 20, of which 14 were waited for; matrix products, arithmetic and copies ran while one was open for 0% of the time, Pallas kernels for 18%

profile of v15, /device:TPU:128, one launch (start us, length us, event | category | flops | bytes accessed | tf_op | source)
XLA Modules:
  0.0 66.3 jit_solution(2728418666670673441)
XLA Ops:
  0.0 0.0 collective-permute-start.9
  0.0 3.3 %attend.1 = (bf16[16,6144]{1,0:T(8,128)(2,1)S(1)}, bf16[16,6144]{1,0:T(8,128)(2,1)S(1)}, bf16[448,6144]{1,0:T(8,128)(2,1)S(1)}) custom-call(s32[16]{0:T(128)} %lengths_in.1, bf16[16,6144]{1,0:T(8,128)(2,1)} %q_in.1, bf16[1024,512]{1,0:T(8,128)(2,1)} %k_in.1, bf16[1024,512]{1,0:T(8,128)(2,1)} %v_in.1, f32[1,6144]{1,0:T(1,128)} %bitcast.4, bf16[448,6144]{1,0:T(8,128)(2,1)} %down.3), custom_call_target="tpu_custom_call" | custom-call | tf_op jit(solution)/shard_map/attend/pallas_call | solution.py:125
  3.4 1.6 %collective-permute-start = (bf16[16,6144]{1,0:T(8,128)(2,1)S(1)}, bf16[16,6144]{1,0:T(8,128)(2,1)S(1)}, u32[]{:S(2)}, u32[]{:S(2)}) collective-permute-start(bf16[16,6144]{1,0:T(8,128)(2,1)S(1)} %get-tuple-element.21.one), channel_id=1, source_target_pairs={{0,16},{8,72},{16,0},{24,88},{32,48},{40,104},{48,32},{56,120},{64... | collective-permute-start | bytes 589832 | tf_op jit(solution)/shard_map/gather_snear/ppermute | solution.py:47
  4.9 2.1 %collective-permute-start.1 = (bf16[16,6144]{1,0:T(8,128)(2,1)S(1)}, bf16[16,6144]{1,0:T(8,128)(2,1)S(1)}, u32[]{:S(2)}, u32[]{:S(2)}) collective-permute-start(bf16[16,6144]{1,0:T(8,128)(2,1)S(1)} %get-tuple-element.21.one), channel_id=1, source_target_pairs={{0,48},{8,200},{16,32},{24,216},{32,16},{40,232},{48,0},{56,248},{... | collective-permute-start | bytes 589832 | tf_op jit(solution)/shard_map/gather_swrap/ppermute | solution.py:47
  7.0 0.6 collective-permute-start.2
  7.7 1.4 %collective-permute-done.two = bf16[16,6144]{1,0:T(8,128)(2,1)S(1)} collective-permute-done((bf16[16,6144]{1,0:T(8,128)(2,1)S(1)}, bf16[16,6144]{1,0:T(8,128)(2,1)S(1)}, u32[]{:S(2)}, u32[]{:S(2)}) %collective-permute-start) | collective-permute-done | bytes 196640 | tf_op jit(solution)/shard_map/gather_snear/ppermute | solution.py:47
  9.1 3.1 %collective-permute-start.4 = (bf16[32,6144]{1,0:T(8,128)(2,1)S(1)}, bf16[32,6144]{1,0:T(8,128)(2,1)S(1)}, u32[]{:S(2)}, u32[]{:S(2)}) collective-permute-start(bf16[32,6144]{1,0:T(8,128)(2,1)S(1)} %pack.2.args_0_), channel_id=1, source_target_pairs={{0,192},{8,56},{16,208},{24,40},{32,224},{40,24},{48,240},{56,8},{... | collective-permute-start | bytes 1179656 | tf_op jit(solution)/shard_map/gather_twrap/ppermute | solution.py:47
  12.2 0.1 collective-permute-start.3
  12.4 0.3 collective-permute-done.1.one
  12.7 1.8 %collective-permute-done.2.two = bf16[16,6144]{1,0:T(8,128)(2,1)S(1)} collective-permute-done((bf16[16,6144]{1,0:T(8,128)(2,1)S(1)}, bf16[16,6144]{1,0:T(8,128)(2,1)S(1)}, u32[]{:S(2)}, u32[]{:S(2)}) %collective-permute-start.2) | collective-permute-done | bytes 196640 | tf_op jit(solution)/shard_map/gather_sfar/ppermute | solution.py:47
  14.5 3.1 %collective-permute-start.6 = (bf16[32,6144]{1,0:T(8,128)(2,1)S(1)}, bf16[32,6144]{1,0:T(8,128)(2,1)S(1)}, u32[]{:S(2)}, u32[]{:S(2)}) collective-permute-start(bf16[32,6144]{1,0:T(8,128)(2,1)S(1)} %pack.3.after.args_1_), channel_id=1, source_target_pairs={{0,192},{8,56},{16,208},{24,40},{32,224},{40,24},{48,240},{56,8},{... | collective-permute-start | bytes 1179656 | tf_op jit(solution)/shard_map/gather_twrap/ppermute | solution.py:47
  17.6 0.1 collective-permute-start.5
  17.7 0.5 collective-permute-done.4.refs_1_.args_4_
  18.2 1.8 %collective-permute-done.3.refs_0_ = bf16[32,6144]{1,0:T(8,128)(2,1)S(1)} collective-permute-done((bf16[32,6144]{1,0:T(8,128)(2,1)S(1)}, bf16[32,6144]{1,0:T(8,128)(2,1)S(1)}, u32[]{:S(2)}, u32[]{:S(2)}) %collective-permute-start.3) | collective-permute-done | bytes 393248 | tf_op jit(solution)/shard_map/gather_tnear/ppermute | solution.py:47
  20.0 1.2 %collective-permute-start.7 = (bf16[32,6144]{1,0:T(8,128)(2,1)S(1)}, bf16[32,6144]{1,0:T(8,128)(2,1)S(1)}, u32[]{:S(2)}, u32[]{:S(2)}) collective-permute-start(bf16[32,6144]{1,0:T(8,128)(2,1)S(1)} %hand.2.args_2_), channel_id=1, source_target_pairs={{0,192},{8,56},{16,208},{24,40},{32,224},{40,24},{48,240},{56,8},{... | collective-permute-start | bytes 1179656 | tf_op jit(solution)/shard_map/gather2_twrap/ppermute | solution.py:47
  21.2 2.3 %collective-permute-done.6.args_5_ = bf16[32,6144]{1,0:T(8,128)(2,1)S(1)} collective-permute-done((bf16[32,6144]{1,0:T(8,128)(2,1)S(1)}, bf16[32,6144]{1,0:T(8,128)(2,1)S(1)}, u32[]{:S(2)}, u32[]{:S(2)}) %collective-permute-start.6) | collective-permute-done | bytes 393248 | tf_op jit(solution)/shard_map/gather_twrap/ppermute | solution.py:47
  23.6 0.4 collective-permute-start.8
  23.9 0.0 collective-permute-done.9.args_9_.refs_1_
  23.9 0.0 collective-permute-start.10
  24.0 2.6 %fetch.1.args_8_ = bf16[448,6144]{1,0:T(8,128)(2,1)S(1)} custom-call(bf16[448,6144]{1,0:T(8,128)(2,1)} %bitcast.6, bf16[32,6144]{1,0:T(8,128)(2,1)S(1)} %pack.3.after.args_1_), custom_call_target="tpu_custom_call" | custom-call | flops 99999997952 | bytes 11010048 | tf_op jit(solution)/shard_map/fetch/pallas_call | solution.py:155
  26.5 2.5 %collective-permute-done.7.args_6_ = bf16[32,6144]{1,0:T(8,128)(2,1)S(1)} collective-permute-done((bf16[32,6144]{1,0:T(8,128)(2,1)S(1)}, bf16[32,6144]{1,0:T(8,128)(2,1)S(1)}, u32[]{:S(2)}, u32[]{:S(2)}) %collective-permute-start.7) | collective-permute-done | bytes 393248 | tf_op jit(solution)/shard_map/gather2_twrap/ppermute | solution.py:47
  29.0 2.3 %collective-permute-done.8.args_7_ = bf16[32,6144]{1,0:T(8,128)(2,1)S(1)} collective-permute-done((bf16[32,6144]{1,0:T(8,128)(2,1)S(1)}, bf16[32,6144]{1,0:T(8,128)(2,1)S(1)}, u32[]{:S(2)}, u32[]{:S(2)}) %collective-permute-start.8) | collective-permute-done | bytes 393248 | tf_op jit(solution)/shard_map/gather2_tnear/ppermute | solution.py:47
  31.4 3.1 %up.1.hidden = bf16[256,896]{1,0:T(8,128)(2,1)S(1)} custom-call(bf16[32,6144]{1,0:T(8,128)(2,1)S(1)} %pack.2.args_0_, bf16[32,6144]{1,0:T(8,128)(2,1)S(1)} %pack.3.after.args_1_, bf16[32,6144]{1,0:T(8,128)(2,1)S(1)} %hand.2.args_2_, bf16[32,6144]{1,0:T(8,128)(2,1)S(1)} %collective-permute-done.5.args_3_, ...), custom_call_target="tpu_custom_call" | custom-call | flops 2818572288 | bytes 3145728 | tf_op jit(solution)/shard_map/up/pallas_call | solution.py:184
  34.5 2.0 %down.5 = (bf16[32,6144]{1,0:T(8,128)(2,1)S(1)}, bf16[32,6144]{1,0:T(8,128)(2,1)S(1)}) custom-call(bf16[256,896]{1,0:T(8,128)(2,1)S(1)} %up.1.hidden, bf16[448,6144]{1,0:T(8,128)(2,1)S(1)} %hand.3.one, bf16[448,6144]{1,0:T(8,128)(2,1)S(1)} %collective-permute-done.10.two), custom_call_target="tpu_custom_call" | custom-call | flops 704643072 | bytes 786432 | tf_op jit(solution)/shard_map/down/pallas_call | solution.py:208
  36.5 1.0 %collective-permute-start.13 = (bf16[32,6144]{1,0:T(8,128)(2,1)S(1)}, bf16[32,6144]{1,0:T(8,128)(2,1)S(1)}, u32[]{:S(2)}, u32[]{:S(2)}) collective-permute-start(bf16[32,6144]{1,0:T(8,128)(2,1)S(1)} %get-tuple-element.28), channel_id=1, source_target_pairs={{0,16},{8,72},{16,0},{24,88},{32,48},{40,104},{48,32},{56,120},{64... | collective-permute-start | bytes 1179656 | tf_op jit(solution)/shard_map/reduce2_snear/ppermute | solution.py:47
  37.5 1.5 %collective-permute-start.12 = (bf16[32,6144]{1,0:T(8,128)(2,1)S(1)}, bf16[32,6144]{1,0:T(8,128)(2,1)S(1)}, u32[]{:S(2)}, u32[]{:S(2)}) collective-permute-start(bf16[32,6144]{1,0:T(8,128)(2,1)S(1)} %get-tuple-element.26), channel_id=1, source_target_pairs={{0,48},{8,200},{16,32},{24,216},{32,16},{40,232},{48,0},{56,248},{... | collective-permute-start | bytes 1179656 | tf_op jit(solution)/shard_map/reduce2_swrap/ppermute | solution.py:47
  39.1 2.6 %down.4 = (bf16[32,6144]{1,0:T(8,128)(2,1)S(1)}, bf16[32,6144]{1,0:T(8,128)(2,1)S(1)}, bf16[32,6144]{1,0:T(8,128)(2,1)S(1)}, bf16[32,6144]{1,0:T(8,128)(2,1)S(1)...) custom-call(bf16[256,896]{1,0:T(8,128)(2,1)S(1)} %up.1.hidden, bf16[448,6144]{1,0:T(8,128)(2,1)S(1)} %hand.3.one, ...), custom_call_target="tpu_custom_call" | custom-call | flops 2113929216 | bytes 2359296 | tf_op jit(solution)/shard_map/down/pallas_call | solution.py:208
  41.7 1.8 %collective-permute-start.11 = (bf16[32,6144]{1,0:T(8,128)(2,1)S(1)}, bf16[32,6144]{1,0:T(8,128)(2,1)S(1)}, u32[]{:S(2)}, u32[]{:S(2)}) collective-permute-start(bf16[32,6144]{1,0:T(8,128)(2,1)S(1)} %get-tuple-element.24), channel_id=1, source_target_pairs={{0,48},{8,200},{16,32},{24,216},{32,16},{40,232},{48,0},{56,248},{... | collective-permute-start | bytes 1179656 | tf_op jit(solution)/shard_map/reduce_swrap/ppermute | solution.py:47
  43.5 0.0 collective-permute-start.15
  43.5 0.9 %collective-permute-done.13.arrived = bf16[32,6144]{1,0:T(8,128)(2,1)S(1)} collective-permute-done((bf16[32,6144]{1,0:T(8,128)(2,1)S(1)}, bf16[32,6144]{1,0:T(8,128)(2,1)S(1)}, u32[]{:S(2)}, u32[]{:S(2)}) %collective-permute-start.13) | collective-permute-done | bytes 393248 | tf_op jit(solution)/shard_map/reduce2_snear/ppermute | solution.py:47
  44.4 0.1 merge.2.refs_0_
  44.5 2.1 %collective-permute-start.16 = (bf16[32,6144]{1,0:T(8,128)(2,1)S(1)}, bf16[32,6144]{1,0:T(8,128)(2,1)S(1)}, u32[]{:S(2)}, u32[]{:S(2)}) collective-permute-start(bf16[32,6144]{1,0:T(8,128)(2,1)S(1)} %merge.2.refs_0_), channel_id=1, source_target_pairs={{0,48},{8,200},{16,32},{24,216},{32,16},{40,232},{48,0},{56,248},{... | collective-permute-start | bytes 1179656 | tf_op jit(solution)/shard_map/reduce_swrap/ppermute | solution.py:47
  46.6 0.0 collective-permute-done.12.arrived
  46.6 0.1 merge.3
  46.7 0.1 collective-permute-start.14
  46.8 3.9 %collective-permute-done.11.refs_0_.direct = bf16[32,6144]{1,0:T(8,128)(2,1)S(1)} collective-permute-done((bf16[32,6144]{1,0:T(8,128)(2,1)S(1)}, bf16[32,6144]{1,0:T(8,128)(2,1)S(1)}, u32[]{:S(2)}, u32[]{:S(2)}) %collective-permute-start.11) | collective-permute-done | bytes 393248 | tf_op jit(solution)/shard_map/reduce_swrap/ppermute | solution.py:47
  50.8 0.5 collective-permute-done.15.direct
  51.3 3.7 %collective-permute-done.16.back = bf16[32,6144]{1,0:T(8,128)(2,1)S(1)} collective-permute-done((bf16[32,6144]{1,0:T(8,128)(2,1)S(1)}, bf16[32,6144]{1,0:T(8,128)(2,1)S(1)}, u32[]{:S(2)}, u32[]{:S(2)}) %collective-permute-start.16) | collective-permute-done | bytes 393248 | tf_op jit(solution)/shard_map/reduce_swrap/ppermute | solution.py:47
  55.0 0.1 finish.2
  55.1 3.1 %collective-permute-start.17 = (bf16[16,6144]{1,0:T(8,128)(2,1)S(1)}, bf16[16,6144]{1,0:T(8,128)(2,1)S(1)}, u32[]{:S(2)}, u32[]{:S(2)}) collective-permute-start(bf16[16,6144]{1,0:T(8,128)(2,1)S(1)} %get-tuple-element.31.refs_0_), channel_id=1, source_target_pairs={{0,192},{8,56},{16,208},{24,40},{32,224},{40,24},{48,240},{56,8},{... | collective-permute-start | bytes 589832 | tf_op jit(solution)/shard_map/home_twrap/ppermute | solution.py:47
  58.2 0.0 collective-permute-start.18
  58.2 0.0 collective-permute-done.14.back
  58.2 0.1 finish.3
  58.4 1.2 %collective-permute-start.19 = (bf16[16,6144]{1,0:T(8,128)(2,1)S(1)}, bf16[16,6144]{1,0:T(8,128)(2,1)S(1)}, u32[]{:S(2)}, u32[]{:S(2)}) collective-permute-start(bf16[16,6144]{1,0:T(8,128)(2,1)S(1)} %get-tuple-element.34), channel_id=1, source_target_pairs={{0,64},{8,24},{16,80},{24,8},{32,96},{40,56},{48,112},{56,40},{64,... | collective-permute-start | bytes 589832 | tf_op jit(solution)/shard_map/home_tnear/ppermute | solution.py:47
  60.2 3.3 %collective-permute-done.17.refs_2_ = bf16[16,6144]{1,0:T(8,128)(2,1)S(1)} collective-permute-done((bf16[16,6144]{1,0:T(8,128)(2,1)S(1)}, bf16[16,6144]{1,0:T(8,128)(2,1)S(1)}, u32[]{:S(2)}, u32[]{:S(2)}) %collective-permute-start.17) | collective-permute-done | bytes 196640 | tf_op jit(solution)/shard_map/home_twrap/ppermute | solution.py:47
  63.5 1.9 %collective-permute-done.18.refs_3_ = bf16[16,6144]{1,0:T(8,128)(2,1)S(1)} collective-permute-done((bf16[16,6144]{1,0:T(8,128)(2,1)S(1)}, bf16[16,6144]{1,0:T(8,128)(2,1)S(1)}, u32[]{:S(2)}, u32[]{:S(2)}) %collective-permute-start.18) | collective-permute-done | bytes 196640 | tf_op jit(solution)/shard_map/home_tfar/ppermute | solution.py:47
  65.4 0.1 collect.1
  65.5 0.8 %select_convert_fusion = bf16[16,6144]{1,0:T(8,128)(2,1)} fusion(f32[16,6144]{1,0:T(8,128)S(1)} %collect.1, bf16[16,6144]{1,0:T(8,128)(2,1)S(1)} %collective-permute-done.19, pred[16]{0:T(512)(128)(4,1)S(1)} %iota_compare_fusion), kind=kLoop, calls=%fused_computation | loop fusion | flops 393216 | bytes 786448 | tf_op jit(solution)/shard_map/convert_element_type | solution.py:349
  (8 shorter events, 0.1 us)
Async XLA Ops:
  0.0 23.9 %collective-permute-start.9 = (bf16[448,6144]{1,0:T(8,128)(2,1)}, bf16[448,6144]{1,0:T(8,128)(2,1)S(1)}, u32[]{:S(2)}, u32[]{:S(2)}) collective-permute-start(bf16[448,6144]{1,0:T(8,128)(2,1)} %bitcast.5), channel_id=1, source_target_pairs={{0,8},{8,0},{16,24},{24,16},{32,40},{40,32},{48,56},{56,48},{64,72... | collective-permute-start | bytes 16515080 | tf_op jit(solution)/shard_map/up_core/ppermute | solution.py:47
  3.4 5.8 %collective-permute-start = (bf16[16,6144]{1,0:T(8,128)(2,1)S(1)}, bf16[16,6144]{1,0:T(8,128)(2,1)S(1)}, u32[]{:S(2)}, u32[]{:S(2)}) collective-permute-start(bf16[16,6144]{1,0:T(8,128)(2,1)S(1)} %get-tuple-element.21.one), channel_id=1, source_target_pairs={{0,16},{8,72},{16,0},{24,88},{32,48},{40,104},{48,32},{56,120},{64... | collective-permute-start | bytes 589832 | tf_op jit(solution)/shard_map/gather_snear/ppermute | solution.py:47
  4.9 7.7 %collective-permute-start.1 = (bf16[16,6144]{1,0:T(8,128)(2,1)S(1)}, bf16[16,6144]{1,0:T(8,128)(2,1)S(1)}, u32[]{:S(2)}, u32[]{:S(2)}) collective-permute-start(bf16[16,6144]{1,0:T(8,128)(2,1)S(1)} %get-tuple-element.21.one), channel_id=1, source_target_pairs={{0,48},{8,200},{16,32},{24,216},{32,16},{40,232},{48,0},{56,248},{... | collective-permute-start | bytes 589832 | tf_op jit(solution)/shard_map/gather_swrap/ppermute | solution.py:47
  7.0 7.4 %collective-permute-start.2 = (bf16[16,6144]{1,0:T(8,128)(2,1)S(1)}, bf16[16,6144]{1,0:T(8,128)(2,1)S(1)}, u32[]{:S(2)}, u32[]{:S(2)}) collective-permute-start(bf16[16,6144]{1,0:T(8,128)(2,1)S(1)} %get-tuple-element.21.one), channel_id=1, source_target_pairs={{0,32},{8,136},{16,48},{24,152},{32,0},{40,168},{48,16},{56,184},{... | collective-permute-start | bytes 589832 | tf_op jit(solution)/shard_map/gather_sfar/ppermute | solution.py:47
  9.1 9.1 %collective-permute-start.4 = (bf16[32,6144]{1,0:T(8,128)(2,1)S(1)}, bf16[32,6144]{1,0:T(8,128)(2,1)S(1)}, u32[]{:S(2)}, u32[]{:S(2)}) collective-permute-start(bf16[32,6144]{1,0:T(8,128)(2,1)S(1)} %pack.2.args_0_), channel_id=1, source_target_pairs={{0,192},{8,56},{16,208},{24,40},{32,224},{40,24},{48,240},{56,8},{... | collective-permute-start | bytes 1179656 | tf_op jit(solution)/shard_map/gather_twrap/ppermute | solution.py:47
  12.2 7.8 %collective-permute-start.3 = (bf16[32,6144]{1,0:T(8,128)(2,1)S(1)}, bf16[32,6144]{1,0:T(8,128)(2,1)S(1)}, u32[]{:S(2)}, u32[]{:S(2)}) collective-permute-start(bf16[32,6144]{1,0:T(8,128)(2,1)S(1)} %pack.2.args_0_), channel_id=1, source_target_pairs={{0,64},{8,24},{16,80},{24,8},{32,96},{40,56},{48,112},{56,40},{64,... | collective-permute-start | bytes 1179656 | tf_op jit(solution)/shard_map/gather_tnear/ppermute | solution.py:47
  14.5 9.1 %collective-permute-start.6 = (bf16[32,6144]{1,0:T(8,128)(2,1)S(1)}, bf16[32,6144]{1,0:T(8,128)(2,1)S(1)}, u32[]{:S(2)}, u32[]{:S(2)}) collective-permute-start(bf16[32,6144]{1,0:T(8,128)(2,1)S(1)} %pack.3.after.args_1_), channel_id=1, source_target_pairs={{0,192},{8,56},{16,208},{24,40},{32,224},{40,24},{48,240},{56,8},{... | collective-permute-start | bytes 1179656 | tf_op jit(solution)/shard_map/gather_twrap/ppermute | solution.py:47
  17.6 8.9 %collective-permute-start.5 = (bf16[32,6144]{1,0:T(8,128)(2,1)S(1)}, bf16[32,6144]{1,0:T(8,128)(2,1)S(1)}, u32[]{:S(2)}, u32[]{:S(2)}) collective-permute-start(bf16[32,6144]{1,0:T(8,128)(2,1)S(1)} %pack.3.after.args_1_), channel_id=1, source_target_pairs={{0,64},{8,24},{16,80},{24,8},{32,96},{40,56},{48,112},{56,40},{64,... | collective-permute-start | bytes 1179656 | tf_op jit(solution)/shard_map/gather_tnear/ppermute | solution.py:47
  20.0 9.0 %collective-permute-start.7 = (bf16[32,6144]{1,0:T(8,128)(2,1)S(1)}, bf16[32,6144]{1,0:T(8,128)(2,1)S(1)}, u32[]{:S(2)}, u32[]{:S(2)}) collective-permute-start(bf16[32,6144]{1,0:T(8,128)(2,1)S(1)} %hand.2.args_2_), channel_id=1, source_target_pairs={{0,192},{8,56},{16,208},{24,40},{32,224},{40,24},{48,240},{56,8},{... | collective-permute-start | bytes 1179656 | tf_op jit(solution)/shard_map/gather2_twrap/ppermute | solution.py:47
  23.6 7.8 %collective-permute-start.8 = (bf16[32,6144]{1,0:T(8,128)(2,1)S(1)}, bf16[32,6144]{1,0:T(8,128)(2,1)S(1)}, u32[]{:S(2)}, u32[]{:S(2)}) collective-permute-start(bf16[32,6144]{1,0:T(8,128)(2,1)S(1)} %collective-permute-done.6.args_5_), channel_id=1, source_target_pairs={{0,64},{8,24},{16,80},{24,8},{32,96},{40,56},{48,112},{56,40},{64,... | collective-permute-start | bytes 1179656 | tf_op jit(solution)/shard_map/gather2_tnear/ppermute | solution.py:47
  23.9 10.5 %collective-permute-start.10 = (bf16[448,6144]{1,0:T(8,128)(2,1)S(1)}, bf16[448,6144]{1,0:T(8,128)(2,1)S(1)}, u32[]{:S(2)}, u32[]{:S(2)}) collective-permute-start(bf16[448,6144]{1,0:T(8,128)(2,1)S(1)} %hand.3.one), channel_id=1, source_target_pairs={{0,8},{8,0},{16,24},{24,16},{32,40},{40,32},{48,56},{56,48},{64,72... | collective-permute-start | bytes 16515080 | tf_op jit(solution)/shard_map/down_core/ppermute | solution.py:47
  36.5 7.9 %collective-permute-start.13 = (bf16[32,6144]{1,0:T(8,128)(2,1)S(1)}, bf16[32,6144]{1,0:T(8,128)(2,1)S(1)}, u32[]{:S(2)}, u32[]{:S(2)}) collective-permute-start(bf16[32,6144]{1,0:T(8,128)(2,1)S(1)} %get-tuple-element.28), channel_id=1, source_target_pairs={{0,16},{8,72},{16,0},{24,88},{32,48},{40,104},{48,32},{56,120},{64... | collective-permute-start | bytes 1179656 | tf_op jit(solution)/shard_map/reduce2_snear/ppermute | solution.py:47
  37.5 9.1 %collective-permute-start.12 = (bf16[32,6144]{1,0:T(8,128)(2,1)S(1)}, bf16[32,6144]{1,0:T(8,128)(2,1)S(1)}, u32[]{:S(2)}, u32[]{:S(2)}) collective-permute-start(bf16[32,6144]{1,0:T(8,128)(2,1)S(1)} %get-tuple-element.26), channel_id=1, source_target_pairs={{0,48},{8,200},{16,32},{24,216},{32,16},{40,232},{48,0},{56,248},{... | collective-permute-start | bytes 1179656 | tf_op jit(solution)/shard_map/reduce2_swrap/ppermute | solution.py:47
  41.7 9.1 %collective-permute-start.11 = (bf16[32,6144]{1,0:T(8,128)(2,1)S(1)}, bf16[32,6144]{1,0:T(8,128)(2,1)S(1)}, u32[]{:S(2)}, u32[]{:S(2)}) collective-permute-start(bf16[32,6144]{1,0:T(8,128)(2,1)S(1)} %get-tuple-element.24), channel_id=1, source_target_pairs={{0,48},{8,200},{16,32},{24,216},{32,16},{40,232},{48,0},{56,248},{... | collective-permute-start | bytes 1179656 | tf_op jit(solution)/shard_map/reduce_swrap/ppermute | solution.py:47
  43.5 7.8 %collective-permute-start.15 = (bf16[32,6144]{1,0:T(8,128)(2,1)S(1)}, bf16[32,6144]{1,0:T(8,128)(2,1)S(1)}, u32[]{:S(2)}, u32[]{:S(2)}) collective-permute-start(bf16[32,6144]{1,0:T(8,128)(2,1)S(1)} %get-tuple-element.30), channel_id=1, source_target_pairs={{0,16},{8,72},{16,0},{24,88},{32,48},{40,104},{48,32},{56,120},{64... | collective-permute-start | bytes 1179656 | tf_op jit(solution)/shard_map/reduce_snear/ppermute | solution.py:47
  44.5 10.5 %collective-permute-start.16 = (bf16[32,6144]{1,0:T(8,128)(2,1)S(1)}, bf16[32,6144]{1,0:T(8,128)(2,1)S(1)}, u32[]{:S(2)}, u32[]{:S(2)}) collective-permute-start(bf16[32,6144]{1,0:T(8,128)(2,1)S(1)} %merge.2.refs_0_), channel_id=1, source_target_pairs={{0,48},{8,200},{16,32},{24,216},{32,16},{40,232},{48,0},{56,248},{... | collective-permute-start | bytes 1179656 | tf_op jit(solution)/shard_map/reduce_swrap/ppermute | solution.py:47
  46.7 11.5 %collective-permute-start.14 = (bf16[32,6144]{1,0:T(8,128)(2,1)S(1)}, bf16[32,6144]{1,0:T(8,128)(2,1)S(1)}, u32[]{:S(2)}, u32[]{:S(2)}) collective-permute-start(bf16[32,6144]{1,0:T(8,128)(2,1)S(1)} %merge.3), channel_id=1, source_target_pairs={{0,16},{8,72},{16,0},{24,88},{32,48},{40,104},{48,32},{56,120},{64... | collective-permute-start | bytes 1179656 | tf_op jit(solution)/shard_map/reduce_snear/ppermute | solution.py:47
  55.1 8.4 %collective-permute-start.17 = (bf16[16,6144]{1,0:T(8,128)(2,1)S(1)}, bf16[16,6144]{1,0:T(8,128)(2,1)S(1)}, u32[]{:S(2)}, u32[]{:S(2)}) collective-permute-start(bf16[16,6144]{1,0:T(8,128)(2,1)S(1)} %get-tuple-element.31.refs_0_), channel_id=1, source_target_pairs={{0,192},{8,56},{16,208},{24,40},{32,224},{40,24},{48,240},{56,8},{... | collective-permute-start | bytes 589832 | tf_op jit(solution)/shard_map/home_twrap/ppermute | solution.py:47
  58.2 7.2 %collective-permute-start.18 = (bf16[16,6144]{1,0:T(8,128)(2,1)S(1)}, bf16[16,6144]{1,0:T(8,128)(2,1)S(1)}, u32[]{:S(2)}, u32[]{:S(2)}) collective-permute-start(bf16[16,6144]{1,0:T(8,128)(2,1)S(1)} %get-tuple-element.33), channel_id=1, source_target_pairs={{0,128},{8,40},{16,144},{24,56},{32,160},{40,8},{48,176},{56,24},{... | collective-permute-start | bytes 589832 | tf_op jit(solution)/shard_map/home_tfar/ppermute | solution.py:47
  58.4 7.1 %collective-permute-start.19 = (bf16[16,6144]{1,0:T(8,128)(2,1)S(1)}, bf16[16,6144]{1,0:T(8,128)(2,1)S(1)}, u32[]{:S(2)}, u32[]{:S(2)}) collective-permute-start(bf16[16,6144]{1,0:T(8,128)(2,1)S(1)} %get-tuple-element.34), channel_id=1, source_target_pairs={{0,64},{8,24},{16,80},{24,8},{32,96},{40,56},{48,112},{56,40},{64,... | collective-permute-start | bytes 589832 | tf_op jit(solution)/shard_map/home_tnear/ppermute | solution.py:47

commit v16 on v15

--- a/solution.py
+++ b/solution.py
@@ -344,7 +344,7 @@
     own, home_near = finish(early, direct_early, back_early, jnp.float32, after=(home_wrap,))
     home_wrap, home_far = send(home_wrap, "twrap", "home"), send(home_far, "tfar", "home")
     home_near = send(home_near, "tnear", "home")
-    mixed = collect(attended, own, home_wrap, home_far)
+    mixed = collect(attended, own, home_far, home_wrap)
     live = jnp.arange(SLOTS, dtype=jnp.int32)[:, None] < counts[0]
     return jnp.where(live, mixed + home_near.astype(jnp.float32), jnp.float32(0.0)).astype(jnp.bfloat16)
 

time: 66.4 us -> 65.8 us (level)
  transfers between devices with their start and end apart: 20 -> 20, of which waited for: 14 -> 15; matrix products, arithmetic and copies ran while one was open for 0% -> 0% of each run, Pallas kernels for 18% -> 19%
where the time goes in v16:
time: 65.8 us; the launch traced here: 65.7 us
  waiting for transfers between devices  26.8 us (41%)
  starting transfers between devices  23 us (35%)
  Pallas kernels  14.3 us (22%)
  other arithmetic  0.77 us (1%)
  between operations  0.77 us (1%)
    ppermute x20, waiting for transfers between devices, send(): return lax.ppermute(value, 'dp', ROUTES[route])  26.8 us
    ppermute x20, starting transfers between devices, send(): return lax.ppermute(value, 'dp', ROUTES[route])  23 us
    pallas_call x2, Pallas kernels, project_down(): pl.pallas_call(functools.partial(down_kernel, begin), out_shape=[jax.Shap...  4.66 us
    pallas_call x1, Pallas kernels, attend(): pl.pallas_call(attend_kernel, out_shape=(jax.ShapeDtypeStruct((SLOTS, D),...  3.34 us
    pallas_call x1, Pallas kernels, project_up(): pl.pallas_call(up_kernel, out_shape=jax.ShapeDtypeStruct((rows, 2 * HIDDE...  3.12 us
    pallas_call x1, Pallas kernels, fetch(): pl.pallas_call(fetch_kernel, out_shape=jax.ShapeDtypeStruct((HIDDEN, D),...  2.57 us
  transfers between devices with their start and end apart: 20, of which 15 were waited for; matrix products, arithmetic and copies ran while one was open for 0% of the time, Pallas kernels for 19%

profile of v16, /device:TPU:128, one launch (start us, length us, event | category | flops | bytes accessed | tf_op | source)
XLA Modules:
  0.0 65.7 jit_solution(13745795250663498829)
XLA Ops:
  0.0 0.0 collective-permute-start.9
  0.0 3.3 %attend.1 = (bf16[16,6144]{1,0:T(8,128)(2,1)S(1)}, bf16[16,6144]{1,0:T(8,128)(2,1)S(1)}, bf16[448,6144]{1,0:T(8,128)(2,1)S(1)}) custom-call(s32[16]{0:T(128)} %lengths_in.1, bf16[16,6144]{1,0:T(8,128)(2,1)} %q_in.1, bf16[1024,512]{1,0:T(8,128)(2,1)} %k_in.1, bf16[1024,512]{1,0:T(8,128)(2,1)} %v_in.1, f32[1,6144]{1,0:T(1,128)} %bitcast.4, bf16[448,6144]{1,0:T(8,128)(2,1)} %down.3), custom_call_target="tpu_custom_call" | custom-call | tf_op jit(solution)/shard_map/attend/pallas_call | solution.py:125
  3.4 1.6 %collective-permute-start = (bf16[16,6144]{1,0:T(8,128)(2,1)S(1)}, bf16[16,6144]{1,0:T(8,128)(2,1)S(1)}, u32[]{:S(2)}, u32[]{:S(2)}) collective-permute-start(bf16[16,6144]{1,0:T(8,128)(2,1)S(1)} %get-tuple-element.21.one), channel_id=1, source_target_pairs={{0,16},{8,72},{16,0},{24,88},{32,48},{40,104},{48,32},{56,120},{64... | collective-permute-start | bytes 589832 | tf_op jit(solution)/shard_map/gather_snear/ppermute | solution.py:47
  4.9 2.1 %collective-permute-start.1 = (bf16[16,6144]{1,0:T(8,128)(2,1)S(1)}, bf16[16,6144]{1,0:T(8,128)(2,1)S(1)}, u32[]{:S(2)}, u32[]{:S(2)}) collective-permute-start(bf16[16,6144]{1,0:T(8,128)(2,1)S(1)} %get-tuple-element.21.one), channel_id=1, source_target_pairs={{0,48},{8,200},{16,32},{24,216},{32,16},{40,232},{48,0},{56,248},{... | collective-permute-start | bytes 589832 | tf_op jit(solution)/shard_map/gather_swrap/ppermute | solution.py:47
  7.0 0.6 collective-permute-start.2
  7.7 1.4 %collective-permute-done.two = bf16[16,6144]{1,0:T(8,128)(2,1)S(1)} collective-permute-done((bf16[16,6144]{1,0:T(8,128)(2,1)S(1)}, bf16[16,6144]{1,0:T(8,128)(2,1)S(1)}, u32[]{:S(2)}, u32[]{:S(2)}) %collective-permute-start) | collective-permute-done | bytes 196640 | tf_op jit(solution)/shard_map/gather_snear/ppermute | solution.py:47
  9.1 3.1 %collective-permute-start.4 = (bf16[32,6144]{1,0:T(8,128)(2,1)S(1)}, bf16[32,6144]{1,0:T(8,128)(2,1)S(1)}, u32[]{:S(2)}, u32[]{:S(2)}) collective-permute-start(bf16[32,6144]{1,0:T(8,128)(2,1)S(1)} %pack.2.args_0_), channel_id=1, source_target_pairs={{0,192},{8,56},{16,208},{24,40},{32,224},{40,24},{48,240},{56,8},{... | collective-permute-start | bytes 1179656 | tf_op jit(solution)/shard_map/gather_twrap/ppermute | solution.py:47
  12.2 0.1 collective-permute-start.3
  12.4 0.3 collective-permute-done.1.one
  12.7 1.8 %collective-permute-done.2.two = bf16[16,6144]{1,0:T(8,128)(2,1)S(1)} collective-permute-done((bf16[16,6144]{1,0:T(8,128)(2,1)S(1)}, bf16[16,6144]{1,0:T(8,128)(2,1)S(1)}, u32[]{:S(2)}, u32[]{:S(2)}) %collective-permute-start.2) | collective-permute-done | bytes 196640 | tf_op jit(solution)/shard_map/gather_sfar/ppermute | solution.py:47
  14.5 3.1 %collective-permute-start.6 = (bf16[32,6144]{1,0:T(8,128)(2,1)S(1)}, bf16[32,6144]{1,0:T(8,128)(2,1)S(1)}, u32[]{:S(2)}, u32[]{:S(2)}) collective-permute-start(bf16[32,6144]{1,0:T(8,128)(2,1)S(1)} %pack.3.after.args_1_), channel_id=1, source_target_pairs={{0,192},{8,56},{16,208},{24,40},{32,224},{40,24},{48,240},{56,8},{... | collective-permute-start | bytes 1179656 | tf_op jit(solution)/shard_map/gather_twrap/ppermute | solution.py:47
  17.6 0.1 collective-permute-start.5
  17.7 0.5 collective-permute-done.4.refs_1_.args_4_
  18.2 1.8 %collective-permute-done.3.refs_0_ = bf16[32,6144]{1,0:T(8,128)(2,1)S(1)} collective-permute-done((bf16[32,6144]{1,0:T(8,128)(2,1)S(1)}, bf16[32,6144]{1,0:T(8,128)(2,1)S(1)}, u32[]{:S(2)}, u32[]{:S(2)}) %collective-permute-start.3) | collective-permute-done | bytes 393248 | tf_op jit(solution)/shard_map/gather_tnear/ppermute | solution.py:47
  20.0 1.2 %collective-permute-start.7 = (bf16[32,6144]{1,0:T(8,128)(2,1)S(1)}, bf16[32,6144]{1,0:T(8,128)(2,1)S(1)}, u32[]{:S(2)}, u32[]{:S(2)}) collective-permute-start(bf16[32,6144]{1,0:T(8,128)(2,1)S(1)} %hand.2.args_2_), channel_id=1, source_target_pairs={{0,192},{8,56},{16,208},{24,40},{32,224},{40,24},{48,240},{56,8},{... | collective-permute-start | bytes 1179656 | tf_op jit(solution)/shard_map/gather2_twrap/ppermute | solution.py:47
  21.2 2.3 %collective-permute-done.6.args_5_ = bf16[32,6144]{1,0:T(8,128)(2,1)S(1)} collective-permute-done((bf16[32,6144]{1,0:T(8,128)(2,1)S(1)}, bf16[32,6144]{1,0:T(8,128)(2,1)S(1)}, u32[]{:S(2)}, u32[]{:S(2)}) %collective-permute-start.6) | collective-permute-done | bytes 393248 | tf_op jit(solution)/shard_map/gather_twrap/ppermute | solution.py:47
  23.6 0.4 collective-permute-start.8
  23.9 0.0 collective-permute-done.9.args_9_.refs_1_
  23.9 0.0 collective-permute-start.10
  24.0 2.6 %fetch.1.args_8_ = bf16[448,6144]{1,0:T(8,128)(2,1)S(1)} custom-call(bf16[448,6144]{1,0:T(8,128)(2,1)} %bitcast.6, bf16[32,6144]{1,0:T(8,128)(2,1)S(1)} %pack.3.after.args_1_), custom_call_target="tpu_custom_call" | custom-call | flops 99999997952 | bytes 11010048 | tf_op jit(solution)/shard_map/fetch/pallas_call | solution.py:155
  26.5 2.5 %collective-permute-done.7.args_6_ = bf16[32,6144]{1,0:T(8,128)(2,1)S(1)} collective-permute-done((bf16[32,6144]{1,0:T(8,128)(2,1)S(1)}, bf16[32,6144]{1,0:T(8,128)(2,1)S(1)}, u32[]{:S(2)}, u32[]{:S(2)}) %collective-permute-start.7) | collective-permute-done | bytes 393248 | tf_op jit(solution)/shard_map/gather2_twrap/ppermute | solution.py:47
  29.0 2.3 %collective-permute-done.8.args_7_ = bf16[32,6144]{1,0:T(8,128)(2,1)S(1)} collective-permute-done((bf16[32,6144]{1,0:T(8,128)(2,1)S(1)}, bf16[32,6144]{1,0:T(8,128)(2,1)S(1)}, u32[]{:S(2)}, u32[]{:S(2)}) %collective-permute-start.8) | collective-permute-done | bytes 393248 | tf_op jit(solution)/shard_map/gather2_tnear/ppermute | solution.py:47
  31.4 3.1 %up.1.hidden = bf16[256,896]{1,0:T(8,128)(2,1)S(1)} custom-call(bf16[32,6144]{1,0:T(8,128)(2,1)S(1)} %pack.2.args_0_, bf16[32,6144]{1,0:T(8,128)(2,1)S(1)} %pack.3.after.args_1_, bf16[32,6144]{1,0:T(8,128)(2,1)S(1)} %hand.2.args_2_, bf16[32,6144]{1,0:T(8,128)(2,1)S(1)} %collective-permute-done.5.args_3_, ...), custom_call_target="tpu_custom_call" | custom-call | flops 2818572288 | bytes 3145728 | tf_op jit(solution)/shard_map/up/pallas_call | solution.py:184
  34.5 2.0 %down.5 = (bf16[32,6144]{1,0:T(8,128)(2,1)S(1)}, bf16[32,6144]{1,0:T(8,128)(2,1)S(1)}) custom-call(bf16[256,896]{1,0:T(8,128)(2,1)S(1)} %up.1.hidden, bf16[448,6144]{1,0:T(8,128)(2,1)S(1)} %hand.3.one, bf16[448,6144]{1,0:T(8,128)(2,1)S(1)} %collective-permute-done.10.two), custom_call_target="tpu_custom_call" | custom-call | flops 704643072 | bytes 786432 | tf_op jit(solution)/shard_map/down/pallas_call | solution.py:208
  36.5 1.0 %collective-permute-start.13 = (bf16[32,6144]{1,0:T(8,128)(2,1)S(1)}, bf16[32,6144]{1,0:T(8,128)(2,1)S(1)}, u32[]{:S(2)}, u32[]{:S(2)}) collective-permute-start(bf16[32,6144]{1,0:T(8,128)(2,1)S(1)} %get-tuple-element.28), channel_id=1, source_target_pairs={{0,16},{8,72},{16,0},{24,88},{32,48},{40,104},{48,32},{56,120},{64... | collective-permute-start | bytes 1179656 | tf_op jit(solution)/shard_map/reduce2_snear/ppermute | solution.py:47
  37.5 1.5 %collective-permute-start.12 = (bf16[32,6144]{1,0:T(8,128)(2,1)S(1)}, bf16[32,6144]{1,0:T(8,128)(2,1)S(1)}, u32[]{:S(2)}, u32[]{:S(2)}) collective-permute-start(bf16[32,6144]{1,0:T(8,128)(2,1)S(1)} %get-tuple-element.26), channel_id=1, source_target_pairs={{0,48},{8,200},{16,32},{24,216},{32,16},{40,232},{48,0},{56,248},{... | collective-permute-start | bytes 1179656 | tf_op jit(solution)/shard_map/reduce2_swrap/ppermute | solution.py:47
  39.1 2.6 %down.4 = (bf16[32,6144]{1,0:T(8,128)(2,1)S(1)}, bf16[32,6144]{1,0:T(8,128)(2,1)S(1)}, bf16[32,6144]{1,0:T(8,128)(2,1)S(1)}, bf16[32,6144]{1,0:T(8,128)(2,1)S(1)...) custom-call(bf16[256,896]{1,0:T(8,128)(2,1)S(1)} %up.1.hidden, bf16[448,6144]{1,0:T(8,128)(2,1)S(1)} %hand.3.one, ...), custom_call_target="tpu_custom_call" | custom-call | flops 2113929216 | bytes 2359296 | tf_op jit(solution)/shard_map/down/pallas_call | solution.py:208
  41.7 1.8 %collective-permute-start.11 = (bf16[32,6144]{1,0:T(8,128)(2,1)S(1)}, bf16[32,6144]{1,0:T(8,128)(2,1)S(1)}, u32[]{:S(2)}, u32[]{:S(2)}) collective-permute-start(bf16[32,6144]{1,0:T(8,128)(2,1)S(1)} %get-tuple-element.24), channel_id=1, source_target_pairs={{0,48},{8,200},{16,32},{24,216},{32,16},{40,232},{48,0},{56,248},{... | collective-permute-start | bytes 1179656 | tf_op jit(solution)/shard_map/reduce_swrap/ppermute | solution.py:47
  43.5 0.9 %collective-permute-done.13.arrived = bf16[32,6144]{1,0:T(8,128)(2,1)S(1)} collective-permute-done((bf16[32,6144]{1,0:T(8,128)(2,1)S(1)}, bf16[32,6144]{1,0:T(8,128)(2,1)S(1)}, u32[]{:S(2)}, u32[]{:S(2)}) %collective-permute-start.13) | collective-permute-done | bytes 393248 | tf_op jit(solution)/shard_map/reduce2_snear/ppermute | solution.py:47
  44.4 0.1 merge.2.refs_0_
  44.5 2.1 %collective-permute-start.16 = (bf16[32,6144]{1,0:T(8,128)(2,1)S(1)}, bf16[32,6144]{1,0:T(8,128)(2,1)S(1)}, u32[]{:S(2)}, u32[]{:S(2)}) collective-permute-start(bf16[32,6144]{1,0:T(8,128)(2,1)S(1)} %merge.2.refs_0_), channel_id=1, source_target_pairs={{0,48},{8,200},{16,32},{24,216},{32,16},{40,232},{48,0},{56,248},{... | collective-permute-start | bytes 1179656 | tf_op jit(solution)/shard_map/reduce_swrap/ppermute | solution.py:47
  46.6 0.0 collective-permute-done.12.arrived
  46.6 0.1 merge.3
  46.7 0.1 collective-permute-start.14
  46.8 3.9 %collective-permute-done.11.refs_0_.direct = bf16[32,6144]{1,0:T(8,128)(2,1)S(1)} collective-permute-done((bf16[32,6144]{1,0:T(8,128)(2,1)S(1)}, bf16[32,6144]{1,0:T(8,128)(2,1)S(1)}, u32[]{:S(2)}, u32[]{:S(2)}) %collective-permute-start.11) | collective-permute-done | bytes 393248 | tf_op jit(solution)/shard_map/reduce_swrap/ppermute | solution.py:47
  50.8 0.5 collective-permute-done.15.direct
  51.3 3.7 %collective-permute-done.16.back = bf16[32,6144]{1,0:T(8,128)(2,1)S(1)} collective-permute-done((bf16[32,6144]{1,0:T(8,128)(2,1)S(1)}, bf16[32,6144]{1,0:T(8,128)(2,1)S(1)}, u32[]{:S(2)}, u32[]{:S(2)}) %collective-permute-start.16) | collective-permute-done | bytes 393248 | tf_op jit(solution)/shard_map/reduce_swrap/ppermute | solution.py:47
  55.0 0.1 finish.2
  55.1 2.7 %collective-permute-start.17 = (bf16[16,6144]{1,0:T(8,128)(2,1)S(1)}, bf16[16,6144]{1,0:T(8,128)(2,1)S(1)}, u32[]{:S(2)}, u32[]{:S(2)}) collective-permute-start(bf16[16,6144]{1,0:T(8,128)(2,1)S(1)} %get-tuple-element.33), channel_id=1, source_target_pairs={{0,128},{8,40},{16,144},{24,56},{32,160},{40,8},{48,176},{56,24},{... | collective-permute-start | bytes 589832 | tf_op jit(solution)/shard_map/home_tfar/ppermute | solution.py:47
  57.8 0.5 collective-permute-start.18
  58.3 0.0 collective-permute-done.14.back
  58.3 0.1 finish.3
  58.5 0.8 %collective-permute-start.19 = (bf16[16,6144]{1,0:T(8,128)(2,1)S(1)}, bf16[16,6144]{1,0:T(8,128)(2,1)S(1)}, u32[]{:S(2)}, u32[]{:S(2)}) collective-permute-start(bf16[16,6144]{1,0:T(8,128)(2,1)S(1)} %get-tuple-element.34), channel_id=1, source_target_pairs={{0,64},{8,24},{16,80},{24,8},{32,96},{40,56},{48,112},{56,40},{64,... | collective-permute-start | bytes 589832 | tf_op jit(solution)/shard_map/home_tnear/ppermute | solution.py:47
  60.0 2.4 %collective-permute-done.17.refs_2_ = bf16[16,6144]{1,0:T(8,128)(2,1)S(1)} collective-permute-done((bf16[16,6144]{1,0:T(8,128)(2,1)S(1)}, bf16[16,6144]{1,0:T(8,128)(2,1)S(1)}, u32[]{:S(2)}, u32[]{:S(2)}) %collective-permute-start.17) | collective-permute-done | bytes 196640 | tf_op jit(solution)/shard_map/home_tfar/ppermute | solution.py:47
  62.4 2.3 %collective-permute-done.18.refs_3_ = bf16[16,6144]{1,0:T(8,128)(2,1)S(1)} collective-permute-done((bf16[16,6144]{1,0:T(8,128)(2,1)S(1)}, bf16[16,6144]{1,0:T(8,128)(2,1)S(1)}, u32[]{:S(2)}, u32[]{:S(2)}) %collective-permute-start.18) | collective-permute-done | bytes 196640 | tf_op jit(solution)/shard_map/home_twrap/ppermute | solution.py:47
  64.7 0.1 collect.1
  64.8 0.1 collective-permute-done.19
  64.9 0.8 %select_convert_fusion = bf16[16,6144]{1,0:T(8,128)(2,1)} fusion(f32[16,6144]{1,0:T(8,128)S(1)} %collect.1, bf16[16,6144]{1,0:T(8,128)(2,1)S(1)} %collective-permute-done.19, pred[16]{0:T(512)(128)(4,1)S(1)} %iota_compare_fusion), kind=kLoop, calls=%fused_computation | loop fusion | flops 393216 | bytes 786448 | tf_op jit(solution)/shard_map/convert_element_type | solution.py:349
  (8 shorter events, 0.1 us)
Async XLA Ops:
  0.0 23.9 %collective-permute-start.9 = (bf16[448,6144]{1,0:T(8,128)(2,1)}, bf16[448,6144]{1,0:T(8,128)(2,1)S(1)}, u32[]{:S(2)}, u32[]{:S(2)}) collective-permute-start(bf16[448,6144]{1,0:T(8,128)(2,1)} %bitcast.5), channel_id=1, source_target_pairs={{0,8},{8,0},{16,24},{24,16},{32,40},{40,32},{48,56},{56,48},{64,72... | collective-permute-start | bytes 16515080 | tf_op jit(solution)/shard_map/up_core/ppermute | solution.py:47
  3.4 5.8 %collective-permute-start = (bf16[16,6144]{1,0:T(8,128)(2,1)S(1)}, bf16[16,6144]{1,0:T(8,128)(2,1)S(1)}, u32[]{:S(2)}, u32[]{:S(2)}) collective-permute-start(bf16[16,6144]{1,0:T(8,128)(2,1)S(1)} %get-tuple-element.21.one), channel_id=1, source_target_pairs={{0,16},{8,72},{16,0},{24,88},{32,48},{40,104},{48,32},{56,120},{64... | collective-permute-start | bytes 589832 | tf_op jit(solution)/shard_map/gather_snear/ppermute | solution.py:47
  4.9 7.7 %collective-permute-start.1 = (bf16[16,6144]{1,0:T(8,128)(2,1)S(1)}, bf16[16,6144]{1,0:T(8,128)(2,1)S(1)}, u32[]{:S(2)}, u32[]{:S(2)}) collective-permute-start(bf16[16,6144]{1,0:T(8,128)(2,1)S(1)} %get-tuple-element.21.one), channel_id=1, source_target_pairs={{0,48},{8,200},{16,32},{24,216},{32,16},{40,232},{48,0},{56,248},{... | collective-permute-start | bytes 589832 | tf_op jit(solution)/shard_map/gather_swrap/ppermute | solution.py:47
  7.0 7.4 %collective-permute-start.2 = (bf16[16,6144]{1,0:T(8,128)(2,1)S(1)}, bf16[16,6144]{1,0:T(8,128)(2,1)S(1)}, u32[]{:S(2)}, u32[]{:S(2)}) collective-permute-start(bf16[16,6144]{1,0:T(8,128)(2,1)S(1)} %get-tuple-element.21.one), channel_id=1, source_target_pairs={{0,32},{8,136},{16,48},{24,152},{32,0},{40,168},{48,16},{56,184},{... | collective-permute-start | bytes 589832 | tf_op jit(solution)/shard_map/gather_sfar/ppermute | solution.py:47
  9.1 9.1 %collective-permute-start.4 = (bf16[32,6144]{1,0:T(8,128)(2,1)S(1)}, bf16[32,6144]{1,0:T(8,128)(2,1)S(1)}, u32[]{:S(2)}, u32[]{:S(2)}) collective-permute-start(bf16[32,6144]{1,0:T(8,128)(2,1)S(1)} %pack.2.args_0_), channel_id=1, source_target_pairs={{0,192},{8,56},{16,208},{24,40},{32,224},{40,24},{48,240},{56,8},{... | collective-permute-start | bytes 1179656 | tf_op jit(solution)/shard_map/gather_twrap/ppermute | solution.py:47
  12.2 7.8 %collective-permute-start.3 = (bf16[32,6144]{1,0:T(8,128)(2,1)S(1)}, bf16[32,6144]{1,0:T(8,128)(2,1)S(1)}, u32[]{:S(2)}, u32[]{:S(2)}) collective-permute-start(bf16[32,6144]{1,0:T(8,128)(2,1)S(1)} %pack.2.args_0_), channel_id=1, source_target_pairs={{0,64},{8,24},{16,80},{24,8},{32,96},{40,56},{48,112},{56,40},{64,... | collective-permute-start | bytes 1179656 | tf_op jit(solution)/shard_map/gather_tnear/ppermute | solution.py:47
  14.5 9.1 %collective-permute-start.6 = (bf16[32,6144]{1,0:T(8,128)(2,1)S(1)}, bf16[32,6144]{1,0:T(8,128)(2,1)S(1)}, u32[]{:S(2)}, u32[]{:S(2)}) collective-permute-start(bf16[32,6144]{1,0:T(8,128)(2,1)S(1)} %pack.3.after.args_1_), channel_id=1, source_target_pairs={{0,192},{8,56},{16,208},{24,40},{32,224},{40,24},{48,240},{56,8},{... | collective-permute-start | bytes 1179656 | tf_op jit(solution)/shard_map/gather_twrap/ppermute | solution.py:47
  17.6 8.9 %collective-permute-start.5 = (bf16[32,6144]{1,0:T(8,128)(2,1)S(1)}, bf16[32,6144]{1,0:T(8,128)(2,1)S(1)}, u32[]{:S(2)}, u32[]{:S(2)}) collective-permute-start(bf16[32,6144]{1,0:T(8,128)(2,1)S(1)} %pack.3.after.args_1_), channel_id=1, source_target_pairs={{0,64},{8,24},{16,80},{24,8},{32,96},{40,56},{48,112},{56,40},{64,... | collective-permute-start | bytes 1179656 | tf_op jit(solution)/shard_map/gather_tnear/ppermute | solution.py:47
  20.0 9.0 %collective-permute-start.7 = (bf16[32,6144]{1,0:T(8,128)(2,1)S(1)}, bf16[32,6144]{1,0:T(8,128)(2,1)S(1)}, u32[]{:S(2)}, u32[]{:S(2)}) collective-permute-start(bf16[32,6144]{1,0:T(8,128)(2,1)S(1)} %hand.2.args_2_), channel_id=1, source_target_pairs={{0,192},{8,56},{16,208},{24,40},{32,224},{40,24},{48,240},{56,8},{... | collective-permute-start | bytes 1179656 | tf_op jit(solution)/shard_map/gather2_twrap/ppermute | solution.py:47
  23.6 7.8 %collective-permute-start.8 = (bf16[32,6144]{1,0:T(8,128)(2,1)S(1)}, bf16[32,6144]{1,0:T(8,128)(2,1)S(1)}, u32[]{:S(2)}, u32[]{:S(2)}) collective-permute-start(bf16[32,6144]{1,0:T(8,128)(2,1)S(1)} %collective-permute-done.6.args_5_), channel_id=1, source_target_pairs={{0,64},{8,24},{16,80},{24,8},{32,96},{40,56},{48,112},{56,40},{64,... | collective-permute-start | bytes 1179656 | tf_op jit(solution)/shard_map/gather2_tnear/ppermute | solution.py:47
  23.9 10.5 %collective-permute-start.10 = (bf16[448,6144]{1,0:T(8,128)(2,1)S(1)}, bf16[448,6144]{1,0:T(8,128)(2,1)S(1)}, u32[]{:S(2)}, u32[]{:S(2)}) collective-permute-start(bf16[448,6144]{1,0:T(8,128)(2,1)S(1)} %hand.3.one), channel_id=1, source_target_pairs={{0,8},{8,0},{16,24},{24,16},{32,40},{40,32},{48,56},{56,48},{64,72... | collective-permute-start | bytes 16515080 | tf_op jit(solution)/shard_map/down_core/ppermute | solution.py:47
  36.5 7.9 %collective-permute-start.13 = (bf16[32,6144]{1,0:T(8,128)(2,1)S(1)}, bf16[32,6144]{1,0:T(8,128)(2,1)S(1)}, u32[]{:S(2)}, u32[]{:S(2)}) collective-permute-start(bf16[32,6144]{1,0:T(8,128)(2,1)S(1)} %get-tuple-element.28), channel_id=1, source_target_pairs={{0,16},{8,72},{16,0},{24,88},{32,48},{40,104},{48,32},{56,120},{64... | collective-permute-start | bytes 1179656 | tf_op jit(solution)/shard_map/reduce2_snear/ppermute | solution.py:47
  37.5 9.1 %collective-permute-start.12 = (bf16[32,6144]{1,0:T(8,128)(2,1)S(1)}, bf16[32,6144]{1,0:T(8,128)(2,1)S(1)}, u32[]{:S(2)}, u32[]{:S(2)}) collective-permute-start(bf16[32,6144]{1,0:T(8,128)(2,1)S(1)} %get-tuple-element.26), channel_id=1, source_target_pairs={{0,48},{8,200},{16,32},{24,216},{32,16},{40,232},{48,0},{56,248},{... | collective-permute-start | bytes 1179656 | tf_op jit(solution)/shard_map/reduce2_swrap/ppermute | solution.py:47
  41.7 9.1 %collective-permute-start.11 = (bf16[32,6144]{1,0:T(8,128)(2,1)S(1)}, bf16[32,6144]{1,0:T(8,128)(2,1)S(1)}, u32[]{:S(2)}, u32[]{:S(2)}) collective-permute-start(bf16[32,6144]{1,0:T(8,128)(2,1)S(1)} %get-tuple-element.24), channel_id=1, source_target_pairs={{0,48},{8,200},{16,32},{24,216},{32,16},{40,232},{48,0},{56,248},{... | collective-permute-start | bytes 1179656 | tf_op jit(solution)/shard_map/reduce_swrap/ppermute | solution.py:47
  43.5 7.8 %collective-permute-start.15 = (bf16[32,6144]{1,0:T(8,128)(2,1)S(1)}, bf16[32,6144]{1,0:T(8,128)(2,1)S(1)}, u32[]{:S(2)}, u32[]{:S(2)}) collective-permute-start(bf16[32,6144]{1,0:T(8,128)(2,1)S(1)} %get-tuple-element.30), channel_id=1, source_target_pairs={{0,16},{8,72},{16,0},{24,88},{32,48},{40,104},{48,32},{56,120},{64... | collective-permute-start | bytes 1179656 | tf_op jit(solution)/shard_map/reduce_snear/ppermute | solution.py:47
  44.5 10.5 %collective-permute-start.16 = (bf16[32,6144]{1,0:T(8,128)(2,1)S(1)}, bf16[32,6144]{1,0:T(8,128)(2,1)S(1)}, u32[]{:S(2)}, u32[]{:S(2)}) collective-permute-start(bf16[32,6144]{1,0:T(8,128)(2,1)S(1)} %merge.2.refs_0_), channel_id=1, source_target_pairs={{0,48},{8,200},{16,32},{24,216},{32,16},{40,232},{48,0},{56,248},{... | collective-permute-start | bytes 1179656 | tf_op jit(solution)/shard_map/reduce_swrap/ppermute | solution.py:47
  46.7 11.6 %collective-permute-start.14 = (bf16[32,6144]{1,0:T(8,128)(2,1)S(1)}, bf16[32,6144]{1,0:T(8,128)(2,1)S(1)}, u32[]{:S(2)}, u32[]{:S(2)}) collective-permute-start(bf16[32,6144]{1,0:T(8,128)(2,1)S(1)} %merge.3), channel_id=1, source_target_pairs={{0,16},{8,72},{16,0},{24,88},{32,48},{40,104},{48,32},{56,120},{64... | collective-permute-start | bytes 1179656 | tf_op jit(solution)/shard_map/reduce_snear/ppermute | solution.py:47
  55.1 7.3 %collective-permute-start.17 = (bf16[16,6144]{1,0:T(8,128)(2,1)S(1)}, bf16[16,6144]{1,0:T(8,128)(2,1)S(1)}, u32[]{:S(2)}, u32[]{:S(2)}) collective-permute-start(bf16[16,6144]{1,0:T(8,128)(2,1)S(1)} %get-tuple-element.33), channel_id=1, source_target_pairs={{0,128},{8,40},{16,144},{24,56},{32,160},{40,8},{48,176},{56,24},{... | collective-permute-start | bytes 589832 | tf_op jit(solution)/shard_map/home_tfar/ppermute | solution.py:47
  57.8 6.9 %collective-permute-start.18 = (bf16[16,6144]{1,0:T(8,128)(2,1)S(1)}, bf16[16,6144]{1,0:T(8,128)(2,1)S(1)}, u32[]{:S(2)}, u32[]{:S(2)}) collective-permute-start(bf16[16,6144]{1,0:T(8,128)(2,1)S(1)} %get-tuple-element.31.refs_0_), channel_id=1, source_target_pairs={{0,192},{8,56},{16,208},{24,40},{32,224},{40,24},{48,240},{56,8},{... | collective-permute-start | bytes 589832 | tf_op jit(solution)/shard_map/home_twrap/ppermute | solution.py:47
  58.5 6.4 %collective-permute-start.19 = (bf16[16,6144]{1,0:T(8,128)(2,1)S(1)}, bf16[16,6144]{1,0:T(8,128)(2,1)S(1)}, u32[]{:S(2)}, u32[]{:S(2)}) collective-permute-start(bf16[16,6144]{1,0:T(8,128)(2,1)S(1)} %get-tuple-element.34), channel_id=1, source_target_pairs={{0,64},{8,24},{16,80},{24,8},{32,96},{40,56},{48,112},{56,40},{64,... | collective-permute-start | bytes 589832 | tf_op jit(solution)/shard_map/home_tnear/ppermute | solution.py:47

commit v17 on v16

--- a/solution.py
+++ b/solution.py
@@ -321,8 +321,8 @@
     late = pack(by_wrap, by_far)
     early_n, late_w = send(early, "tnear", "gather"), send(late, "twrap", "gather")
     late_n, early_w = send(late, "tnear", "gather"), send(early, "twrap", "gather")
-    early_n = hand(early_n, early_w)
-    early_f, late_f = send(early_n, "twrap", "gather2"), send(late_w, "tnear", "gather2")
+    early_w = hand(early_w, early_n)
+    early_f, late_f = send(early_w, "tnear", "gather2"), send(late_n, "twrap", "gather2")
     down_held = hand(down_held, up_other)
     down_other = send(down_held, "core", "down")
     up_held = fetch(up_own, late)

time: 65.8 us -> 66 us (level)
  starting transfers between devices: 23 us -> 25.5 us
  waiting for transfers between devices: 26.8 us -> 24.5 us
    ppermute x20, starting transfers between devices: 23 us -> 25.5 us  [send(): return lax.ppermute(value, 'dp', ROUTES[route])]
    ppermute x20, waiting for transfers between devices: 26.8 us -> 24.5 us  [send(): return lax.ppermute(value, 'dp', ROUTES[route])]
  transfers between devices with their start and end apart: 20 -> 20, of which waited for: 15 -> 13; matrix products, arithmetic and copies ran while one was open for 0% -> 0% of each run, Pallas kernels for 19% -> 19%
where the time goes in v17:
time: 66 us; the launch traced here: 65.9 us
  starting transfers between devices  25.5 us (39%)
  waiting for transfers between devices  24.5 us (37%)
  Pallas kernels  14.3 us (22%)
  other arithmetic  0.77 us (1%)
  between operations  0.77 us (1%)
    ppermute x20, starting transfers between devices, send(): return lax.ppermute(value, 'dp', ROUTES[route])  25.5 us
    ppermute x20, waiting for transfers between devices, send(): return lax.ppermute(value, 'dp', ROUTES[route])  24.5 us
    pallas_call x2, Pallas kernels, project_down(): pl.pallas_call(functools.partial(down_kernel, begin), out_shape=[jax.Shap...  4.66 us
    pallas_call x1, Pallas kernels, attend(): pl.pallas_call(attend_kernel, out_shape=(jax.ShapeDtypeStruct((SLOTS, D),...  3.34 us
    pallas_call x1, Pallas kernels, project_up(): pl.pallas_call(up_kernel, out_shape=jax.ShapeDtypeStruct((rows, 2 * HIDDE...  3.13 us
    pallas_call x1, Pallas kernels, fetch(): pl.pallas_call(fetch_kernel, out_shape=jax.ShapeDtypeStruct((HIDDEN, D),...  2.57 us
  transfers between devices with their start and end apart: 20, of which 13 were waited for; matrix products, arithmetic and copies ran while one was open for 0% of the time, Pallas kernels for 19%

profile of v17, /device:TPU:128, one launch (start us, length us, event | category | flops | bytes accessed | tf_op | source)
XLA Modules:
  0.0 65.9 jit_solution(3105751899034317914)
XLA Ops:
  0.0 0.0 collective-permute-start.9
  0.0 3.3 %attend.1 = (bf16[16,6144]{1,0:T(8,128)(2,1)S(1)}, bf16[16,6144]{1,0:T(8,128)(2,1)S(1)}, bf16[448,6144]{1,0:T(8,128)(2,1)S(1)}) custom-call(s32[16]{0:T(128)} %lengths_in.1, bf16[16,6144]{1,0:T(8,128)(2,1)} %q_in.1, bf16[1024,512]{1,0:T(8,128)(2,1)} %k_in.1, bf16[1024,512]{1,0:T(8,128)(2,1)} %v_in.1, f32[1,6144]{1,0:T(1,128)} %bitcast.4, bf16[448,6144]{1,0:T(8,128)(2,1)} %down.3), custom_call_target="tpu_custom_call" | custom-call | tf_op jit(solution)/shard_map/attend/pallas_call | solution.py:125
  3.4 1.6 %collective-permute-start = (bf16[16,6144]{1,0:T(8,128)(2,1)S(1)}, bf16[16,6144]{1,0:T(8,128)(2,1)S(1)}, u32[]{:S(2)}, u32[]{:S(2)}) collective-permute-start(bf16[16,6144]{1,0:T(8,128)(2,1)S(1)} %get-tuple-element.21.one), channel_id=1, source_target_pairs={{0,16},{8,72},{16,0},{24,88},{32,48},{40,104},{48,32},{56,120},{64... | collective-permute-start | bytes 589832 | tf_op jit(solution)/shard_map/gather_snear/ppermute | solution.py:47
  4.9 2.1 %collective-permute-start.1 = (bf16[16,6144]{1,0:T(8,128)(2,1)S(1)}, bf16[16,6144]{1,0:T(8,128)(2,1)S(1)}, u32[]{:S(2)}, u32[]{:S(2)}) collective-permute-start(bf16[16,6144]{1,0:T(8,128)(2,1)S(1)} %get-tuple-element.21.one), channel_id=1, source_target_pairs={{0,48},{8,200},{16,32},{24,216},{32,16},{40,232},{48,0},{56,248},{... | collective-permute-start | bytes 589832 | tf_op jit(solution)/shard_map/gather_swrap/ppermute | solution.py:47
  7.0 0.6 collective-permute-start.2
  7.7 1.4 %collective-permute-done.two = bf16[16,6144]{1,0:T(8,128)(2,1)S(1)} collective-permute-done((bf16[16,6144]{1,0:T(8,128)(2,1)S(1)}, bf16[16,6144]{1,0:T(8,128)(2,1)S(1)}, u32[]{:S(2)}, u32[]{:S(2)}) %collective-permute-start) | collective-permute-done | bytes 196640 | tf_op jit(solution)/shard_map/gather_snear/ppermute | solution.py:47
  9.1 1.7 %collective-permute-start.3 = (bf16[32,6144]{1,0:T(8,128)(2,1)S(1)}, bf16[32,6144]{1,0:T(8,128)(2,1)S(1)}, u32[]{:S(2)}, u32[]{:S(2)}) collective-permute-start(bf16[32,6144]{1,0:T(8,128)(2,1)S(1)} %pack.2.args_0_), channel_id=1, source_target_pairs={{0,64},{8,24},{16,80},{24,8},{32,96},{40,56},{48,112},{56,40},{64,... | collective-permute-start | bytes 1179656 | tf_op jit(solution)/shard_map/gather_tnear/ppermute | solution.py:47
  10.8 2.2 %collective-permute-start.5 = (bf16[32,6144]{1,0:T(8,128)(2,1)S(1)}, bf16[32,6144]{1,0:T(8,128)(2,1)S(1)}, u32[]{:S(2)}, u32[]{:S(2)}) collective-permute-start(bf16[32,6144]{1,0:T(8,128)(2,1)S(1)} %pack.2.args_0_), channel_id=1, source_target_pairs={{0,192},{8,56},{16,208},{24,40},{32,224},{40,24},{48,240},{56,8},{... | collective-permute-start | bytes 1179656 | tf_op jit(solution)/shard_map/gather_twrap/ppermute | solution.py:47
  13.0 0.0 collective-permute-done.1.one
  13.0 1.7 %collective-permute-done.2.two = bf16[16,6144]{1,0:T(8,128)(2,1)S(1)} collective-permute-done((bf16[16,6144]{1,0:T(8,128)(2,1)S(1)}, bf16[16,6144]{1,0:T(8,128)(2,1)S(1)}, u32[]{:S(2)}, u32[]{:S(2)}) %collective-permute-start.2) | collective-permute-done | bytes 196640 | tf_op jit(solution)/shard_map/gather_sfar/ppermute | solution.py:47
  14.7 1.7 %collective-permute-start.4 = (bf16[32,6144]{1,0:T(8,128)(2,1)S(1)}, bf16[32,6144]{1,0:T(8,128)(2,1)S(1)}, u32[]{:S(2)}, u32[]{:S(2)}) collective-permute-start(bf16[32,6144]{1,0:T(8,128)(2,1)S(1)} %pack.3.after.args_1_), channel_id=1, source_target_pairs={{0,64},{8,24},{16,80},{24,8},{32,96},{40,56},{48,112},{56,40},{64,... | collective-permute-start | bytes 1179656 | tf_op jit(solution)/shard_map/gather_tnear/ppermute | solution.py:47
  16.4 2.2 %collective-permute-start.6 = (bf16[32,6144]{1,0:T(8,128)(2,1)S(1)}, bf16[32,6144]{1,0:T(8,128)(2,1)S(1)}, u32[]{:S(2)}, u32[]{:S(2)}) collective-permute-start(bf16[32,6144]{1,0:T(8,128)(2,1)S(1)} %pack.3.after.args_1_), channel_id=1, source_target_pairs={{0,192},{8,56},{16,208},{24,40},{32,224},{40,24},{48,240},{56,8},{... | collective-permute-start | bytes 1179656 | tf_op jit(solution)/shard_map/gather_twrap/ppermute | solution.py:47
  18.5 0.0 collective-permute-done.3.refs_1_.args_2_
  18.5 1.2 %collective-permute-done.5.refs_0_ = bf16[32,6144]{1,0:T(8,128)(2,1)S(1)} collective-permute-done((bf16[32,6144]{1,0:T(8,128)(2,1)S(1)}, bf16[32,6144]{1,0:T(8,128)(2,1)S(1)}, u32[]{:S(2)}, u32[]{:S(2)}) %collective-permute-start.5) | collective-permute-done | bytes 393248 | tf_op jit(solution)/shard_map/gather_twrap/ppermute | solution.py:47
  19.8 0.0 collective-permute-start.7
  19.8 2.8 %collective-permute-done.4.args_3_ = bf16[32,6144]{1,0:T(8,128)(2,1)S(1)} collective-permute-done((bf16[32,6144]{1,0:T(8,128)(2,1)S(1)}, bf16[32,6144]{1,0:T(8,128)(2,1)S(1)}, u32[]{:S(2)}, u32[]{:S(2)}) %collective-permute-start.4) | collective-permute-done | bytes 393248 | tf_op jit(solution)/shard_map/gather_tnear/ppermute | solution.py:47
  22.6 3.0 %collective-permute-start.8 = (bf16[32,6144]{1,0:T(8,128)(2,1)S(1)}, bf16[32,6144]{1,0:T(8,128)(2,1)S(1)}, u32[]{:S(2)}, u32[]{:S(2)}) collective-permute-start(bf16[32,6144]{1,0:T(8,128)(2,1)S(1)} %collective-permute-done.4.args_3_), channel_id=1, source_target_pairs={{0,192},{8,56},{16,208},{24,40},{32,224},{40,24},{48,240},{56,8},{... | collective-permute-start | bytes 1179656 | tf_op jit(solution)/shard_map/gather2_twrap/ppermute | solution.py:47
  25.6 0.0 collective-permute-done.9.args_9_.refs_1_
  25.6 0.0 collective-permute-start.10
  25.6 2.6 %fetch.1.args_8_ = bf16[448,6144]{1,0:T(8,128)(2,1)S(1)} custom-call(bf16[448,6144]{1,0:T(8,128)(2,1)} %bitcast.6, bf16[32,6144]{1,0:T(8,128)(2,1)S(1)} %pack.3.after.args_1_), custom_call_target="tpu_custom_call" | custom-call | flops 99999997952 | bytes 11010048 | tf_op jit(solution)/shard_map/fetch/pallas_call | solution.py:155
  28.2 0.0 collective-permute-done.7.args_6_
  28.2 3.4 %collective-permute-done.8.args_7_ = bf16[32,6144]{1,0:T(8,128)(2,1)S(1)} collective-permute-done((bf16[32,6144]{1,0:T(8,128)(2,1)S(1)}, bf16[32,6144]{1,0:T(8,128)(2,1)S(1)}, u32[]{:S(2)}, u32[]{:S(2)}) %collective-permute-start.8) | collective-permute-done | bytes 393248 | tf_op jit(solution)/shard_map/gather2_twrap/ppermute | solution.py:47
  31.6 3.1 %up.1.hidden = bf16[256,896]{1,0:T(8,128)(2,1)S(1)} custom-call(bf16[32,6144]{1,0:T(8,128)(2,1)S(1)} %pack.2.args_0_, bf16[32,6144]{1,0:T(8,128)(2,1)S(1)} %pack.3.after.args_1_, bf16[32,6144]{1,0:T(8,128)(2,1)S(1)} %collective-permute-done.3.refs_1_.args_2_, bf16[32,6144]{1,0:T(8,128)(2,1)S(1)} %collective-permute-done.4.args_3_, ...), custom_call_target="tpu_custom_call" | custom-call | flops 2818572288 | bytes 3145728 | tf_op jit(solution)/shard_map/up/pallas_call | solution.py:184
  34.7 0.0 collective-permute-done.10.two
  34.7 2.0 %down.5 = (bf16[32,6144]{1,0:T(8,128)(2,1)S(1)}, bf16[32,6144]{1,0:T(8,128)(2,1)S(1)}) custom-call(bf16[256,896]{1,0:T(8,128)(2,1)S(1)} %up.1.hidden, bf16[448,6144]{1,0:T(8,128)(2,1)S(1)} %hand.3.one, bf16[448,6144]{1,0:T(8,128)(2,1)S(1)} %collective-permute-done.10.two), custom_call_target="tpu_custom_call" | custom-call | flops 704643072 | bytes 786432 | tf_op jit(solution)/shard_map/down/pallas_call | solution.py:208
  36.7 1.1 %collective-permute-start.13 = (bf16[32,6144]{1,0:T(8,128)(2,1)S(1)}, bf16[32,6144]{1,0:T(8,128)(2,1)S(1)}, u32[]{:S(2)}, u32[]{:S(2)}) collective-permute-start(bf16[32,6144]{1,0:T(8,128)(2,1)S(1)} %get-tuple-element.28), channel_id=1, source_target_pairs={{0,16},{8,72},{16,0},{24,88},{32,48},{40,104},{48,32},{56,120},{64... | collective-permute-start | bytes 1179656 | tf_op jit(solution)/shard_map/reduce2_snear/ppermute | solution.py:47
  37.8 1.2 %collective-permute-start.12 = (bf16[32,6144]{1,0:T(8,128)(2,1)S(1)}, bf16[32,6144]{1,0:T(8,128)(2,1)S(1)}, u32[]{:S(2)}, u32[]{:S(2)}) collective-permute-start(bf16[32,6144]{1,0:T(8,128)(2,1)S(1)} %get-tuple-element.26), channel_id=1, source_target_pairs={{0,48},{8,200},{16,32},{24,216},{32,16},{40,232},{48,0},{56,248},{... | collective-permute-start | bytes 1179656 | tf_op jit(solution)/shard_map/reduce2_swrap/ppermute | solution.py:47
  39.1 2.6 %down.4 = (bf16[32,6144]{1,0:T(8,128)(2,1)S(1)}, bf16[32,6144]{1,0:T(8,128)(2,1)S(1)}, bf16[32,6144]{1,0:T(8,128)(2,1)S(1)}, bf16[32,6144]{1,0:T(8,128)(2,1)S(1)...) custom-call(bf16[256,896]{1,0:T(8,128)(2,1)S(1)} %up.1.hidden, bf16[448,6144]{1,0:T(8,128)(2,1)S(1)} %hand.3.one, ...), custom_call_target="tpu_custom_call" | custom-call | flops 2113929216 | bytes 2359296 | tf_op jit(solution)/shard_map/down/pallas_call | solution.py:208
  41.7 2.1 %collective-permute-start.11 = (bf16[32,6144]{1,0:T(8,128)(2,1)S(1)}, bf16[32,6144]{1,0:T(8,128)(2,1)S(1)}, u32[]{:S(2)}, u32[]{:S(2)}) collective-permute-start(bf16[32,6144]{1,0:T(8,128)(2,1)S(1)} %get-tuple-element.24), channel_id=1, source_target_pairs={{0,48},{8,200},{16,32},{24,216},{32,16},{40,232},{48,0},{56,248},{... | collective-permute-start | bytes 1179656 | tf_op jit(solution)/shard_map/reduce_swrap/ppermute | solution.py:47
  43.8 0.8 %collective-permute-done.13.arrived = bf16[32,6144]{1,0:T(8,128)(2,1)S(1)} collective-permute-done((bf16[32,6144]{1,0:T(8,128)(2,1)S(1)}, bf16[32,6144]{1,0:T(8,128)(2,1)S(1)}, u32[]{:S(2)}, u32[]{:S(2)}) %collective-permute-start.13) | collective-permute-done | bytes 393248 | tf_op jit(solution)/shard_map/reduce2_snear/ppermute | solution.py:47
  44.6 0.1 merge.2.refs_0_
  44.7 2.0 %collective-permute-start.16 = (bf16[32,6144]{1,0:T(8,128)(2,1)S(1)}, bf16[32,6144]{1,0:T(8,128)(2,1)S(1)}, u32[]{:S(2)}, u32[]{:S(2)}) collective-permute-start(bf16[32,6144]{1,0:T(8,128)(2,1)S(1)} %merge.2.refs_0_), channel_id=1, source_target_pairs={{0,48},{8,200},{16,32},{24,216},{32,16},{40,232},{48,0},{56,248},{... | collective-permute-start | bytes 1179656 | tf_op jit(solution)/shard_map/reduce_swrap/ppermute | solution.py:47
  46.7 0.1 collective-permute-done.12.arrived
  46.8 0.1 merge.3
  46.9 0.1 collective-permute-start.14
  47.0 4.0 %collective-permute-done.11.refs_0_.direct = bf16[32,6144]{1,0:T(8,128)(2,1)S(1)} collective-permute-done((bf16[32,6144]{1,0:T(8,128)(2,1)S(1)}, bf16[32,6144]{1,0:T(8,128)(2,1)S(1)}, u32[]{:S(2)}, u32[]{:S(2)}) %collective-permute-start.11) | collective-permute-done | bytes 393248 | tf_op jit(solution)/shard_map/reduce_swrap/ppermute | solution.py:47
  51.0 0.5 collective-permute-done.15.direct
  51.6 3.7 %collective-permute-done.16.back = bf16[32,6144]{1,0:T(8,128)(2,1)S(1)} collective-permute-done((bf16[32,6144]{1,0:T(8,128)(2,1)S(1)}, bf16[32,6144]{1,0:T(8,128)(2,1)S(1)}, u32[]{:S(2)}, u32[]{:S(2)}) %collective-permute-start.16) | collective-permute-done | bytes 393248 | tf_op jit(solution)/shard_map/reduce_swrap/ppermute | solution.py:47
  55.2 0.1 finish.2
  55.4 2.1 %collective-permute-start.17 = (bf16[16,6144]{1,0:T(8,128)(2,1)S(1)}, bf16[16,6144]{1,0:T(8,128)(2,1)S(1)}, u32[]{:S(2)}, u32[]{:S(2)}) collective-permute-start(bf16[16,6144]{1,0:T(8,128)(2,1)S(1)} %get-tuple-element.33), channel_id=1, source_target_pairs={{0,128},{8,40},{16,144},{24,56},{32,160},{40,8},{48,176},{56,24},{... | collective-permute-start | bytes 589832 | tf_op jit(solution)/shard_map/home_tfar/ppermute | solution.py:47
  57.5 1.1 %collective-permute-start.18 = (bf16[16,6144]{1,0:T(8,128)(2,1)S(1)}, bf16[16,6144]{1,0:T(8,128)(2,1)S(1)}, u32[]{:S(2)}, u32[]{:S(2)}) collective-permute-start(bf16[16,6144]{1,0:T(8,128)(2,1)S(1)} %get-tuple-element.31.refs_0_), channel_id=1, source_target_pairs={{0,192},{8,56},{16,208},{24,40},{32,224},{40,24},{48,240},{56,8},{... | collective-permute-start | bytes 589832 | tf_op jit(solution)/shard_map/home_twrap/ppermute | solution.py:47
  58.6 0.1 finish.3
  58.7 0.8 %collective-permute-start.19 = (bf16[16,6144]{1,0:T(8,128)(2,1)S(1)}, bf16[16,6144]{1,0:T(8,128)(2,1)S(1)}, u32[]{:S(2)}, u32[]{:S(2)}) collective-permute-start(bf16[16,6144]{1,0:T(8,128)(2,1)S(1)} %get-tuple-element.34), channel_id=1, source_target_pairs={{0,64},{8,24},{16,80},{24,8},{32,96},{40,56},{48,112},{56,40},{64,... | collective-permute-start | bytes 589832 | tf_op jit(solution)/shard_map/home_tnear/ppermute | solution.py:47
  60.2 2.5 %collective-permute-done.17.refs_2_ = bf16[16,6144]{1,0:T(8,128)(2,1)S(1)} collective-permute-done((bf16[16,6144]{1,0:T(8,128)(2,1)S(1)}, bf16[16,6144]{1,0:T(8,128)(2,1)S(1)}, u32[]{:S(2)}, u32[]{:S(2)}) %collective-permute-start.17) | collective-permute-done | bytes 196640 | tf_op jit(solution)/shard_map/home_tfar/ppermute | solution.py:47
  62.7 2.1 %collective-permute-done.18.refs_3_ = bf16[16,6144]{1,0:T(8,128)(2,1)S(1)} collective-permute-done((bf16[16,6144]{1,0:T(8,128)(2,1)S(1)}, bf16[16,6144]{1,0:T(8,128)(2,1)S(1)}, u32[]{:S(2)}, u32[]{:S(2)}) %collective-permute-start.18) | collective-permute-done | bytes 196640 | tf_op jit(solution)/shard_map/home_twrap/ppermute | solution.py:47
  64.8 0.1 collect.1
  64.8 0.3 collective-permute-done.19
  65.1 0.8 %select_convert_fusion = bf16[16,6144]{1,0:T(8,128)(2,1)} fusion(f32[16,6144]{1,0:T(8,128)S(1)} %collect.1, bf16[16,6144]{1,0:T(8,128)(2,1)S(1)} %collective-permute-done.19, pred[16]{0:T(512)(128)(4,1)S(1)} %iota_compare_fusion), kind=kLoop, calls=%fused_computation | loop fusion | flops 393216 | bytes 786448 | tf_op jit(solution)/shard_map/convert_element_type | solution.py:349
  (8 shorter events, 0.1 us)
Async XLA Ops:
  0.0 25.6 %collective-permute-start.9 = (bf16[448,6144]{1,0:T(8,128)(2,1)}, bf16[448,6144]{1,0:T(8,128)(2,1)S(1)}, u32[]{:S(2)}, u32[]{:S(2)}) collective-permute-start(bf16[448,6144]{1,0:T(8,128)(2,1)} %bitcast.5), channel_id=1, source_target_pairs={{0,8},{8,0},{16,24},{24,16},{32,40},{40,32},{48,56},{56,48},{64,72... | collective-permute-start | bytes 16515080 | tf_op jit(solution)/shard_map/up_core/ppermute | solution.py:47
  3.4 5.8 %collective-permute-start = (bf16[16,6144]{1,0:T(8,128)(2,1)S(1)}, bf16[16,6144]{1,0:T(8,128)(2,1)S(1)}, u32[]{:S(2)}, u32[]{:S(2)}) collective-permute-start(bf16[16,6144]{1,0:T(8,128)(2,1)S(1)} %get-tuple-element.21.one), channel_id=1, source_target_pairs={{0,16},{8,72},{16,0},{24,88},{32,48},{40,104},{48,32},{56,120},{64... | collective-permute-start | bytes 589832 | tf_op jit(solution)/shard_map/gather_snear/ppermute | solution.py:47
  4.9 8.1 %collective-permute-start.1 = (bf16[16,6144]{1,0:T(8,128)(2,1)S(1)}, bf16[16,6144]{1,0:T(8,128)(2,1)S(1)}, u32[]{:S(2)}, u32[]{:S(2)}) collective-permute-start(bf16[16,6144]{1,0:T(8,128)(2,1)S(1)} %get-tuple-element.21.one), channel_id=1, source_target_pairs={{0,48},{8,200},{16,32},{24,216},{32,16},{40,232},{48,0},{56,248},{... | collective-permute-start | bytes 589832 | tf_op jit(solution)/shard_map/gather_swrap/ppermute | solution.py:47
  7.0 7.6 %collective-permute-start.2 = (bf16[16,6144]{1,0:T(8,128)(2,1)S(1)}, bf16[16,6144]{1,0:T(8,128)(2,1)S(1)}, u32[]{:S(2)}, u32[]{:S(2)}) collective-permute-start(bf16[16,6144]{1,0:T(8,128)(2,1)S(1)} %get-tuple-element.21.one), channel_id=1, source_target_pairs={{0,32},{8,136},{16,48},{24,152},{32,0},{40,168},{48,16},{56,184},{... | collective-permute-start | bytes 589832 | tf_op jit(solution)/shard_map/gather_sfar/ppermute | solution.py:47
  9.1 9.4 %collective-permute-start.3 = (bf16[32,6144]{1,0:T(8,128)(2,1)S(1)}, bf16[32,6144]{1,0:T(8,128)(2,1)S(1)}, u32[]{:S(2)}, u32[]{:S(2)}) collective-permute-start(bf16[32,6144]{1,0:T(8,128)(2,1)S(1)} %pack.2.args_0_), channel_id=1, source_target_pairs={{0,64},{8,24},{16,80},{24,8},{32,96},{40,56},{48,112},{56,40},{64,... | collective-permute-start | bytes 1179656 | tf_op jit(solution)/shard_map/gather_tnear/ppermute | solution.py:47
  10.8 9.0 %collective-permute-start.5 = (bf16[32,6144]{1,0:T(8,128)(2,1)S(1)}, bf16[32,6144]{1,0:T(8,128)(2,1)S(1)}, u32[]{:S(2)}, u32[]{:S(2)}) collective-permute-start(bf16[32,6144]{1,0:T(8,128)(2,1)S(1)} %pack.2.args_0_), channel_id=1, source_target_pairs={{0,192},{8,56},{16,208},{24,40},{32,224},{40,24},{48,240},{56,8},{... | collective-permute-start | bytes 1179656 | tf_op jit(solution)/shard_map/gather_twrap/ppermute | solution.py:47
  14.7 7.9 %collective-permute-start.4 = (bf16[32,6144]{1,0:T(8,128)(2,1)S(1)}, bf16[32,6144]{1,0:T(8,128)(2,1)S(1)}, u32[]{:S(2)}, u32[]{:S(2)}) collective-permute-start(bf16[32,6144]{1,0:T(8,128)(2,1)S(1)} %pack.3.after.args_1_), channel_id=1, source_target_pairs={{0,64},{8,24},{16,80},{24,8},{32,96},{40,56},{48,112},{56,40},{64,... | collective-permute-start | bytes 1179656 | tf_op jit(solution)/shard_map/gather_tnear/ppermute | solution.py:47
  16.4 11.8 %collective-permute-start.6 = (bf16[32,6144]{1,0:T(8,128)(2,1)S(1)}, bf16[32,6144]{1,0:T(8,128)(2,1)S(1)}, u32[]{:S(2)}, u32[]{:S(2)}) collective-permute-start(bf16[32,6144]{1,0:T(8,128)(2,1)S(1)} %pack.3.after.args_1_), channel_id=1, source_target_pairs={{0,192},{8,56},{16,208},{24,40},{32,224},{40,24},{48,240},{56,8},{... | collective-permute-start | bytes 1179656 | tf_op jit(solution)/shard_map/gather_twrap/ppermute | solution.py:47
  19.8 8.4 %collective-permute-start.7 = (bf16[32,6144]{1,0:T(8,128)(2,1)S(1)}, bf16[32,6144]{1,0:T(8,128)(2,1)S(1)}, u32[]{:S(2)}, u32[]{:S(2)}) collective-permute-start(bf16[32,6144]{1,0:T(8,128)(2,1)S(1)} %hand.2.args_4_), channel_id=1, source_target_pairs={{0,64},{8,24},{16,80},{24,8},{32,96},{40,56},{48,112},{56,40},{64,... | collective-permute-start | bytes 1179656 | tf_op jit(solution)/shard_map/gather2_tnear/ppermute | solution.py:47
  22.6 9.0 %collective-permute-start.8 = (bf16[32,6144]{1,0:T(8,128)(2,1)S(1)}, bf16[32,6144]{1,0:T(8,128)(2,1)S(1)}, u32[]{:S(2)}, u32[]{:S(2)}) collective-permute-start(bf16[32,6144]{1,0:T(8,128)(2,1)S(1)} %collective-permute-done.4.args_3_), channel_id=1, source_target_pairs={{0,192},{8,56},{16,208},{24,40},{32,224},{40,24},{48,240},{56,8},{... | collective-permute-start | bytes 1179656 | tf_op jit(solution)/shard_map/gather2_twrap/ppermute | solution.py:47
  25.6 9.1 %collective-permute-start.10 = (bf16[448,6144]{1,0:T(8,128)(2,1)S(1)}, bf16[448,6144]{1,0:T(8,128)(2,1)S(1)}, u32[]{:S(2)}, u32[]{:S(2)}) collective-permute-start(bf16[448,6144]{1,0:T(8,128)(2,1)S(1)} %hand.3.one), channel_id=1, source_target_pairs={{0,8},{8,0},{16,24},{24,16},{32,40},{40,32},{48,56},{56,48},{64,72... | collective-permute-start | bytes 16515080 | tf_op jit(solution)/shard_map/down_core/ppermute | solution.py:47
  36.7 7.9 %collective-permute-start.13 = (bf16[32,6144]{1,0:T(8,128)(2,1)S(1)}, bf16[32,6144]{1,0:T(8,128)(2,1)S(1)}, u32[]{:S(2)}, u32[]{:S(2)}) collective-permute-start(bf16[32,6144]{1,0:T(8,128)(2,1)S(1)} %get-tuple-element.28), channel_id=1, source_target_pairs={{0,16},{8,72},{16,0},{24,88},{32,48},{40,104},{48,32},{56,120},{64... | collective-permute-start | bytes 1179656 | tf_op jit(solution)/shard_map/reduce2_snear/ppermute | solution.py:47
  37.8 9.0 %collective-permute-start.12 = (bf16[32,6144]{1,0:T(8,128)(2,1)S(1)}, bf16[32,6144]{1,0:T(8,128)(2,1)S(1)}, u32[]{:S(2)}, u32[]{:S(2)}) collective-permute-start(bf16[32,6144]{1,0:T(8,128)(2,1)S(1)} %get-tuple-element.26), channel_id=1, source_target_pairs={{0,48},{8,200},{16,32},{24,216},{32,16},{40,232},{48,0},{56,248},{... | collective-permute-start | bytes 1179656 | tf_op jit(solution)/shard_map/reduce2_swrap/ppermute | solution.py:47
  41.7 9.3 %collective-permute-start.11 = (bf16[32,6144]{1,0:T(8,128)(2,1)S(1)}, bf16[32,6144]{1,0:T(8,128)(2,1)S(1)}, u32[]{:S(2)}, u32[]{:S(2)}) collective-permute-start(bf16[32,6144]{1,0:T(8,128)(2,1)S(1)} %get-tuple-element.24), channel_id=1, source_target_pairs={{0,48},{8,200},{16,32},{24,216},{32,16},{40,232},{48,0},{56,248},{... | collective-permute-start | bytes 1179656 | tf_op jit(solution)/shard_map/reduce_swrap/ppermute | solution.py:47
  43.8 7.8 %collective-permute-start.15 = (bf16[32,6144]{1,0:T(8,128)(2,1)S(1)}, bf16[32,6144]{1,0:T(8,128)(2,1)S(1)}, u32[]{:S(2)}, u32[]{:S(2)}) collective-permute-start(bf16[32,6144]{1,0:T(8,128)(2,1)S(1)} %get-tuple-element.30), channel_id=1, source_target_pairs={{0,16},{8,72},{16,0},{24,88},{32,48},{40,104},{48,32},{56,120},{64... | collective-permute-start | bytes 1179656 | tf_op jit(solution)/shard_map/reduce_snear/ppermute | solution.py:47
  44.7 10.5 %collective-permute-start.16 = (bf16[32,6144]{1,0:T(8,128)(2,1)S(1)}, bf16[32,6144]{1,0:T(8,128)(2,1)S(1)}, u32[]{:S(2)}, u32[]{:S(2)}) collective-permute-start(bf16[32,6144]{1,0:T(8,128)(2,1)S(1)} %merge.2.refs_0_), channel_id=1, source_target_pairs={{0,48},{8,200},{16,32},{24,216},{32,16},{40,232},{48,0},{56,248},{... | collective-permute-start | bytes 1179656 | tf_op jit(solution)/shard_map/reduce_swrap/ppermute | solution.py:47
  46.9 11.7 %collective-permute-start.14 = (bf16[32,6144]{1,0:T(8,128)(2,1)S(1)}, bf16[32,6144]{1,0:T(8,128)(2,1)S(1)}, u32[]{:S(2)}, u32[]{:S(2)}) collective-permute-start(bf16[32,6144]{1,0:T(8,128)(2,1)S(1)} %merge.3), channel_id=1, source_target_pairs={{0,16},{8,72},{16,0},{24,88},{32,48},{40,104},{48,32},{56,120},{64... | collective-permute-start | bytes 1179656 | tf_op jit(solution)/shard_map/reduce_snear/ppermute | solution.py:47
  55.4 7.3 %collective-permute-start.17 = (bf16[16,6144]{1,0:T(8,128)(2,1)S(1)}, bf16[16,6144]{1,0:T(8,128)(2,1)S(1)}, u32[]{:S(2)}, u32[]{:S(2)}) collective-permute-start(bf16[16,6144]{1,0:T(8,128)(2,1)S(1)} %get-tuple-element.33), channel_id=1, source_target_pairs={{0,128},{8,40},{16,144},{24,56},{32,160},{40,8},{48,176},{56,24},{... | collective-permute-start | bytes 589832 | tf_op jit(solution)/shard_map/home_tfar/ppermute | solution.py:47
  57.5 7.3 %collective-permute-start.18 = (bf16[16,6144]{1,0:T(8,128)(2,1)S(1)}, bf16[16,6144]{1,0:T(8,128)(2,1)S(1)}, u32[]{:S(2)}, u32[]{:S(2)}) collective-permute-start(bf16[16,6144]{1,0:T(8,128)(2,1)S(1)} %get-tuple-element.31.refs_0_), channel_id=1, source_target_pairs={{0,192},{8,56},{16,208},{24,40},{32,224},{40,24},{48,240},{56,8},{... | collective-permute-start | bytes 589832 | tf_op jit(solution)/shard_map/home_twrap/ppermute | solution.py:47
  58.7 6.4 %collective-permute-start.19 = (bf16[16,6144]{1,0:T(8,128)(2,1)S(1)}, bf16[16,6144]{1,0:T(8,128)(2,1)S(1)}, u32[]{:S(2)}, u32[]{:S(2)}) collective-permute-start(bf16[16,6144]{1,0:T(8,128)(2,1)S(1)} %get-tuple-element.34), channel_id=1, source_target_pairs={{0,64},{8,24},{16,80},{24,8},{32,96},{40,56},{48,112},{56,40},{64,... | collective-permute-start | bytes 589832 | tf_op jit(solution)/shard_map/home_tnear/ppermute | solution.py:47

commit v18 on v16

--- a/solution.py
+++ b/solution.py
@@ -167,7 +167,7 @@
 def up_kernel(*args):
     blocks, up, hidden = args[:8], args[8:10], args[10]
     lows, highs = slice(0, SLOTS), slice(SLOTS, PAIR)
-    order = [(part, half) for part in (0, 1) for half in (lows, highs)]
+    order = [(0, lows), (0, highs), (1, highs), (1, lows)]
     rows = jnp.concatenate([blocks[2 * t + part][half, :] for part, half in order for t in range(SIDE)], axis=0)
     value = lax.dot_general(
         jnp.concatenate([w[...] for w in up], axis=0),
@@ -318,7 +318,7 @@
     )
     by_wrap, by_far, by_near = [send(normed, r, "gather") for r in ("swrap", "sfar", "snear")]
     early = pack(normed, by_near)
-    late = pack(by_wrap, by_far)
+    late = pack(by_far, by_wrap)
     early_n, late_w = send(early, "tnear", "gather"), send(late, "twrap", "gather")
     late_n, early_w = send(late, "tnear", "gather"), send(early, "twrap", "gather")
     early_n = hand(early_n, early_w)

time: 65.8 us -> 68.3 us (1.038)
  waiting for transfers between devices: 26.8 us -> 30.6 us
  starting transfers between devices: 23 us -> 21.7 us
    ppermute x20, waiting for transfers between devices: 26.8 us -> 30.6 us  [send(): return lax.ppermute(value, 'dp', ROUTES[route])]
    ppermute x20, starting transfers between devices: 23 us -> 21.7 us  [send(): return lax.ppermute(value, 'dp', ROUTES[route])]
  transfers between devices with their start and end apart: 20 -> 20, of which waited for: 15 -> 14; matrix products, arithmetic and copies ran while one was open for 0% -> 0% of each run, Pallas kernels for 19% -> 18%
where the time goes in v18:
time: 68.3 us; the launch traced here: 68.1 us
  waiting for transfers between devices  30.6 us (45%)
  starting transfers between devices  21.7 us (32%)
  Pallas kernels  14.3 us (21%)
  other arithmetic  0.77 us (1%)
  between operations  0.77 us (1%)
    ppermute x20, waiting for transfers between devices, send(): return lax.ppermute(value, 'dp', ROUTES[route])  30.6 us
    ppermute x20, starting transfers between devices, send(): return lax.ppermute(value, 'dp', ROUTES[route])  21.7 us
    pallas_call x2, Pallas kernels, project_down(): pl.pallas_call(functools.partial(down_kernel, begin), out_shape=[jax.Shap...  4.66 us
    pallas_call x1, Pallas kernels, attend(): pl.pallas_call(attend_kernel, out_shape=(jax.ShapeDtypeStruct((SLOTS, D),...  3.34 us
    pallas_call x1, Pallas kernels, project_up(): pl.pallas_call(up_kernel, out_shape=jax.ShapeDtypeStruct((rows, 2 * HIDDE...  3.13 us
    pallas_call x1, Pallas kernels, fetch(): pl.pallas_call(fetch_kernel, out_shape=jax.ShapeDtypeStruct((HIDDEN, D),...  2.57 us
  transfers between devices with their start and end apart: 20, of which 14 were waited for; matrix products, arithmetic and copies ran while one was open for 0% of the time, Pallas kernels for 18%

profile of v18, /device:TPU:128, one launch (start us, length us, event | category | flops | bytes accessed | tf_op | source)
XLA Modules:
  0.0 68.1 jit_solution(12779713084225499511)
XLA Ops:
  0.0 0.0 collective-permute-start.9
  0.0 3.3 %attend.1 = (bf16[16,6144]{1,0:T(8,128)(2,1)S(1)}, bf16[16,6144]{1,0:T(8,128)(2,1)S(1)}, bf16[448,6144]{1,0:T(8,128)(2,1)S(1)}) custom-call(s32[16]{0:T(128)} %lengths_in.1, bf16[16,6144]{1,0:T(8,128)(2,1)} %q_in.1, bf16[1024,512]{1,0:T(8,128)(2,1)} %k_in.1, bf16[1024,512]{1,0:T(8,128)(2,1)} %v_in.1, f32[1,6144]{1,0:T(1,128)} %bitcast.4, bf16[448,6144]{1,0:T(8,128)(2,1)} %down.3), custom_call_target="tpu_custom_call" | custom-call | tf_op jit(solution)/shard_map/attend/pallas_call | solution.py:125
  3.4 1.6 %collective-permute-start = (bf16[16,6144]{1,0:T(8,128)(2,1)S(1)}, bf16[16,6144]{1,0:T(8,128)(2,1)S(1)}, u32[]{:S(2)}, u32[]{:S(2)}) collective-permute-start(bf16[16,6144]{1,0:T(8,128)(2,1)S(1)} %get-tuple-element.21.one), channel_id=1, source_target_pairs={{0,16},{8,72},{16,0},{24,88},{32,48},{40,104},{48,32},{56,120},{64... | collective-permute-start | bytes 589832 | tf_op jit(solution)/shard_map/gather_snear/ppermute | solution.py:47
  4.9 2.7 %collective-permute-start.1 = (bf16[16,6144]{1,0:T(8,128)(2,1)S(1)}, bf16[16,6144]{1,0:T(8,128)(2,1)S(1)}, u32[]{:S(2)}, u32[]{:S(2)}) collective-permute-start(bf16[16,6144]{1,0:T(8,128)(2,1)S(1)} %get-tuple-element.21.one), channel_id=1, source_target_pairs={{0,32},{8,136},{16,48},{24,152},{32,0},{40,168},{48,16},{56,184},{... | collective-permute-start | bytes 589832 | tf_op jit(solution)/shard_map/gather_sfar/ppermute | solution.py:47
  7.7 0.5 collective-permute-start.2
  8.1 1.0 %collective-permute-done.two = bf16[16,6144]{1,0:T(8,128)(2,1)S(1)} collective-permute-done((bf16[16,6144]{1,0:T(8,128)(2,1)S(1)}, bf16[16,6144]{1,0:T(8,128)(2,1)S(1)}, u32[]{:S(2)}, u32[]{:S(2)}) %collective-permute-start) | collective-permute-done | bytes 196640 | tf_op jit(solution)/shard_map/gather_snear/ppermute | solution.py:47
  9.1 3.1 %collective-permute-start.4 = (bf16[32,6144]{1,0:T(8,128)(2,1)S(1)}, bf16[32,6144]{1,0:T(8,128)(2,1)S(1)}, u32[]{:S(2)}, u32[]{:S(2)}) collective-permute-start(bf16[32,6144]{1,0:T(8,128)(2,1)S(1)} %pack.2.args_0_), channel_id=1, source_target_pairs={{0,192},{8,56},{16,208},{24,40},{32,224},{40,24},{48,240},{56,8},{... | collective-permute-start | bytes 1179656 | tf_op jit(solution)/shard_map/gather_twrap/ppermute | solution.py:47
  12.2 0.1 collective-permute-start.3
  12.4 1.1 %collective-permute-done.1.one = bf16[16,6144]{1,0:T(8,128)(2,1)S(1)} collective-permute-done((bf16[16,6144]{1,0:T(8,128)(2,1)S(1)}, bf16[16,6144]{1,0:T(8,128)(2,1)S(1)}, u32[]{:S(2)}, u32[]{:S(2)}) %collective-permute-start.1) | collective-permute-done | bytes 196640 | tf_op jit(solution)/shard_map/gather_sfar/ppermute | solution.py:47
  13.5 4.1 %collective-permute-done.2.two = bf16[16,6144]{1,0:T(8,128)(2,1)S(1)} collective-permute-done((bf16[16,6144]{1,0:T(8,128)(2,1)S(1)}, bf16[16,6144]{1,0:T(8,128)(2,1)S(1)}, u32[]{:S(2)}, u32[]{:S(2)}) %collective-permute-start.2) | collective-permute-done | bytes 196640 | tf_op jit(solution)/shard_map/gather_swrap/ppermute | solution.py:47
  17.6 3.1 %collective-permute-start.6 = (bf16[32,6144]{1,0:T(8,128)(2,1)S(1)}, bf16[32,6144]{1,0:T(8,128)(2,1)S(1)}, u32[]{:S(2)}, u32[]{:S(2)}) collective-permute-start(bf16[32,6144]{1,0:T(8,128)(2,1)S(1)} %pack.3.after.args_1_), channel_id=1, source_target_pairs={{0,192},{8,56},{16,208},{24,40},{32,224},{40,24},{48,240},{56,8},{... | collective-permute-start | bytes 1179656 | tf_op jit(solution)/shard_map/gather_twrap/ppermute | solution.py:47
  20.7 0.1 collective-permute-start.5
  20.9 0.0 collective-permute-done.4.refs_1_.args_4_
  20.9 0.0 collective-permute-done.3.refs_0_
  20.9 1.1 %collective-permute-start.7 = (bf16[32,6144]{1,0:T(8,128)(2,1)S(1)}, bf16[32,6144]{1,0:T(8,128)(2,1)S(1)}, u32[]{:S(2)}, u32[]{:S(2)}) collective-permute-start(bf16[32,6144]{1,0:T(8,128)(2,1)S(1)} %hand.2.args_2_), channel_id=1, source_target_pairs={{0,192},{8,56},{16,208},{24,40},{32,224},{40,24},{48,240},{56,8},{... | collective-permute-start | bytes 1179656 | tf_op jit(solution)/shard_map/gather2_twrap/ppermute | solution.py:47
  21.9 4.8 %collective-permute-done.6.args_5_ = bf16[32,6144]{1,0:T(8,128)(2,1)S(1)} collective-permute-done((bf16[32,6144]{1,0:T(8,128)(2,1)S(1)}, bf16[32,6144]{1,0:T(8,128)(2,1)S(1)}, u32[]{:S(2)}, u32[]{:S(2)}) %collective-permute-start.6) | collective-permute-done | bytes 393248 | tf_op jit(solution)/shard_map/gather_twrap/ppermute | solution.py:47
  26.7 0.4 collective-permute-start.8
  27.1 0.0 collective-permute-done.9.args_9_.refs_1_
  27.1 2.6 %fetch.1.args_8_ = bf16[448,6144]{1,0:T(8,128)(2,1)S(1)} custom-call(bf16[448,6144]{1,0:T(8,128)(2,1)} %bitcast.6, bf16[32,6144]{1,0:T(8,128)(2,1)S(1)} %pack.3.after.args_1_), custom_call_target="tpu_custom_call" | custom-call | flops 99999997952 | bytes 11010048 | tf_op jit(solution)/shard_map/fetch/pallas_call | solution.py:155
  29.7 1.3 %collective-permute-done.7.args_6_ = bf16[32,6144]{1,0:T(8,128)(2,1)S(1)} collective-permute-done((bf16[32,6144]{1,0:T(8,128)(2,1)S(1)}, bf16[32,6144]{1,0:T(8,128)(2,1)S(1)}, u32[]{:S(2)}, u32[]{:S(2)}) %collective-permute-start.7) | collective-permute-done | bytes 393248 | tf_op jit(solution)/shard_map/gather2_twrap/ppermute | solution.py:47
  30.9 3.6 %collective-permute-done.8.args_7_ = bf16[32,6144]{1,0:T(8,128)(2,1)S(1)} collective-permute-done((bf16[32,6144]{1,0:T(8,128)(2,1)S(1)}, bf16[32,6144]{1,0:T(8,128)(2,1)S(1)}, u32[]{:S(2)}, u32[]{:S(2)}) %collective-permute-start.8) | collective-permute-done | bytes 393248 | tf_op jit(solution)/shard_map/gather2_tnear/ppermute | solution.py:47
  34.5 3.1 %up.1.hidden = bf16[256,896]{1,0:T(8,128)(2,1)S(1)} custom-call(bf16[32,6144]{1,0:T(8,128)(2,1)S(1)} %pack.2.args_0_, bf16[32,6144]{1,0:T(8,128)(2,1)S(1)} %pack.3.after.args_1_, bf16[32,6144]{1,0:T(8,128)(2,1)S(1)} %hand.2.args_2_, bf16[32,6144]{1,0:T(8,128)(2,1)S(1)} %collective-permute-done.5.args_3_, ...), custom_call_target="tpu_custom_call" | custom-call | flops 2818572288 | bytes 3145728 | tf_op jit(solution)/shard_map/up/pallas_call | solution.py:184
  37.6 0.0 collective-permute-done.10.two
  37.6 2.0 %down.5 = (bf16[32,6144]{1,0:T(8,128)(2,1)S(1)}, bf16[32,6144]{1,0:T(8,128)(2,1)S(1)}) custom-call(bf16[256,896]{1,0:T(8,128)(2,1)S(1)} %up.1.hidden, bf16[448,6144]{1,0:T(8,128)(2,1)S(1)} %hand.3.one, bf16[448,6144]{1,0:T(8,128)(2,1)S(1)} %collective-permute-done.10.two), custom_call_target="tpu_custom_call" | custom-call | flops 704643072 | bytes 786432 | tf_op jit(solution)/shard_map/down/pallas_call | solution.py:208
  39.7 0.1 collective-permute-start.13
  39.8 0.6 collective-permute-start.12
  40.4 2.6 %down.4 = (bf16[32,6144]{1,0:T(8,128)(2,1)S(1)}, bf16[32,6144]{1,0:T(8,128)(2,1)S(1)}, bf16[32,6144]{1,0:T(8,128)(2,1)S(1)}, bf16[32,6144]{1,0:T(8,128)(2,1)S(1)...) custom-call(bf16[256,896]{1,0:T(8,128)(2,1)S(1)} %up.1.hidden, bf16[448,6144]{1,0:T(8,128)(2,1)S(1)} %hand.3.one, ...), custom_call_target="tpu_custom_call" | custom-call | flops 2113929216 | bytes 2359296 | tf_op jit(solution)/shard_map/down/pallas_call | solution.py:208
  43.0 3.0 %collective-permute-start.11 = (bf16[32,6144]{1,0:T(8,128)(2,1)S(1)}, bf16[32,6144]{1,0:T(8,128)(2,1)S(1)}, u32[]{:S(2)}, u32[]{:S(2)}) collective-permute-start(bf16[32,6144]{1,0:T(8,128)(2,1)S(1)} %get-tuple-element.24), channel_id=1, source_target_pairs={{0,48},{8,200},{16,32},{24,216},{32,16},{40,232},{48,0},{56,248},{... | collective-permute-start | bytes 1179656 | tf_op jit(solution)/shard_map/reduce_swrap/ppermute | solution.py:47
  46.0 0.5 collective-permute-start.15
  46.5 1.0 %collective-permute-done.13.arrived = bf16[32,6144]{1,0:T(8,128)(2,1)S(1)} collective-permute-done((bf16[32,6144]{1,0:T(8,128)(2,1)S(1)}, bf16[32,6144]{1,0:T(8,128)(2,1)S(1)}, u32[]{:S(2)}, u32[]{:S(2)}) %collective-permute-start.13) | collective-permute-done | bytes 393248 | tf_op jit(solution)/shard_map/reduce2_snear/ppermute | solution.py:47
  47.5 0.1 merge.2.refs_0_
  47.6 0.1 collective-permute-start.16
  47.7 1.3 %collective-permute-done.12.arrived = bf16[32,6144]{1,0:T(8,128)(2,1)S(1)} collective-permute-done((bf16[32,6144]{1,0:T(8,128)(2,1)S(1)}, bf16[32,6144]{1,0:T(8,128)(2,1)S(1)}, u32[]{:S(2)}, u32[]{:S(2)}) %collective-permute-start.12) | collective-permute-done | bytes 393248 | tf_op jit(solution)/shard_map/reduce2_swrap/ppermute | solution.py:47
  49.0 0.1 merge.3
  49.1 0.6 collective-permute-start.14
  49.8 3.5 %collective-permute-done.11.refs_0_.direct = bf16[32,6144]{1,0:T(8,128)(2,1)S(1)} collective-permute-done((bf16[32,6144]{1,0:T(8,128)(2,1)S(1)}, bf16[32,6144]{1,0:T(8,128)(2,1)S(1)}, u32[]{:S(2)}, u32[]{:S(2)}) %collective-permute-start.11) | collective-permute-done | bytes 393248 | tf_op jit(solution)/shard_map/reduce_swrap/ppermute | solution.py:47
  53.2 0.5 collective-permute-done.15.direct
  53.8 3.7 %collective-permute-done.16.back = bf16[32,6144]{1,0:T(8,128)(2,1)S(1)} collective-permute-done((bf16[32,6144]{1,0:T(8,128)(2,1)S(1)}, bf16[32,6144]{1,0:T(8,128)(2,1)S(1)}, u32[]{:S(2)}, u32[]{:S(2)}) %collective-permute-start.16) | collective-permute-done | bytes 393248 | tf_op jit(solution)/shard_map/reduce_swrap/ppermute | solution.py:47
  57.5 0.1 finish.2
  57.6 2.7 %collective-permute-start.17 = (bf16[16,6144]{1,0:T(8,128)(2,1)S(1)}, bf16[16,6144]{1,0:T(8,128)(2,1)S(1)}, u32[]{:S(2)}, u32[]{:S(2)}) collective-permute-start(bf16[16,6144]{1,0:T(8,128)(2,1)S(1)} %get-tuple-element.33), channel_id=1, source_target_pairs={{0,128},{8,40},{16,144},{24,56},{32,160},{40,8},{48,176},{56,24},{... | collective-permute-start | bytes 589832 | tf_op jit(solution)/shard_map/home_tfar/ppermute | solution.py:47
  60.3 0.5 collective-permute-start.18
  60.8 0.1 finish.3
  61.0 0.8 %collective-permute-start.19 = (bf16[16,6144]{1,0:T(8,128)(2,1)S(1)}, bf16[16,6144]{1,0:T(8,128)(2,1)S(1)}, u32[]{:S(2)}, u32[]{:S(2)}) collective-permute-start(bf16[16,6144]{1,0:T(8,128)(2,1)S(1)} %get-tuple-element.34), channel_id=1, source_target_pairs={{0,64},{8,24},{16,80},{24,8},{32,96},{40,56},{48,112},{56,40},{64,... | collective-permute-start | bytes 589832 | tf_op jit(solution)/shard_map/home_tnear/ppermute | solution.py:47
  62.5 2.4 %collective-permute-done.17.refs_2_ = bf16[16,6144]{1,0:T(8,128)(2,1)S(1)} collective-permute-done((bf16[16,6144]{1,0:T(8,128)(2,1)S(1)}, bf16[16,6144]{1,0:T(8,128)(2,1)S(1)}, u32[]{:S(2)}, u32[]{:S(2)}) %collective-permute-start.17) | collective-permute-done | bytes 196640 | tf_op jit(solution)/shard_map/home_tfar/ppermute | solution.py:47
  64.9 2.3 %collective-permute-done.18.refs_3_ = bf16[16,6144]{1,0:T(8,128)(2,1)S(1)} collective-permute-done((bf16[16,6144]{1,0:T(8,128)(2,1)S(1)}, bf16[16,6144]{1,0:T(8,128)(2,1)S(1)}, u32[]{:S(2)}, u32[]{:S(2)}) %collective-permute-start.18) | collective-permute-done | bytes 196640 | tf_op jit(solution)/shard_map/home_twrap/ppermute | solution.py:47
  67.2 0.1 collect.1
  67.3 0.1 collective-permute-done.19
  67.4 0.8 %select_convert_fusion = bf16[16,6144]{1,0:T(8,128)(2,1)} fusion(f32[16,6144]{1,0:T(8,128)S(1)} %collect.1, bf16[16,6144]{1,0:T(8,128)(2,1)S(1)} %collective-permute-done.19, pred[16]{0:T(512)(128)(4,1)S(1)} %iota_compare_fusion), kind=kLoop, calls=%fused_computation | loop fusion | flops 393216 | bytes 786448 | tf_op jit(solution)/shard_map/convert_element_type | solution.py:349
  (8 shorter events, 0.1 us)
Async XLA Ops:
  0.0 27.1 %collective-permute-start.9 = (bf16[448,6144]{1,0:T(8,128)(2,1)}, bf16[448,6144]{1,0:T(8,128)(2,1)S(1)}, u32[]{:S(2)}, u32[]{:S(2)}) collective-permute-start(bf16[448,6144]{1,0:T(8,128)(2,1)} %bitcast.5), channel_id=1, source_target_pairs={{0,8},{8,0},{16,24},{24,16},{32,40},{40,32},{48,56},{56,48},{64,72... | collective-permute-start | bytes 16515080 | tf_op jit(solution)/shard_map/up_core/ppermute | solution.py:47
  3.4 5.8 %collective-permute-start = (bf16[16,6144]{1,0:T(8,128)(2,1)S(1)}, bf16[16,6144]{1,0:T(8,128)(2,1)S(1)}, u32[]{:S(2)}, u32[]{:S(2)}) collective-permute-start(bf16[16,6144]{1,0:T(8,128)(2,1)S(1)} %get-tuple-element.21.one), channel_id=1, source_target_pairs={{0,16},{8,72},{16,0},{24,88},{32,48},{40,104},{48,32},{56,120},{64... | collective-permute-start | bytes 589832 | tf_op jit(solution)/shard_map/gather_snear/ppermute | solution.py:47
  4.9 8.6 %collective-permute-start.1 = (bf16[16,6144]{1,0:T(8,128)(2,1)S(1)}, bf16[16,6144]{1,0:T(8,128)(2,1)S(1)}, u32[]{:S(2)}, u32[]{:S(2)}) collective-permute-start(bf16[16,6144]{1,0:T(8,128)(2,1)S(1)} %get-tuple-element.21.one), channel_id=1, source_target_pairs={{0,32},{8,136},{16,48},{24,152},{32,0},{40,168},{48,16},{56,184},{... | collective-permute-start | bytes 589832 | tf_op jit(solution)/shard_map/gather_sfar/ppermute | solution.py:47
  7.7 9.9 %collective-permute-start.2 = (bf16[16,6144]{1,0:T(8,128)(2,1)S(1)}, bf16[16,6144]{1,0:T(8,128)(2,1)S(1)}, u32[]{:S(2)}, u32[]{:S(2)}) collective-permute-start(bf16[16,6144]{1,0:T(8,128)(2,1)S(1)} %get-tuple-element.21.one), channel_id=1, source_target_pairs={{0,48},{8,200},{16,32},{24,216},{32,16},{40,232},{48,0},{56,248},{... | collective-permute-start | bytes 589832 | tf_op jit(solution)/shard_map/gather_swrap/ppermute | solution.py:47
  9.1 11.7 %collective-permute-start.4 = (bf16[32,6144]{1,0:T(8,128)(2,1)S(1)}, bf16[32,6144]{1,0:T(8,128)(2,1)S(1)}, u32[]{:S(2)}, u32[]{:S(2)}) collective-permute-start(bf16[32,6144]{1,0:T(8,128)(2,1)S(1)} %pack.2.args_0_), channel_id=1, source_target_pairs={{0,192},{8,56},{16,208},{24,40},{32,224},{40,24},{48,240},{56,8},{... | collective-permute-start | bytes 1179656 | tf_op jit(solution)/shard_map/gather_twrap/ppermute | solution.py:47
  12.2 8.6 %collective-permute-start.3 = (bf16[32,6144]{1,0:T(8,128)(2,1)S(1)}, bf16[32,6144]{1,0:T(8,128)(2,1)S(1)}, u32[]{:S(2)}, u32[]{:S(2)}) collective-permute-start(bf16[32,6144]{1,0:T(8,128)(2,1)S(1)} %pack.2.args_0_), channel_id=1, source_target_pairs={{0,64},{8,24},{16,80},{24,8},{32,96},{40,56},{48,112},{56,40},{64,... | collective-permute-start | bytes 1179656 | tf_op jit(solution)/shard_map/gather_tnear/ppermute | solution.py:47
  17.6 9.1 %collective-permute-start.6 = (bf16[32,6144]{1,0:T(8,128)(2,1)S(1)}, bf16[32,6144]{1,0:T(8,128)(2,1)S(1)}, u32[]{:S(2)}, u32[]{:S(2)}) collective-permute-start(bf16[32,6144]{1,0:T(8,128)(2,1)S(1)} %pack.3.after.args_1_), channel_id=1, source_target_pairs={{0,192},{8,56},{16,208},{24,40},{32,224},{40,24},{48,240},{56,8},{... | collective-permute-start | bytes 1179656 | tf_op jit(solution)/shard_map/gather_twrap/ppermute | solution.py:47
  20.7 8.9 %collective-permute-start.5 = (bf16[32,6144]{1,0:T(8,128)(2,1)S(1)}, bf16[32,6144]{1,0:T(8,128)(2,1)S(1)}, u32[]{:S(2)}, u32[]{:S(2)}) collective-permute-start(bf16[32,6144]{1,0:T(8,128)(2,1)S(1)} %pack.3.after.args_1_), channel_id=1, source_target_pairs={{0,64},{8,24},{16,80},{24,8},{32,96},{40,56},{48,112},{56,40},{64,... | collective-permute-start | bytes 1179656 | tf_op jit(solution)/shard_map/gather_tnear/ppermute | solution.py:47
  20.9 10.0 %collective-permute-start.7 = (bf16[32,6144]{1,0:T(8,128)(2,1)S(1)}, bf16[32,6144]{1,0:T(8,128)(2,1)S(1)}, u32[]{:S(2)}, u32[]{:S(2)}) collective-permute-start(bf16[32,6144]{1,0:T(8,128)(2,1)S(1)} %hand.2.args_2_), channel_id=1, source_target_pairs={{0,192},{8,56},{16,208},{24,40},{32,224},{40,24},{48,240},{56,8},{... | collective-permute-start | bytes 1179656 | tf_op jit(solution)/shard_map/gather2_twrap/ppermute | solution.py:47
  26.7 7.8 %collective-permute-start.8 = (bf16[32,6144]{1,0:T(8,128)(2,1)S(1)}, bf16[32,6144]{1,0:T(8,128)(2,1)S(1)}, u32[]{:S(2)}, u32[]{:S(2)}) collective-permute-start(bf16[32,6144]{1,0:T(8,128)(2,1)S(1)} %collective-permute-done.6.args_5_), channel_id=1, source_target_pairs={{0,64},{8,24},{16,80},{24,8},{32,96},{40,56},{48,112},{56,40},{64,... | collective-permute-start | bytes 1179656 | tf_op jit(solution)/shard_map/gather2_tnear/ppermute | solution.py:47
  27.1 10.5 %collective-permute-start.10 = (bf16[448,6144]{1,0:T(8,128)(2,1)S(1)}, bf16[448,6144]{1,0:T(8,128)(2,1)S(1)}, u32[]{:S(2)}, u32[]{:S(2)}) collective-permute-start(bf16[448,6144]{1,0:T(8,128)(2,1)S(1)} %hand.3.one), channel_id=1, source_target_pairs={{0,8},{8,0},{16,24},{24,16},{32,40},{40,32},{48,56},{56,48},{64,72... | collective-permute-start | bytes 16515080 | tf_op jit(solution)/shard_map/down_core/ppermute | solution.py:47
  39.7 7.9 %collective-permute-start.13 = (bf16[32,6144]{1,0:T(8,128)(2,1)S(1)}, bf16[32,6144]{1,0:T(8,128)(2,1)S(1)}, u32[]{:S(2)}, u32[]{:S(2)}) collective-permute-start(bf16[32,6144]{1,0:T(8,128)(2,1)S(1)} %get-tuple-element.28), channel_id=1, source_target_pairs={{0,16},{8,72},{16,0},{24,88},{32,48},{40,104},{48,32},{56,120},{64... | collective-permute-start | bytes 1179656 | tf_op jit(solution)/shard_map/reduce2_snear/ppermute | solution.py:47
  39.8 9.3 %collective-permute-start.12 = (bf16[32,6144]{1,0:T(8,128)(2,1)S(1)}, bf16[32,6144]{1,0:T(8,128)(2,1)S(1)}, u32[]{:S(2)}, u32[]{:S(2)}) collective-permute-start(bf16[32,6144]{1,0:T(8,128)(2,1)S(1)} %get-tuple-element.26), channel_id=1, source_target_pairs={{0,48},{8,200},{16,32},{24,216},{32,16},{40,232},{48,0},{56,248},{... | collective-permute-start | bytes 1179656 | tf_op jit(solution)/shard_map/reduce2_swrap/ppermute | solution.py:47
  43.0 10.2 %collective-permute-start.11 = (bf16[32,6144]{1,0:T(8,128)(2,1)S(1)}, bf16[32,6144]{1,0:T(8,128)(2,1)S(1)}, u32[]{:S(2)}, u32[]{:S(2)}) collective-permute-start(bf16[32,6144]{1,0:T(8,128)(2,1)S(1)} %get-tuple-element.24), channel_id=1, source_target_pairs={{0,48},{8,200},{16,32},{24,216},{32,16},{40,232},{48,0},{56,248},{... | collective-permute-start | bytes 1179656 | tf_op jit(solution)/shard_map/reduce_swrap/ppermute | solution.py:47
  46.0 7.8 %collective-permute-start.15 = (bf16[32,6144]{1,0:T(8,128)(2,1)S(1)}, bf16[32,6144]{1,0:T(8,128)(2,1)S(1)}, u32[]{:S(2)}, u32[]{:S(2)}) collective-permute-start(bf16[32,6144]{1,0:T(8,128)(2,1)S(1)} %get-tuple-element.30), channel_id=1, source_target_pairs={{0,16},{8,72},{16,0},{24,88},{32,48},{40,104},{48,32},{56,120},{64... | collective-permute-start | bytes 1179656 | tf_op jit(solution)/shard_map/reduce_snear/ppermute | solution.py:47
  47.6 9.8 %collective-permute-start.16 = (bf16[32,6144]{1,0:T(8,128)(2,1)S(1)}, bf16[32,6144]{1,0:T(8,128)(2,1)S(1)}, u32[]{:S(2)}, u32[]{:S(2)}) collective-permute-start(bf16[32,6144]{1,0:T(8,128)(2,1)S(1)} %merge.2.refs_0_), channel_id=1, source_target_pairs={{0,48},{8,200},{16,32},{24,216},{32,16},{40,232},{48,0},{56,248},{... | collective-permute-start | bytes 1179656 | tf_op jit(solution)/shard_map/reduce_swrap/ppermute | solution.py:47
  49.1 11.7 %collective-permute-start.14 = (bf16[32,6144]{1,0:T(8,128)(2,1)S(1)}, bf16[32,6144]{1,0:T(8,128)(2,1)S(1)}, u32[]{:S(2)}, u32[]{:S(2)}) collective-permute-start(bf16[32,6144]{1,0:T(8,128)(2,1)S(1)} %merge.3), channel_id=1, source_target_pairs={{0,16},{8,72},{16,0},{24,88},{32,48},{40,104},{48,32},{56,120},{64... | collective-permute-start | bytes 1179656 | tf_op jit(solution)/shard_map/reduce_snear/ppermute | solution.py:47
  57.6 7.3 %collective-permute-start.17 = (bf16[16,6144]{1,0:T(8,128)(2,1)S(1)}, bf16[16,6144]{1,0:T(8,128)(2,1)S(1)}, u32[]{:S(2)}, u32[]{:S(2)}) collective-permute-start(bf16[16,6144]{1,0:T(8,128)(2,1)S(1)} %get-tuple-element.33), channel_id=1, source_target_pairs={{0,128},{8,40},{16,144},{24,56},{32,160},{40,8},{48,176},{56,24},{... | collective-permute-start | bytes 589832 | tf_op jit(solution)/shard_map/home_tfar/ppermute | solution.py:47
  60.3 6.9 %collective-permute-start.18 = (bf16[16,6144]{1,0:T(8,128)(2,1)S(1)}, bf16[16,6144]{1,0:T(8,128)(2,1)S(1)}, u32[]{:S(2)}, u32[]{:S(2)}) collective-permute-start(bf16[16,6144]{1,0:T(8,128)(2,1)S(1)} %get-tuple-element.31.refs_0_), channel_id=1, source_target_pairs={{0,192},{8,56},{16,208},{24,40},{32,224},{40,24},{48,240},{56,8},{... | collective-permute-start | bytes 589832 | tf_op jit(solution)/shard_map/home_twrap/ppermute | solution.py:47
  61.0 6.4 %collective-permute-start.19 = (bf16[16,6144]{1,0:T(8,128)(2,1)S(1)}, bf16[16,6144]{1,0:T(8,128)(2,1)S(1)}, u32[]{:S(2)}, u32[]{:S(2)}) collective-permute-start(bf16[16,6144]{1,0:T(8,128)(2,1)S(1)} %get-tuple-element.34), channel_id=1, source_target_pairs={{0,64},{8,24},{16,80},{24,8},{32,96},{40,56},{48,112},{56,40},{64,... | collective-permute-start | bytes 589832 | tf_op jit(solution)/shard_map/home_tnear/ppermute | solution.py:47
